TPU v7x, 32 devices: a whole 2x2x4 slice. The times are simulated.
32 devices in a mesh: dp: 8 (over z, core), space: 4 (over y, x).
Axes of the slice: x: 2, y: 2, z: 4, core: 2. Of those that a mesh axis runs over, the one named last changes fastest.
Arguments:
- volume: bfloat16 [8, 16, 32, 32, 128], P('dp', 'space'), may hold values from -6 to 6
- kernel: bfloat16 [3, 3, 3, 128, 256], replicated, may hold values from -0.109375 to 0.109375
- cotangent: bfloat16 [8, 8, 16, 16, 256], P('dp', 'space'), may hold values from -6 to 6
Outputs:
- switched: bfloat16 [8, 256, 2048], P('dp', 'space')
- volume_grad: bfloat16 [8, 16, 32, 32, 128], P('dp', 'space')
- kernel_grad: float32 [3, 3, 3, 128, 256], P(None, None, None, 'dp')
All inputs are finite; a program needn't handle non-finite values.
Results may differ from a plain program's by a relative error of at most 0.0049.
Values may be sent and summed in bfloat16 or wider, within the bound.
No kernel may reach another device: no remote copies, remote signals or barrier semaphores. Data moves between devices by JAX's collectives and lax.ppermute only.
A program may use at most 64 MiB of HBM per device.

v0:
```python
import math

import jax
import jax.numpy as jnp
from jax import lax
from jax.sharding import PartitionSpec as P


def from_behind(value, axis, steps):
    count = lax.axis_size(axis)
    first, last = (max(0, -steps), min(count, count - steps))
    return lax.ppermute(value, axis, [(source, source + steps) for source in range(first, last)])


def body(volume, kernel, cotangent):
    below = from_behind(volume[:, -1:], "space", 1)
    extended = jnp.concatenate([below, volume], axis=1)
    preact = lax.conv_general_dilated(
        extended,
        kernel,
        (2, 2, 2),
        ((0, 0), (1, 1), (1, 1)),
        dimension_numbers=("NDHWC", "DHWIO", "NDHWC"),
        preferred_element_type=jnp.float32,
    )
    sigmoid_z = jax.nn.sigmoid(preact)
    activated = (preact * sigmoid_z).astype(jnp.bfloat16)
    slope = sigmoid_z * (1.0 + preact * (1.0 - sigmoid_z))
    grad_pre = (cotangent.astype(jnp.float32) * slope).astype(jnp.bfloat16)
    samples, planes, rows, cols, chans = activated.shape
    channel_major = jnp.transpose(activated, (0, 4, 1, 2, 3)).reshape(
        samples, chans, planes * rows * cols
    )
    switched = lax.all_to_all(channel_major, "space", split_axis=1, concat_axis=2, tiled=True)
    flipped = kernel[::-1, ::-1, ::-1]
    above = from_behind(grad_pre[:, :1], "space", -1)
    grad_ext = jnp.concatenate([grad_pre, above], axis=1)
    data_grad = lax.conv_general_dilated(
        grad_ext,
        flipped,
        (1, 1, 1),
        ((1, 0), (1, 2), (1, 2)),
        lhs_dilation=(2, 2, 2),
        dimension_numbers=("NDHWC", "DHWOI", "NDHWC"),
        preferred_element_type=jnp.float32,
    )
    volume_grad = data_grad.astype(jnp.bfloat16)
    kernel_part = lax.conv_general_dilated(
        extended,
        grad_pre,
        (1, 1, 1),
        ((0, 0), (1, 0), (1, 0)),
        rhs_dilation=(2, 2, 2),
        dimension_numbers=("CDHWN", "IDHWO", "DHWNC"),
        preferred_element_type=jnp.float32,
    )
    count = lax.axis_size("dp") * lax.axis_size("space") * planes * rows * cols
    kernel_part = kernel_part * (1.0 / math.sqrt(count))
    summed = lax.psum(kernel_part, "space")
    kernel_grad = lax.psum_scatter(summed, "dp", scatter_dimension=3, tiled=True)
    return (switched, volume_grad, kernel_grad)


def solution(mesh):
    in_specs = (P("dp", "space", None, None, None), P(), P("dp", "space", None, None, None))
    out_specs = (
        P("dp", "space", None),
        P("dp", "space", None, None, None),
        P(None, None, None, "dp", None),
    )
    return jax.shard_map(body, mesh=mesh, in_specs=in_specs, out_specs=out_specs, check_vma=False)
```

profile of v0, /device:TPU:0, one launch (start us, length us, event | category | flops | bytes accessed | tf_op | source)
XLA Modules:
  0.0 144.4 jit_solution(10874244779314807320)
XLA Ops:
  7.2 1.1 slice.13
  8.4 0.6 copy.64
  8.9 4.9 %collective-permute-start = (bf16[1,1,32,32,128]{4,0,3,2,1:T(2,128)(2,1)S(1)}, bf16[1,1,32,32,128]{4,0,3,2,1:T(2,128)(2,1)S(1)}, u32[]{:S(2)}, u32[]{:S(2)}) collective-permute-start(bf16[1,1,32,32,128]{4,0,3,2,1:T(2,128)(2,1)S(1)} %copy.64), channel_id=1, source_target_pairs={{0,1},{1,2},{2,3},{4,5},{5,6},{6,7},{8,9},{9,10},{10,11},{12,13},{... | collective-permute-start | bytes 786440 | tf_op jit(solution)/shard_map/ppermute | solution.py:12
  13.8 11.1 %collective-permute-done = bf16[1,1,32,32,128]{4,0,3,2,1:T(2,128)(2,1)S(1)} collective-permute-done((bf16[1,1,32,32,128]{4,0,3,2,1:T(2,128)(2,1)S(1)}, bf16[1,1,32,32,128]{4,0,3,2,1:T(2,128)(2,1)S(1)}, u32[]{:S(2)}, u32[]{:S(2)}) %collective-permute-start) | collective-permute-done | bytes 262176 | tf_op jit(solution)/shard_map/ppermute | solution.py:12
  25.0 0.5 constant_dynamic-update-slice_fusion.1
  25.5 2.6 %constant_dynamic-update-slice_fusion = bf16[1,5,32,32,128]{4,0,3,2,1:T(2,128)(2,1)S(1)} fusion(bf16[1,5,32,32,128]{4,0,3,2,1:T(2,128)(2,1)S(1)} %constant_dynamic-update-slice_fusion.1, bf16[1,4,32,32,128]{4,3,2,1,0:T(8,128)(2,1)S(1)} %copy-done.1), kind=kLoop, calls=%fused_computation.31 | loop fusion | bytes 3145728 | tf_op jit(solution)/shard_map/concatenate | solution.py:17
  28.1 1.5 %copy.65 = bf16[1,5,32,32,128]{4,2,3,1,0:T(8,128)(2,1)S(1)} copy(bf16[1,5,32,32,128]{4,0,3,2,1:T(2,128)(2,1)S(1)} %constant_dynamic-update-slice_fusion) | data formatting | bytes 2621440
  29.6 0.4 pad.clone
  30.0 1.3 copy.42
  31.3 0.2 slice.14
  31.5 2.5 %add_multiply_fusion = (f32[2,16,8,3,256]{4,2,3,1,0:T(8,128)S(1)}, bf16[2,16,8,3,256]{4,2,3,1,0:T(8,128)(2,1)}) fusion(bf16[3,3,3,128,256]{4,3,2,1,0:T(8,128)(2,1)S(1)} %copy-done, bf16[5,32,1,7,2,128]{5,3,4,1,0,2:T(8,128)(2,1)S(1)} %slice.14, bf16[5,32,1,8,6,128]{5,3,4,1,0,2:T(8,128)(2,1)S(1)} %copy.42, pred[8,3]{0,1:T(4,128)(4,1)S(1)} %copy-done.5), kind=kOutput, calls=%fused_computation.21 | convolution fusion | flops 1340473344 | bytes 5488664 | tf_op jit(solution)/shard_map/conv_general_dilated | solution.py:18
  34.0 0.2 copy.48
  34.3 0.2 fusion.20
  34.4 8.7 %convolution_multiply_fusion = f32[3,3,3,128,256]{4,3,2,1,0:T(8,128)} fusion(bf16[1,5,32,32,128]{4,0,3,2,1:T(2,128)(2,1)S(1)} %constant_dynamic-update-slice_fusion, bf16[1,2,16,16,256]{4,2,3,1,0:T(8,128)(2,1)S(1)} %fusion.20), kind=kOutput, calls=%fused_computation.9 | convolution fusion | flops 869498880 | bytes 5111808 | tf_op jit(solution)/shard_map/conv_general_dilated | solution.py:48
  43.1 1.4 collective-permute-start.1
  44.6 0.1 copy.43
  44.7 0.1 copy.44
  44.8 0.5 copy.45
  45.3 0.5 broadcast.56
  45.8 2.2 %reduce = bf16[256,512]{1,0:T(8,128)(2,1)S(1)} reduce(bf16[256,1,512]{2,1,0:T(2,128)(2,1)S(1)} %bitcast.53, bf16[]{:T(256)} %broadcast.56), dimensions={1}, to_apply=%bitcast.34.reduce_sub_computation | reduce | bytes 524290
  48.0 0.9 reshape.37
  48.9 6.8 %all-to-all-start = ((bf16[4,2,16384]{2,1,0:T(2,128)(2,1)}), bf16[4,2,16384]{2,1,0:T(2,128)(2,1)S(1)}, u32[]{:S(2)}, u32[]{:S(2)}) async-start(bf16[4,2,16384]{2,1,0:T(2,128)(2,1)} %reshape.37), calls=%async_computation | async-start | bytes 524288 | tf_op jit(solution)/shard_map/all_to_all | solution.py:34
  55.7 0.2 copy.50
  56.0 0.1 fusion.35
  56.1 33.3 %reduce-scatter.2.cloned.1.call-done = f32[3,3,3,16,256]{4,3,2,1,0:T(8,128)} async-done(((f32[3,3,3,128,256]{4,3,2,1,0:T(8,128)}), f32[3,3,3,16,256]{4,3,2,1,0:T(8,128)}) %reduce-scatter.2.cloned.1.call-update) | async-done | bytes 442384 | tf_op jit(solution)/shard_map/reduce_scatter | solution.py:60
  89.4 2.9 %select_convert_fusion = bf16[4,32,8,6,128]{4,2,3,1,0:T(8,128)(2,1)S(1)} fusion(bf16[3,3,3,128,256]{4,3,2,1,0:T(8,128)(2,1)S(1)} %copy-done, pred[8,6]{0,1:T(8,128)(4,1)S(1)} %copy-done.3, bf16[3,16,8,4,256]{4,2,3,1,0:T(8,128)(2,1)S(1)} %fusion.35), kind=kOutput, calls=%fused_computation.2 | convolution fusion | flops 1332215808 | bytes 4128816 | tf_op jit(solution)/shard_map/conv_general_dilated | solution.py:38
  92.3 0.4 copy.51
  92.8 1.4 copy.53
  94.2 0.3 reshape.38
  94.5 0.7 copy.58
  95.2 40.5 %all-reduce.2.cloned.1.call-done = f32[3,3,3,16,256]{4,3,2,1,0:T(8,128)} async-done(((f32[3,3,3,16,256]{4,3,2,1,0:T(8,128)}), f32[3,3,3,16,256]{4,3,2,1,0:T(8,128)}) %all-reduce.2.cloned.1.call-update) | async-done | bytes 442384 | tf_op jit(solution)/shard_map/psum | solution.py:59
  135.8 1.8 %copy.68 = f32[3,3,3,16,256]{4,3,2,1,0:T(8,128)} copy(f32[3,3,3,16,256]{4,3,2,1,0:T(8,128)} %all-reduce.2.cloned.1.call-done) | data formatting | bytes 884736
  (25 shorter events, 0.4 us)
Async XLA Ops:
  7.2 24.3 %copy-start = (bf16[3,3,3,128,256]{4,3,2,1,0:T(8,128)(2,1)S(1)}, bf16[3,3,3,128,256]{4,3,2,1,0:T(8,128)(2,1)}, u32[]{:S(2)}) copy-start(bf16[3,3,3,128,256]{4,3,2,1,0:T(8,128)(2,1)} %param.4) | copy-start | bytes 5308420
  7.2 18.3 %copy-start.1 = (bf16[1,4,32,32,128]{4,3,2,1,0:T(8,128)(2,1)S(1)}, bf16[1,4,32,32,128]{4,3,2,1,0:T(8,128)(2,1)}, u32[]{:S(2)}) copy-start(bf16[1,4,32,32,128]{4,3,2,1,0:T(8,128)(2,1)} %param.3) | copy-start | bytes 3145732
  7.2 82.2 %reduce-scatter.2.cloned.1.call-start = ((), (), s32[]{:S(2)}) async-start(), calls=%async_computation.2 | async-start | bytes 3981312 | tf_op jit(solution)/shard_map/reduce_scatter | solution.py:60
  8.9 16.0 %collective-permute-start = (bf16[1,1,32,32,128]{4,0,3,2,1:T(2,128)(2,1)S(1)}, bf16[1,1,32,32,128]{4,0,3,2,1:T(2,128)(2,1)S(1)}, u32[]{:S(2)}, u32[]{:S(2)}) collective-permute-start(bf16[1,1,32,32,128]{4,0,3,2,1:T(2,128)(2,1)S(1)} %copy.64), channel_id=1, source_target_pairs={{0,1},{1,2},{2,3},{4,5},{5,6},{6,7},{8,9},{9,10},{10,11},{12,13},{... | collective-permute-start | bytes 786440 | tf_op jit(solution)/shard_map/ppermute | solution.py:12
  30.0 1.5 %copy-start.5 = (pred[8,3]{0,1:T(4,128)(4,1)S(1)}, pred[8,3]{0,1:T(4,128)(4,1)}, u32[]{:S(2)}) copy-start(pred[8,3]{0,1:T(4,128)(4,1)} %constant.14) | copy-start | bytes 76
  31.5 2.7 %copy-start.4 = (bf16[1,2,16,16,256]{4,3,2,1,0:T(8,128)(2,1)S(1)}, bf16[1,2,16,16,256]{4,3,2,1,0:T(8,128)(2,1)}, u32[]{:S(2)}) copy-start(bf16[1,2,16,16,256]{4,3,2,1,0:T(8,128)(2,1)} %param.5) | copy-start | bytes 786436
  43.1 1.5 %copy-start.2 = (bf16[2,16,8,3,256]{4,2,3,1,0:T(8,128)(2,1)S(1)}, bf16[2,16,8,3,256]{4,2,3,1,0:T(8,128)(2,1)}, u32[]{:S(2)}) copy-start(bf16[2,16,8,3,256]{4,2,3,1,0:T(8,128)(2,1)} %get-tuple-element.13) | copy-start | bytes 1179652
  43.1 12.5 %collective-permute-start.1 = (bf16[1,1,16,16,256]{4,2,3,1,0:T(8,128)(2,1)S(1)}, bf16[1,1,16,16,256]{4,2,3,1,0:T(8,128)(2,1)S(1)}, u32[]{:S(2)}, u32[]{:S(2)}) collective-permute-start(bf16[1,1,16,16,256]{4,2,3,1,0:T(8,128)(2,1)S(1)} %slice.17), channel_id=1, source_target_pairs={{1,0},{2,1},{3,2},{5,4},{6,5},{7,6},{9,8},{10,9},{11,10},{13,12},{... | collective-permute-start | bytes 393224 | tf_op jit(solution)/shard_map/ppermute | solution.py:12
  48.9 45.3 %all-to-all-start = ((bf16[4,2,16384]{2,1,0:T(2,128)(2,1)}), bf16[4,2,16384]{2,1,0:T(2,128)(2,1)S(1)}, u32[]{:S(2)}, u32[]{:S(2)}) async-start(bf16[4,2,16384]{2,1,0:T(2,128)(2,1)} %reshape.37), calls=%async_computation | async-start | bytes 524288 | tf_op jit(solution)/shard_map/all_to_all | solution.py:34
  55.6 33.7 %copy-start.3 = (pred[8,6]{0,1:T(8,128)(4,1)S(1)}, pred[8,6]{0,1:T(8,128)(4,1)}, u32[]{:S(2)}) copy-start(pred[8,6]{0,1:T(8,128)(4,1)} %constant.15) | copy-start | bytes 148
  55.6 80.1 %all-reduce.2.cloned.1.call-start = ((), (), s32[]{:S(2)}) async-start(), calls=%async_computation.3 | async-start | bytes 884736 | tf_op jit(solution)/shard_map/psum | solution.py:59
Sparse Core Ops, SparseCore 0:
  43.3 46.0 reduce-scatter.1
  92.6 43.0 all-reduce.1
where the time goes:
time: 145 us; the launch traced here: 144 us
  waiting for transfers between devices  85 us (59%)
  local copies, waits for them, and re-layouts  15.5 us (11%)
  between operations  14.3 us (10%)
  matrix products  14.1 us (10%)
  starting transfers between devices  13.1 us (9%)
  other arithmetic  2.48 us (2%)
    psum x1, waiting for transfers between devices, body(): summed = lax.psum(kernel_part, 'space')  40.5 us
    reduce_scatter x1, waiting for transfers between devices, body(): lax.psum_scatter(summed, 'dp', scatter_dimension=3, tiled=True)  33.3 us
    ppermute x2, waiting for transfers between devices, from_behind(): lax.ppermute(value, axis, [(source, source + steps) for source in range(f...  11.1 us
    conv_general_dilated x1, matrix products, body(): lax.conv_general_dilated(extended, grad_pre, (1, 1, 1), ((0, 0), (1, 0),...  8.67 us
    unnamed x21, local copies, waits for them, and re-layouts  7.54 us
    all_to_all x1, starting transfers between devices, body(): lax.all_to_all(channel_major, 'space', split_axis=1, concat_axis=2, tiled...  6.76 us
    ppermute x2, starting transfers between devices, from_behind(): lax.ppermute(value, axis, [(source, source + steps) for source in range(f...  6.3 us
    concatenate x2, local copies, waits for them, and re-layouts, body(): extended = jnp.concatenate([below, volume], axis=1)  2.97 us
  transfers between devices with their start and end apart: 5, of which 3 were waited for; matrix products, arithmetic and copies ran while one was open for 7% of the time, Pallas kernels for 0%

commit v1 on v0

--- a/solution.py
+++ b/solution.py
@@ -5,11 +5,48 @@
 from jax import lax
 from jax.sharding import PartitionSpec as P
 
+BF16 = jnp.bfloat16
+F32 = jnp.float32
+
 
 def from_behind(value, axis, steps):
     count = lax.axis_size(axis)
     first, last = (max(0, -steps), min(count, count - steps))
     return lax.ppermute(value, axis, [(source, source + steps) for source in range(first, last)])
+
+
+def reduce_kernel_grad(part):
+    taps, chans_in, chans_out = part.shape
+    dp, space = lax.axis_size("dp"), lax.axis_size("space")
+    cores = 2 if dp % 2 == 0 else 1
+    chips = dp // cores
+    padded = -(-taps // space) * space
+    block = chans_in // dp
+    share = padded // space
+    part = jnp.pad(part, ((0, padded - taps), (0, 0), (0, 0)))
+    pieces = part.reshape(space, share, chips, cores, block, chans_out)
+    pieces = pieces.transpose(3, 0, 2, 1, 4, 5)
+    if cores == 2:
+        core = lax.axis_index("dp") % 2
+        mine = lax.dynamic_index_in_dim(pieces, core, 0, keepdims=False)
+        other = lax.dynamic_index_in_dim(pieces, 1 - core, 0, keepdims=False).astype(BF16)
+        got = lax.ppermute(other, "dp", [(i, i ^ 1) for i in range(dp)])
+        total = mine + got.astype(F32)
+    else:
+        total = pieces[0]
+    rows = share * block
+    total = total.reshape(space, chips * rows, chans_out).astype(BF16)
+    got = lax.all_to_all(total, "space", 0, 0, tiled=True)
+    total = jnp.sum(got.astype(F32), axis=0).astype(BF16)
+    if chips > 1:
+        groups = [[chip * cores + core for chip in range(chips)] for core in range(cores)]
+        got = lax.all_to_all(
+            total.reshape(chips, rows, chans_out), "dp", 0, 0, axis_index_groups=groups, tiled=True
+        )
+        total = jnp.sum(got.astype(F32), axis=0).astype(BF16)
+    spread = jnp.broadcast_to(total.reshape(1, rows, chans_out), (space, rows, chans_out))
+    full = lax.all_to_all(spread, "space", 0, 0, tiled=True)
+    return full.reshape(padded, block, chans_out)[:taps].astype(F32)
 
 
 def body(volume, kernel, cotangent):
@@ -56,9 +93,9 @@
     )
     count = lax.axis_size("dp") * lax.axis_size("space") * planes * rows * cols
     kernel_part = kernel_part * (1.0 / math.sqrt(count))
-    summed = lax.psum(kernel_part, "space")
-    kernel_grad = lax.psum_scatter(summed, "dp", scatter_dimension=3, tiled=True)
-    return (switched, volume_grad, kernel_grad)
+    kd, kh, kw, ci, co = kernel_part.shape
+    kernel_grad = reduce_kernel_grad(kernel_part.reshape(kd * kh * kw, ci, co))
+    return (switched, volume_grad, kernel_grad.reshape(kd, kh, kw, -1, co))
 
 
 def solution(mesh):

time: 145 us -> 98.3 us (0.68)
  waiting for transfers between devices: 85 us -> 29.6 us
  between operations: 14.3 us -> 0.96 us
  starting transfers between devices: 13.1 us -> 24.8 us
  local copies, waits for them, and re-layouts: 15.5 us -> 21.7 us
  other arithmetic: 2.48 us -> 8.17 us
  matrix products: 14.1 us -> 12.5 us
    psum x1 -> x0, waiting for transfers between devices: 40.5 us -> none  [body(): summed = lax.psum(kernel_part, 'space')]
    reduce_scatter x1 -> x0, waiting for transfers between devices: 33.3 us -> none  [body(): lax.psum_scatter(summed, 'dp', scatter_dimension=3, tiled=True)]
    all_to_all x0 -> x3, waiting for transfers between devices: none -> 15.5 us  [the longest x1 11.2 us: reduce_kernel_grad(): got = lax.all_to_all(total, 'space', 0, 0, tiled=True)]
    all_to_all x0 -> x3, starting transfers between devices: none -> 13.7 us  [the longest x1 4.87 us: reduce_kernel_grad(): lax.all_to_all(total.reshape(chips, rows, chans_out), 'dp', 0, 0, axis_in...]
    all_to_all x1, starting transfers between devices: 6.76 us -> 4.04 us  [body(): lax.all_to_all(channel_major, 'space', split_axis=1, concat_axis=2, tiled...]
    ppermute x0 -> x1, waiting for transfers between devices: none -> 2.58 us  [reduce_kernel_grad(): got = lax.ppermute(other, 'dp', [(i, i ^ 1) for i in range(dp)])]
    convert_element_type x0 -> x1, other arithmetic: none -> 2.12 us  [reduce_kernel_grad(): total = total.reshape(space, chips * rows, chans_out).astype(BF16)]
    unnamed x21 -> x20, local copies, waits for them, and re-layouts: 7.54 us -> 9.48 us
  transfers between devices with their start and end apart: 5 -> 7, of which waited for: 3 -> 6; matrix products, arithmetic and copies ran while one was open for 7% -> 15% of each run, Pallas kernels for 0% -> 0%
where the time goes in v1:
time: 98.3 us; the launch traced here: 97.6 us
  waiting for transfers between devices  29.6 us (30%)
  starting transfers between devices  24.8 us (25%)
  local copies, waits for them, and re-layouts  21.7 us (22%)
  matrix products  12.5 us (13%)
  other arithmetic  8.17 us (8%)
    all_to_all x1, waiting for transfers between devices, reduce_kernel_grad(): got = lax.all_to_all(total, 'space', 0, 0, tiled=True)  11.2 us
    ppermute x2, waiting for transfers between devices, from_behind(): lax.ppermute(value, axis, [(source, source + steps) for source in range(f...  10.4 us
    unnamed x20, local copies, waits for them, and re-layouts  9.48 us
    conv_general_dilated x1, matrix products, body(): lax.conv_general_dilated(extended, grad_pre, (1, 1, 1), ((0, 0), (1, 0),...  7.06 us
    ppermute x2, starting transfers between devices, from_behind(): lax.ppermute(value, axis, [(source, source + steps) for source in range(f...  6.94 us
    all_to_all x1, starting transfers between devices, reduce_kernel_grad(): lax.all_to_all(total.reshape(chips, rows, chans_out), 'dp', 0, 0, axis_in...  4.87 us
    all_to_all x1, starting transfers between devices, reduce_kernel_grad(): got = lax.all_to_all(total, 'space', 0, 0, tiled=True)  4.82 us
    all_to_all x1, starting transfers between devices, body(): lax.all_to_all(channel_major, 'space', split_axis=1, concat_axis=2, tiled...  4.04 us
  transfers between devices with their start and end apart: 7, of which 6 were waited for; matrix products, arithmetic and copies ran while one was open for 15% of the time, Pallas kernels for 0%

profile of v1, /device:TPU:0, one launch (start us, length us, event | category | flops | bytes accessed | tf_op | source)
XLA Modules:
  0.0 97.6 jit_solution(3160207283375353230)
XLA Ops:
  0.7 1.1 %slice.17 = bf16[1,1,32,32,128]{4,3,2,1,0:T(8,128)(2,1)S(1)} slice(bf16[1,4,32,32,128]{4,3,2,1,0:T(8,128)(2,1)} %param.3), slice={[0:1], [3:4], [0:32], [0:32], [0:128]} | slice | bytes 524288 | tf_op jit(solution)/shard_map/slice | solution.py:53
  2.3 5.7 %collective-permute-start = (bf16[1,1,32,32,128]{4,0,3,2,1:T(2,128)(2,1)S(1)}, bf16[1,1,32,32,128]{4,0,3,2,1:T(2,128)(2,1)}, u32[]{:S(2)}, u32[]{:S(2)}) collective-permute-start(bf16[1,1,32,32,128]{4,0,3,2,1:T(2,128)(2,1)S(1)} %copy.88), channel_id=1, source_target_pairs={{0,1},{1,2},{2,3},{4,5},{5,6},{6,7},{8,9},{9,10},{10,11},{12,13},{... | collective-permute-start | bytes 786440 | tf_op jit(solution)/shard_map/ppermute | solution.py:15
  8.0 10.4 %collective-permute-done = bf16[1,1,32,32,128]{4,0,3,2,1:T(2,128)(2,1)} collective-permute-done((bf16[1,1,32,32,128]{4,0,3,2,1:T(2,128)(2,1)S(1)}, bf16[1,1,32,32,128]{4,0,3,2,1:T(2,128)(2,1)}, u32[]{:S(2)}, u32[]{:S(2)}) %collective-permute-start) | collective-permute-done | bytes 262176 | tf_op jit(solution)/shard_map/ppermute | solution.py:15
  18.4 1.6 %constant_dynamic-update-slice_fusion.1 = bf16[1,5,32,32,128]{4,0,3,2,1:T(2,128)(2,1)S(1)} fusion(bf16[1,1,32,32,128]{4,0,3,2,1:T(2,128)(2,1)} %collective-permute-done), kind=kLoop, calls=%fused_computation.36 | loop fusion | bytes 786432
  20.0 2.6 %constant_dynamic-update-slice_fusion = bf16[1,5,32,32,128]{4,0,3,2,1:T(2,128)(2,1)S(1)} fusion(bf16[1,5,32,32,128]{4,0,3,2,1:T(2,128)(2,1)S(1)} %constant_dynamic-update-slice_fusion.1, bf16[1,4,32,32,128]{4,3,2,1,0:T(8,128)(2,1)S(1)} %copy-done.2), kind=kLoop, calls=%fused_computation.35 | loop fusion | bytes 3145728 | tf_op jit(solution)/shard_map/concatenate | solution.py:54
  22.6 1.5 %copy.89 = bf16[1,5,32,32,128]{4,2,3,1,0:T(8,128)(2,1)S(1)} copy(bf16[1,5,32,32,128]{4,0,3,2,1:T(2,128)(2,1)S(1)} %constant_dynamic-update-slice_fusion) | data formatting | bytes 2621440
  24.5 1.3 %copy.63 = bf16[5,32,1,8,6,128]{5,3,4,1,0,2:T(8,128)(2,1)S(1)} copy(bf16[5,32,1,8,6,128]{5,1,4,3,0,2:T(8,128)(2,1)S(1)} %bitcast.68) | data formatting | bytes 3932160 | tf_op jit(solution)/shard_map/conv_general_dilated | solution.py:55
  26.0 2.5 %add_multiply_fusion = (f32[2,16,8,3,256]{4,2,3,1,0:T(8,128)S(1)}, bf16[2,16,8,3,256]{4,2,3,1,0:T(8,128)(2,1)}) fusion(bf16[3,3,3,128,256]{4,3,2,1,0:T(8,128)(2,1)S(1)} %copy-done, bf16[5,32,1,7,2,128]{5,3,4,1,0,2:T(8,128)(2,1)S(1)} %slice.18, bf16[5,32,1,8,6,128]{5,3,4,1,0,2:T(8,128)(2,1)S(1)} %copy.63, pred[8,3]{0,1:T(4,128)(4,1)S(1)} %copy-done.5), kind=kOutput, calls=%fused_computation.25 | convolution fusion | flops 1340473344 | bytes 5488664 | tf_op jit(solution)/shard_map/conv_general_dilated | solution.py:55
  28.9 7.1 %convolution_multiply_fusion = f32[3,3,3,128,256]{4,3,2,1,0:T(8,128)S(1)} fusion(bf16[1,5,32,32,128]{4,0,3,2,1:T(2,128)(2,1)S(1)} %constant_dynamic-update-slice_fusion, bf16[1,2,16,16,256]{4,2,3,1,0:T(8,128)(2,1)S(1)} %fusion.22), kind=kOutput, calls=%fused_computation.9 | convolution fusion | flops 869498880 | bytes 5111808 | tf_op jit(solution)/shard_map/conv_general_dilated | solution.py:85
  36.5 1.8 %copy-done.1 = f32[28,128,256]{2,1,0:T(8,128)} copy-done((f32[28,128,256]{2,1,0:T(8,128)}, f32[28,128,256]{2,1,0:T(8,128)S(1)}, u32[]{:S(2)}) %copy-start.1) | copy-done | bytes 3670040
  38.5 2.6 %collective-permute-done.2 = bf16[4,4,7,16,256]{4,3,1,2,0:T(8,128)(2,1)} collective-permute-done((bf16[4,4,7,16,256]{4,3,1,2,0:T(8,128)(2,1)S(1)}, bf16[4,4,7,16,256]{4,3,1,2,0:T(8,128)(2,1)}, u32[]{:S(2)}, u32[]{:S(2)}) %collective-permute-start.2) | collective-permute-done | bytes 917536 | tf_op jit(solution)/shard_map/ppermute | solution.py:33
  41.1 2.1 %fusion.8 = bf16[4,4,7,16,256]{4,3,1,2,0:T(8,128)(2,1)S(1)} fusion(bf16[4,4,7,16,256]{4,3,1,2,0:T(8,128)(2,1)} %collective-permute-done.2, f32[4,7,4,2,16,256]{5,4,3,2,1,0:T(8,128)} %bitcast.67, s32[]{:T(128)S(6)} %select_n.15), kind=kLoop, calls=%fused_computation.11 | loop fusion | flops 1376256 | bytes 3670020 | tf_op jit(solution)/shard_map/convert_element_type | solution.py:38
  43.2 1.0 %copy.75 = bf16[4,4,7,16,256]{4,3,2,1,0:T(8,128)(2,1)} copy(bf16[4,4,7,16,256]{4,3,1,2,0:T(8,128)(2,1)S(1)} %fusion.8) | data formatting | bytes 1835008 | tf_op jit(solution)/shard_map/convert_element_type | solution.py:38
  44.2 4.8 %all-to-all-start.1 = ((bf16[4,448,256]{2,1,0:T(8,128)(2,1)}), bf16[4,448,256]{2,1,0:T(8,128)(2,1)S(1)}, u32[]{:S(2)}, u32[]{:S(2)}) async-start(bf16[4,448,256]{2,1,0:T(8,128)(2,1)} %bitcast.19), calls=%async_computation.1 | async-start | bytes 1835008 | tf_op jit(solution)/shard_map/all_to_all | solution.py:39
  49.0 1.3 %collective-permute-start.1 = (bf16[1,1,16,16,256]{4,2,3,1,0:T(8,128)(2,1)S(1)}, bf16[1,1,16,16,256]{4,2,3,1,0:T(8,128)(2,1)}, u32[]{:S(2)}, u32[]{:S(2)}) collective-permute-start(bf16[1,1,16,16,256]{4,2,3,1,0:T(8,128)(2,1)S(1)} %slice.21), channel_id=1, source_target_pairs={{1,0},{2,1},{3,2},{5,4},{6,5},{7,6},{9,8},{10,9},{11,10},{13,12},{... | collective-permute-start | bytes 393224 | tf_op jit(solution)/shard_map/ppermute | solution.py:15
  50.3 1.1 %copy.64 = bf16[2,16,8,3,256]{4,1,3,2,0:T(8,128)(2,1)S(1)} copy(bf16[2,16,8,3,256]{4,2,3,1,0:T(8,128)(2,1)} %get-tuple-element.16) | data formatting | bytes 786432 | tf_op jit(solution)/shard_map/convert_element_type | solution.py:64
  51.4 11.2 %all-to-all-done.1 = bf16[4,448,256]{2,1,0:T(8,128)(2,1)S(1)} async-done(((bf16[4,448,256]{2,1,0:T(8,128)(2,1)}), bf16[4,448,256]{2,1,0:T(8,128)(2,1)S(1)}, u32[]{:S(2)}, u32[]{:S(2)}) %all-to-all-start.1) | async-done | bytes 917536 | tf_op jit(solution)/shard_map/all_to_all | solution.py:39
  62.6 0.9 reduce_sum.24
  63.5 4.9 %all-to-all-start.2 = ((bf16[4,112,256]{2,1,0:T(8,128)(2,1)}), bf16[4,112,256]{2,1,0:T(8,128)(2,1)}, u32[]{:S(2)}, u32[]{:S(2)}) async-start(bf16[4,112,256]{2,1,0:T(8,128)(2,1)} %bitcast.79), calls=%async_computation.2 | async-start | bytes 458752 | tf_op jit(solution)/shard_map/all_to_all | solution.py:43
  69.5 2.2 %reduce.2 = bf16[256,512]{1,0:T(8,128)(2,1)S(1)} reduce(bf16[256,1,512]{2,1,0:T(2,128)(2,1)S(1)} %bitcast.75, bf16[]{:T(256)} %broadcast.60), dimensions={1}, to_apply=%bitcast.53.reduce_sub_computation | reduce | bytes 524290
  71.7 0.9 reshape.68
  72.6 0.9 maximum_bitcast_fusion
  73.9 2.4 %all-to-all-done.2 = bf16[4,112,256]{2,1,0:T(8,128)(2,1)} async-done(((bf16[4,112,256]{2,1,0:T(8,128)(2,1)}), bf16[4,112,256]{2,1,0:T(8,128)(2,1)}, u32[]{:S(2)}, u32[]{:S(2)}) %all-to-all-start.2) | async-done | bytes 229408 | tf_op jit(solution)/shard_map/all_to_all | solution.py:43
  76.3 4.0 %all-to-all-start = ((bf16[4,2,16384]{2,1,0:T(2,128)(2,1)}), bf16[4,2,16384]{2,1,0:T(2,128)(2,1)}, u32[]{:S(2)}, u32[]{:S(2)}) async-start(bf16[4,2,16384]{2,1,0:T(2,128)(2,1)} %reshape.68), calls=%async_computation | async-start | bytes 524288 | tf_op jit(solution)/shard_map/all_to_all | solution.py:71
  80.3 2.9 %select_convert_fusion = bf16[4,32,8,6,128]{4,2,3,1,0:T(8,128)(2,1)S(1)} fusion(bf16[3,3,3,128,256]{4,3,2,1,0:T(8,128)(2,1)S(1)} %copy-done, pred[8,6]{0,1:T(8,128)(4,1)S(1)} %copy-done.3, bf16[3,16,8,4,256]{4,2,3,1,0:T(8,128)(2,1)S(1)} %fusion.37), kind=kOutput, calls=%fused_computation.2 | convolution fusion | flops 1332215808 | bytes 4128816 | tf_op jit(solution)/shard_map/conv_general_dilated | solution.py:75
  83.7 1.0 %reduce_sum.25 = bf16[112,256]{1,0:T(8,128)(2,1)S(1)} reduce(bf16[4,112,256]{2,1,0:T(8,128)(2,1)} %all-to-all-done.2, bf16[]{:T(256)} %constant.38.clone.1), dimensions={0}, to_apply=%region_1.2 | reduce | flops 86016 | bytes 286722 | tf_op jit(solution)/shard_map/reduce_sum | solution.py:46
  84.6 1.1 %all-to-all-done = bf16[4,2,16384]{2,1,0:T(2,128)(2,1)} async-done(((bf16[4,2,16384]{2,1,0:T(2,128)(2,1)}), bf16[4,2,16384]{2,1,0:T(2,128)(2,1)}, u32[]{:S(2)}, u32[]{:S(2)}) %all-to-all-start) | async-done | bytes 262176 | tf_op jit(solution)/shard_map/all_to_all | solution.py:71
  86.4 4.0 %all-to-all-start.3 = ((bf16[4,112,256]{2,1,0:T(8,128)(2,1)}), bf16[4,112,256]{2,1,0:T(8,128)(2,1)}, u32[]{:S(2)}, u32[]{:S(2)}) async-start(bf16[4,112,256]{2,1,0:T(8,128)(2,1)} %broadcast_in_dim.2), calls=%async_computation.3 | async-start | bytes 458752 | tf_op jit(solution)/shard_map/all_to_all | solution.py:48
  90.6 1.4 %copy.76 = bf16[1,4,32,32,128]{4,3,2,1,0:T(8,128)(2,1)} copy(bf16[1,4,32,32,128]{4,2,3,1,0:T(8,128)(2,1)S(1)} %slice_bitcast_fusion) | data formatting | bytes 2097152
  91.9 1.2 %reshape.69 = bf16[256,1,512]{2,1,0:T(2,128)(2,1)S(1)} reshape(bf16[4,2,16384]{2,1,0:T(2,128)(2,1)} %all-to-all-done) | data formatting | bytes 524288
  93.9 1.9 %all-to-all-done.3 = bf16[4,112,256]{2,1,0:T(8,128)(2,1)} async-done(((bf16[4,112,256]{2,1,0:T(8,128)(2,1)}), bf16[4,112,256]{2,1,0:T(8,128)(2,1)}, u32[]{:S(2)}, u32[]{:S(2)}) %all-to-all-start.3) | async-done | bytes 229408 | tf_op jit(solution)/shard_map/all_to_all | solution.py:48
  95.8 1.0 slice.24
  (35 shorter events, 6.5 us)
Async XLA Ops:
  0.6 25.3 %copy-start = (bf16[3,3,3,128,256]{4,3,2,1,0:T(8,128)(2,1)S(1)}, bf16[3,3,3,128,256]{4,3,2,1,0:T(8,128)(2,1)}, u32[]{:S(2)}) copy-start(bf16[3,3,3,128,256]{4,3,2,1,0:T(8,128)(2,1)} %param.4) | copy-start | bytes 5308420
  0.6 19.3 %copy-start.2 = (bf16[1,4,32,32,128]{4,3,2,1,0:T(8,128)(2,1)S(1)}, bf16[1,4,32,32,128]{4,3,2,1,0:T(8,128)(2,1)}, u32[]{:S(2)}) copy-start(bf16[1,4,32,32,128]{4,3,2,1,0:T(8,128)(2,1)} %param.3) | copy-start | bytes 3145732
  2.3 16.0 %collective-permute-start = (bf16[1,1,32,32,128]{4,0,3,2,1:T(2,128)(2,1)S(1)}, bf16[1,1,32,32,128]{4,0,3,2,1:T(2,128)(2,1)}, u32[]{:S(2)}, u32[]{:S(2)}) collective-permute-start(bf16[1,1,32,32,128]{4,0,3,2,1:T(2,128)(2,1)S(1)} %copy.88), channel_id=1, source_target_pairs={{0,1},{1,2},{2,3},{4,5},{5,6},{6,7},{8,9},{9,10},{10,11},{12,13},{... | collective-permute-start | bytes 786440 | tf_op jit(solution)/shard_map/ppermute | solution.py:15
  24.5 1.5 %copy-start.5 = (pred[8,3]{0,1:T(4,128)(4,1)S(1)}, pred[8,3]{0,1:T(4,128)(4,1)}, u32[]{:S(2)}) copy-start(pred[8,3]{0,1:T(4,128)(4,1)} %constant.51) | copy-start | bytes 76
  26.0 2.7 %copy-start.4 = (bf16[1,2,16,16,256]{4,3,2,1,0:T(8,128)(2,1)S(1)}, bf16[1,2,16,16,256]{4,3,2,1,0:T(8,128)(2,1)}, u32[]{:S(2)}) copy-start(bf16[1,2,16,16,256]{4,3,2,1,0:T(8,128)(2,1)} %param.5) | copy-start | bytes 786436
  36.5 1.8 %copy-start.1 = (f32[28,128,256]{2,1,0:T(8,128)}, f32[28,128,256]{2,1,0:T(8,128)S(1)}, u32[]{:S(2)}) copy-start(f32[28,128,256]{2,1,0:T(8,128)S(1)} %pad.4) | copy-start | bytes 11010052
  38.4 2.7 %collective-permute-start.2 = (bf16[4,4,7,16,256]{4,3,1,2,0:T(8,128)(2,1)S(1)}, bf16[4,4,7,16,256]{4,3,1,2,0:T(8,128)(2,1)}, u32[]{:S(2)}, u32[]{:S(2)}) collective-permute-start(bf16[4,4,7,16,256]{4,3,1,2,0:T(8,128)(2,1)S(1)} %fusion.14), channel_id=1, source_target_pairs={{0,4},{4,0},{8,12},{12,8},{16,20},{20,16},{24,28},{28,24},{1,5},{5... | collective-permute-start | bytes 2752520 | tf_op jit(solution)/shard_map/ppermute | solution.py:33
  44.2 18.4 %all-to-all-start.1 = ((bf16[4,448,256]{2,1,0:T(8,128)(2,1)}), bf16[4,448,256]{2,1,0:T(8,128)(2,1)S(1)}, u32[]{:S(2)}, u32[]{:S(2)}) async-start(bf16[4,448,256]{2,1,0:T(8,128)(2,1)} %bitcast.19), calls=%async_computation.1 | async-start | bytes 1835008 | tf_op jit(solution)/shard_map/all_to_all | solution.py:39
  49.0 23.5 %collective-permute-start.1 = (bf16[1,1,16,16,256]{4,2,3,1,0:T(8,128)(2,1)S(1)}, bf16[1,1,16,16,256]{4,2,3,1,0:T(8,128)(2,1)}, u32[]{:S(2)}, u32[]{:S(2)}) collective-permute-start(bf16[1,1,16,16,256]{4,2,3,1,0:T(8,128)(2,1)S(1)} %slice.21), channel_id=1, source_target_pairs={{1,0},{2,1},{3,2},{5,4},{6,5},{7,6},{9,8},{10,9},{11,10},{13,12},{... | collective-permute-start | bytes 393224 | tf_op jit(solution)/shard_map/ppermute | solution.py:15
  63.5 12.8 %all-to-all-start.2 = ((bf16[4,112,256]{2,1,0:T(8,128)(2,1)}), bf16[4,112,256]{2,1,0:T(8,128)(2,1)}, u32[]{:S(2)}, u32[]{:S(2)}) async-start(bf16[4,112,256]{2,1,0:T(8,128)(2,1)} %bitcast.79), calls=%async_computation.2 | async-start | bytes 458752 | tf_op jit(solution)/shard_map/all_to_all | solution.py:43
  72.5 7.8 %copy-start.3 = (pred[8,6]{0,1:T(8,128)(4,1)S(1)}, pred[8,6]{0,1:T(8,128)(4,1)}, u32[]{:S(2)}) copy-start(pred[8,6]{0,1:T(8,128)(4,1)} %constant.52) | copy-start | bytes 148
  76.3 9.5 %all-to-all-start = ((bf16[4,2,16384]{2,1,0:T(2,128)(2,1)}), bf16[4,2,16384]{2,1,0:T(2,128)(2,1)}, u32[]{:S(2)}, u32[]{:S(2)}) async-start(bf16[4,2,16384]{2,1,0:T(2,128)(2,1)} %reshape.68), calls=%async_computation | async-start | bytes 524288 | tf_op jit(solution)/shard_map/all_to_all | solution.py:71
  86.4 9.4 %all-to-all-start.3 = ((bf16[4,112,256]{2,1,0:T(8,128)(2,1)}), bf16[4,112,256]{2,1,0:T(8,128)(2,1)}, u32[]{:S(2)}, u32[]{:S(2)}) async-start(bf16[4,112,256]{2,1,0:T(8,128)(2,1)} %broadcast_in_dim.2), calls=%async_computation.3 | async-start | bytes 458752 | tf_op jit(solution)/shard_map/all_to_all | solution.py:48

commit v2 on v0

--- a/solution.py
+++ b/solution.py
@@ -5,11 +5,72 @@
 from jax import lax
 from jax.sharding import PartitionSpec as P
 
+BF16 = jnp.bfloat16
+F32 = jnp.float32
+
 
 def from_behind(value, axis, steps):
     count = lax.axis_size(axis)
     first, last = (max(0, -steps), min(count, count - steps))
     return lax.ppermute(value, axis, [(source, source + steps) for source in range(first, last)])
+
+
+def chip_groups():
+    dp = lax.axis_size("dp")
+    cores = 2 if dp % 2 == 0 else 1
+    return cores, dp // cores, [list(range(core, dp, cores)) for core in range(cores)]
+
+
+def add_cores(part):
+    units, chans_in, lanes = part.shape
+    cores, chips, _ = chip_groups()
+    pieces = part.reshape(units, chips, cores, chans_in // (chips * cores), lanes)
+    if cores == 1:
+        return pieces[:, :, 0]
+    core = lax.axis_index("dp") % 2
+    mine = lax.dynamic_index_in_dim(pieces, core, 2, keepdims=False)
+    other = lax.dynamic_index_in_dim(pieces, 1 - core, 2, keepdims=False).astype(BF16)
+    got = lax.ppermute(other, "dp", [(i, i ^ 1) for i in range(cores * chips)])
+    return mine + got.astype(F32)
+
+
+def scatter_space(total):
+    space = lax.axis_size("space")
+    units, rows, lanes = total.shape
+    share = -(-units // space)
+    total = jnp.pad(total.astype(BF16), ((0, share * space - units), (0, 0), (0, 0)))
+    got = lax.all_to_all(total.reshape(space, share * rows, lanes), "space", 0, 0, tiled=True)
+    return jnp.sum(got.astype(F32), axis=0).reshape(share, rows, lanes)
+
+
+def scatter_chips(total):
+    units, chips, block, lanes = total.shape
+    if chips == 1:
+        return total[:, 0]
+    _, _, groups = chip_groups()
+    moved = jnp.swapaxes(total, 0, 1).astype(BF16).reshape(chips, units * block, lanes)
+    got = lax.all_to_all(moved, "dp", 0, 0, axis_index_groups=groups, tiled=True)
+    return jnp.sum(got.astype(F32), axis=0).reshape(units, block, lanes)
+
+
+def reduce_kernel_grad(part, late):
+    space = lax.axis_size("space")
+    early = part.shape[0] - late
+    first = add_cores(part[:early])
+    second = add_cores(part[early:])
+    units, chips, block, lanes = first.shape
+    first = scatter_space(first.reshape(units, chips * block, lanes))
+    second = scatter_chips(second)
+    first = scatter_chips(first.reshape(-1, chips, block, lanes))
+    second = scatter_space(second)
+    both = jnp.concatenate([first, second], axis=0).astype(BF16)
+    share = both.shape[0]
+    spread = jnp.broadcast_to(both.reshape(1, share * block, lanes), (space, share * block, lanes))
+    full = lax.all_to_all(spread, "space", 0, 0, tiled=True).reshape(space, share, block, lanes)
+    cut = first.shape[0]
+    early_full = full[:, :cut].reshape(-1, block, lanes)[:early]
+    late_full = full[:, cut:].reshape(-1, block, lanes)[:late]
+    return jnp.concatenate([early_full, late_full], axis=0).astype(F32)
 
 
 def body(volume, kernel, cotangent):
@@ -56,9 +117,14 @@
     )
     count = lax.axis_size("dp") * lax.axis_size("space") * planes * rows * cols
     kernel_part = kernel_part * (1.0 / math.sqrt(count))
-    summed = lax.psum(kernel_part, "space")
-    kernel_grad = lax.psum_scatter(summed, "dp", scatter_dimension=3, tiled=True)
-    return (switched, volume_grad, kernel_grad)
+    kd, kh, kw, ci, co = kernel_part.shape
+    lanes = 128 if co % 128 == 0 else co
+    halves = co // lanes
+    units = kernel_part.reshape(kd * kh * kw, ci, halves, lanes).swapaxes(1, 2)
+    units = units.reshape(-1, ci, lanes)
+    total = reduce_kernel_grad(units, kh * kw * halves)
+    kernel_grad = total.reshape(kd * kh * kw, halves, -1, lanes).swapaxes(1, 2)
+    return (switched, volume_grad, kernel_grad.reshape(kd, kh, kw, -1, co))
 
 
 def solution(mesh):

time: 145 us -> 121 us (0.83)
  waiting for transfers between devices: 85 us -> 30 us
  starting transfers between devices: 13.1 us -> 32.4 us
  local copies, waits for them, and re-layouts: 15.5 us -> 34.4 us
  between operations: 14.3 us -> 1.01 us
  other arithmetic: 2.48 us -> 8.06 us
    psum x1 -> x0, waiting for transfers between devices: 40.5 us -> none  [body(): summed = lax.psum(kernel_part, 'space')]
    reduce_scatter x1 -> x0, waiting for transfers between devices: 33.3 us -> none  [body(): lax.psum_scatter(summed, 'dp', scatter_dimension=3, tiled=True)]
    all_to_all x0 -> x5, starting transfers between devices: none -> 20.8 us  [the longest x2 8.55 us: scatter_chips(): lax.all_to_all(moved, 'dp', 0, 0, axis_index_groups=groups, tiled=True)]
    all_to_all x0 -> x5, waiting for transfers between devices: none -> 18.5 us  [the longest x2 12 us: scatter_chips(): lax.all_to_all(moved, 'dp', 0, 0, axis_index_groups=groups, tiled=True)]
    reshape x0 -> x4, local copies, waits for them, and re-layouts: none -> 9.19 us  [the longest x2 7.84 us: body(): units = kernel_part.reshape(kd * kh * kw, ci, halves, lanes).swapaxes(1, 2)]
    convert_element_type x0 -> x2, other arithmetic: none -> 3.53 us  [the longest x1 2.48 us: scatter_space(): total.astype(BF16)]
    all_to_all x1, starting transfers between devices: 6.76 us -> 4.19 us  [body(): lax.all_to_all(channel_major, 'space', split_axis=1, concat_axis=2, tiled...]
    convert_element_type x0 -> x4, local copies, waits for them, and re-layouts: none -> 2.47 us  [the longest x2 1.43 us: scatter_chips(): jnp.swapaxes(total, 0, 1).astype(BF16).reshape(chips, units * block, lanes)]
  transfers between devices with their start and end apart: 5 -> 10, of which waited for: 3 -> 6; matrix products, arithmetic and copies ran while one was open for 7% -> 18% of each run, Pallas kernels for 0% -> 0%
where the time goes in v2:
time: 121 us; the launch traced here: 120 us
  local copies, waits for them, and re-layouts  34.4 us (28%)
  starting transfers between devices  32.4 us (27%)
  waiting for transfers between devices  30 us (25%)
  matrix products  14.1 us (12%)
  other arithmetic  8.06 us (7%)
    all_to_all x2, waiting for transfers between devices, scatter_chips(): lax.all_to_all(moved, 'dp', 0, 0, axis_index_groups=groups, tiled=True)  12 us
    ppermute x2, waiting for transfers between devices, from_behind(): lax.ppermute(value, axis, [(source, source + steps) for source in range(f...  10.4 us
    unnamed x22, local copies, waits for them, and re-layouts  9.73 us
    conv_general_dilated x1, matrix products, body(): lax.conv_general_dilated(extended, grad_pre, (1, 1, 1), ((0, 0), (1, 0),...  8.66 us
    all_to_all x2, starting transfers between devices, scatter_chips(): lax.all_to_all(moved, 'dp', 0, 0, axis_index_groups=groups, tiled=True)  8.55 us
    all_to_all x2, starting transfers between devices, scatter_space(): lax.all_to_all(total.reshape(space, share * rows, lanes), 'space', 0, 0,...  8.19 us
    reshape x2, local copies, waits for them, and re-layouts, body(): units = kernel_part.reshape(kd * kh * kw, ci, halves, lanes).swapaxes(1, 2)  7.84 us
    ppermute x2, starting transfers between devices, from_behind(): lax.ppermute(value, axis, [(source, source + steps) for source in range(f...  6.93 us
  transfers between devices with their start and end apart: 10, of which 6 were waited for; matrix products, arithmetic and copies ran while one was open for 18% of the time, Pallas kernels for 0%

profile of v2, /device:TPU:0, one launch (start us, length us, event | category | flops | bytes accessed | tf_op | source)
XLA Modules:
  0.0 120.0 jit_solution(9865039943993172599)
XLA Ops:
  0.7 1.1 slice.35
  2.3 5.7 %collective-permute-start = (bf16[1,1,32,32,128]{4,0,3,2,1:T(2,128)(2,1)S(1)}, bf16[1,1,32,32,128]{4,0,3,2,1:T(2,128)(2,1)}, u32[]{:S(2)}, u32[]{:S(2)}) collective-permute-start(bf16[1,1,32,32,128]{4,0,3,2,1:T(2,128)(2,1)S(1)} %copy.95), channel_id=1, source_target_pairs={{0,1},{1,2},{2,3},{4,5},{5,6},{6,7},{8,9},{9,10},{10,11},{12,13},{... | collective-permute-start | bytes 786440 | tf_op jit(solution)/shard_map/ppermute | solution.py:15
  8.0 10.4 %collective-permute-done = bf16[1,1,32,32,128]{4,0,3,2,1:T(2,128)(2,1)} collective-permute-done((bf16[1,1,32,32,128]{4,0,3,2,1:T(2,128)(2,1)S(1)}, bf16[1,1,32,32,128]{4,0,3,2,1:T(2,128)(2,1)}, u32[]{:S(2)}, u32[]{:S(2)}) %collective-permute-start) | collective-permute-done | bytes 262176 | tf_op jit(solution)/shard_map/ppermute | solution.py:15
  18.4 1.6 %constant_dynamic-update-slice_fusion.1 = bf16[1,5,32,32,128]{4,0,3,2,1:T(2,128)(2,1)S(1)} fusion(bf16[1,1,32,32,128]{4,0,3,2,1:T(2,128)(2,1)} %collective-permute-done), kind=kLoop, calls=%fused_computation.45 | loop fusion | bytes 786432
  20.0 2.6 %constant_dynamic-update-slice_fusion = bf16[1,5,32,32,128]{4,0,3,2,1:T(2,128)(2,1)S(1)} fusion(bf16[1,5,32,32,128]{4,0,3,2,1:T(2,128)(2,1)S(1)} %constant_dynamic-update-slice_fusion.1, bf16[1,4,32,32,128]{4,3,2,1,0:T(8,128)(2,1)S(1)} %copy-done.2), kind=kLoop, calls=%fused_computation.44 | loop fusion | bytes 3145728 | tf_op jit(solution)/shard_map/concatenate | solution.py:78
  22.6 1.5 %copy.97 = bf16[1,5,32,32,128]{4,2,3,1,0:T(8,128)(2,1)S(1)} copy(bf16[1,5,32,32,128]{4,0,3,2,1:T(2,128)(2,1)S(1)} %constant_dynamic-update-slice_fusion) | data formatting | bytes 2621440
  24.5 1.3 %copy.68 = bf16[5,32,1,8,6,128]{5,3,4,1,0,2:T(8,128)(2,1)S(1)} copy(bf16[5,32,1,8,6,128]{5,1,4,3,0,2:T(8,128)(2,1)S(1)} %bitcast.90) | data formatting | bytes 3932160 | tf_op jit(solution)/shard_map/conv_general_dilated | solution.py:79
  26.0 2.5 %add_multiply_fusion = (f32[2,16,8,3,256]{4,2,3,1,0:T(8,128)S(1)}, bf16[2,16,8,3,256]{4,2,3,1,0:T(8,128)(2,1)}) fusion(bf16[3,3,3,128,256]{4,3,2,1,0:T(8,128)(2,1)S(1)} %copy-done, bf16[5,32,1,7,2,128]{5,3,4,1,0,2:T(8,128)(2,1)S(1)} %slice.36, bf16[5,32,1,8,6,128]{5,3,4,1,0,2:T(8,128)(2,1)S(1)} %copy.68, pred[8,3]{0,1:T(4,128)(4,1)S(1)} %copy-done.6), kind=kOutput, calls=%fused_computation.25 | convolution fusion | flops 1340473344 | bytes 5488664 | tf_op jit(solution)/shard_map/conv_general_dilated | solution.py:79
  28.9 8.7 %convolution_multiply_fusion = f32[3,3,3,128,256]{4,3,2,1,0:T(8,128)} fusion(bf16[1,5,32,32,128]{4,0,3,2,1:T(2,128)(2,1)S(1)} %constant_dynamic-update-slice_fusion, bf16[1,2,16,16,256]{4,2,3,1,0:T(8,128)(2,1)S(1)} %fusion.23), kind=kOutput, calls=%fused_computation.10 | convolution fusion | flops 869498880 | bytes 5111808 | tf_op jit(solution)/shard_map/conv_general_dilated | solution.py:109
  37.5 5.4 %reshape.76 = f32[27,128,2,128]{3,2,1,0:T(2,128)} reshape(f32[3,3,3,128,256]{4,3,2,1,0:T(8,128)} %convolution_multiply_fusion) | data formatting | bytes 7077888 | tf_op jit(solution)/shard_map/reshape | solution.py:123
  42.9 2.5 %copy.96 = f32[27,128,2,128]{3,1,2,0:T(8,128)S(1)} copy(f32[27,128,2,128]{3,2,1,0:T(2,128)} %reshape.76) | data formatting | bytes 7077888 | tf_op jit(solution)/shard_map/reshape | solution.py:123
  45.8 1.4 %copy-done.1 = f32[18,2,128,128]{3,2,1,0:T(8,128)} copy-done((f32[18,2,128,128]{3,2,1,0:T(8,128)}, f32[18,2,128,128]{3,2,1,0:T(8,128)S(1)}, u32[]{:S(2)}) %copy-start.1) | copy-done | bytes 2359320
  48.7 1.1 fusion.27
  50.5 4.9 %all-to-all-start.3 = ((bf16[4,288,128]{2,1,0:T(8,128)(2,1)}), bf16[4,288,128]{2,1,0:T(8,128)(2,1)S(1)}, u32[]{:S(2)}, u32[]{:S(2)}) async-start(bf16[4,288,128]{2,1,0:T(8,128)(2,1)} %bitcast.26), calls=%async_computation.3 | async-start | bytes 589824 | tf_op jit(solution)/shard_map/all_to_all | solution.py:52
  55.4 2.5 %fusion.13 = bf16[36,4,16,128]{3,2,1,0:T(8,128)(2,1)} fusion(bf16[36,4,16,128]{3,2,1,0:T(8,128)(2,1)} %collective-permute-done.2, f32[36,4,2,16,128]{4,3,2,1,0:T(8,128)} %bitcast.92, s32[]{:T(128)S(6)} %select_n.20), kind=kLoop, calls=%fused_computation.17 | loop fusion | flops 884736 | bytes 2359300 | tf_op jit(solution)/shard_map/convert_element_type | solution.py:41
  57.9 7.3 %all-to-all-done.3 = bf16[4,288,128]{2,1,0:T(8,128)(2,1)S(1)} async-done(((bf16[4,288,128]{2,1,0:T(8,128)(2,1)}), bf16[4,288,128]{2,1,0:T(8,128)(2,1)S(1)}, u32[]{:S(2)}, u32[]{:S(2)}) %all-to-all-start.3) | async-done | bytes 294944 | tf_op jit(solution)/shard_map/all_to_all | solution.py:52
  65.2 4.8 %all-to-all-start.1 = ((bf16[4,576,128]{2,1,0:T(8,128)(2,1)}), bf16[4,576,128]{2,1,0:T(8,128)(2,1)S(1)}, u32[]{:S(2)}, u32[]{:S(2)}) async-start(bf16[4,576,128]{2,1,0:T(8,128)(2,1)} %bitcast.17), calls=%async_computation.1 | async-start | bytes 1179648 | tf_op jit(solution)/shard_map/all_to_all | solution.py:42
  70.7 1.3 %collective-permute-start.1 = (bf16[1,1,16,16,256]{4,2,3,1,0:T(8,128)(2,1)}, bf16[1,1,16,16,256]{4,2,3,1,0:T(8,128)(2,1)}, u32[]{:S(2)}, u32[]{:S(2)}) collective-permute-start(bf16[1,1,16,16,256]{4,2,3,1,0:T(8,128)(2,1)} %slice.39), channel_id=1, source_target_pairs={{1,0},{2,1},{3,2},{5,4},{6,5},{7,6},{9,8},{10,9},{11,10},{13,12},{... | collective-permute-start | bytes 393224 | tf_op jit(solution)/shard_map/ppermute | solution.py:15
  72.0 1.1 copy.69
  73.7 4.6 %all-to-all-done.1 = bf16[4,576,128]{2,1,0:T(8,128)(2,1)S(1)} async-done(((bf16[4,576,128]{2,1,0:T(8,128)(2,1)}), bf16[4,576,128]{2,1,0:T(8,128)(2,1)S(1)}, u32[]{:S(2)}, u32[]{:S(2)}) %all-to-all-start.1) | async-done | bytes 589856 | tf_op jit(solution)/shard_map/all_to_all | solution.py:42
  78.3 3.4 %all-to-all-start.4 = ((bf16[4,80,128]{2,1,0:T(8,128)(2,1)}), bf16[4,80,128]{2,1,0:T(8,128)(2,1)S(1)}, u32[]{:S(2)}, u32[]{:S(2)}) async-start(bf16[4,80,128]{2,1,0:T(8,128)(2,1)} %bitcast.28), calls=%async_computation.4 | async-start | bytes 163840 | tf_op jit(solution)/shard_map/all_to_all | solution.py:42
  82.8 2.2 %reduce.4 = bf16[256,512]{1,0:T(8,128)(2,1)S(1)} reduce(bf16[256,1,512]{2,1,0:T(2,128)(2,1)S(1)} %bitcast.100, bf16[]{:T(256)} %broadcast.59), dimensions={1}, to_apply=%bitcast.74.reduce_sub_computation | reduce | bytes 524290
  87.3 3.7 %all-to-all-start.2 = ((bf16[4,144,128]{2,1,0:T(8,128)(2,1)}), bf16[4,144,128]{2,1,0:T(8,128)(2,1)S(1)}, u32[]{:S(2)}, u32[]{:S(2)}) async-start(bf16[4,144,128]{2,1,0:T(8,128)(2,1)} %bitcast.20), calls=%async_computation.2 | async-start | bytes 294912 | tf_op jit(solution)/shard_map/all_to_all | solution.py:52
  92.3 4.6 %all-to-all-done.2 = bf16[4,144,128]{2,1,0:T(8,128)(2,1)S(1)} async-done(((bf16[4,144,128]{2,1,0:T(8,128)(2,1)}), bf16[4,144,128]{2,1,0:T(8,128)(2,1)S(1)}, u32[]{:S(2)}, u32[]{:S(2)}) %all-to-all-start.2) | async-done | bytes 147488 | tf_op jit(solution)/shard_map/all_to_all | solution.py:52
  96.9 4.2 %all-to-all-start = ((bf16[4,2,16384]{2,1,0:T(2,128)(2,1)}), bf16[4,2,16384]{2,1,0:T(2,128)(2,1)}, u32[]{:S(2)}, u32[]{:S(2)}) async-start(bf16[4,2,16384]{2,1,0:T(2,128)(2,1)} %reshape.121), calls=%async_computation | async-start | bytes 524288 | tf_op jit(solution)/shard_map/all_to_all | solution.py:95
  101.1 2.9 %select_convert_fusion = bf16[4,32,8,6,128]{4,2,3,1,0:T(8,128)(2,1)S(1)} fusion(bf16[3,3,3,128,256]{4,3,2,1,0:T(8,128)(2,1)S(1)} %copy-done, pred[8,6]{0,1:T(8,128)(4,1)S(1)} %copy-done.4, bf16[3,16,8,4,256]{4,2,3,1,0:T(8,128)(2,1)S(1)} %fusion.40), kind=kOutput, calls=%fused_computation.3 | convolution fusion | flops 1332215808 | bytes 4128816 | tf_op jit(solution)/shard_map/conv_general_dilated | solution.py:99
  105.4 1.2 all-to-all-done
  107.3 4.0 %all-to-all-start.5 = ((bf16[4,224,128]{2,1,0:T(8,128)(2,1)}), bf16[4,224,128]{2,1,0:T(8,128)(2,1)}, u32[]{:S(2)}, u32[]{:S(2)}) async-start(bf16[4,224,128]{2,1,0:T(8,128)(2,1)} %broadcast_in_dim.2), calls=%async_computation.5 | async-start | bytes 458752 | tf_op jit(solution)/shard_map/all_to_all | solution.py:69
  111.5 1.4 %copy.83 = bf16[1,4,32,32,128]{4,3,2,1,0:T(8,128)(2,1)} copy(bf16[1,4,32,32,128]{4,2,3,1,0:T(8,128)(2,1)S(1)} %slice_bitcast_fusion) | data formatting | bytes 2097152
  112.8 1.2 reshape.122
  114.8 1.9 %all-to-all-done.5 = bf16[4,224,128]{2,1,0:T(8,128)(2,1)} async-done(((bf16[4,224,128]{2,1,0:T(8,128)(2,1)}), bf16[4,224,128]{2,1,0:T(8,128)(2,1)}, u32[]{:S(2)}, u32[]{:S(2)}) %all-to-all-start.5) | async-done | bytes 229408 | tf_op jit(solution)/shard_map/all_to_all | solution.py:69
  118.9 1.1 reshape.106
  (58 shorter events, 15.2 us)
Async XLA Ops:
  0.6 25.3 %copy-start = (bf16[3,3,3,128,256]{4,3,2,1,0:T(8,128)(2,1)S(1)}, bf16[3,3,3,128,256]{4,3,2,1,0:T(8,128)(2,1)}, u32[]{:S(2)}) copy-start(bf16[3,3,3,128,256]{4,3,2,1,0:T(8,128)(2,1)} %param.4) | copy-start | bytes 5308420
  0.6 19.3 %copy-start.2 = (bf16[1,4,32,32,128]{4,3,2,1,0:T(8,128)(2,1)S(1)}, bf16[1,4,32,32,128]{4,3,2,1,0:T(8,128)(2,1)}, u32[]{:S(2)}) copy-start(bf16[1,4,32,32,128]{4,3,2,1,0:T(8,128)(2,1)} %param.3) | copy-start | bytes 3145732
  2.3 16.0 %collective-permute-start = (bf16[1,1,32,32,128]{4,0,3,2,1:T(2,128)(2,1)S(1)}, bf16[1,1,32,32,128]{4,0,3,2,1:T(2,128)(2,1)}, u32[]{:S(2)}, u32[]{:S(2)}) collective-permute-start(bf16[1,1,32,32,128]{4,0,3,2,1:T(2,128)(2,1)S(1)} %copy.95), channel_id=1, source_target_pairs={{0,1},{1,2},{2,3},{4,5},{5,6},{6,7},{8,9},{9,10},{10,11},{12,13},{... | collective-permute-start | bytes 786440 | tf_op jit(solution)/shard_map/ppermute | solution.py:15
  24.5 1.5 %copy-start.6 = (pred[8,3]{0,1:T(4,128)(4,1)S(1)}, pred[8,3]{0,1:T(4,128)(4,1)}, u32[]{:S(2)}) copy-start(pred[8,3]{0,1:T(4,128)(4,1)} %constant.59) | copy-start | bytes 76
  26.0 2.7 %copy-start.5 = (bf16[1,2,16,16,256]{4,3,2,1,0:T(8,128)(2,1)S(1)}, bf16[1,2,16,16,256]{4,3,2,1,0:T(8,128)(2,1)}, u32[]{:S(2)}) copy-start(bf16[1,2,16,16,256]{4,3,2,1,0:T(8,128)(2,1)} %param.5) | copy-start | bytes 786436
  45.6 3.1 %collective-permute-start.3 = (bf16[18,4,16,128]{3,2,1,0:T(8,128)(2,1)S(1)}, bf16[18,4,16,128]{3,2,1,0:T(8,128)(2,1)}, u32[]{:S(2)}, u32[]{:S(2)}) collective-permute-start(bf16[18,4,16,128]{3,2,1,0:T(8,128)(2,1)S(1)} %fusion.26), channel_id=1, source_target_pairs={{0,4},{4,0},{8,12},{12,8},{16,20},{20,16},{24,28},{28,24},{1,5},{5... | collective-permute-start | bytes 884744 | tf_op jit(solution)/shard_map/ppermute | solution.py:33
  45.8 1.4 %copy-start.1 = (f32[18,2,128,128]{3,2,1,0:T(8,128)}, f32[18,2,128,128]{3,2,1,0:T(8,128)S(1)}, u32[]{:S(2)}) copy-start(f32[18,2,128,128]{3,2,1,0:T(8,128)S(1)} %slice.42) | copy-start | bytes 7077892
  48.2 7.2 %collective-permute-start.2 = (bf16[36,4,16,128]{3,2,1,0:T(8,128)(2,1)}, bf16[36,4,16,128]{3,2,1,0:T(8,128)(2,1)}, u32[]{:S(2)}, u32[]{:S(2)}) collective-permute-start(bf16[36,4,16,128]{3,2,1,0:T(8,128)(2,1)} %fusion.20), channel_id=1, source_target_pairs={{0,4},{4,0},{8,12},{12,8},{16,20},{20,16},{24,28},{28,24},{1,5},{5... | collective-permute-start | bytes 1769480 | tf_op jit(solution)/shard_map/ppermute | solution.py:33
  50.5 14.7 %all-to-all-start.3 = ((bf16[4,288,128]{2,1,0:T(8,128)(2,1)}), bf16[4,288,128]{2,1,0:T(8,128)(2,1)S(1)}, u32[]{:S(2)}, u32[]{:S(2)}) async-start(bf16[4,288,128]{2,1,0:T(8,128)(2,1)} %bitcast.26), calls=%async_computation.3 | async-start | bytes 589824 | tf_op jit(solution)/shard_map/all_to_all | solution.py:52
  65.2 13.1 %all-to-all-start.1 = ((bf16[4,576,128]{2,1,0:T(8,128)(2,1)}), bf16[4,576,128]{2,1,0:T(8,128)(2,1)S(1)}, u32[]{:S(2)}, u32[]{:S(2)}) async-start(bf16[4,576,128]{2,1,0:T(8,128)(2,1)} %bitcast.17), calls=%async_computation.1 | async-start | bytes 1179648 | tf_op jit(solution)/shard_map/all_to_all | solution.py:42
  70.7 20.3 %collective-permute-start.1 = (bf16[1,1,16,16,256]{4,2,3,1,0:T(8,128)(2,1)}, bf16[1,1,16,16,256]{4,2,3,1,0:T(8,128)(2,1)}, u32[]{:S(2)}, u32[]{:S(2)}) collective-permute-start(bf16[1,1,16,16,256]{4,2,3,1,0:T(8,128)(2,1)} %slice.39), channel_id=1, source_target_pairs={{1,0},{2,1},{3,2},{5,4},{6,5},{7,6},{9,8},{10,9},{11,10},{13,12},{... | collective-permute-start | bytes 393224 | tf_op jit(solution)/shard_map/ppermute | solution.py:15
  78.3 8.3 %all-to-all-start.4 = ((bf16[4,80,128]{2,1,0:T(8,128)(2,1)}), bf16[4,80,128]{2,1,0:T(8,128)(2,1)S(1)}, u32[]{:S(2)}, u32[]{:S(2)}) async-start(bf16[4,80,128]{2,1,0:T(8,128)(2,1)} %bitcast.28), calls=%async_computation.4 | async-start | bytes 163840 | tf_op jit(solution)/shard_map/all_to_all | solution.py:42
  86.7 0.6 copy-start.3
  87.3 9.6 %all-to-all-start.2 = ((bf16[4,144,128]{2,1,0:T(8,128)(2,1)}), bf16[4,144,128]{2,1,0:T(8,128)(2,1)S(1)}, u32[]{:S(2)}, u32[]{:S(2)}) async-start(bf16[4,144,128]{2,1,0:T(8,128)(2,1)} %bitcast.20), calls=%async_computation.2 | async-start | bytes 294912 | tf_op jit(solution)/shard_map/all_to_all | solution.py:52
  91.9 9.2 %copy-start.4 = (pred[8,6]{0,1:T(8,128)(4,1)S(1)}, pred[8,6]{0,1:T(8,128)(4,1)}, u32[]{:S(2)}) copy-start(pred[8,6]{0,1:T(8,128)(4,1)} %constant.60) | copy-start | bytes 148
  96.9 9.7 %all-to-all-start = ((bf16[4,2,16384]{2,1,0:T(2,128)(2,1)}), bf16[4,2,16384]{2,1,0:T(2,128)(2,1)}, u32[]{:S(2)}, u32[]{:S(2)}) async-start(bf16[4,2,16384]{2,1,0:T(2,128)(2,1)} %reshape.121), calls=%async_computation | async-start | bytes 524288 | tf_op jit(solution)/shard_map/all_to_all | solution.py:95
  107.3 9.4 %all-to-all-start.5 = ((bf16[4,224,128]{2,1,0:T(8,128)(2,1)}), bf16[4,224,128]{2,1,0:T(8,128)(2,1)}, u32[]{:S(2)}, u32[]{:S(2)}) async-start(bf16[4,224,128]{2,1,0:T(8,128)(2,1)} %broadcast_in_dim.2), calls=%async_computation.5 | async-start | bytes 458752 | tf_op jit(solution)/shard_map/all_to_all | solution.py:69

commit v3 on v0

v3 whole, which is shorter than its diff:
```python
import functools
import math

import jax
import jax.numpy as jnp
from jax import lax
from jax.experimental import pallas as pl
from jax.experimental.pallas import tpu as pltpu
from jax.sharding import PartitionSpec as P

BF16 = jnp.bfloat16
F32 = jnp.float32
VMEM_LIMIT = 40 * 1024 * 1024


def params():
    return pltpu.CompilerParams(vmem_limit_bytes=VMEM_LIMIT)


def call(kernel, out_shape, scratch=(), flops=0, moved=0):
    return pl.pallas_call(
        kernel,
        out_shape=out_shape,
        scratch_shapes=list(scratch),
        compiler_params=params(),
        cost_estimate=pl.CostEstimate(flops=flops, bytes_accessed=moved, transcendentals=0),
    )


def spread_plane(plane, wide):
    height, width, chans = plane.shape
    cells = height * width
    half = width // 2
    wide[pl.ds(8, cells), :] = plane.reshape(cells, chans).astype(F32)
    left = wide[pl.ds(7, cells // 2, stride=2), :]
    even = wide[pl.ds(8, cells // 2, stride=2), :]
    odd = wide[pl.ds(9, cells // 2, stride=2), :]
    column = lax.broadcasted_iota(jnp.int32, left.shape, 0) % half
    left = jnp.where(column == 0, 0.0, left)
    joined = jnp.concatenate([left.astype(BF16), even.astype(BF16), odd.astype(BF16)], axis=1)
    joined = joined.reshape(height // 2, 2, half, 3 * chans)
    return joined[:, 0], joined[:, 1]


def tap_rows(even, odd, plane, kh):
    height = even.shape[1]
    picked = even[plane] if kh == 1 else odd[plane, pl.ds(0 if kh == 0 else 1, height)]
    return picked.reshape(height * even.shape[2], even.shape[3])


def halo_kernel(plane_ref, kernel_ref, share_ref, wide):
    _, _, height, width, chans = plane_ref.shape
    even, odd = spread_plane(plane_ref[0, 0], wide)
    above = jnp.concatenate([jnp.zeros_like(odd[:1]), odd[:-1]], axis=0)
    total = None
    for kh, rows in enumerate((above, even, odd)):
        lhs = rows.reshape(height * width // 4, 3 * chans)
        rhs = kernel_ref[0, kh].reshape(3 * chans, kernel_ref.shape[-1])
        term = jnp.dot(lhs, rhs, preferred_element_type=F32)
        total = term if total is None else total + term
    share_ref[...] = total.astype(BF16)


def halo_share(volume, kernel):
    _, planes, height, width, chans = volume.shape
    co = kernel.shape[-1]
    cells = height * width // 4
    return pl.pallas_call(
        halo_kernel,
        grid=(1,),
        out_shape=jax.ShapeDtypeStruct((cells, co), BF16),
        in_specs=[
            pl.BlockSpec((1, 1, height, width, chans), lambda i: (0, planes - 1, 0, 0, 0)),
            pl.BlockSpec((1, 3, 3, chans, co), lambda i: (0, 0, 0, 0, 0)),
        ],
        out_specs=pl.BlockSpec((cells, co), lambda i: (0, 0)),
        scratch_shapes=[pltpu.VMEM((height * width + 16, chans), F32)],
        compiler_params=params(),
        cost_estimate=pl.CostEstimate(
            flops=2 * cells * 9 * chans * co, bytes_accessed=2**20, transcendentals=0
        ),
    )(volume, kernel)


def preact_kernel(volume_ref, kernel_ref, preact_ref, even_ref, odd_ref, wide):
    _, planes, height, width, chans = volume_ref.shape
    cells = height * width // 4
    outs = planes // 2
    for plane in range(planes):
        even, odd = spread_plane(volume_ref[0, plane], wide)
        even_ref[plane] = even
        odd_ref[plane, pl.ds(0, 1)] = jnp.zeros_like(odd[:1])
        odd_ref[plane, pl.ds(1, height // 2)] = odd
    co = kernel_ref.shape[-1]
    total = None
    for kd in (1, 2):
        for kh in range(3):
            lhs = [tap_rows(even_ref, odd_ref, 2 * d - 1 + kd, kh) for d in range(outs)]
            rhs = kernel_ref[kd, kh].reshape(3 * chans, co)
            term = jnp.dot(jnp.concatenate(lhs, axis=0), rhs, preferred_element_type=F32)
            total = term if total is None else total + term
    preact_ref[...] = total
    if outs > 1:
        total = preact_ref[pl.ds(cells, (outs - 1) * cells), :]
        for kh in range(3):
            lhs = [tap_rows(even_ref, odd_ref, 2 * d - 1, kh) for d in range(1, outs)]
            rhs = kernel_ref[0, kh].reshape(3 * chans, co)
            total += jnp.dot(jnp.concatenate(lhs, axis=0), rhs, preferred_element_type=F32)
        preact_ref[pl.ds(cells, (outs - 1) * cells), :] = total


def partial_preact(volume, kernel):
    _, planes, height, width, chans = volume.shape
    co = kernel.shape[-1]
    cells = height * width // 4
    h2, w2 = height // 2, width // 2
    return call(
        preact_kernel,
        (
            jax.ShapeDtypeStruct((planes // 2 * cells, co), F32),
            jax.ShapeDtypeStruct((planes, h2, w2, 3 * chans), BF16),
            jax.ShapeDtypeStruct((planes, h2 + 1, w2, 3 * chans), BF16),
        ),
        [pltpu.VMEM((height * width + 16, chans), F32)],
        flops=2 * planes // 2 * cells * 27 * chans * co,
        moved=6 * 2**20,
    )(volume, kernel)


def activation_kernel(preact_ref, share_ref, cotangent_ref, grad_ref, flipped_ref):
    cells = share_ref.shape[0]
    count = preact_ref.shape[0] // cells
    for d in range(count):
        rows = pl.ds(d * cells, cells)
        value = preact_ref[rows, :]
        if d == 0:
            value = value + share_ref[...].astype(F32)
        sig = jax.nn.sigmoid(value)
        slope = sig * (1.0 + value * (1.0 - sig))
        grad_ref[rows, :] = (cotangent_ref[rows, :].astype(F32) * slope).astype(BF16)
        flipped_ref[:, rows] = (value * sig).T.astype(BF16)


def activation(preact, share, cotangent):
    cells, co = preact.shape
    return call(
        activation_kernel,
        (
            jax.ShapeDtypeStruct((cells, co), BF16),
            jax.ShapeDtypeStruct((co, cells), BF16),
        ),
        flops=20 * cells * co,
        moved=2 * 2**20,
    )(preact, share, cotangent)


def store_units(product, scale, core, cores, chips, put):
    chans = product.shape[0] // 3
    co = product.shape[1]
    block = chans // (cores * chips)
    halves = co // 128
    product = product * scale
    for kw in range(3):
        for half in range(halves):
            unit = product[kw * chans : (kw + 1) * chans, half * 128 : (half + 1) * 128]
            unit = unit.reshape(chips, cores, block, 128)
            for chip in range(chips):
                first = unit[chip, 0]
                last = unit[chip, cores - 1]
                keep = jnp.where(core == 0, first, last)
                send = jnp.where(core == 0, last, first)
                put(kw * halves + half, chip, keep, send)


def kernel_grad_kernel(kds, chip_major, cores, chips, scale, *refs):
    even_ref, odd_ref, grads_ref = refs[:3]
    above_ref = refs[3] if 0 in kds else None
    keep_ref, send_ref = refs[-2:]
    outs = even_ref.shape[0] // 2
    cells = even_ref.shape[1] * even_ref.shape[2]
    core = lax.axis_index("dp") % cores
    per_row = 3 * (grads_ref.shape[1] // 128)
    for place, kd in enumerate(kds):
        if kd == 0:
            planes = [2 * d - 1 for d in range(1, outs + 1)]
            rhs = [grads_ref[pl.ds(d * cells, cells), :] for d in range(1, outs)] + [above_ref[...]]
            rhs = jnp.concatenate(rhs, axis=0)
        else:
            planes = [2 * d - 1 + kd for d in range(outs)]
            rhs = grads_ref[...]
        for kh in range(3):
            lhs = [tap_rows(even_ref, odd_ref, plane, kh) for plane in planes]
            product = lax.dot_general(
                jnp.concatenate(lhs, axis=0), rhs, (((0,), (0,)), ((), ())), preferred_element_type=F32
            )

            def put(unit, chip, keep, send, base=(place * 3 + kh) * per_row):
                where = (chip, base + unit) if chip_major else (base + unit, chip)
                keep_ref[where] = keep
                send_ref[where] = send.astype(BF16)

            store_units(product, scale, core, cores, chips, put)


def kernel_grad_part(even, odd, grads, above, kds, chip_major, cores, chips, scale):
    chans = even.shape[-1] // 3
    co = grads.shape[-1]
    units = len(kds) * 9 * (co // 128)
    block = chans // (cores * chips)
    shape = (chips, units, block, 128) if chip_major else (units, chips, block, 128)
    operands = (even, odd, grads) + ((above,) if 0 in kds else ())
    return call(
        functools.partial(kernel_grad_kernel, kds, chip_major, cores, chips, scale),
        (jax.ShapeDtypeStruct(shape, F32), jax.ShapeDtypeStruct(shape, BF16)),
        flops=2 * grads.shape[0] * len(kds) * 9 * chans * co,
        moved=6 * 2**20,
    )(*operands)


def volume_grad_kernel(grads_ref, above_ref, kernel_ref, out_ref, shifted, wide):
    planes, h2, _, width, chans = out_ref.shape
    w2 = width // 2
    cells = h2 * w2
    outs = planes // 2
    co = grads_ref.shape[1]
    here, right = [], []
    for d in range(outs + 1):
        plane = grads_ref[pl.ds(d * cells, cells), :] if d < outs else above_ref[...]
        shifted[pl.ds(0, cells), :] = plane.astype(F32)
        moved = shifted[pl.ds(1, cells), :]
        column = lax.broadcasted_iota(jnp.int32, moved.shape, 0) % w2
        moved = jnp.where(column == w2 - 1, 0.0, moved).astype(BF16)
        here.append(plane)
        right.append(moved)

    def down(rows):
        return jnp.concatenate([rows[w2:], jnp.zeros((w2, co), BF16)], axis=0)

    contract = (((1,), (1,)), ((), ()))
    for plane in range(planes):
        d = plane // 2
        depth = [(1, d)] if plane % 2 == 0 else [(2, d), (0, d + 1)]
        for odd_row in range(2):
            taps = [(1, False)] if odd_row == 0 else [(2, False), (0, True)]
            both, right_only = None, None
            for kd, source in depth:
                for kh, lower in taps:
                    lhs = down(here[source]) if lower else here[source]
                    rhs = kernel_ref[kd, kh, pl.ds(1, 2)].reshape(2 * chans, co)
                    term = lax.dot_general(lhs, rhs, contract, preferred_element_type=F32)
                    both = term if both is None else both + term
                    lhs = down(right[source]) if lower else right[source]
                    term = lax.dot_general(lhs, kernel_ref[kd, kh, 0], contract, preferred_element_type=F32)
                    right_only = term if right_only is None else right_only + term
            wide[pl.ds(0, cells, stride=2), :] = both[:, :chans]
            wide[pl.ds(1, cells, stride=2), :] = both[:, chans:] + right_only
            out_ref[plane, :, odd_row] = wide[...].reshape(h2, width, chans).astype(BF16)


def volume_grad_of(grads, above, kernel, height, width):
    cells, co = grads.shape
    chans = kernel.shape[3]
    planes = 2 * cells * 4 // (height * width)
    shape = (planes, height // 2, 2, width, chans)
    return call(
        volume_grad_kernel,
        jax.ShapeDtypeStruct(shape, BF16),
        [
            pltpu.VMEM((height * width // 4 + 8, co), F32),
            pltpu.VMEM((height * width // 2, chans), F32),
        ],
        flops=2 * cells * 27 * chans * co,
        moved=4 * 2**20,
    )(grads, above, kernel)


def bits_of(count):
    bits = count.bit_length() - 1
    assert 1 << bits == count
    return bits


def exchange(value, partner):
    dp, space = lax.axis_size("dp"), lax.axis_size("space")
    pairs = []
    for i in range(dp):
        for j in range(space):
            to_dp, to_space = partner(i, j)
            pairs.append((i * space + j, to_dp * space + to_space))
    return lax.ppermute(value, ("dp", "space"), pairs)


def space_bit(stage, odd_core):
    bits = bits_of(lax.axis_size("space"))
    return bits - 1 - stage if odd_core else stage


def space_partner(stage, cores):
    return lambda i, j: (i, j ^ (1 << space_bit(stage, cores == 2 and i % 2 == 1)))


def my_space_bit(stage, cores):
    index = lax.axis_index("space")
    even = (index >> space_bit(stage, False)) & 1
    odd = (index >> space_bit(stage, True)) & 1
    return jnp.where(lax.axis_index("dp") % cores == 1, odd, even) if cores == 2 else even


def halve(value, bit):
    value = value.reshape((2, value.shape[0] // 2) + value.shape[1:])
    keep = lax.dynamic_index_in_dim(value, bit, 0, keepdims=False)
    send = lax.dynamic_index_in_dim(value, 1 - bit, 0, keepdims=False)
    return keep, send.astype(BF16)


def scatter_space(value, cores):
    for stage in range(bits_of(lax.axis_size("space"))):
        keep, send = halve(value, my_space_bit(stage, cores))
        value = keep + exchange(send, space_partner(stage, cores)).astype(F32)
    return value


def scatter_chips(value, cores, chips):
    order = list(range(bits_of(chips)))
    if order:
        rest = value.shape[1:]
        value = value.reshape((2,) * len(order) + rest)
        value = jnp.transpose(
            value, tuple(reversed(order)) + tuple(range(len(order), len(order) + len(rest)))
        )
        value = value.reshape((chips,) + rest)
    chip = lax.axis_index("dp") // cores
    for bit in order:
        keep, send = halve(value, (chip >> bit) & 1)
        got = exchange(send, lambda i, j, bit=bit: (i ^ (cores << bit), j))
        value = keep + got.astype(F32)
    return value[0]


def gather_space(value, cores):
    value = value[None]
    for stage in reversed(range(bits_of(lax.axis_size("space")))):
        got = exchange(value, space_partner(stage, cores))
        bit = my_space_bit(stage, cores)
        value = jnp.where(
            bit == 0, jnp.concatenate([value, got], 0), jnp.concatenate([got, value], 0)
        )
    return value


def neighbour(value, steps):
    count = lax.axis_size("space")
    first, last = (max(0, -steps), min(count, count - steps))
    return lax.ppermute(value, "space", [(source, source + steps) for source in range(first, last)])


def add_cores(keep, send, cores):
    if cores == 1:
        return keep
    return keep + exchange(send, lambda i, j: (i ^ 1, j)).astype(F32)


def reduce_parts(early, late, cores, chips):
    space = lax.axis_size("space")
    units, _, block, lanes = early.shape
    extra = -units % space
    early = jnp.pad(early, ((0, extra), (0, 0), (0, 0), (0, 0)))
    early = scatter_space(early, cores)
    early = scatter_chips(jnp.swapaxes(early, 0, 1), cores, chips)
    late_units = late.shape[1]
    late = scatter_chips(late, cores, chips)
    late = jnp.pad(late, ((0, -late_units % space), (0, 0), (0, 0)))
    late = scatter_space(late, cores)
    full = gather_space(jnp.concatenate([early, late], axis=0).astype(BF16), cores)
    cut = early.shape[0]
    early = full[:, :cut].reshape(-1, block, lanes)[:units]
    late = full[:, cut:].reshape(-1, block, lanes)[:late_units]
    return early, late


def body(volume, kernel, cotangent):
    samples, planes, height, width, ci = volume.shape
    co = kernel.shape[-1]
    assert samples == 1
    dp, space = lax.axis_size("dp"), lax.axis_size("space")
    cores = 2 if dp % 2 == 0 else 1
    chips = dp // cores
    outs = planes // 2
    cells = height * width // 4
    scale = 1.0 / math.sqrt(dp * space * samples * outs * cells)

    share = neighbour(halo_share(volume, kernel), 1)
    preact, even, odd = partial_preact(volume, kernel)
    grads, flipped = activation(preact, share, cotangent.reshape(outs * cells, co))
    above = neighbour(grads[:cells], -1)

    early = kernel_grad_part(even, odd, grads, None, (1, 2), False, cores, chips, scale)
    early = add_cores(*early, cores)
    late = kernel_grad_part(even, odd, grads, above, (0,), True, cores, chips, scale)
    late = add_cores(*late, cores)
    early, late = reduce_parts(early, late, cores, chips)

    switched = lax.all_to_all(
        flipped.reshape(space, co // space, outs * cells), "space", 0, 0, tiled=True
    )
    switched = jnp.swapaxes(switched, 0, 1).reshape(1, co // space, space * outs * cells)

    volume_grad = volume_grad_of(grads, above, kernel, height, width).reshape(volume.shape)

    lanes = late.shape[-1]
    taps = jnp.concatenate([late, early], axis=0).reshape(3, 3, 3, co // lanes, ci // dp, lanes)
    kernel_grad = jnp.swapaxes(taps, 3, 4).reshape(3, 3, 3, ci // dp, co).astype(F32)
    return (switched, volume_grad, kernel_grad)


def solution(mesh):
    in_specs = (P("dp", "space", None, None, None), P(), P("dp", "space", None, None, None))
    out_specs = (
        P("dp", "space", None),
        P("dp", "space", None, None, None),
        P(None, None, None, "dp", None),
    )
    return jax.shard_map(body, mesh=mesh, in_specs=in_specs, out_specs=out_specs, check_vma=False)
```

time: 145 us -> 69.3 us (0.48)
  waiting for transfers between devices: 85 us -> 23.4 us
  starting transfers between devices: 13.1 us -> 30 us
  matrix products: 14.1 us -> 0 us
  between operations: 14.3 us -> 0.91 us
  local copies, waits for them, and re-layouts: 15.5 us -> 4.88 us
  Pallas kernels: 0 us -> 7.49 us
    psum x1 -> x0, waiting for transfers between devices: 40.5 us -> none  [body(): summed = lax.psum(kernel_part, 'space')]
    reduce_scatter x1 -> x0, waiting for transfers between devices: 33.3 us -> none  [body(): lax.psum_scatter(summed, 'dp', scatter_dimension=3, tiled=True)]
    ppermute x2 -> x14, starting transfers between devices: 6.3 us -> 26.6 us  [the longest x12 20.3 us: exchange(): return lax.ppermute(value, ('dp', 'space'), pairs)]
    conv_general_dilated x3 -> x0, matrix products: 14.1 us -> none  [the longest x1 8.67 us: body(): lax.conv_general_dilated(extended, grad_pre, (1, 1, 1), ((0, 0), (1, 0),...]
    ppermute x2 -> x14, waiting for transfers between devices: 11.1 us -> 22.8 us  [the longest x12 15.4 us: exchange(): return lax.ppermute(value, ('dp', 'space'), pairs)]
    pallas_call x0 -> x6, Pallas kernels: none -> 7.49 us  [the longest x1 2.59 us: volume_grad_of(): call(volume_grad_kernel, jax.ShapeDtypeStruct(shape, BF16), [pltpu.VMEM((...]
    unnamed x21 -> x12, local copies, waits for them, and re-layouts: 7.54 us -> 3.52 us
    all_to_all x1, starting transfers between devices: 6.76 us -> 3.41 us  [body(): lax.all_to_all(flipped.reshape(space, co // space, outs * cells), 'space'...]
  transfers between devices with their start and end apart: 5 -> 15, of which waited for: 3 -> 9; matrix products, arithmetic and copies ran while one was open for 7% -> 4% of each run, Pallas kernels for 0% -> 8%
where the time goes in v3:
time: 69.3 us; the launch traced here: 69 us
  starting transfers between devices  30 us (43%)
  waiting for transfers between devices  23.4 us (34%)
  Pallas kernels  7.49 us (11%)
  local copies, waits for them, and re-layouts  4.88 us (7%)
  other arithmetic  2.3 us (3%)
  between operations  0.91 us (1%)
    ppermute x12, starting transfers between devices, exchange(): return lax.ppermute(value, ('dp', 'space'), pairs)  20.3 us
    ppermute x12, waiting for transfers between devices, exchange(): return lax.ppermute(value, ('dp', 'space'), pairs)  15.4 us
    ppermute x2, waiting for transfers between devices, neighbour(): lax.ppermute(value, 'space', [(source, source + steps) for source in rang...  7.37 us
    ppermute x2, starting transfers between devices, neighbour(): lax.ppermute(value, 'space', [(source, source + steps) for source in rang...  6.27 us
    unnamed x12, local copies, waits for them, and re-layouts  3.52 us
    all_to_all x1, starting transfers between devices, body(): lax.all_to_all(flipped.reshape(space, co // space, outs * cells), 'space'...  3.41 us
    pallas_call x1, Pallas kernels, volume_grad_of(): call(volume_grad_kernel, jax.ShapeDtypeStruct(shape, BF16), [pltpu.VMEM((...  2.59 us
    pallas_call x2, Pallas kernels, kernel_grad_part(): call(functools.partial(kernel_grad_kernel, kds, chip_major, cores, chips,...  2.19 us
  transfers between devices with their start and end apart: 15, of which 9 were waited for; matrix products, arithmetic and copies ran while one was open for 4% of the time, Pallas kernels for 8%

profile of v3, /device:TPU:0, one launch (start us, length us, event | category | flops | bytes accessed | tf_op | source)
XLA Modules:
  0.0 69.0 jit_solution(2607932641972899841)
XLA Ops:
  0.6 1.5 %copy-done = bf16[3,3,3,128,256]{4,3,2,1,0:T(8,128)(2,1)S(1)} copy-done((bf16[3,3,3,128,256]{4,3,2,1,0:T(8,128)(2,1)S(1)}, bf16[3,3,3,128,256]{4,3,2,1,0:T(8,128)(2,1)}, u32[]{:S(2)}) %copy-start) | copy-done | bytes 1769496
  2.1 1.2 %copy-done.2 = bf16[1,4,32,32,128]{4,3,2,1,0:T(8,128)(2,1)S(1)} copy-done((bf16[1,4,32,32,128]{4,3,2,1,0:T(8,128)(2,1)S(1)}, bf16[1,4,32,32,128]{4,3,2,1,0:T(8,128)(2,1)}, u32[]{:S(2)}) %copy-start.2) | copy-done | bytes 1048600
  3.7 5.0 %collective-permute-start = (bf16[256,256]{1,0:T(8,128)(2,1)S(1)}, bf16[256,256]{1,0:T(8,128)(2,1)S(1)}, u32[]{:S(2)}, u32[]{:S(2)}) collective-permute-start(bf16[256,256]{1,0:T(8,128)(2,1)S(1)} %shard_map.59), channel_id=1, source_target_pairs={{0,1},{1,2},{2,3},{4,5},{5,6},{6,7},{8,9},{9,10},{10,11},{12,13},{... | collective-permute-start | bytes 393224 | tf_op jit(solution)/shard_map/ppermute | solution.py:354
  8.7 1.4 %shard_map.58 = (f32[512,256]{1,0:T(8,128)S(1)}, bf16[4,16,16,384]{3,2,1,0:T(8,128)(2,1)S(1)}, bf16[4,17,16,384]{3,2,1,0:T(8,128)(2,1)S(1)}) custom-call(bf16[1,4,32,32,128]{4,3,2,1,0:T(8,128)(2,1)S(1)} %copy-done.2, bf16[3,3,3,128,256]{4,3,2,1,0:T(8,128)(2,1)S(1)} %copy-done), custom_call_target="tpu_custom_call" | custom-call | flops 905969664 | bytes 6291456 | tf_op jit(solution)/shard_map/pallas_call | solution.py:117
  10.1 1.3 %collective-permute-done.share_ref = bf16[256,256]{1,0:T(8,128)(2,1)S(1)} collective-permute-done((bf16[256,256]{1,0:T(8,128)(2,1)S(1)}, bf16[256,256]{1,0:T(8,128)(2,1)S(1)}, u32[]{:S(2)}, u32[]{:S(2)}) %collective-permute-start) | collective-permute-done | bytes 131104 | tf_op jit(solution)/shard_map/ppermute | solution.py:354
  11.4 1.0 %shard_map.60 = (bf16[512,256]{1,0:T(8,128)(2,1)S(1)}, bf16[256,512]{1,0:T(8,128)(2,1)}) custom-call(f32[512,256]{1,0:T(8,128)S(1)} %get-tuple-element.12.preact_ref, bf16[256,256]{1,0:T(8,128)(2,1)S(1)} %collective-permute-done.share_ref, bf16[512,256]{1,0:T(8,128)(2,1)S(1)} %bitcast.56), custom_call_target="tpu_custom_call" | custom-call | flops 2621440 | bytes 2097152 | tf_op jit(solution)/shard_map/pallas_call | solution.py:146
  12.4 1.3 %collective-permute-start.1 = (bf16[256,256]{1,0:T(8,128)(2,1)S(1)}, bf16[256,256]{1,0:T(8,128)(2,1)S(1)}, u32[]{:S(2)}, u32[]{:S(2)}) collective-permute-start(bf16[256,256]{1,0:T(8,128)(2,1)S(1)} %slice.12), channel_id=1, source_target_pairs={{1,0},{2,1},{3,2},{5,4},{6,5},{7,6},{9,8},{10,9},{11,10},{13,12},{... | collective-permute-start | bytes 393224 | tf_op jit(solution)/shard_map/ppermute | solution.py:354
  13.7 6.0 %collective-permute-done.1.above_ref.refs_3_ = bf16[256,256]{1,0:T(8,128)(2,1)S(1)} collective-permute-done((bf16[256,256]{1,0:T(8,128)(2,1)S(1)}, bf16[256,256]{1,0:T(8,128)(2,1)S(1)}, u32[]{:S(2)}, u32[]{:S(2)}) %collective-permute-start.1) | collective-permute-done | bytes 131104 | tf_op jit(solution)/shard_map/ppermute | solution.py:354
  19.7 0.5 shard_map.63
  20.3 0.8 %copy-done.3 = f32[4,18,16,128]{3,2,1,0:T(8,128)} copy-done((f32[4,18,16,128]{3,2,1,0:T(8,128)}, f32[4,18,16,128]{3,2,1,0:T(8,128)S(1)}, u32[]{:S(2)}) %copy-start.3) | copy-done | bytes 589848
  21.1 1.7 %shard_map.62 = (f32[36,4,16,128]{3,2,1,0:T(8,128)S(1)}, bf16[36,4,16,128]{3,2,1,0:T(8,128)(2,1)}) custom-call(bf16[4,16,16,384]{3,2,1,0:T(8,128)(2,1)S(1)} %get-tuple-element.15.refs_0_, bf16[4,17,16,384]{3,2,1,0:T(8,128)(2,1)S(1)} %get-tuple-element.16.refs_1_, bf16[512,256]{1,0:T(8,128)(2,1)S(1)} %get-tuple-element.14.grads_ref.refs_2_), custom_call_target="tpu_custom_call" | custom-call | flops 603979776 | bytes 6291456 | tf_op jit(solution)/shard_map/pallas_call | solution.py:212
  22.8 0.5 collective-permute-start.2
  23.3 1.0 %convert_add_fusion.1 = f32[4,18,16,128]{3,2,1,0:T(8,128)S(1)} fusion(f32[4,18,16,128]{3,2,1,0:T(8,128)S(1)} %copy-done.4, bf16[4,18,16,128]{3,2,1,0:T(8,128)(2,1)} %collective-permute-done.7), kind=kLoop, calls=%fused_computation.2 | loop fusion | flops 294912 | bytes 1474560 | tf_op jit(solution)/shard_map/add | solution.py:360
  24.3 1.6 %collective-permute-start.8 = (bf16[2,18,16,128]{3,2,1,0:T(8,128)(2,1)S(1)}, bf16[2,18,16,128]{3,2,1,0:T(8,128)(2,1)S(1)}, u32[]{:S(2)}, u32[]{:S(2)}) collective-permute-start(bf16[2,18,16,128]{3,2,1,0:T(8,128)(2,1)S(1)} %fusion.3), channel_id=1, source_target_pairs={{0,8},{1,9},{2,10},{3,11},{4,12},{5,13},{6,14},{7,15},{8,0},{9,1},... | collective-permute-start | bytes 442376 | tf_op jit(solution)/shard_map/ppermute | solution.py:290
  26.0 4.2 %collective-permute-done.8 = bf16[2,18,16,128]{3,2,1,0:T(8,128)(2,1)S(1)} collective-permute-done((bf16[2,18,16,128]{3,2,1,0:T(8,128)(2,1)S(1)}, bf16[2,18,16,128]{3,2,1,0:T(8,128)(2,1)S(1)}, u32[]{:S(2)}, u32[]{:S(2)}) %collective-permute-start.8) | collective-permute-done | bytes 147488 | tf_op jit(solution)/shard_map/ppermute | solution.py:290
  30.2 2.7 %collective-permute-start.9 = (bf16[1,18,16,128]{3,2,1,0:T(8,128)(2,1)S(1)}, bf16[1,18,16,128]{3,2,1,0:T(8,128)(2,1)S(1)}, u32[]{:S(2)}, u32[]{:S(2)}) collective-permute-start(bf16[1,18,16,128]{3,2,1,0:T(8,128)(2,1)S(1)} %dynamic-slice_convert_fusion.3), channel_id=1, source_target_pairs={{0,16},{1,17},{2,18},{3,19},{4,20},{5,21},{6,22},{7,23},{8,24},{9,... | collective-permute-start | bytes 221192 | tf_op jit(solution)/shard_map/ppermute | solution.py:290
  33.2 3.0 %collective-permute-start.3 = (bf16[18,4,16,128]{3,2,1,0:T(8,128)(2,1)S(1)}, bf16[18,4,16,128]{3,2,1,0:T(8,128)(2,1)S(1)}, u32[]{:S(2)}, u32[]{:S(2)}) collective-permute-start(bf16[18,4,16,128]{3,2,1,0:T(8,128)(2,1)S(1)} %fusion), channel_id=1, source_target_pairs={{0,1},{1,0},{2,3},{3,2},{4,6},{5,7},{6,4},{7,5},{8,9},{9,8},{10,11... | collective-permute-start | bytes 884744 | tf_op jit(solution)/shard_map/ppermute | solution.py:290
  36.2 2.4 %collective-permute-start.10 = (bf16[10,16,128]{2,1,0:T(8,128)(2,1)S(1)}, bf16[10,16,128]{2,1,0:T(8,128)(2,1)S(1)}, u32[]{:S(2)}, u32[]{:S(2)}) collective-permute-start(bf16[10,16,128]{2,1,0:T(8,128)(2,1)S(1)} %fusion.5), channel_id=1, source_target_pairs={{0,1},{1,0},{2,3},{3,2},{4,6},{5,7},{6,4},{7,5},{8,9},{9,8},{10,11... | collective-permute-start | bytes 122888 | tf_op jit(solution)/shard_map/ppermute | solution.py:290
  38.6 2.2 %collective-permute-done.3 = bf16[18,4,16,128]{3,2,1,0:T(8,128)(2,1)S(1)} collective-permute-done((bf16[18,4,16,128]{3,2,1,0:T(8,128)(2,1)S(1)}, bf16[18,4,16,128]{3,2,1,0:T(8,128)(2,1)S(1)}, u32[]{:S(2)}, u32[]{:S(2)}) %collective-permute-start.3) | collective-permute-done | bytes 294944 | tf_op jit(solution)/shard_map/ppermute | solution.py:290
  41.0 2.1 %collective-permute-start.4 = (bf16[9,4,16,128]{3,2,1,0:T(8,128)(2,1)S(1)}, bf16[9,4,16,128]{3,2,1,0:T(8,128)(2,1)S(1)}, u32[]{:S(2)}, u32[]{:S(2)}) collective-permute-start(bf16[9,4,16,128]{3,2,1,0:T(8,128)(2,1)S(1)} %fusion.2), channel_id=1, source_target_pairs={{0,2},{1,3},{2,0},{3,1},{4,5},{5,4},{6,7},{7,6},{8,10},{9,11},{10,... | collective-permute-start | bytes 442376 | tf_op jit(solution)/shard_map/ppermute | solution.py:290
  43.1 3.1 %collective-permute-done.4 = bf16[9,4,16,128]{3,2,1,0:T(8,128)(2,1)S(1)} collective-permute-done((bf16[9,4,16,128]{3,2,1,0:T(8,128)(2,1)S(1)}, bf16[9,4,16,128]{3,2,1,0:T(8,128)(2,1)S(1)}, u32[]{:S(2)}, u32[]{:S(2)}) %collective-permute-start.4) | collective-permute-done | bytes 147488 | tf_op jit(solution)/shard_map/ppermute | solution.py:290
  46.3 1.6 %collective-permute-start.5 = (bf16[2,9,16,128]{3,2,1,0:T(8,128)(2,1)S(1)}, bf16[2,9,16,128]{3,2,1,0:T(8,128)(2,1)S(1)}, u32[]{:S(2)}, u32[]{:S(2)}) collective-permute-start(bf16[2,9,16,128]{3,2,1,0:T(8,128)(2,1)S(1)} %fusion.4), channel_id=1, source_target_pairs={{0,8},{1,9},{2,10},{3,11},{4,12},{5,13},{6,14},{7,15},{8,0},{9,1},... | collective-permute-start | bytes 221192 | tf_op jit(solution)/shard_map/ppermute | solution.py:290
  47.9 2.0 %collective-permute-start.11 = (bf16[5,16,128]{2,1,0:T(8,128)(2,1)S(1)}, bf16[5,16,128]{2,1,0:T(8,128)(2,1)S(1)}, u32[]{:S(2)}, u32[]{:S(2)}) collective-permute-start(bf16[5,16,128]{2,1,0:T(8,128)(2,1)S(1)} %fusion.7), channel_id=1, source_target_pairs={{0,2},{1,3},{2,0},{3,1},{4,5},{5,4},{6,7},{7,6},{8,10},{9,11},{10,... | collective-permute-start | bytes 61448 | tf_op jit(solution)/shard_map/ppermute | solution.py:290
  50.0 1.1 %collective-permute-done.5 = bf16[2,9,16,128]{3,2,1,0:T(8,128)(2,1)S(1)} collective-permute-done((bf16[2,9,16,128]{3,2,1,0:T(8,128)(2,1)S(1)}, bf16[2,9,16,128]{3,2,1,0:T(8,128)(2,1)S(1)}, u32[]{:S(2)}, u32[]{:S(2)}) %collective-permute-start.5) | collective-permute-done | bytes 73760 | tf_op jit(solution)/shard_map/ppermute | solution.py:290
  51.7 4.3 %collective-permute-done.6 = bf16[1,9,16,128]{3,2,1,0:T(8,128)(2,1)S(1)} collective-permute-done((bf16[1,9,16,128]{3,2,1,0:T(8,128)(2,1)S(1)}, bf16[1,9,16,128]{3,2,1,0:T(8,128)(2,1)S(1)}, u32[]{:S(2)}, u32[]{:S(2)}) %collective-permute-start.6) | collective-permute-done | bytes 36896 | tf_op jit(solution)/shard_map/ppermute | solution.py:290
  56.1 2.1 %collective-permute-start.12 = (bf16[1,14,16,128]{3,2,1,0:T(8,128)(2,1)S(1)}, bf16[1,14,16,128]{3,2,1,0:T(8,128)(2,1)S(1)}, u32[]{:S(2)}, u32[]{:S(2)}) collective-permute-start(bf16[1,14,16,128]{3,2,1,0:T(8,128)(2,1)S(1)} %pad_maximum_fusion.1), channel_id=1, source_target_pairs={{0,2},{1,3},{2,0},{3,1},{4,5},{5,4},{6,7},{7,6},{8,10},{9,11},{10,... | collective-permute-start | bytes 172040 | tf_op jit(solution)/shard_map/ppermute | solution.py:290
  58.2 3.4 %all-to-all-start = ((bf16[4,64,512]{2,1,0:T(8,128)(2,1)}), bf16[4,64,512]{2,1,0:T(8,128)(2,1)S(1)}, u32[]{:S(2)}, u32[]{:S(2)}) async-start(bf16[4,64,512]{2,1,0:T(8,128)(2,1)} %bitcast.1), calls=%async_computation | async-start | bytes 524288 | tf_op jit(solution)/shard_map/all_to_all | solution.py:403
  61.6 2.0 %collective-permute-start.13 = (bf16[2,14,16,128]{3,2,1,0:T(8,128)(2,1)S(1)}, bf16[2,14,16,128]{3,2,1,0:T(8,128)(2,1)S(1)}, u32[]{:S(2)}, u32[]{:S(2)}) collective-permute-start(bf16[2,14,16,128]{3,2,1,0:T(8,128)(2,1)S(1)} %maximum_select_fusion.1), channel_id=1, source_target_pairs={{0,1},{1,0},{2,3},{3,2},{4,6},{5,7},{6,4},{7,5},{8,9},{9,8},{10,11... | collective-permute-start | bytes 344072 | tf_op jit(solution)/shard_map/ppermute | solution.py:290
  63.7 2.6 %shard_map.61 = bf16[4,16,2,32,128]{4,3,2,1,0:T(8,128)(2,1)} custom-call(bf16[512,256]{1,0:T(8,128)(2,1)S(1)} %get-tuple-element.14.grads_ref.refs_2_, bf16[256,256]{1,0:T(8,128)(2,1)S(1)} %collective-permute-done.1.above_ref.refs_3_, bf16[3,3,3,128,256]{4,3,2,1,0:T(8,128)(2,1)S(1)} %copy-done.1), custom_call_target="tpu_custom_call" | custom-call | flops 905969664 | bytes 4194304 | tf_op jit(solution)/shard_map/pallas_call | solution.py:265
  66.3 0.7 all-to-all-done
  67.2 0.9 %reshape.106 = bf16[1,64,2048]{2,1,0:T(8,128)(2,1)} reshape(bf16[64,4,512]{2,1,0:T(4,128)(2,1)S(1)} %copy.11) | data formatting | bytes 524288 | tf_op jit(solution)/shard_map/reshape | solution.py:406
  68.2 0.8 %copy_bitcast_fusion = f32[3,3,3,16,256]{4,3,2,1,0:T(8,128)} fusion(bf16[3,3,3,2,16,128]{5,4,3,2,1,0:T(8,128)(2,1)S(1)} %bitcast.66), kind=kLoop, calls=%fused_computation.4 | loop fusion | flops 110592 | bytes 663552 | tf_op jit(solution)/shard_map/convert_element_type | solution.py:412
  (47 shorter events, 1.9 us)
Async XLA Ops:
  0.6 1.5 %copy-start = (bf16[3,3,3,128,256]{4,3,2,1,0:T(8,128)(2,1)S(1)}, bf16[3,3,3,128,256]{4,3,2,1,0:T(8,128)(2,1)}, u32[]{:S(2)}) copy-start(bf16[3,3,3,128,256]{4,3,2,1,0:T(8,128)(2,1)} %kernel_ref.5) | copy-start | bytes 5308420
  2.1 1.2 %copy-start.2 = (bf16[1,4,32,32,128]{4,3,2,1,0:T(8,128)(2,1)S(1)}, bf16[1,4,32,32,128]{4,3,2,1,0:T(8,128)(2,1)}, u32[]{:S(2)}) copy-start(bf16[1,4,32,32,128]{4,3,2,1,0:T(8,128)(2,1)} %plane_ref.1) | copy-start | bytes 3145732
  3.7 7.7 %copy-start.5 = (bf16[1,2,16,16,256]{4,3,2,1,0:T(8,128)(2,1)S(1)}, bf16[1,2,16,16,256]{4,3,2,1,0:T(8,128)(2,1)}, u32[]{:S(2)}) copy-start(bf16[1,2,16,16,256]{4,3,2,1,0:T(8,128)(2,1)} %param.5) | copy-start | bytes 786436
  3.7 7.7 %collective-permute-start = (bf16[256,256]{1,0:T(8,128)(2,1)S(1)}, bf16[256,256]{1,0:T(8,128)(2,1)S(1)}, u32[]{:S(2)}, u32[]{:S(2)}) collective-permute-start(bf16[256,256]{1,0:T(8,128)(2,1)S(1)} %shard_map.59), channel_id=1, source_target_pairs={{0,1},{1,2},{2,3},{4,5},{5,6},{6,7},{8,9},{9,10},{10,11},{12,13},{... | collective-permute-start | bytes 393224 | tf_op jit(solution)/shard_map/ppermute | solution.py:354
  12.4 7.3 %collective-permute-start.1 = (bf16[256,256]{1,0:T(8,128)(2,1)S(1)}, bf16[256,256]{1,0:T(8,128)(2,1)S(1)}, u32[]{:S(2)}, u32[]{:S(2)}) collective-permute-start(bf16[256,256]{1,0:T(8,128)(2,1)S(1)} %slice.12), channel_id=1, source_target_pairs={{1,0},{2,1},{3,2},{5,4},{6,5},{7,6},{9,8},{10,9},{11,10},{13,12},{... | collective-permute-start | bytes 393224 | tf_op jit(solution)/shard_map/ppermute | solution.py:354
  20.3 0.8 %copy-start.3 = (f32[4,18,16,128]{3,2,1,0:T(8,128)}, f32[4,18,16,128]{3,2,1,0:T(8,128)S(1)}, u32[]{:S(2)}) copy-start(f32[4,18,16,128]{3,2,1,0:T(8,128)S(1)} %get-tuple-element.19) | copy-start | bytes 1769476
  21.1 2.2 %collective-permute-start.7 = (bf16[4,18,16,128]{3,2,1,0:T(8,128)(2,1)S(1)}, bf16[4,18,16,128]{3,2,1,0:T(8,128)(2,1)}, u32[]{:S(2)}, u32[]{:S(2)}) collective-permute-start(bf16[4,18,16,128]{3,2,1,0:T(8,128)(2,1)S(1)} %get-tuple-element.20), channel_id=1, source_target_pairs={{0,4},{1,5},{2,6},{3,7},{4,0},{5,1},{6,2},{7,3},{8,12},{9,13},{10,... | collective-permute-start | bytes 884744 | tf_op jit(solution)/shard_map/ppermute | solution.py:290
  21.1 2.2 %copy-start.4 = (f32[4,18,16,128]{3,2,1,0:T(8,128)S(1)}, f32[4,18,16,128]{3,2,1,0:T(8,128)}, u32[]{:S(2)}) copy-start(f32[4,18,16,128]{3,2,1,0:T(8,128)} %copy-done.3) | copy-start | bytes 1769476
  22.8 10.1 %collective-permute-start.2 = (bf16[36,4,16,128]{3,2,1,0:T(8,128)(2,1)}, bf16[36,4,16,128]{3,2,1,0:T(8,128)(2,1)S(1)}, u32[]{:S(2)}, u32[]{:S(2)}) collective-permute-start(bf16[36,4,16,128]{3,2,1,0:T(8,128)(2,1)} %get-tuple-element.18), channel_id=1, source_target_pairs={{0,4},{1,5},{2,6},{3,7},{4,0},{5,1},{6,2},{7,3},{8,12},{9,13},{10,... | collective-permute-start | bytes 1769480 | tf_op jit(solution)/shard_map/ppermute | solution.py:290
  24.3 5.8 %collective-permute-start.8 = (bf16[2,18,16,128]{3,2,1,0:T(8,128)(2,1)S(1)}, bf16[2,18,16,128]{3,2,1,0:T(8,128)(2,1)S(1)}, u32[]{:S(2)}, u32[]{:S(2)}) collective-permute-start(bf16[2,18,16,128]{3,2,1,0:T(8,128)(2,1)S(1)} %fusion.3), channel_id=1, source_target_pairs={{0,8},{1,9},{2,10},{3,11},{4,12},{5,13},{6,14},{7,15},{8,0},{9,1},... | collective-permute-start | bytes 442376 | tf_op jit(solution)/shard_map/ppermute | solution.py:290
  30.2 5.9 %collective-permute-start.9 = (bf16[1,18,16,128]{3,2,1,0:T(8,128)(2,1)S(1)}, bf16[1,18,16,128]{3,2,1,0:T(8,128)(2,1)S(1)}, u32[]{:S(2)}, u32[]{:S(2)}) collective-permute-start(bf16[1,18,16,128]{3,2,1,0:T(8,128)(2,1)S(1)} %dynamic-slice_convert_fusion.3), channel_id=1, source_target_pairs={{0,16},{1,17},{2,18},{3,19},{4,20},{5,21},{6,22},{7,23},{8,24},{9,... | collective-permute-start | bytes 221192 | tf_op jit(solution)/shard_map/ppermute | solution.py:290
  33.2 7.7 %collective-permute-start.3 = (bf16[18,4,16,128]{3,2,1,0:T(8,128)(2,1)S(1)}, bf16[18,4,16,128]{3,2,1,0:T(8,128)(2,1)S(1)}, u32[]{:S(2)}, u32[]{:S(2)}) collective-permute-start(bf16[18,4,16,128]{3,2,1,0:T(8,128)(2,1)S(1)} %fusion), channel_id=1, source_target_pairs={{0,1},{1,0},{2,3},{3,2},{4,6},{5,7},{6,4},{7,5},{8,9},{9,8},{10,11... | collective-permute-start | bytes 884744 | tf_op jit(solution)/shard_map/ppermute | solution.py:290
  36.2 6.9 %collective-permute-start.10 = (bf16[10,16,128]{2,1,0:T(8,128)(2,1)S(1)}, bf16[10,16,128]{2,1,0:T(8,128)(2,1)S(1)}, u32[]{:S(2)}, u32[]{:S(2)}) collective-permute-start(bf16[10,16,128]{2,1,0:T(8,128)(2,1)S(1)} %fusion.5), channel_id=1, source_target_pairs={{0,1},{1,0},{2,3},{3,2},{4,6},{5,7},{6,4},{7,5},{8,9},{9,8},{10,11... | collective-permute-start | bytes 122888 | tf_op jit(solution)/shard_map/ppermute | solution.py:290
  41.0 5.2 %collective-permute-start.4 = (bf16[9,4,16,128]{3,2,1,0:T(8,128)(2,1)S(1)}, bf16[9,4,16,128]{3,2,1,0:T(8,128)(2,1)S(1)}, u32[]{:S(2)}, u32[]{:S(2)}) collective-permute-start(bf16[9,4,16,128]{3,2,1,0:T(8,128)(2,1)S(1)} %fusion.2), channel_id=1, source_target_pairs={{0,2},{1,3},{2,0},{3,1},{4,5},{5,4},{6,7},{7,6},{8,10},{9,11},{10,... | collective-permute-start | bytes 442376 | tf_op jit(solution)/shard_map/ppermute | solution.py:290
  46.2 17.5 %copy-start.1 = (bf16[3,3,3,128,256]{4,3,2,1,0:T(8,128)(2,1)S(1)}, bf16[3,3,3,128,256]{4,3,2,1,0:T(8,128)(2,1)}, u32[]{:S(2)}) copy-start(bf16[3,3,3,128,256]{4,3,2,1,0:T(8,128)(2,1)} %kernel_ref.5) | copy-start | bytes 5308420
  46.3 4.8 %collective-permute-start.5 = (bf16[2,9,16,128]{3,2,1,0:T(8,128)(2,1)S(1)}, bf16[2,9,16,128]{3,2,1,0:T(8,128)(2,1)S(1)}, u32[]{:S(2)}, u32[]{:S(2)}) collective-permute-start(bf16[2,9,16,128]{3,2,1,0:T(8,128)(2,1)S(1)} %fusion.4), channel_id=1, source_target_pairs={{0,8},{1,9},{2,10},{3,11},{4,12},{5,13},{6,14},{7,15},{8,0},{9,1},... | collective-permute-start | bytes 221192 | tf_op jit(solution)/shard_map/ppermute | solution.py:290
  47.9 3.8 %collective-permute-start.11 = (bf16[5,16,128]{2,1,0:T(8,128)(2,1)S(1)}, bf16[5,16,128]{2,1,0:T(8,128)(2,1)S(1)}, u32[]{:S(2)}, u32[]{:S(2)}) collective-permute-start(bf16[5,16,128]{2,1,0:T(8,128)(2,1)S(1)} %fusion.7), channel_id=1, source_target_pairs={{0,2},{1,3},{2,0},{3,1},{4,5},{5,4},{6,7},{7,6},{8,10},{9,11},{10,... | collective-permute-start | bytes 61448 | tf_op jit(solution)/shard_map/ppermute | solution.py:290
  51.2 4.9 %collective-permute-start.6 = (bf16[1,9,16,128]{3,2,1,0:T(8,128)(2,1)S(1)}, bf16[1,9,16,128]{3,2,1,0:T(8,128)(2,1)S(1)}, u32[]{:S(2)}, u32[]{:S(2)}) collective-permute-start(bf16[1,9,16,128]{3,2,1,0:T(8,128)(2,1)S(1)} %dynamic-slice_convert_fusion.6), channel_id=1, source_target_pairs={{0,16},{1,17},{2,18},{3,19},{4,20},{5,21},{6,22},{7,23},{8,24},{9,... | collective-permute-start | bytes 110600 | tf_op jit(solution)/shard_map/ppermute | solution.py:290
  56.1 5.5 %collective-permute-start.12 = (bf16[1,14,16,128]{3,2,1,0:T(8,128)(2,1)S(1)}, bf16[1,14,16,128]{3,2,1,0:T(8,128)(2,1)S(1)}, u32[]{:S(2)}, u32[]{:S(2)}) collective-permute-start(bf16[1,14,16,128]{3,2,1,0:T(8,128)(2,1)S(1)} %pad_maximum_fusion.1), channel_id=1, source_target_pairs={{0,2},{1,3},{2,0},{3,1},{4,5},{5,4},{6,7},{7,6},{8,10},{9,11},{10,... | collective-permute-start | bytes 172040 | tf_op jit(solution)/shard_map/ppermute | solution.py:290
  58.2 8.8 %all-to-all-start = ((bf16[4,64,512]{2,1,0:T(8,128)(2,1)}), bf16[4,64,512]{2,1,0:T(8,128)(2,1)S(1)}, u32[]{:S(2)}, u32[]{:S(2)}) async-start(bf16[4,64,512]{2,1,0:T(8,128)(2,1)} %bitcast.1), calls=%async_computation | async-start | bytes 524288 | tf_op jit(solution)/shard_map/all_to_all | solution.py:403
  61.6 6.4 %collective-permute-start.13 = (bf16[2,14,16,128]{3,2,1,0:T(8,128)(2,1)S(1)}, bf16[2,14,16,128]{3,2,1,0:T(8,128)(2,1)S(1)}, u32[]{:S(2)}, u32[]{:S(2)}) collective-permute-start(bf16[2,14,16,128]{3,2,1,0:T(8,128)(2,1)S(1)} %maximum_select_fusion.1), channel_id=1, source_target_pairs={{0,1},{1,0},{2,3},{3,2},{4,6},{5,7},{6,4},{7,5},{8,9},{9,8},{10,11... | collective-permute-start | bytes 344072 | tf_op jit(solution)/shard_map/ppermute | solution.py:290

commit v4 on v3

--- a/solution.py
+++ b/solution.py
@@ -10,21 +10,24 @@
 
 BF16 = jnp.bfloat16
 F32 = jnp.float32
-VMEM_LIMIT = 40 * 1024 * 1024
-
-
-def params():
-    return pltpu.CompilerParams(vmem_limit_bytes=VMEM_LIMIT)
-
-
-def call(kernel, out_shape, scratch=(), flops=0, moved=0):
+VMEM_LIMIT = 20 * 1024 * 1024
+VMEM_WHOLE = 60 * 1024 * 1024
+
+
+def call(kernel, out_shape, scratch=(), in_specs=None, limit=VMEM_LIMIT):
+    extra = {} if in_specs is None else {"in_specs": in_specs}
     return pl.pallas_call(
         kernel,
         out_shape=out_shape,
         scratch_shapes=list(scratch),
-        compiler_params=params(),
-        cost_estimate=pl.CostEstimate(flops=flops, bytes_accessed=moved, transcendentals=0),
+        compiler_params=pltpu.CompilerParams(vmem_limit_bytes=limit),
+        cost_estimate=pl.CostEstimate(flops=1000, bytes_accessed=1000, transcendentals=0),
+        **extra,
     )
+
+
+def after(value, *others):
+    return lax.optimization_barrier((value,) + others)[0]
 
 
 def spread_plane(plane, wide):
@@ -48,14 +51,51 @@
     return picked.reshape(height * even.shape[2], even.shape[3])
 
 
-def halo_kernel(plane_ref, kernel_ref, share_ref, wide):
-    _, _, height, width, chans = plane_ref.shape
-    even, odd = spread_plane(plane_ref[0, 0], wide)
+def bits_of(count):
+    bits = count.bit_length() - 1
+    assert 1 << bits == count
+    return bits
+
+
+def odd_core(cores):
+    return lax.axis_index("dp") % cores == 1 if cores == 2 else False
+
+
+def reverse_bits(value, bits):
+    return sum(((value >> bit) & 1) << (bits - 1 - bit) for bit in range(bits))
+
+
+def staged_place(target, space, cores):
+    return jnp.where(odd_core(cores), target, reverse_bits(target, bits_of(space)))
+
+
+def relative_place(source, space, cores):
+    bits = bits_of(space)
+    off = source ^ lax.axis_index("space")
+    return jnp.where(odd_core(cores), reverse_bits(off, bits), off)
+
+
+def relative_group(group, space, cores):
+    bits = bits_of(space)
+    index = lax.axis_index("space")
+    mine = jnp.where(odd_core(cores), index, reverse_bits(index, bits))
+    return group ^ mine
+
+
+def halo_kernel(volume_ref, kernel_ref, share_ref, plane, weights, wide, sems):
+    planes, height, width, chans = volume_ref.shape[1:]
+    first = pltpu.make_async_copy(volume_ref.at[0, planes - 1], plane, sems.at[0])
+    second = pltpu.make_async_copy(kernel_ref.at[0], weights, sems.at[1])
+    first.start()
+    second.start()
+    first.wait()
+    even, odd = spread_plane(plane[...], wide)
     above = jnp.concatenate([jnp.zeros_like(odd[:1]), odd[:-1]], axis=0)
+    second.wait()
     total = None
     for kh, rows in enumerate((above, even, odd)):
         lhs = rows.reshape(height * width // 4, 3 * chans)
-        rhs = kernel_ref[0, kh].reshape(3 * chans, kernel_ref.shape[-1])
+        rhs = weights[kh].reshape(3 * chans, weights.shape[-1])
         term = jnp.dot(lhs, rhs, preferred_element_type=F32)
         total = term if total is None else total + term
     share_ref[...] = total.astype(BF16)
@@ -64,47 +104,58 @@
 def halo_share(volume, kernel):
     _, planes, height, width, chans = volume.shape
     co = kernel.shape[-1]
-    cells = height * width // 4
-    return pl.pallas_call(
+    return call(
         halo_kernel,
-        grid=(1,),
-        out_shape=jax.ShapeDtypeStruct((cells, co), BF16),
-        in_specs=[
-            pl.BlockSpec((1, 1, height, width, chans), lambda i: (0, planes - 1, 0, 0, 0)),
-            pl.BlockSpec((1, 3, 3, chans, co), lambda i: (0, 0, 0, 0, 0)),
+        jax.ShapeDtypeStruct((height * width // 4, co), BF16),
+        [
+            pltpu.VMEM((height, width, chans), BF16),
+            pltpu.VMEM((3, 3, chans, co), BF16),
+            pltpu.VMEM((height * width + 16, chans), F32),
+            pltpu.SemaphoreType.DMA((2,)),
         ],
-        out_specs=pl.BlockSpec((cells, co), lambda i: (0, 0)),
-        scratch_shapes=[pltpu.VMEM((height * width + 16, chans), F32)],
-        compiler_params=params(),
-        cost_estimate=pl.CostEstimate(
-            flops=2 * cells * 9 * chans * co, bytes_accessed=2**20, transcendentals=0
-        ),
+        [pl.BlockSpec(memory_space=pltpu.HBM)] * 2,
+        VMEM_WHOLE,
     )(volume, kernel)
 
 
-def preact_kernel(volume_ref, kernel_ref, preact_ref, even_ref, odd_ref, wide):
-    _, planes, height, width, chans = volume_ref.shape
+def preact_kernel(volume_ref, kernel_ref, preact_ref, even_ref, odd_ref, slab, weights, wide, sems):
+    planes, height, width, chans = volume_ref.shape[1:]
     cells = height * width // 4
     outs = planes // 2
+    copies = [
+        pltpu.make_async_copy(volume_ref.at[0, plane], slab.at[plane], sems.at[plane])
+        for plane in range(planes)
+    ]
+    loads = {
+        kd: pltpu.make_async_copy(kernel_ref.at[kd], weights.at[kd], sems.at[planes + kd])
+        for kd in range(3)
+    }
+    for copy in copies:
+        copy.start()
+    for kd in (1, 2, 0):
+        loads[kd].start()
     for plane in range(planes):
-        even, odd = spread_plane(volume_ref[0, plane], wide)
+        copies[plane].wait()
+        even, odd = spread_plane(slab[plane], wide)
         even_ref[plane] = even
         odd_ref[plane, pl.ds(0, 1)] = jnp.zeros_like(odd[:1])
         odd_ref[plane, pl.ds(1, height // 2)] = odd
     co = kernel_ref.shape[-1]
     total = None
     for kd in (1, 2):
+        loads[kd].wait()
         for kh in range(3):
             lhs = [tap_rows(even_ref, odd_ref, 2 * d - 1 + kd, kh) for d in range(outs)]
-            rhs = kernel_ref[kd, kh].reshape(3 * chans, co)
+            rhs = weights[kd, kh].reshape(3 * chans, co)
             term = jnp.dot(jnp.concatenate(lhs, axis=0), rhs, preferred_element_type=F32)
             total = term if total is None else total + term
     preact_ref[...] = total
+    loads[0].wait()
     if outs > 1:
         total = preact_ref[pl.ds(cells, (outs - 1) * cells), :]
         for kh in range(3):
             lhs = [tap_rows(even_ref, odd_ref, 2 * d - 1, kh) for d in range(1, outs)]
-            rhs = kernel_ref[0, kh].reshape(3 * chans, co)
+            rhs = weights[0, kh].reshape(3 * chans, co)
             total += jnp.dot(jnp.concatenate(lhs, axis=0), rhs, preferred_element_type=F32)
         preact_ref[pl.ds(cells, (outs - 1) * cells), :] = total
 
@@ -121,15 +172,21 @@
             jax.ShapeDtypeStruct((planes, h2, w2, 3 * chans), BF16),
             jax.ShapeDtypeStruct((planes, h2 + 1, w2, 3 * chans), BF16),
         ),
-        [pltpu.VMEM((height * width + 16, chans), F32)],
-        flops=2 * planes // 2 * cells * 27 * chans * co,
-        moved=6 * 2**20,
+        [
+            pltpu.VMEM(volume.shape[1:], BF16),
+            pltpu.VMEM(kernel.shape, BF16),
+            pltpu.VMEM((height * width + 16, chans), F32),
+            pltpu.SemaphoreType.DMA((planes + 3,)),
+        ],
+        [pl.BlockSpec(memory_space=pltpu.HBM)] * 2,
     )(volume, kernel)
 
 
-def activation_kernel(preact_ref, share_ref, cotangent_ref, grad_ref, flipped_ref):
-    cells = share_ref.shape[0]
+def activation_kernel(space, cores, preact_ref, share_ref, cotangent_ref, grad_ref, flipped_ref):
+    cells, co = share_ref.shape
     count = preact_ref.shape[0] // cells
+    group = co // space
+    strips = cells // 128
     for d in range(count):
         rows = pl.ds(d * cells, cells)
         value = preact_ref[rows, :]
@@ -138,20 +195,72 @@
         sig = jax.nn.sigmoid(value)
         slope = sig * (1.0 + value * (1.0 - sig))
         grad_ref[rows, :] = (cotangent_ref[rows, :].astype(F32) * slope).astype(BF16)
-        flipped_ref[:, rows] = (value * sig).T.astype(BF16)
-
-
-def activation(preact, share, cotangent):
+        flipped = (value * sig).T.astype(BF16)
+        for target in range(space):
+            place = staged_place(target, space, cores)
+            for strip in range(strips):
+                flipped_ref[place, d * strips + strip] = flipped[
+                    target * group : (target + 1) * group, strip * 128 : (strip + 1) * 128
+                ]
+
+
+def activation(preact, share, cotangent, space, cores):
     cells, co = preact.shape
     return call(
-        activation_kernel,
+        functools.partial(activation_kernel, space, cores),
         (
             jax.ShapeDtypeStruct((cells, co), BF16),
-            jax.ShapeDtypeStruct((co, cells), BF16),
+            jax.ShapeDtypeStruct((space, cells // 128, co // space, 128), BF16),
         ),
-        flops=20 * cells * co,
-        moved=2 * 2**20,
     )(preact, share, cotangent)
+
+
+def switched_kernel(space, cores, kept_ref, got_ref, out_ref):
+    half = space // 2
+    strips = kept_ref.shape[0] // half
+    for source in range(space):
+        place = relative_place(source, space, cores)
+        for strip in range(strips):
+            column = (source * strips + strip) * 128
+            far = place // half
+            row = (place % half) * strips + strip
+            out_ref[:, column : column + 128] = jnp.where(far == 1, got_ref[row], kept_ref[row])
+
+
+def switched_of(kept, got, space, cores):
+    half = space // 2
+    group = kept.shape[-2]
+    kept = kept.reshape(-1, group, 128)
+    got = got.reshape(-1, group, 128)
+    return call(
+        functools.partial(switched_kernel, space, cores),
+        jax.ShapeDtypeStruct((group, 2 * kept.shape[0] * 128), BF16),
+    )(kept, got)
+
+
+def kernel_grad_out_kernel(space, cores, early_units, late_units, pieces_ref, out_ref):
+    block = pieces_ref.shape[2]
+    halves = out_ref.shape[-1] // 128
+    early_share = -(-early_units // space)
+    late_share = -(-late_units // space)
+    for group in range(space):
+        place = relative_group(group, space, cores)
+        for unit in range(early_share + late_share):
+            late = unit >= early_share
+            index = group * late_share + unit - early_share if late else group * early_share + unit
+            if index >= (late_units if late else early_units):
+                continue
+            index = index if late else index + late_units
+            tap, half = divmod(index, halves)
+            out_ref[tap, :, half * 128 : (half + 1) * 128] = pieces_ref[place, unit].astype(F32)
+
+
+def kernel_grad_out(pieces, early_units, late_units, space, cores, co):
+    taps = (early_units + late_units) * 128 // co
+    return call(
+        functools.partial(kernel_grad_out_kernel, space, cores, early_units, late_units),
+        jax.ShapeDtypeStruct((taps, pieces.shape[2], co), F32),
+    )(pieces)
 
 
 def store_units(product, scale, core, cores, chips, put):
@@ -212,8 +321,6 @@
     return call(
         functools.partial(kernel_grad_kernel, kds, chip_major, cores, chips, scale),
         (jax.ShapeDtypeStruct(shape, F32), jax.ShapeDtypeStruct(shape, BF16)),
-        flops=2 * grads.shape[0] * len(kds) * 9 * chans * co,
-        moved=6 * 2**20,
     )(*operands)
 
 
@@ -269,15 +376,7 @@
             pltpu.VMEM((height * width // 4 + 8, co), F32),
             pltpu.VMEM((height * width // 2, chans), F32),
         ],
-        flops=2 * cells * 27 * chans * co,
-        moved=4 * 2**20,
     )(grads, above, kernel)
-
-
-def bits_of(count):
-    bits = count.bit_length() - 1
-    assert 1 << bits == count
-    return bits
 
 
 def exchange(value, partner):
@@ -290,62 +389,44 @@
     return lax.ppermute(value, ("dp", "space"), pairs)
 
 
-def space_bit(stage, odd_core):
+def exchange_space(value, stage, cores):
     bits = bits_of(lax.axis_size("space"))
-    return bits - 1 - stage if odd_core else stage
-
-
-def space_partner(stage, cores):
-    return lambda i, j: (i, j ^ (1 << space_bit(stage, cores == 2 and i % 2 == 1)))
-
-
-def my_space_bit(stage, cores):
+
+    def partner(i, j):
+        bit = bits - 1 - stage if cores == 2 and i % 2 == 1 else stage
+        return i, j ^ (1 << bit)
+
+    return exchange(value, partner)
+
+
+def exchange_chips(value, bit, cores):
+    return exchange(value, lambda i, j: (i ^ (cores << bit), j))
+
+
+def space_bit(stage, cores):
+    bits = bits_of(lax.axis_size("space"))
     index = lax.axis_index("space")
-    even = (index >> space_bit(stage, False)) & 1
-    odd = (index >> space_bit(stage, True)) & 1
-    return jnp.where(lax.axis_index("dp") % cores == 1, odd, even) if cores == 2 else even
-
-
-def halve(value, bit):
+    even, odd = (index >> stage) & 1, (index >> (bits - 1 - stage)) & 1
+    return jnp.where(odd_core(cores), odd, even)
+
+
+def chip_bit(bit, cores):
+    return ((lax.axis_index("dp") // cores) >> bit) & 1
+
+
+def pick(value, bit):
     value = value.reshape((2, value.shape[0] // 2) + value.shape[1:])
-    keep = lax.dynamic_index_in_dim(value, bit, 0, keepdims=False)
-    send = lax.dynamic_index_in_dim(value, 1 - bit, 0, keepdims=False)
-    return keep, send.astype(BF16)
-
-
-def scatter_space(value, cores):
-    for stage in range(bits_of(lax.axis_size("space"))):
-        keep, send = halve(value, my_space_bit(stage, cores))
-        value = keep + exchange(send, space_partner(stage, cores)).astype(F32)
-    return value
-
-
-def scatter_chips(value, cores, chips):
-    order = list(range(bits_of(chips)))
-    if order:
-        rest = value.shape[1:]
-        value = value.reshape((2,) * len(order) + rest)
-        value = jnp.transpose(
-            value, tuple(reversed(order)) + tuple(range(len(order), len(order) + len(rest)))
-        )
-        value = value.reshape((chips,) + rest)
-    chip = lax.axis_index("dp") // cores
-    for bit in order:
-        keep, send = halve(value, (chip >> bit) & 1)
-        got = exchange(send, lambda i, j, bit=bit: (i ^ (cores << bit), j))
-        value = keep + got.astype(F32)
-    return value[0]
-
-
-def gather_space(value, cores):
-    value = value[None]
-    for stage in reversed(range(bits_of(lax.axis_size("space")))):
-        got = exchange(value, space_partner(stage, cores))
-        bit = my_space_bit(stage, cores)
-        value = jnp.where(
-            bit == 0, jnp.concatenate([value, got], 0), jnp.concatenate([got, value], 0)
-        )
-    return value
+    return lax.dynamic_index_in_dim(value, bit, 0, keepdims=False)
+
+
+def by_nearest(value, chips):
+    count = bits_of(chips)
+    if count < 2:
+        return value
+    rest = value.shape[1:]
+    value = value.reshape((2,) * count + rest)
+    order = tuple(reversed(range(count))) + tuple(range(count, count + len(rest)))
+    return jnp.transpose(value, order).reshape((chips,) + rest)
 
 
 def neighbour(value, steps):
@@ -360,22 +441,56 @@
     return keep + exchange(send, lambda i, j: (i ^ 1, j)).astype(F32)
 
 
-def reduce_parts(early, late, cores, chips):
-    space = lax.axis_size("space")
-    units, _, block, lanes = early.shape
-    extra = -units % space
-    early = jnp.pad(early, ((0, extra), (0, 0), (0, 0), (0, 0)))
-    early = scatter_space(early, cores)
-    early = scatter_chips(jnp.swapaxes(early, 0, 1), cores, chips)
-    late_units = late.shape[1]
-    late = scatter_chips(late, cores, chips)
-    late = jnp.pad(late, ((0, -late_units % space), (0, 0), (0, 0)))
-    late = scatter_space(late, cores)
-    full = gather_space(jnp.concatenate([early, late], axis=0).astype(BF16), cores)
-    cut = early.shape[0]
-    early = full[:, :cut].reshape(-1, block, lanes)[:units]
-    late = full[:, cut:].reshape(-1, block, lanes)[:late_units]
-    return early, late
+def pad_units(value, space):
+    extra = -value.shape[0] % space
+    return jnp.pad(value, ((0, extra),) + ((0, 0),) * (value.ndim - 1)) if extra else value
+
+
+def rows_of(value):
+    return value.reshape(-1, value.shape[-1])
+
+
+def early_chain(value, cores, chips):
+    for stage in range(bits_of(lax.axis_size("space"))):
+        bit = space_bit(stage, cores)
+        sent = pick(value, 1 - bit).astype(BF16)
+        got = exchange_space(sent, stage, cores)
+        got = after(got, *(yield sent))
+        value = pick(value, bit) + got.astype(F32)
+    value = by_nearest(jnp.swapaxes(value, 0, 1), chips)
+    for stage in range(bits_of(chips)):
+        bit = chip_bit(stage, cores)
+        sent = pick(value, 1 - bit).astype(BF16)
+        got = exchange_chips(sent, stage, cores)
+        got = after(got, *(yield sent))
+        value = pick(value, bit) + got.astype(F32)
+    return value[0]
+
+
+def late_chain(value, switch, cores, chips):
+    value = by_nearest(value, chips)
+    for stage in range(bits_of(chips)):
+        bit = chip_bit(stage, cores)
+        sent = pick(value, 1 - bit).astype(BF16)
+        got = exchange_chips(sent, stage, cores)
+        got = after(got, *(yield sent))
+        value = pick(value, bit) + got.astype(F32)
+    value = pad_units(value[0], lax.axis_size("space"))
+    stay, moved = switch[None], None
+    for stage in range(bits_of(lax.axis_size("space"))):
+        bit = space_bit(stage, cores)
+        if moved is not None:
+            stay = jnp.concatenate([stay, moved], axis=0)
+        halves = stay.reshape((stay.shape[0], 2, stay.shape[1] // 2) + stay.shape[2:])
+        out = lax.dynamic_index_in_dim(halves, 1 - bit, 1, keepdims=False)
+        stay = lax.dynamic_index_in_dim(halves, bit, 1, keepdims=False)
+        sent = pick(value, 1 - bit).astype(BF16)
+        got = exchange_space(jnp.concatenate([rows_of(sent), rows_of(out)], axis=0), stage, cores)
+        got = after(got, *(yield sent))
+        cut = sent.size // sent.shape[-1]
+        moved = got[cut:].reshape(out.shape)
+        value = pick(value, bit) + got[:cut].reshape(sent.shape).astype(F32)
+    return value, stay, moved
 
 
 def body(volume, kernel, cotangent):
@@ -391,26 +506,54 @@
 
     share = neighbour(halo_share(volume, kernel), 1)
     preact, even, odd = partial_preact(volume, kernel)
-    grads, flipped = activation(preact, share, cotangent.reshape(outs * cells, co))
-    above = neighbour(grads[:cells], -1)
+    grads, flipped = activation(preact, share, cotangent.reshape(outs * cells, co), space, cores)
+    first = grads[:cells]
+    grads, first = lax.optimization_barrier((grads, first))
+    above = neighbour(first, -1)
 
     early = kernel_grad_part(even, odd, grads, None, (1, 2), False, cores, chips, scale)
-    early = add_cores(*early, cores)
+    early_units = early[0].shape[0]
+    ahead = early_chain(pad_units(add_cores(*early, cores), space), cores, chips)
+    token = next(ahead)
+
+    above = after(above, token)
     late = kernel_grad_part(even, odd, grads, above, (0,), True, cores, chips, scale)
-    late = add_cores(*late, cores)
-    early, late = reduce_parts(early, late, cores, chips)
-
-    switched = lax.all_to_all(
-        flipped.reshape(space, co // space, outs * cells), "space", 0, 0, tiled=True
+    late_units = late[0].shape[1]
+    behind = late_chain(add_cores(*late, cores), flipped, cores, chips)
+    late_token = next(behind)
+
+    volume_grad = volume_grad_of(grads, after(above, late_token), kernel, height, width)
+    tokens = (late_token, volume_grad)
+    early_total = late_total = None
+    while early_total is None or late_total is None:
+        if early_total is None:
+            try:
+                tokens = (ahead.send(tokens),)
+            except StopIteration as end:
+                early_total = end.value
+                tokens = (early_total,)
+        if late_total is None:
+            try:
+                tokens = (behind.send(tokens),)
+            except StopIteration as end:
+                late_total, kept, arrived = end.value
+                tokens = (late_total,)
+
+    pieces = jnp.concatenate([early_total, late_total], axis=0).astype(BF16)[None]
+    switched = None
+    for stage in reversed(range(bits_of(space))):
+        got = exchange_space(pieces, stage, cores)
+        if switched is None:
+            switched = switched_of(after(kept, pieces), arrived, space, cores)
+            got = after(got, switched)
+        pieces = jnp.concatenate([pieces, got], axis=0)
+    kernel_grad = kernel_grad_out(pieces, early_units, late_units, space, cores, co)
+
+    return (
+        switched[None],
+        volume_grad.reshape(volume.shape),
+        kernel_grad.reshape(3, 3, 3, ci // dp, co),
     )
-    switched = jnp.swapaxes(switched, 0, 1).reshape(1, co // space, space * outs * cells)
-
-    volume_grad = volume_grad_of(grads, above, kernel, height, width).reshape(volume.shape)
-
-    lanes = late.shape[-1]
-    taps = jnp.concatenate([late, early], axis=0).reshape(3, 3, 3, co // lanes, ci // dp, lanes)
-    kernel_grad = jnp.swapaxes(taps, 3, 4).reshape(3, 3, 3, ci // dp, co).astype(F32)
-    return (switched, volume_grad, kernel_grad)
 
 
 def solution(mesh):

time: 69.3 us -> 60.6 us (0.87)
  waiting for transfers between devices: 23.4 us -> 17.5 us
  Pallas kernels: 7.49 us -> 12 us
  starting transfers between devices: 30 us -> 25.7 us
  local copies, waits for them, and re-layouts: 4.88 us -> 1.45 us
    ppermute x2, waiting for transfers between devices: 7.37 us -> 3.55 us  [neighbour(): lax.ppermute(value, 'space', [(source, source + steps) for source in rang...]
    all_to_all x1 -> x0, starting transfers between devices: 3.41 us -> none  [body(): lax.all_to_all(flipped.reshape(space, co // space, outs * cells), 'space'...]
    unnamed x12 -> x22, local copies, waits for them, and re-layouts: 3.52 us -> 0.35 us
    pallas_call x2 -> x4, Pallas kernels: 1.33 us -> 4.22 us  [the longest x1 2.32 us: halo_share(): call(halo_kernel, jax.ShapeDtypeStruct((height * width // 4, co), BF16),...]
    pallas_call x1, Pallas kernels: 1.38 us -> 2.98 us  [partial_preact(): call(preact_kernel, (jax.ShapeDtypeStruct((planes // 2 * cells, co), F32)...]
    ppermute x12, waiting for transfers between devices: 15.4 us -> 14 us  [exchange(): return lax.ppermute(value, ('dp', 'space'), pairs)]
    add x2, other arithmetic: 1.22 us -> 2.4 us  [add_cores(): return keep + exchange(send, lambda i, j: (i ^ 1, j)).astype(F32)]
    ppermute x12, starting transfers between devices: 20.3 us -> 19.4 us  [exchange(): return lax.ppermute(value, ('dp', 'space'), pairs)]
  transfers between devices with their start and end apart: 15 -> 14, of which waited for: 9 -> 9; matrix products, arithmetic and copies ran while one was open for 4% -> 6% of each run, Pallas kernels for 8% -> 11%
where the time goes in v4:
time: 60.6 us; the launch traced here: 60.3 us
  starting transfers between devices  25.7 us (42%)
  waiting for transfers between devices  17.5 us (29%)
  Pallas kernels  12 us (20%)
  other arithmetic  2.71 us (4%)
  local copies, waits for them, and re-layouts  1.45 us (2%)
  between operations  1.02 us (2%)
    ppermute x12, starting transfers between devices, exchange(): return lax.ppermute(value, ('dp', 'space'), pairs)  19.4 us
    ppermute x12, waiting for transfers between devices, exchange(): return lax.ppermute(value, ('dp', 'space'), pairs)  14 us
    ppermute x2, starting transfers between devices, neighbour(): lax.ppermute(value, 'space', [(source, source + steps) for source in rang...  6.27 us
    ppermute x2, waiting for transfers between devices, neighbour(): lax.ppermute(value, 'space', [(source, source + steps) for source in rang...  3.55 us
    pallas_call x1, Pallas kernels, partial_preact(): call(preact_kernel, (jax.ShapeDtypeStruct((planes // 2 * cells, co), F32)...  2.98 us
    pallas_call x1, Pallas kernels, volume_grad_of(): call(volume_grad_kernel, jax.ShapeDtypeStruct(shape, BF16), [pltpu.VMEM((...  2.59 us
    add x2, other arithmetic, add_cores(): return keep + exchange(send, lambda i, j: (i ^ 1, j)).astype(F32)  2.4 us
    pallas_call x1, Pallas kernels, halo_share(): call(halo_kernel, jax.ShapeDtypeStruct((height * width // 4, co), BF16),...  2.32 us
  transfers between devices with their start and end apart: 14, of which 9 were waited for; matrix products, arithmetic and copies ran while one was open for 6% of the time, Pallas kernels for 11%

profile of v4, /device:TPU:0, one launch (start us, length us, event | category | flops | bytes accessed | tf_op | source)
XLA Modules:
  0.0 60.3 jit_solution(6649391146845816441)
XLA Ops:
  0.6 2.3 %shard_map.59 = bf16[256,256]{1,0:T(8,128)(2,1)} custom-call(bf16[1,4,32,32,128]{4,3,2,1,0:T(8,128)(2,1)} %volume_ref.3, bf16[3,3,3,128,256]{4,3,2,1,0:T(8,128)(2,1)} %kernel_ref.5), custom_call_target="tpu_custom_call" | custom-call | flops 1000 | bytes 1000 | tf_op jit(solution)/shard_map/pallas_call | solution.py:107
  3.0 5.0 %collective-permute-start = (bf16[256,256]{1,0:T(8,128)(2,1)}, bf16[256,256]{1,0:T(8,128)(2,1)S(1)}, u32[]{:S(2)}, u32[]{:S(2)}) collective-permute-start(bf16[256,256]{1,0:T(8,128)(2,1)} %shard_map.59), channel_id=1, source_target_pairs={{0,1},{1,2},{2,3},{4,5},{5,6},{6,7},{8,9},{9,10},{10,11},{12,13},{... | collective-permute-start | bytes 393224 | tf_op jit(solution)/shard_map/ppermute | solution.py:435
  8.0 3.0 %shard_map.58 = (f32[512,256]{1,0:T(8,128)S(1)}, bf16[4,16,16,384]{3,2,1,0:T(8,128)(2,1)S(1)}, bf16[4,17,16,384]{3,2,1,0:T(8,128)(2,1)S(1)}) custom-call(bf16[1,4,32,32,128]{4,3,2,1,0:T(8,128)(2,1)S(1)} %copy-done.1, bf16[3,3,3,128,256]{4,3,2,1,0:T(8,128)(2,1)S(1)} %copy-done), custom_call_target="tpu_custom_call" | custom-call | flops 1000 | bytes 1000 | tf_op jit(solution)/shard_map/pallas_call | solution.py:168
  11.3 1.7 %shard_map.61 = (f32[36,4,16,128]{3,2,1,0:T(8,128)S(1)}, bf16[36,4,16,128]{3,2,1,0:T(8,128)(2,1)}) custom-call(bf16[4,16,16,384]{3,2,1,0:T(8,128)(2,1)S(1)} %get-tuple-element.25.refs_0_, bf16[4,17,16,384]{3,2,1,0:T(8,128)(2,1)S(1)} %get-tuple-element.26.refs_1_, bf16[512,256]{1,0:T(8,128)(2,1)S(1)} %get-tuple-element.28.refs_2_.grads_ref), custom_call_target="tpu_custom_call" | custom-call | flops 1000 | bytes 1000 | tf_op jit(solution)/shard_map/pallas_call | solution.py:321
  13.1 1.3 %collective-permute-start.1 = (bf16[256,256]{1,0:T(8,128)(2,1)S(1)}, bf16[256,256]{1,0:T(8,128)(2,1)S(1)}, u32[]{:S(2)}, u32[]{:S(2)}) collective-permute-start(bf16[256,256]{1,0:T(8,128)(2,1)S(1)} %slice.15), channel_id=1, source_target_pairs={{1,0},{2,1},{3,2},{5,4},{6,5},{7,6},{9,8},{10,9},{11,10},{13,12},{... | collective-permute-start | bytes 393224 | tf_op jit(solution)/shard_map/ppermute | solution.py:435
  14.4 1.0 %collective-permute-done.2 = bf16[36,4,16,128]{3,2,1,0:T(8,128)(2,1)} collective-permute-done((bf16[36,4,16,128]{3,2,1,0:T(8,128)(2,1)}, bf16[36,4,16,128]{3,2,1,0:T(8,128)(2,1)}, u32[]{:S(2)}, u32[]{:S(2)}) %collective-permute-start.2) | collective-permute-done | bytes 589856 | tf_op jit(solution)/shard_map/ppermute | solution.py:389
  15.4 1.4 %convert_add_fusion = f32[36,4,16,128]{3,2,1,0:T(8,128)S(1)} fusion(f32[36,4,16,128]{3,2,1,0:T(8,128)S(1)} %get-tuple-element.30, bf16[36,4,16,128]{3,2,1,0:T(8,128)(2,1)} %collective-permute-done.2), kind=kLoop, calls=%fused_computation | loop fusion | flops 589824 | bytes 2949120 | tf_op jit(solution)/shard_map/add | solution.py:441
  16.8 0.8 %fusion = bf16[18,4,16,128]{3,2,1,0:T(8,128)(2,1)} fusion(f32[2,18,4,16,128]{4,3,2,1,0:T(8,128)S(1)} %bitcast.51, s32[]{:T(128)S(6)} %select_n.77), kind=kLoop, calls=%fused_computation.8 | loop fusion | bytes 589828 | tf_op jit(solution)/shard_map/convert_element_type | solution.py:456
  17.7 0.3 copy-done.9
  18.0 3.5 %collective-permute-done.1.refs_3_.above_ref = bf16[256,256]{1,0:T(8,128)(2,1)S(1)} collective-permute-done((bf16[256,256]{1,0:T(8,128)(2,1)S(1)}, bf16[256,256]{1,0:T(8,128)(2,1)S(1)}, u32[]{:S(2)}, u32[]{:S(2)}) %collective-permute-start.1) | collective-permute-done | bytes 131104 | tf_op jit(solution)/shard_map/ppermute | solution.py:435
  21.5 0.5 shard_map.62
  22.2 2.7 %collective-permute-start.5 = (bf16[18,4,16,128]{3,2,1,0:T(8,128)(2,1)}, bf16[18,4,16,128]{3,2,1,0:T(8,128)(2,1)S(1)}, u32[]{:S(2)}, u32[]{:S(2)}) collective-permute-start(bf16[18,4,16,128]{3,2,1,0:T(8,128)(2,1)} %fusion), channel_id=1, source_target_pairs={{0,1},{1,0},{2,3},{3,2},{4,6},{5,7},{6,4},{7,5},{8,9},{9,8},{10,11... | collective-permute-start | bytes 884744 | tf_op jit(solution)/shard_map/ppermute | solution.py:389
  24.9 1.0 %convert_add_fusion.1 = f32[4,18,16,128]{3,2,1,0:T(8,128)S(1)} fusion(f32[4,18,16,128]{3,2,1,0:T(8,128)S(1)} %get-tuple-element.33, bf16[4,18,16,128]{3,2,1,0:T(8,128)(2,1)} %collective-permute-done.3), kind=kLoop, calls=%fused_computation.2 | loop fusion | flops 294912 | bytes 1474560 | tf_op jit(solution)/shard_map/add | solution.py:441
  26.0 1.6 %collective-permute-start.4 = (bf16[2,18,16,128]{3,2,1,0:T(8,128)(2,1)S(1)}, bf16[2,18,16,128]{3,2,1,0:T(8,128)(2,1)S(1)}, u32[]{:S(2)}, u32[]{:S(2)}) collective-permute-start(bf16[2,18,16,128]{3,2,1,0:T(8,128)(2,1)S(1)} %fusion.1), channel_id=1, source_target_pairs={{0,8},{1,9},{2,10},{3,11},{4,12},{5,13},{6,14},{7,15},{8,0},{9,1},... | collective-permute-start | bytes 442376 | tf_op jit(solution)/shard_map/ppermute | solution.py:389
  27.6 2.6 %shard_map.63 = bf16[4,16,2,32,128]{4,3,2,1,0:T(8,128)(2,1)} custom-call(bf16[512,256]{1,0:T(8,128)(2,1)S(1)} %get-tuple-element.28.refs_2_.grads_ref, bf16[256,256]{1,0:T(8,128)(2,1)S(1)} %collective-permute-done.1.refs_3_.above_ref, bf16[3,3,3,128,256]{4,3,2,1,0:T(8,128)(2,1)S(1)} %copy-done), custom_call_target="tpu_custom_call" | custom-call | flops 1000 | bytes 1000 | tf_op jit(solution)/shard_map/pallas_call | solution.py:372
  30.3 1.7 %collective-permute-start.7 = (bf16[9,4,16,128]{3,2,1,0:T(8,128)(2,1)S(1)}, bf16[9,4,16,128]{3,2,1,0:T(8,128)(2,1)S(1)}, u32[]{:S(2)}, u32[]{:S(2)}) collective-permute-start(bf16[9,4,16,128]{3,2,1,0:T(8,128)(2,1)S(1)} %fusion.2), channel_id=1, source_target_pairs={{0,2},{1,3},{2,0},{3,1},{4,5},{5,4},{6,7},{7,6},{8,10},{9,11},{10,... | collective-permute-start | bytes 442376 | tf_op jit(solution)/shard_map/ppermute | solution.py:389
  32.1 2.7 %collective-permute-start.6 = (bf16[1,18,16,128]{3,2,1,0:T(8,128)(2,1)S(1)}, bf16[1,18,16,128]{3,2,1,0:T(8,128)(2,1)S(1)}, u32[]{:S(2)}, u32[]{:S(2)}) collective-permute-start(bf16[1,18,16,128]{3,2,1,0:T(8,128)(2,1)S(1)} %dynamic-slice_convert_fusion.3), channel_id=1, source_target_pairs={{0,16},{1,17},{2,18},{3,19},{4,20},{5,21},{6,22},{7,23},{8,24},{9,... | collective-permute-start | bytes 221192 | tf_op jit(solution)/shard_map/ppermute | solution.py:389
  34.7 0.8 %collective-permute-done.7 = bf16[9,4,16,128]{3,2,1,0:T(8,128)(2,1)S(1)} collective-permute-done((bf16[9,4,16,128]{3,2,1,0:T(8,128)(2,1)S(1)}, bf16[9,4,16,128]{3,2,1,0:T(8,128)(2,1)S(1)}, u32[]{:S(2)}, u32[]{:S(2)}) %collective-permute-start.7) | collective-permute-done | bytes 147488 | tf_op jit(solution)/shard_map/ppermute | solution.py:389
  35.6 1.3 %collective-permute-start.9 = (bf16[2,9,16,128]{3,2,1,0:T(8,128)(2,1)S(1)}, bf16[2,9,16,128]{3,2,1,0:T(8,128)(2,1)S(1)}, u32[]{:S(2)}, u32[]{:S(2)}) collective-permute-start(bf16[2,9,16,128]{3,2,1,0:T(8,128)(2,1)S(1)} %fusion.5), channel_id=1, source_target_pairs={{0,8},{1,9},{2,10},{3,11},{4,12},{5,13},{6,14},{7,15},{8,0},{9,1},... | collective-permute-start | bytes 221192 | tf_op jit(solution)/shard_map/ppermute | solution.py:389
  36.9 0.7 %collective-permute-done.6 = bf16[1,18,16,128]{3,2,1,0:T(8,128)(2,1)S(1)} collective-permute-done((bf16[1,18,16,128]{3,2,1,0:T(8,128)(2,1)S(1)}, bf16[1,18,16,128]{3,2,1,0:T(8,128)(2,1)S(1)}, u32[]{:S(2)}, u32[]{:S(2)}) %collective-permute-start.6) | collective-permute-done | bytes 73760 | tf_op jit(solution)/shard_map/ppermute | solution.py:389
  37.7 1.5 %collective-permute-start.8 = (bf16[672,128]{1,0:T(8,128)(2,1)S(1)}, bf16[672,128]{1,0:T(8,128)(2,1)S(1)}, u32[]{:S(2)}, u32[]{:S(2)}) collective-permute-start(bf16[672,128]{1,0:T(8,128)(2,1)S(1)} %pad_maximum_fusion.1), channel_id=1, source_target_pairs={{0,1},{1,0},{2,3},{3,2},{4,6},{5,7},{6,4},{7,5},{8,9},{9,8},{10,11... | collective-permute-start | bytes 516104 | tf_op jit(solution)/shard_map/ppermute | solution.py:389
  39.2 0.8 %collective-permute-done.9 = bf16[2,9,16,128]{3,2,1,0:T(8,128)(2,1)S(1)} collective-permute-done((bf16[2,9,16,128]{3,2,1,0:T(8,128)(2,1)S(1)}, bf16[2,9,16,128]{3,2,1,0:T(8,128)(2,1)S(1)}, u32[]{:S(2)}, u32[]{:S(2)}) %collective-permute-start.9) | collective-permute-done | bytes 73760 | tf_op jit(solution)/shard_map/ppermute | solution.py:389
  40.1 2.7 %collective-permute-start.10 = (bf16[1,9,16,128]{3,2,1,0:T(8,128)(2,1)S(1)}, bf16[1,9,16,128]{3,2,1,0:T(8,128)(2,1)S(1)}, u32[]{:S(2)}, u32[]{:S(2)}) collective-permute-start(bf16[1,9,16,128]{3,2,1,0:T(8,128)(2,1)S(1)} %dynamic-slice_convert_fusion.5), channel_id=1, source_target_pairs={{0,16},{1,17},{2,18},{3,19},{4,20},{5,21},{6,22},{7,23},{8,24},{9,... | collective-permute-start | bytes 110600 | tf_op jit(solution)/shard_map/ppermute | solution.py:389
  42.7 2.3 %collective-permute-done.10 = bf16[1,9,16,128]{3,2,1,0:T(8,128)(2,1)S(1)} collective-permute-done((bf16[1,9,16,128]{3,2,1,0:T(8,128)(2,1)S(1)}, bf16[1,9,16,128]{3,2,1,0:T(8,128)(2,1)S(1)}, u32[]{:S(2)}, u32[]{:S(2)}) %collective-permute-start.10) | collective-permute-done | bytes 36896 | tf_op jit(solution)/shard_map/ppermute | solution.py:389
  45.1 1.7 %collective-permute-start.11 = (bf16[592,128]{1,0:T(8,128)(2,1)S(1)}, bf16[592,128]{1,0:T(8,128)(2,1)S(1)}, u32[]{:S(2)}, u32[]{:S(2)}) collective-permute-start(bf16[592,128]{1,0:T(8,128)(2,1)S(1)} %pad_maximum_fusion.2), channel_id=1, source_target_pairs={{0,2},{1,3},{2,0},{3,1},{4,5},{5,4},{6,7},{7,6},{8,10},{9,11},{10,... | collective-permute-start | bytes 454664 | tf_op jit(solution)/shard_map/ppermute | solution.py:389
  46.8 3.5 %collective-permute-done.11 = bf16[592,128]{1,0:T(8,128)(2,1)S(1)} collective-permute-done((bf16[592,128]{1,0:T(8,128)(2,1)S(1)}, bf16[592,128]{1,0:T(8,128)(2,1)S(1)}, u32[]{:S(2)}, u32[]{:S(2)}) %collective-permute-start.11) | collective-permute-done | bytes 151584 | tf_op jit(solution)/shard_map/ppermute | solution.py:389
  50.4 1.7 %collective-permute-start.12 = (bf16[1,14,16,128]{3,2,1,0:T(8,128)(2,1)S(1)}, bf16[1,14,16,128]{3,2,1,0:T(8,128)(2,1)S(1)}, u32[]{:S(2)}, u32[]{:S(2)}) collective-permute-start(bf16[1,14,16,128]{3,2,1,0:T(8,128)(2,1)S(1)} %pad_maximum_fusion.4), channel_id=1, source_target_pairs={{0,2},{1,3},{2,0},{3,1},{4,5},{5,4},{6,7},{7,6},{8,10},{9,11},{10,... | collective-permute-start | bytes 172040 | tf_op jit(solution)/shard_map/ppermute | solution.py:389
  52.1 0.8 %shard_map.64 = bf16[64,2048]{1,0:T(8,128)(2,1)} custom-call(bf16[8,64,128]{2,1,0:T(8,128)(2,1)S(1)} %bitcast.48, bf16[8,64,128]{2,1,0:T(8,128)(2,1)S(1)} %bitcast.47), custom_call_target="tpu_custom_call" | custom-call | flops 1000 | bytes 1000 | tf_op jit(solution)/shard_map/pallas_call | solution.py:235
  52.9 1.7 %collective-permute-done.12 = bf16[1,14,16,128]{3,2,1,0:T(8,128)(2,1)S(1)} collective-permute-done((bf16[1,14,16,128]{3,2,1,0:T(8,128)(2,1)S(1)}, bf16[1,14,16,128]{3,2,1,0:T(8,128)(2,1)S(1)}, u32[]{:S(2)}, u32[]{:S(2)}) %collective-permute-start.12) | collective-permute-done | bytes 57376 | tf_op jit(solution)/shard_map/ppermute | solution.py:389
  54.6 1.7 %collective-permute-start.13 = (bf16[2,14,16,128]{3,2,1,0:T(8,128)(2,1)S(1)}, bf16[2,14,16,128]{3,2,1,0:T(8,128)(2,1)S(1)}, u32[]{:S(2)}, u32[]{:S(2)}) collective-permute-start(bf16[2,14,16,128]{3,2,1,0:T(8,128)(2,1)S(1)} %pad_maximum_fusion.3), channel_id=1, source_target_pairs={{0,1},{1,0},{2,3},{3,2},{4,6},{5,7},{6,4},{7,5},{8,9},{9,8},{10,11... | collective-permute-start | bytes 344072 | tf_op jit(solution)/shard_map/ppermute | solution.py:389
  56.3 3.2 %collective-permute-done.13 = bf16[2,14,16,128]{3,2,1,0:T(8,128)(2,1)S(1)} collective-permute-done((bf16[2,14,16,128]{3,2,1,0:T(8,128)(2,1)S(1)}, bf16[2,14,16,128]{3,2,1,0:T(8,128)(2,1)S(1)}, u32[]{:S(2)}, u32[]{:S(2)}) %collective-permute-start.13) | collective-permute-done | bytes 114720 | tf_op jit(solution)/shard_map/ppermute | solution.py:389
  59.5 0.8 %shard_map.65 = f32[27,16,256]{2,1,0:T(8,128)} custom-call(bf16[4,14,16,128]{3,2,1,0:T(8,128)(2,1)S(1)} %pad_maximum_fusion.pieces_ref), custom_call_target="tpu_custom_call" | custom-call | flops 1000 | bytes 1000 | tf_op jit(solution)/shard_map/pallas_call | solution.py:260
  (59 shorter events, 1.1 us)
Async XLA Ops:
  0.6 7.4 %copy-start = (bf16[3,3,3,128,256]{4,3,2,1,0:T(8,128)(2,1)S(1)}, bf16[3,3,3,128,256]{4,3,2,1,0:T(8,128)(2,1)}, u32[]{:S(2)}) copy-start(bf16[3,3,3,128,256]{4,3,2,1,0:T(8,128)(2,1)} %kernel_ref.5) | copy-start | bytes 5308420
  0.6 7.4 %copy-start.1 = (bf16[1,4,32,32,128]{4,3,2,1,0:T(8,128)(2,1)S(1)}, bf16[1,4,32,32,128]{4,3,2,1,0:T(8,128)(2,1)}, u32[]{:S(2)}) copy-start(bf16[1,4,32,32,128]{4,3,2,1,0:T(8,128)(2,1)} %volume_ref.3) | copy-start | bytes 3145732
  3.0 8.0 %copy-start.6 = (bf16[1,2,16,16,256]{4,3,2,1,0:T(8,128)(2,1)S(1)}, bf16[1,2,16,16,256]{4,3,2,1,0:T(8,128)(2,1)}, u32[]{:S(2)}) copy-start(bf16[1,2,16,16,256]{4,3,2,1,0:T(8,128)(2,1)} %param.5) | copy-start | bytes 786436
  3.0 8.0 %collective-permute-start = (bf16[256,256]{1,0:T(8,128)(2,1)}, bf16[256,256]{1,0:T(8,128)(2,1)S(1)}, u32[]{:S(2)}, u32[]{:S(2)}) collective-permute-start(bf16[256,256]{1,0:T(8,128)(2,1)} %shard_map.59), channel_id=1, source_target_pairs={{0,1},{1,2},{2,3},{4,5},{5,6},{6,7},{8,9},{9,10},{10,11},{12,13},{... | collective-permute-start | bytes 393224 | tf_op jit(solution)/shard_map/ppermute | solution.py:435
  11.0 2.0 %copy-start.2 = (bf16[4,17,16,384]{3,2,1,0:T(8,128)(2,1)}, bf16[4,17,16,384]{3,2,1,0:T(8,128)(2,1)S(1)}, u32[]{:S(2)}) copy-start(bf16[4,17,16,384]{3,2,1,0:T(8,128)(2,1)S(1)} %get-tuple-element.26.refs_1_) | copy-start | bytes 2506756
  11.0 2.0 %copy-start.4 = (bf16[4,16,16,384]{3,2,1,0:T(8,128)(2,1)}, bf16[4,16,16,384]{3,2,1,0:T(8,128)(2,1)S(1)}, u32[]{:S(2)}) copy-start(bf16[4,16,16,384]{3,2,1,0:T(8,128)(2,1)S(1)} %get-tuple-element.25.refs_0_) | copy-start | bytes 2359300
  11.3 1.7 %copy-start.7 = (bf16[4,4,64,128]{3,2,1,0:T(8,128)(2,1)}, bf16[4,4,64,128]{3,2,1,0:T(8,128)(2,1)S(1)}, u32[]{:S(2)}) copy-start(bf16[4,4,64,128]{3,2,1,0:T(8,128)(2,1)S(1)} %get-tuple-element.24) | copy-start | bytes 786436
  13.0 2.4 %collective-permute-start.2 = (bf16[36,4,16,128]{3,2,1,0:T(8,128)(2,1)}, bf16[36,4,16,128]{3,2,1,0:T(8,128)(2,1)}, u32[]{:S(2)}, u32[]{:S(2)}) collective-permute-start(bf16[36,4,16,128]{3,2,1,0:T(8,128)(2,1)} %get-tuple-element.31), channel_id=1, source_target_pairs={{0,4},{1,5},{2,6},{3,7},{4,0},{5,1},{6,2},{7,3},{8,12},{9,13},{10,... | collective-permute-start | bytes 1769480 | tf_op jit(solution)/shard_map/ppermute | solution.py:389
  13.1 8.4 %collective-permute-start.1 = (bf16[256,256]{1,0:T(8,128)(2,1)S(1)}, bf16[256,256]{1,0:T(8,128)(2,1)S(1)}, u32[]{:S(2)}, u32[]{:S(2)}) collective-permute-start(bf16[256,256]{1,0:T(8,128)(2,1)S(1)} %slice.15), channel_id=1, source_target_pairs={{1,0},{2,1},{3,2},{5,4},{6,5},{7,6},{9,8},{10,9},{11,10},{13,12},{... | collective-permute-start | bytes 393224 | tf_op jit(solution)/shard_map/ppermute | solution.py:435
  15.4 6.1 %copy-start.3 = (bf16[4,17,16,384]{3,2,1,0:T(8,128)(2,1)S(1)}, bf16[4,17,16,384]{3,2,1,0:T(8,128)(2,1)}, u32[]{:S(2)}) copy-start(bf16[4,17,16,384]{3,2,1,0:T(8,128)(2,1)} %copy-done.2) | copy-start | bytes 2506756
  15.4 6.1 %copy-start.5 = (bf16[4,16,16,384]{3,2,1,0:T(8,128)(2,1)S(1)}, bf16[4,16,16,384]{3,2,1,0:T(8,128)(2,1)}, u32[]{:S(2)}) copy-start(bf16[4,16,16,384]{3,2,1,0:T(8,128)(2,1)} %copy-done.4) | copy-start | bytes 2359300
  16.8 1.2 %copy-start.9 = (f32[36,4,16,128]{3,2,1,0:T(8,128)}, f32[36,4,16,128]{3,2,1,0:T(8,128)S(1)}, u32[]{:S(2)}) copy-start(f32[36,4,16,128]{3,2,1,0:T(8,128)S(1)} %convert_add_fusion) | copy-start | bytes 3538948
  18.0 4.2 %copy-start.8 = (bf16[4,4,64,128]{3,2,1,0:T(8,128)(2,1)S(1)}, bf16[4,4,64,128]{3,2,1,0:T(8,128)(2,1)}, u32[]{:S(2)}) copy-start(bf16[4,4,64,128]{3,2,1,0:T(8,128)(2,1)} %copy-done.7) | copy-start | bytes 786436
  22.0 2.8 %collective-permute-start.3 = (bf16[4,18,16,128]{3,2,1,0:T(8,128)(2,1)S(1)}, bf16[4,18,16,128]{3,2,1,0:T(8,128)(2,1)}, u32[]{:S(2)}, u32[]{:S(2)}) collective-permute-start(bf16[4,18,16,128]{3,2,1,0:T(8,128)(2,1)S(1)} %get-tuple-element.34), channel_id=1, source_target_pairs={{0,4},{1,5},{2,6},{3,7},{4,0},{5,1},{6,2},{7,3},{8,12},{9,13},{10,... | collective-permute-start | bytes 884744 | tf_op jit(solution)/shard_map/ppermute | solution.py:389
  22.2 8.0 %collective-permute-start.5 = (bf16[18,4,16,128]{3,2,1,0:T(8,128)(2,1)}, bf16[18,4,16,128]{3,2,1,0:T(8,128)(2,1)S(1)}, u32[]{:S(2)}, u32[]{:S(2)}) collective-permute-start(bf16[18,4,16,128]{3,2,1,0:T(8,128)(2,1)} %fusion), channel_id=1, source_target_pairs={{0,1},{1,0},{2,3},{3,2},{4,6},{5,7},{6,4},{7,5},{8,9},{9,8},{10,11... | collective-permute-start | bytes 884744 | tf_op jit(solution)/shard_map/ppermute | solution.py:389
  25.9 4.2 %copy-start.10 = (f32[36,4,16,128]{3,2,1,0:T(8,128)S(1)}, f32[36,4,16,128]{3,2,1,0:T(8,128)}, u32[]{:S(2)}) copy-start(f32[36,4,16,128]{3,2,1,0:T(8,128)} %copy-done.9) | copy-start | bytes 3538948
  26.0 6.1 %collective-permute-start.4 = (bf16[2,18,16,128]{3,2,1,0:T(8,128)(2,1)S(1)}, bf16[2,18,16,128]{3,2,1,0:T(8,128)(2,1)S(1)}, u32[]{:S(2)}, u32[]{:S(2)}) collective-permute-start(bf16[2,18,16,128]{3,2,1,0:T(8,128)(2,1)S(1)} %fusion.1), channel_id=1, source_target_pairs={{0,8},{1,9},{2,10},{3,11},{4,12},{5,13},{6,14},{7,15},{8,0},{9,1},... | collective-permute-start | bytes 442376 | tf_op jit(solution)/shard_map/ppermute | solution.py:389
  30.3 5.2 %collective-permute-start.7 = (bf16[9,4,16,128]{3,2,1,0:T(8,128)(2,1)S(1)}, bf16[9,4,16,128]{3,2,1,0:T(8,128)(2,1)S(1)}, u32[]{:S(2)}, u32[]{:S(2)}) collective-permute-start(bf16[9,4,16,128]{3,2,1,0:T(8,128)(2,1)S(1)} %fusion.2), channel_id=1, source_target_pairs={{0,2},{1,3},{2,0},{3,1},{4,5},{5,4},{6,7},{7,6},{8,10},{9,11},{10,... | collective-permute-start | bytes 442376 | tf_op jit(solution)/shard_map/ppermute | solution.py:389
  32.1 5.5 %collective-permute-start.6 = (bf16[1,18,16,128]{3,2,1,0:T(8,128)(2,1)S(1)}, bf16[1,18,16,128]{3,2,1,0:T(8,128)(2,1)S(1)}, u32[]{:S(2)}, u32[]{:S(2)}) collective-permute-start(bf16[1,18,16,128]{3,2,1,0:T(8,128)(2,1)S(1)} %dynamic-slice_convert_fusion.3), channel_id=1, source_target_pairs={{0,16},{1,17},{2,18},{3,19},{4,20},{5,21},{6,22},{7,23},{8,24},{9,... | collective-permute-start | bytes 221192 | tf_op jit(solution)/shard_map/ppermute | solution.py:389
  35.6 4.4 %collective-permute-start.9 = (bf16[2,9,16,128]{3,2,1,0:T(8,128)(2,1)S(1)}, bf16[2,9,16,128]{3,2,1,0:T(8,128)(2,1)S(1)}, u32[]{:S(2)}, u32[]{:S(2)}) collective-permute-start(bf16[2,9,16,128]{3,2,1,0:T(8,128)(2,1)S(1)} %fusion.5), channel_id=1, source_target_pairs={{0,8},{1,9},{2,10},{3,11},{4,12},{5,13},{6,14},{7,15},{8,0},{9,1},... | collective-permute-start | bytes 221192 | tf_op jit(solution)/shard_map/ppermute | solution.py:389
  37.7 7.3 %collective-permute-start.8 = (bf16[672,128]{1,0:T(8,128)(2,1)S(1)}, bf16[672,128]{1,0:T(8,128)(2,1)S(1)}, u32[]{:S(2)}, u32[]{:S(2)}) collective-permute-start(bf16[672,128]{1,0:T(8,128)(2,1)S(1)} %pad_maximum_fusion.1), channel_id=1, source_target_pairs={{0,1},{1,0},{2,3},{3,2},{4,6},{5,7},{6,4},{7,5},{8,9},{9,8},{10,11... | collective-permute-start | bytes 516104 | tf_op jit(solution)/shard_map/ppermute | solution.py:389
  40.1 4.9 %collective-permute-start.10 = (bf16[1,9,16,128]{3,2,1,0:T(8,128)(2,1)S(1)}, bf16[1,9,16,128]{3,2,1,0:T(8,128)(2,1)S(1)}, u32[]{:S(2)}, u32[]{:S(2)}) collective-permute-start(bf16[1,9,16,128]{3,2,1,0:T(8,128)(2,1)S(1)} %dynamic-slice_convert_fusion.5), channel_id=1, source_target_pairs={{0,16},{1,17},{2,18},{3,19},{4,20},{5,21},{6,22},{7,23},{8,24},{9,... | collective-permute-start | bytes 110600 | tf_op jit(solution)/shard_map/ppermute | solution.py:389
  45.1 5.3 %collective-permute-start.11 = (bf16[592,128]{1,0:T(8,128)(2,1)S(1)}, bf16[592,128]{1,0:T(8,128)(2,1)S(1)}, u32[]{:S(2)}, u32[]{:S(2)}) collective-permute-start(bf16[592,128]{1,0:T(8,128)(2,1)S(1)} %pad_maximum_fusion.2), channel_id=1, source_target_pairs={{0,2},{1,3},{2,0},{3,1},{4,5},{5,4},{6,7},{7,6},{8,10},{9,11},{10,... | collective-permute-start | bytes 454664 | tf_op jit(solution)/shard_map/ppermute | solution.py:389
  50.4 4.2 %collective-permute-start.12 = (bf16[1,14,16,128]{3,2,1,0:T(8,128)(2,1)S(1)}, bf16[1,14,16,128]{3,2,1,0:T(8,128)(2,1)S(1)}, u32[]{:S(2)}, u32[]{:S(2)}) collective-permute-start(bf16[1,14,16,128]{3,2,1,0:T(8,128)(2,1)S(1)} %pad_maximum_fusion.4), channel_id=1, source_target_pairs={{0,2},{1,3},{2,0},{3,1},{4,5},{5,4},{6,7},{7,6},{8,10},{9,11},{10,... | collective-permute-start | bytes 172040 | tf_op jit(solution)/shard_map/ppermute | solution.py:389
  54.6 4.9 %collective-permute-start.13 = (bf16[2,14,16,128]{3,2,1,0:T(8,128)(2,1)S(1)}, bf16[2,14,16,128]{3,2,1,0:T(8,128)(2,1)S(1)}, u32[]{:S(2)}, u32[]{:S(2)}) collective-permute-start(bf16[2,14,16,128]{3,2,1,0:T(8,128)(2,1)S(1)} %pad_maximum_fusion.3), channel_id=1, source_target_pairs={{0,1},{1,0},{2,3},{3,2},{4,6},{5,7},{6,4},{7,5},{8,9},{9,8},{10,11... | collective-permute-start | bytes 344072 | tf_op jit(solution)/shard_map/ppermute | solution.py:389

commit v5 on v4

--- a/solution.py
+++ b/solution.py
@@ -11,11 +11,20 @@
 BF16 = jnp.bfloat16
 F32 = jnp.float32
 VMEM_LIMIT = 20 * 1024 * 1024
-VMEM_WHOLE = 60 * 1024 * 1024
-
-
-def call(kernel, out_shape, scratch=(), in_specs=None, limit=VMEM_LIMIT):
+DONE = (8, 128)
+VMEM_WHOLE = 63 * 1024 * 1024
+
+
+def call(kernel, out_shape, scratch=(), in_specs=None, limit=VMEM_LIMIT, order=(), inputs=0):
     extra = {} if in_specs is None else {"in_specs": in_specs}
+    if order:
+        whole = pl.BlockSpec(memory_space=pltpu.VMEM)
+        extra["in_specs"] = [whole] * inputs + [pl.BlockSpec(memory_space=pl.ANY)] * len(order)
+        inner, count = kernel, len(order)
+
+        def kernel(*refs):
+            inner(*refs[:inputs], *refs[inputs + count :])
+
     return pl.pallas_call(
         kernel,
         out_shape=out_shape,
@@ -24,10 +33,6 @@
         cost_estimate=pl.CostEstimate(flops=1000, bytes_accessed=1000, transcendentals=0),
         **extra,
     )
-
-
-def after(value, *others):
-    return lax.optimization_barrier((value,) + others)[0]
 
 
 def spread_plane(plane, wide):
@@ -118,44 +123,29 @@
     )(volume, kernel)
 
 
-def preact_kernel(volume_ref, kernel_ref, preact_ref, even_ref, odd_ref, slab, weights, wide, sems):
+def preact_kernel(volume_ref, kernel_ref, preact_ref, even_ref, odd_ref, wide):
     planes, height, width, chans = volume_ref.shape[1:]
     cells = height * width // 4
     outs = planes // 2
-    copies = [
-        pltpu.make_async_copy(volume_ref.at[0, plane], slab.at[plane], sems.at[plane])
-        for plane in range(planes)
-    ]
-    loads = {
-        kd: pltpu.make_async_copy(kernel_ref.at[kd], weights.at[kd], sems.at[planes + kd])
-        for kd in range(3)
-    }
-    for copy in copies:
-        copy.start()
-    for kd in (1, 2, 0):
-        loads[kd].start()
     for plane in range(planes):
-        copies[plane].wait()
-        even, odd = spread_plane(slab[plane], wide)
+        even, odd = spread_plane(volume_ref[0, plane], wide)
         even_ref[plane] = even
         odd_ref[plane, pl.ds(0, 1)] = jnp.zeros_like(odd[:1])
         odd_ref[plane, pl.ds(1, height // 2)] = odd
     co = kernel_ref.shape[-1]
     total = None
     for kd in (1, 2):
-        loads[kd].wait()
         for kh in range(3):
             lhs = [tap_rows(even_ref, odd_ref, 2 * d - 1 + kd, kh) for d in range(outs)]
-            rhs = weights[kd, kh].reshape(3 * chans, co)
+            rhs = kernel_ref[kd, kh].reshape(3 * chans, co)
             term = jnp.dot(jnp.concatenate(lhs, axis=0), rhs, preferred_element_type=F32)
             total = term if total is None else total + term
     preact_ref[...] = total
-    loads[0].wait()
     if outs > 1:
         total = preact_ref[pl.ds(cells, (outs - 1) * cells), :]
         for kh in range(3):
             lhs = [tap_rows(even_ref, odd_ref, 2 * d - 1, kh) for d in range(1, outs)]
-            rhs = weights[0, kh].reshape(3 * chans, co)
+            rhs = kernel_ref[0, kh].reshape(3 * chans, co)
             total += jnp.dot(jnp.concatenate(lhs, axis=0), rhs, preferred_element_type=F32)
         preact_ref[pl.ds(cells, (outs - 1) * cells), :] = total
 
@@ -172,13 +162,7 @@
             jax.ShapeDtypeStruct((planes, h2, w2, 3 * chans), BF16),
             jax.ShapeDtypeStruct((planes, h2 + 1, w2, 3 * chans), BF16),
         ),
-        [
-            pltpu.VMEM(volume.shape[1:], BF16),
-            pltpu.VMEM(kernel.shape, BF16),
-            pltpu.VMEM((height * width + 16, chans), F32),
-            pltpu.SemaphoreType.DMA((planes + 3,)),
-        ],
-        [pl.BlockSpec(memory_space=pltpu.HBM)] * 2,
+        [pltpu.VMEM((height * width + 16, chans), F32)],
     )(volume, kernel)
 
 
@@ -215,7 +199,8 @@
     )(preact, share, cotangent)
 
 
-def switched_kernel(space, cores, kept_ref, got_ref, out_ref):
+def switched_kernel(space, cores, kept_ref, got_ref, out_ref, done_ref):
+    done_ref[...] = jnp.zeros_like(done_ref)
     half = space // 2
     strips = kept_ref.shape[0] // half
     for source in range(space):
@@ -227,40 +212,160 @@
             out_ref[:, column : column + 128] = jnp.where(far == 1, got_ref[row], kept_ref[row])
 
 
-def switched_of(kept, got, space, cores):
-    half = space // 2
+def switched_of(kept, got, space, cores, order):
     group = kept.shape[-2]
     kept = kept.reshape(-1, group, 128)
     got = got.reshape(-1, group, 128)
     return call(
         functools.partial(switched_kernel, space, cores),
-        jax.ShapeDtypeStruct((group, 2 * kept.shape[0] * 128), BF16),
-    )(kept, got)
-
-
-def kernel_grad_out_kernel(space, cores, early_units, late_units, pieces_ref, out_ref):
-    block = pieces_ref.shape[2]
+        (
+            jax.ShapeDtypeStruct((group, 2 * kept.shape[0] * 128), BF16),
+            jax.ShapeDtypeStruct(DONE, F32),
+        ),
+        order=order,
+        inputs=2,
+    )(kept, got, *order)
+
+
+def side(axis, stage, cores):
+    if axis == "chips":
+        return (lax.axis_index("dp") // cores >> stage) & 1
+    bits = bits_of(lax.axis_size("space"))
+    index = lax.axis_index("space")
+    return jnp.where(odd_core(cores), (index >> (bits - 1 - stage)) & 1, (index >> stage) & 1)
+
+
+def halves_of(shape, axis):
+    units, chips = shape[:2]
+    lead = (1, 2, units // 2 * chips) if axis == "space" else (units * chips // 2, 2, 1)
+    return lead + tuple(shape[2:])
+
+
+def half_shape(shape, axis):
+    units, chips = shape[:2]
+    return ((units // 2, chips) if axis == "space" else (units, chips // 2)) + tuple(shape[2:])
+
+
+def add_kernel(now, then, cores, value_ref, got_ref, *outs):
+    if now is None:
+        total = value_ref[...]
+    else:
+        total = value_ref[:, side(*now, cores)]
+    total = total.reshape(got_ref.shape) + got_ref[...].astype(F32)
+    if then is None:
+        outs[0][...] = total.astype(BF16)
+        return
+    keep_ref, sent_ref = outs
+    keep_ref[...] = total.reshape(keep_ref.shape)
+    sent_ref[...] = keep_ref[:, 1 - side(*then, cores)].reshape(sent_ref.shape).astype(BF16)
+
+
+def add_stage(value, got, now, then, cores, order=()):
+    shape = got.shape
+    if then is None:
+        outs = jax.ShapeDtypeStruct(shape, BF16)
+    else:
+        outs = (
+            jax.ShapeDtypeStruct(halves_of(shape, then[0]), F32),
+            jax.ShapeDtypeStruct(half_shape(shape, then[0]), BF16),
+        )
+    return call(
+        functools.partial(add_kernel, now, then, cores), outs, order=order, inputs=2
+    )(value, got, *order)
+
+
+def switch_kernel(stage, cores, first_ref, *refs):
+    got_ref = refs[0] if len(refs) == 3 else None
+    stay_ref, out_ref = refs[-2:]
+    bit = side("space", stage, cores)
+    sources = first_ref.shape[0]
+    for part, ref in enumerate((first_ref, got_ref)):
+        if ref is not None:
+            for source in range(sources):
+                stay_ref[part * sources + source] = ref[source, bit]
+                out_ref[part * sources + source] = ref[source, 1 - bit]
+
+
+def switch_stage(first, got, stage, cores, order):
+    sources, targets = first.shape[:2]
+    split = (sources, 2, targets // 2) + first.shape[2:]
+    operands = (first.reshape(split),) + ((got.reshape(split),) if got is not None else ())
+    shape = jax.ShapeDtypeStruct((sources * len(operands), targets // 2) + first.shape[2:], BF16)
+    return call(
+        functools.partial(switch_kernel, stage, cores),
+        (shape, shape),
+        order=order,
+        inputs=len(operands),
+    )(*operands, *order)
+
+
+def gather_kernel(early_count, mine_ref, got_ref, out_ref):
+    out_ref[pl.ds(0, early_count)] = mine_ref[pl.ds(0, early_count)]
+    out_ref[pl.ds(early_count, early_count)] = got_ref[pl.ds(0, early_count)]
+    late = mine_ref.shape[0] - early_count
+    rows = pl.ds(early_count, late)
+    total = mine_ref[rows].astype(F32) + got_ref[rows].astype(F32)
+    out_ref[pl.ds(2 * early_count, late)] = total.astype(BF16)
+
+
+def gather_stage(mine, got, early_count, order):
+    shape = (mine.shape[0] + early_count,) + mine.shape[1:]
+    return call(
+        functools.partial(gather_kernel, early_count),
+        jax.ShapeDtypeStruct(shape, BF16),
+        order=order,
+        inputs=2,
+    )(mine, got, *order)
+
+
+def join_kernel(now, cores, value_ref, got_ref, late_ref, out_ref):
+    total = value_ref[:, side(*now, cores)].reshape(got_ref.shape) + got_ref[...].astype(F32)
+    early = total.shape[0]
+    out_ref[pl.ds(0, early)] = total.reshape((early,) + out_ref.shape[1:]).astype(BF16)
+    out_ref[pl.ds(early, late_ref.shape[0])] = late_ref[...].reshape((-1,) + out_ref.shape[1:])
+
+
+def join(value, got, late, now, cores, order):
+    shape = (got.shape[0] + late.shape[0],) + got.shape[2:]
+    return call(
+        functools.partial(join_kernel, now, cores),
+        jax.ShapeDtypeStruct(shape, BF16),
+        order=order,
+        inputs=3,
+    )(value, got, late, *order)
+
+
+def kernel_grad_out_kernel(space, cores, early_units, share, mine_ref, got_ref, out_ref):
     halves = out_ref.shape[-1] // 128
-    early_share = -(-early_units // space)
-    late_share = -(-late_units // space)
+    count = mine_ref.shape[0]
+    late_units = out_ref.shape[0] * halves - early_units
+    near = share * (space // 2)
+
+    def put(index, value):
+        tap, half = divmod(index, halves)
+        out_ref[tap, :, half * 128 : (half + 1) * 128] = value
+
+    for index in range(late_units):
+        row = near + index
+        put(index, mine_ref[row].astype(F32) + got_ref[row].astype(F32))
     for group in range(space):
         place = relative_group(group, space, cores)
-        for unit in range(early_share + late_share):
-            late = unit >= early_share
-            index = group * late_share + unit - early_share if late else group * early_share + unit
-            if index >= (late_units if late else early_units):
-                continue
-            index = index if late else index + late_units
-            tap, half = divmod(index, halves)
-            out_ref[tap, :, half * 128 : (half + 1) * 128] = pieces_ref[place, unit].astype(F32)
-
-
-def kernel_grad_out(pieces, early_units, late_units, space, cores, co):
+        far = place // (space // 2)
+        row = (place % (space // 2)) * share
+        for unit in range(share):
+            index = group * share + unit
+            if index < early_units:
+                value = jnp.where(far == 1, got_ref[row + unit], mine_ref[row + unit])
+                put(late_units + index, value.astype(F32))
+
+
+def kernel_grad_out(mine, got, early_units, late_units, space, cores, co):
     taps = (early_units + late_units) * 128 // co
-    return call(
-        functools.partial(kernel_grad_out_kernel, space, cores, early_units, late_units),
-        jax.ShapeDtypeStruct((taps, pieces.shape[2], co), F32),
-    )(pieces)
+    share = -(-early_units // space)
+    return call(
+        functools.partial(kernel_grad_out_kernel, space, cores, early_units, share),
+        jax.ShapeDtypeStruct((taps, mine.shape[1], co), F32),
+    )(mine, got)
 
 
 def store_units(product, scale, core, cores, chips, put):
@@ -281,9 +386,8 @@
                 put(kw * halves + half, chip, keep, send)
 
 
-def kernel_grad_kernel(kds, chip_major, cores, chips, scale, *refs):
-    even_ref, odd_ref, grads_ref = refs[:3]
-    above_ref = refs[3] if 0 in kds else None
+def kernel_grad_kernel(kds, cores, chips, scale, even_ref, odd_ref, grads_ref, *refs):
+    above_ref = refs[0] if 0 in kds else None
     keep_ref, send_ref = refs[-2:]
     outs = even_ref.shape[0] // 2
     cells = even_ref.shape[1] * even_ref.shape[2]
@@ -304,27 +408,28 @@
             )
 
             def put(unit, chip, keep, send, base=(place * 3 + kh) * per_row):
-                where = (chip, base + unit) if chip_major else (base + unit, chip)
-                keep_ref[where] = keep
-                send_ref[where] = send.astype(BF16)
+                keep_ref[base + unit, chip] = keep
+                send_ref[base + unit, chip] = send.astype(BF16)
 
             store_units(product, scale, core, cores, chips, put)
 
 
-def kernel_grad_part(even, odd, grads, above, kds, chip_major, cores, chips, scale):
+def kernel_grad_part(even, odd, grads, above, kds, cores, chips, scale, order=()):
     chans = even.shape[-1] // 3
     co = grads.shape[-1]
     units = len(kds) * 9 * (co // 128)
-    block = chans // (cores * chips)
-    shape = (chips, units, block, 128) if chip_major else (units, chips, block, 128)
+    shape = (units, chips, chans // (cores * chips), 128)
     operands = (even, odd, grads) + ((above,) if 0 in kds else ())
     return call(
-        functools.partial(kernel_grad_kernel, kds, chip_major, cores, chips, scale),
+        functools.partial(kernel_grad_kernel, kds, cores, chips, scale),
         (jax.ShapeDtypeStruct(shape, F32), jax.ShapeDtypeStruct(shape, BF16)),
-    )(*operands)
-
-
-def volume_grad_kernel(grads_ref, above_ref, kernel_ref, out_ref, shifted, wide):
+        order=order,
+        inputs=len(operands),
+    )(*operands, *order)
+
+
+def volume_grad_kernel(grads_ref, above_ref, kernel_ref, out_ref, done_ref, shifted, wide):
+    done_ref[...] = jnp.zeros_like(done_ref)
     planes, h2, _, width, chans = out_ref.shape
     w2 = width // 2
     cells = h2 * w2
@@ -364,19 +469,21 @@
             out_ref[plane, :, odd_row] = wide[...].reshape(h2, width, chans).astype(BF16)
 
 
-def volume_grad_of(grads, above, kernel, height, width):
+def volume_grad_of(grads, above, kernel, height, width, order=()):
     cells, co = grads.shape
     chans = kernel.shape[3]
     planes = 2 * cells * 4 // (height * width)
     shape = (planes, height // 2, 2, width, chans)
     return call(
         volume_grad_kernel,
-        jax.ShapeDtypeStruct(shape, BF16),
+        (jax.ShapeDtypeStruct(shape, BF16), jax.ShapeDtypeStruct(DONE, F32)),
         [
             pltpu.VMEM((height * width // 4 + 8, co), F32),
             pltpu.VMEM((height * width // 2, chans), F32),
         ],
-    )(grads, above, kernel)
+        order=order,
+        inputs=3,
+    )(grads, above, kernel, *order)
 
 
 def exchange(value, partner):
@@ -403,94 +510,27 @@
     return exchange(value, lambda i, j: (i ^ (cores << bit), j))
 
 
-def space_bit(stage, cores):
-    bits = bits_of(lax.axis_size("space"))
-    index = lax.axis_index("space")
-    even, odd = (index >> stage) & 1, (index >> (bits - 1 - stage)) & 1
-    return jnp.where(odd_core(cores), odd, even)
-
-
-def chip_bit(bit, cores):
-    return ((lax.axis_index("dp") // cores) >> bit) & 1
-
-
-def pick(value, bit):
-    value = value.reshape((2, value.shape[0] // 2) + value.shape[1:])
-    return lax.dynamic_index_in_dim(value, bit, 0, keepdims=False)
-
-
-def by_nearest(value, chips):
-    count = bits_of(chips)
-    if count < 2:
-        return value
-    rest = value.shape[1:]
-    value = value.reshape((2,) * count + rest)
-    order = tuple(reversed(range(count))) + tuple(range(count, count + len(rest)))
-    return jnp.transpose(value, order).reshape((chips,) + rest)
-
-
 def neighbour(value, steps):
     count = lax.axis_size("space")
     first, last = (max(0, -steps), min(count, count - steps))
     return lax.ppermute(value, "space", [(source, source + steps) for source in range(first, last)])
 
 
-def add_cores(keep, send, cores):
+def exchange_stage(value, axis, stage, cores):
+    return exchange_space(value, stage, cores) if axis == "space" else exchange_chips(value, stage, cores)
+
+
+def add_cores(keep, send, then, cores, order=()):
     if cores == 1:
-        return keep
-    return keep + exchange(send, lambda i, j: (i ^ 1, j)).astype(F32)
+        got = jnp.zeros_like(send)
+    else:
+        got = exchange(send, lambda i, j: (i ^ 1, j))
+    return add_stage(keep, got, None, then, cores, order)
 
 
 def pad_units(value, space):
     extra = -value.shape[0] % space
     return jnp.pad(value, ((0, extra),) + ((0, 0),) * (value.ndim - 1)) if extra else value
-
-
-def rows_of(value):
-    return value.reshape(-1, value.shape[-1])
-
-
-def early_chain(value, cores, chips):
-    for stage in range(bits_of(lax.axis_size("space"))):
-        bit = space_bit(stage, cores)
-        sent = pick(value, 1 - bit).astype(BF16)
-        got = exchange_space(sent, stage, cores)
-        got = after(got, *(yield sent))
-        value = pick(value, bit) + got.astype(F32)
-    value = by_nearest(jnp.swapaxes(value, 0, 1), chips)
-    for stage in range(bits_of(chips)):
-        bit = chip_bit(stage, cores)
-        sent = pick(value, 1 - bit).astype(BF16)
-        got = exchange_chips(sent, stage, cores)
-        got = after(got, *(yield sent))
-        value = pick(value, bit) + got.astype(F32)
-    return value[0]
-
-
-def late_chain(value, switch, cores, chips):
-    value = by_nearest(value, chips)
-    for stage in range(bits_of(chips)):
-        bit = chip_bit(stage, cores)
-        sent = pick(value, 1 - bit).astype(BF16)
-        got = exchange_chips(sent, stage, cores)
-        got = after(got, *(yield sent))
-        value = pick(value, bit) + got.astype(F32)
-    value = pad_units(value[0], lax.axis_size("space"))
-    stay, moved = switch[None], None
-    for stage in range(bits_of(lax.axis_size("space"))):
-        bit = space_bit(stage, cores)
-        if moved is not None:
-            stay = jnp.concatenate([stay, moved], axis=0)
-        halves = stay.reshape((stay.shape[0], 2, stay.shape[1] // 2) + stay.shape[2:])
-        out = lax.dynamic_index_in_dim(halves, 1 - bit, 1, keepdims=False)
-        stay = lax.dynamic_index_in_dim(halves, bit, 1, keepdims=False)
-        sent = pick(value, 1 - bit).astype(BF16)
-        got = exchange_space(jnp.concatenate([rows_of(sent), rows_of(out)], axis=0), stage, cores)
-        got = after(got, *(yield sent))
-        cut = sent.size // sent.shape[-1]
-        moved = got[cut:].reshape(out.shape)
-        value = pick(value, bit) + got[:cut].reshape(sent.shape).astype(F32)
-    return value, stay, moved
 
 
 def body(volume, kernel, cotangent):
@@ -503,51 +543,76 @@
     outs = planes // 2
     cells = height * width // 4
     scale = 1.0 / math.sqrt(dp * space * samples * outs * cells)
+    over_space = [("space", stage) for stage in range(bits_of(space))]
+    over_chips = [("chips", stage) for stage in range(bits_of(chips))]
 
     share = neighbour(halo_share(volume, kernel), 1)
     preact, even, odd = partial_preact(volume, kernel)
     grads, flipped = activation(preact, share, cotangent.reshape(outs * cells, co), space, cores)
-    first = grads[:cells]
-    grads, first = lax.optimization_barrier((grads, first))
-    above = neighbour(first, -1)
-
-    early = kernel_grad_part(even, odd, grads, None, (1, 2), False, cores, chips, scale)
+    above = neighbour(grads[:cells], -1)
+
+    early = kernel_grad_part(even, odd, grads, None, (1, 2), cores, chips, scale)
     early_units = early[0].shape[0]
-    ahead = early_chain(pad_units(add_cores(*early, cores), space), cores, chips)
-    token = next(ahead)
-
-    above = after(above, token)
-    late = kernel_grad_part(even, odd, grads, above, (0,), True, cores, chips, scale)
-    late_units = late[0].shape[1]
-    behind = late_chain(add_cores(*late, cores), flipped, cores, chips)
-    late_token = next(behind)
-
-    volume_grad = volume_grad_of(grads, after(above, late_token), kernel, height, width)
-    tokens = (late_token, volume_grad)
-    early_total = late_total = None
-    while early_total is None or late_total is None:
-        if early_total is None:
-            try:
-                tokens = (ahead.send(tokens),)
-            except StopIteration as end:
-                early_total = end.value
-                tokens = (early_total,)
-        if late_total is None:
-            try:
-                tokens = (behind.send(tokens),)
-            except StopIteration as end:
-                late_total, kept, arrived = end.value
-                tokens = (late_total,)
-
-    pieces = jnp.concatenate([early_total, late_total], axis=0).astype(BF16)[None]
+    early = [pad_units(half, space) for half in early]
+    plan = over_space + over_chips
+    late_plan = list(over_chips)
+    switch_plan = list(over_space)
+    value, sent = add_cores(*early, plan[0], cores)
+    late_state = stay = moved = None
+    late_units = volume_grad = None
+    late_ready = None
+    for place, now in enumerate(plan):
+        got = exchange_stage(sent, *now, cores)
+        tokens = []
+        if place == 0:
+            volume_grad, done = volume_grad_of(grads, above, kernel, height, width, (sent,))
+            late = kernel_grad_part(even, odd, grads, above, (0,), cores, chips, scale, (done,))
+            late_units = late[0].shape[0]
+            tokens.append(late[0])
+        elif late_ready is None:
+            if late_state is None:
+                then = late_plan[0] if late_plan else None
+                result = add_cores(*late, then, cores, (sent,))
+            else:
+                then = late_plan[0] if late_plan else None
+                result = add_stage(*late_state, late_now, then, cores, (sent,))
+            if then is None:
+                late_ready = result
+                tokens.append(late_ready)
+            else:
+                late_now = late_plan.pop(0)
+                late_state = (result[0], exchange_stage(result[1], *late_now, cores))
+                tokens.append(result[1])
+        if place >= len(over_space) and switch_plan:
+            _, stage = switch_plan.pop(0)
+            if stay is None:
+                stay = flipped[None]
+            stay, out = switch_stage(stay, moved, stage, cores, (sent,))
+            moved = exchange_space(out, stage, cores)
+            tokens.append(out)
+        if place + 1 < len(plan):
+            value, sent = add_stage(value, got, now, plan[place + 1], cores, tuple(tokens))
+    while late_ready is None:
+        then = late_plan[0] if late_plan else None
+        result = add_stage(*late_state, late_now, then, cores)
+        if then is None:
+            late_ready = result
+        else:
+            late_now = late_plan.pop(0)
+            late_state = (result[0], exchange_stage(result[1], *late_now, cores))
+
+    mine = join(value, got, late_ready, plan[-1], cores, tuple(tokens))
+    share_units = mine.shape[0] - late_units
     switched = None
-    for stage in reversed(range(bits_of(space))):
-        got = exchange_space(pieces, stage, cores)
+    for step, (_, stage) in enumerate(reversed(over_space)):
+        got = exchange_space(mine, stage, cores)
+        order = ()
         if switched is None:
-            switched = switched_of(after(kept, pieces), arrived, space, cores)
-            got = after(got, switched)
-        pieces = jnp.concatenate([pieces, got], axis=0)
-    kernel_grad = kernel_grad_out(pieces, early_units, late_units, space, cores, co)
+            switched, done = switched_of(stay, moved, space, cores, (mine,))
+            order = (done,)
+        if step + 1 < len(over_space):
+            mine = gather_stage(mine, got, share_units << step, order)
+    kernel_grad = kernel_grad_out(mine, got, early_units, late_units, space, cores, co)
 
     return (
         switched[None],

time: 60.6 us -> 53.2 us (0.88)
  starting transfers between devices: 25.7 us -> 22.3 us
  other arithmetic: 2.71 us -> 0 us
  Pallas kernels: 12 us -> 9.95 us
  local copies, waits for them, and re-layouts: 1.45 us -> 2.72 us
    ppermute x12, starting transfers between devices: 19.4 us -> 16 us  [exchange(): return lax.ppermute(value, ('dp', 'space'), pairs)]
    add x7 -> x0, other arithmetic: 2.57 us -> none  [the longest x2 2.4 us: add_cores(): return keep + exchange(send, lambda i, j: (i ^ 1, j)).astype(F32)]
    unnamed x22 -> x8, local copies, waits for them, and re-layouts: 0.35 us -> 2.71 us
    pallas_call x1, Pallas kernels: 2.98 us -> 1.37 us  [partial_preact(): call(preact_kernel, (jax.ShapeDtypeStruct((planes // 2 * cells, co), F32)...]
    convert_element_type x8 -> x0, local copies, waits for them, and re-layouts: 1 us -> none  [the longest x4 0.92 us: early_chain(): sent = pick(value, 1 - bit).astype(BF16)]
    pallas_call x4 -> x15, Pallas kernels: 5.58 us -> 5.3 us  [the longest x1 2.59 us: volume_grad_of(): call(volume_grad_kernel, (jax.ShapeDtypeStruct(shape, BF16), jax.ShapeDty...]
  transfers between devices with their start and end apart: 14 -> 14, of which waited for: 9 -> 9; matrix products, arithmetic and copies ran while one was open for 6% -> 0% of each run, Pallas kernels for 11% -> 11%
where the time goes in v5:
time: 53.2 us; the launch traced here: 52.9 us
  starting transfers between devices  22.3 us (42%)
  waiting for transfers between devices  17.2 us (32%)
  Pallas kernels  9.95 us (19%)
  local copies, waits for them, and re-layouts  2.72 us (5%)
  between operations  0.83 us (2%)
    ppermute x12, starting transfers between devices, exchange(): return lax.ppermute(value, ('dp', 'space'), pairs)  16 us
    ppermute x12, waiting for transfers between devices, exchange(): return lax.ppermute(value, ('dp', 'space'), pairs)  13.8 us
    ppermute x2, starting transfers between devices, neighbour(): lax.ppermute(value, 'space', [(source, source + steps) for source in rang...  6.27 us
    ppermute x2, waiting for transfers between devices, neighbour(): lax.ppermute(value, 'space', [(source, source + steps) for source in rang...  3.44 us
    unnamed x8, local copies, waits for them, and re-layouts  2.71 us
    pallas_call x1, Pallas kernels, volume_grad_of(): call(volume_grad_kernel, (jax.ShapeDtypeStruct(shape, BF16), jax.ShapeDty...  2.59 us
    pallas_call x1, Pallas kernels, halo_share(): call(halo_kernel, jax.ShapeDtypeStruct((height * width // 4, co), BF16),...  2.18 us
    pallas_call x1, Pallas kernels, partial_preact(): call(preact_kernel, (jax.ShapeDtypeStruct((planes // 2 * cells, co), F32)...  1.37 us
  transfers between devices with their start and end apart: 14, of which 9 were waited for; matrix products, arithmetic and copies ran while one was open for 0% of the time, Pallas kernels for 11%

profile of v5, /device:TPU:0, one launch (start us, length us, event | category | flops | bytes accessed | tf_op | source)
XLA Modules:
  0.0 52.9 jit_solution(15571682318660311221)
XLA Ops:
  0.6 2.2 %shard_map.59 = bf16[256,256]{1,0:T(8,128)(2,1)} custom-call(bf16[1,4,32,32,128]{4,3,2,1,0:T(8,128)(2,1)} %volume_ref.3, bf16[3,3,3,128,256]{4,3,2,1,0:T(8,128)(2,1)} %refs_2_.1), custom_call_target="tpu_custom_call" | custom-call | flops 1000 | bytes 1000 | tf_op jit(solution)/shard_map/pallas_call | solution.py:112
  2.8 4.8 %collective-permute-start = (bf16[256,256]{1,0:T(8,128)(2,1)}, bf16[256,256]{1,0:T(8,128)(2,1)S(1)}, u32[]{:S(2)}, u32[]{:S(2)}) collective-permute-start(bf16[256,256]{1,0:T(8,128)(2,1)} %shard_map.59), channel_id=1, source_target_pairs={{0,1},{1,2},{2,3},{4,5},{5,6},{6,7},{8,9},{9,10},{10,11},{12,13},{... | collective-permute-start | bytes 393224 | tf_op jit(solution)/shard_map/ppermute | solution.py:516
  7.7 1.5 %copy-done = bf16[3,3,3,128,256]{4,3,2,1,0:T(8,128)(2,1)S(1)} copy-done((bf16[3,3,3,128,256]{4,3,2,1,0:T(8,128)(2,1)S(1)}, bf16[3,3,3,128,256]{4,3,2,1,0:T(8,128)(2,1)}, u32[]{:S(2)}) %copy-start) | copy-done | bytes 1769496
  9.2 1.2 %copy-done.2 = bf16[1,4,32,32,128]{4,3,2,1,0:T(8,128)(2,1)S(1)} copy-done((bf16[1,4,32,32,128]{4,3,2,1,0:T(8,128)(2,1)S(1)}, bf16[1,4,32,32,128]{4,3,2,1,0:T(8,128)(2,1)}, u32[]{:S(2)}) %copy-start.2) | copy-done | bytes 1048600
  10.4 1.4 %shard_map.58 = (f32[512,256]{1,0:T(8,128)S(1)}, bf16[4,16,16,384]{3,2,1,0:T(8,128)(2,1)S(1)}, bf16[4,17,16,384]{3,2,1,0:T(8,128)(2,1)S(1)}) custom-call(bf16[1,4,32,32,128]{4,3,2,1,0:T(8,128)(2,1)S(1)} %copy-done.2, bf16[3,3,3,128,256]{4,3,2,1,0:T(8,128)(2,1)S(1)} %copy-done), custom_call_target="tpu_custom_call" | custom-call | flops 1000 | bytes 1000 | tf_op jit(solution)/shard_map/pallas_call | solution.py:158
  11.8 0.3 shard_map.60
  12.1 0.8 %shard_map.61 = (f32[36,4,16,128]{3,2,1,0:T(8,128)S(1)}, bf16[36,4,16,128]{3,2,1,0:T(8,128)(2,1)S(1)}) custom-call(bf16[4,16,16,384]{3,2,1,0:T(8,128)(2,1)S(1)} %get-tuple-element.34.even_ref.refs_0_, bf16[4,17,16,384]{3,2,1,0:T(8,128)(2,1)S(1)} %get-tuple-element.35.odd_ref.refs_1_, bf16[512,256]{1,0:T(8,128)(2,1)S(1)} %get-tuple-element.36.grads_ref.refs_0_.refs_2_), custom_call_target="tpu_custom_call" | custom-call | flops 1000 | bytes 1000 | tf_op jit(solution)/shard_map/pallas_call | solution.py:423
  13.0 1.4 %collective-permute-start.3 = (bf16[256,256]{1,0:T(8,128)(2,1)S(1)}, bf16[256,256]{1,0:T(8,128)(2,1)S(1)}, u32[]{:S(2)}, u32[]{:S(2)}) collective-permute-start(bf16[256,256]{1,0:T(8,128)(2,1)S(1)} %slice.3), channel_id=1, source_target_pairs={{1,0},{2,1},{3,2},{5,4},{6,5},{7,6},{9,8},{10,9},{11,10},{13,12},{... | collective-permute-start | bytes 393224 | tf_op jit(solution)/shard_map/ppermute | solution.py:516
  14.4 0.5 %collective-permute-done.1.got_ref = bf16[36,4,16,128]{3,2,1,0:T(8,128)(2,1)S(1)} collective-permute-done((bf16[36,4,16,128]{3,2,1,0:T(8,128)(2,1)S(1)}, bf16[36,4,16,128]{3,2,1,0:T(8,128)(2,1)S(1)}, u32[]{:S(2)}, u32[]{:S(2)}) %collective-permute-start.1) | collective-permute-done | bytes 589856 | tf_op jit(solution)/shard_map/ppermute | solution.py:496
  15.0 0.2 shard_map.62
  15.2 2.2 %collective-permute-start.2 = (bf16[18,4,16,128]{3,2,1,0:T(8,128)(2,1)S(1)}, bf16[18,4,16,128]{3,2,1,0:T(8,128)(2,1)S(1)}, u32[]{:S(2)}, u32[]{:S(2)}) collective-permute-start(bf16[18,4,16,128]{3,2,1,0:T(8,128)(2,1)S(1)} %get-tuple-element.40.refs_3_), channel_id=1, source_target_pairs={{0,1},{1,0},{2,3},{3,2},{4,6},{5,7},{6,4},{7,5},{8,9},{9,8},{10,11... | collective-permute-start | bytes 884744 | tf_op jit(solution)/shard_map/ppermute | solution.py:496
  17.3 3.4 %collective-permute-done.3.refs_1_.refs_3_ = bf16[256,256]{1,0:T(8,128)(2,1)S(1)} collective-permute-done((bf16[256,256]{1,0:T(8,128)(2,1)S(1)}, bf16[256,256]{1,0:T(8,128)(2,1)S(1)}, u32[]{:S(2)}, u32[]{:S(2)}) %collective-permute-start.3) | collective-permute-done | bytes 131104 | tf_op jit(solution)/shard_map/ppermute | solution.py:516
  20.8 2.6 %shard_map.63 = (bf16[4,16,2,32,128]{4,3,2,1,0:T(8,128)(2,1)}, f32[8,128]{1,0:T(8,128)S(1)}) custom-call(bf16[512,256]{1,0:T(8,128)(2,1)S(1)} %get-tuple-element.36.grads_ref.refs_0_.refs_2_, bf16[256,256]{1,0:T(8,128)(2,1)S(1)} %collective-permute-done.3.refs_1_.refs_3_, bf16[3,3,3,128,256]{4,3,2,1,0:T(8,128)(2,1)S(1)} %copy-done.1, ...), custom_call_target="tpu_custom_call" | custom-call | flops 1000 | bytes 1000 | tf_op jit(solution)/shard_map/pallas_call | solution.py:477
  23.4 0.5 shard_map.64
  24.0 0.1 shard_map.65
  24.1 2.3 %collective-permute-start.4 = (bf16[9,4,16,128]{3,2,1,0:T(8,128)(2,1)S(1)}, bf16[9,4,16,128]{3,2,1,0:T(8,128)(2,1)S(1)}, u32[]{:S(2)}, u32[]{:S(2)}) collective-permute-start(bf16[9,4,16,128]{3,2,1,0:T(8,128)(2,1)S(1)} %get-tuple-element.44.refs_2_), channel_id=1, source_target_pairs={{0,2},{1,3},{2,0},{3,1},{4,5},{5,4},{6,7},{7,6},{8,10},{9,11},{10,... | collective-permute-start | bytes 442376 | tf_op jit(solution)/shard_map/ppermute | solution.py:496
  26.4 0.1 shard_map.66
  26.5 1.6 %collective-permute-start.8 = (bf16[18,2,16,128]{3,2,1,0:T(8,128)(2,1)S(1)}, bf16[18,2,16,128]{3,2,1,0:T(8,128)(2,1)S(1)}, u32[]{:S(2)}, u32[]{:S(2)}) collective-permute-start(bf16[18,2,16,128]{3,2,1,0:T(8,128)(2,1)S(1)} %get-tuple-element.46.refs_2_), channel_id=1, source_target_pairs={{0,8},{1,9},{2,10},{3,11},{4,12},{5,13},{6,14},{7,15},{8,0},{9,1},... | collective-permute-start | bytes 442376 | tf_op jit(solution)/shard_map/ppermute | solution.py:496
  28.1 1.4 %collective-permute-done.4.refs_1_ = bf16[9,4,16,128]{3,2,1,0:T(8,128)(2,1)S(1)} collective-permute-done((bf16[9,4,16,128]{3,2,1,0:T(8,128)(2,1)S(1)}, bf16[9,4,16,128]{3,2,1,0:T(8,128)(2,1)S(1)}, u32[]{:S(2)}, u32[]{:S(2)}) %collective-permute-start.4) | collective-permute-done | bytes 147488 | tf_op jit(solution)/shard_map/ppermute | solution.py:496
  29.6 2.3 %collective-permute-start.6 = (bf16[1,2,4,64,128]{4,3,2,1,0:T(8,128)(2,1)S(1)}, bf16[1,2,4,64,128]{4,3,2,1,0:T(8,128)(2,1)S(1)}, u32[]{:S(2)}, u32[]{:S(2)}) collective-permute-start(bf16[1,2,4,64,128]{4,3,2,1,0:T(8,128)(2,1)S(1)} %get-tuple-element.49.refs_3_), channel_id=1, source_target_pairs={{0,1},{1,0},{2,3},{3,2},{4,6},{5,7},{6,4},{7,5},{8,9},{9,8},{10,11... | collective-permute-start | bytes 393224 | tf_op jit(solution)/shard_map/ppermute | solution.py:496
  31.9 1.6 %collective-permute-start.7 = (bf16[9,2,16,128]{3,2,1,0:T(8,128)(2,1)S(1)}, bf16[9,2,16,128]{3,2,1,0:T(8,128)(2,1)S(1)}, u32[]{:S(2)}, u32[]{:S(2)}) collective-permute-start(bf16[9,2,16,128]{3,2,1,0:T(8,128)(2,1)S(1)} %get-tuple-element.47.refs_1_.refs_2_), channel_id=1, source_target_pairs={{0,8},{1,9},{2,10},{3,11},{4,12},{5,13},{6,14},{7,15},{8,0},{9,1},... | collective-permute-start | bytes 221192 | tf_op jit(solution)/shard_map/ppermute | solution.py:496
  33.6 2.7 %collective-permute-start.11 = (bf16[18,1,16,128]{3,2,1,0:T(8,128)(2,1)S(1)}, bf16[18,1,16,128]{3,2,1,0:T(8,128)(2,1)S(1)}, u32[]{:S(2)}, u32[]{:S(2)}) collective-permute-start(bf16[18,1,16,128]{3,2,1,0:T(8,128)(2,1)S(1)} %get-tuple-element.52.refs_2_), channel_id=1, source_target_pairs={{0,16},{1,17},{2,18},{3,19},{4,20},{5,21},{6,22},{7,23},{8,24},{9,... | collective-permute-start | bytes 221192 | tf_op jit(solution)/shard_map/ppermute | solution.py:496
  36.2 0.9 %collective-permute-done.7.refs_1_ = bf16[9,2,16,128]{3,2,1,0:T(8,128)(2,1)S(1)} collective-permute-done((bf16[9,2,16,128]{3,2,1,0:T(8,128)(2,1)S(1)}, bf16[9,2,16,128]{3,2,1,0:T(8,128)(2,1)S(1)}, u32[]{:S(2)}, u32[]{:S(2)}) %collective-permute-start.7) | collective-permute-done | bytes 73760 | tf_op jit(solution)/shard_map/ppermute | solution.py:496
  37.1 2.2 %collective-permute-start.10 = (bf16[9,1,16,128]{3,2,1,0:T(8,128)(2,1)S(1)}, bf16[9,1,16,128]{3,2,1,0:T(8,128)(2,1)S(1)}, u32[]{:S(2)}, u32[]{:S(2)}) collective-permute-start(bf16[9,1,16,128]{3,2,1,0:T(8,128)(2,1)S(1)} %get-tuple-element.53.refs_2_), channel_id=1, source_target_pairs={{0,16},{1,17},{2,18},{3,19},{4,20},{5,21},{6,22},{7,23},{8,24},{9,... | collective-permute-start | bytes 110600 | tf_op jit(solution)/shard_map/ppermute | solution.py:496
  39.3 0.8 %collective-permute-start.9 = (bf16[2,1,4,64,128]{4,3,2,1,0:T(8,128)(2,1)S(1)}, bf16[2,1,4,64,128]{4,3,2,1,0:T(8,128)(2,1)S(1)}, u32[]{:S(2)}, u32[]{:S(2)}) collective-permute-start(bf16[2,1,4,64,128]{4,3,2,1,0:T(8,128)(2,1)S(1)} %get-tuple-element.55.refs_4_), channel_id=1, source_target_pairs={{0,2},{1,3},{2,0},{3,1},{4,5},{5,4},{6,7},{7,6},{8,10},{9,11},{10,... | collective-permute-start | bytes 393224 | tf_op jit(solution)/shard_map/ppermute | solution.py:496
  40.1 0.4 collective-permute-done.11.refs_1_
  40.6 1.5 %collective-permute-done.10.refs_1_ = bf16[9,1,16,128]{3,2,1,0:T(8,128)(2,1)S(1)} collective-permute-done((bf16[9,1,16,128]{3,2,1,0:T(8,128)(2,1)S(1)}, bf16[9,1,16,128]{3,2,1,0:T(8,128)(2,1)S(1)}, u32[]{:S(2)}, u32[]{:S(2)}) %collective-permute-start.10) | collective-permute-done | bytes 36896 | tf_op jit(solution)/shard_map/ppermute | solution.py:496
  42.1 2.2 %collective-permute-done.9 = bf16[2,1,4,64,128]{4,3,2,1,0:T(8,128)(2,1)S(1)} collective-permute-done((bf16[2,1,4,64,128]{4,3,2,1,0:T(8,128)(2,1)S(1)}, bf16[2,1,4,64,128]{4,3,2,1,0:T(8,128)(2,1)S(1)}, u32[]{:S(2)}, u32[]{:S(2)}) %collective-permute-start.9) | collective-permute-done | bytes 131104 | tf_op jit(solution)/shard_map/ppermute | solution.py:496
  44.3 0.8 %shard_map.74 = (bf16[64,2048]{1,0:T(8,128)(2,1)}, f32[8,128]{1,0:T(8,128)S(1)}) custom-call(bf16[8,64,128]{2,1,0:T(8,128)(2,1)S(1)} %bitcast.11, bf16[8,64,128]{2,1,0:T(8,128)(2,1)S(1)} %bitcast.12, bf16[27,16,128]{2,1,0:T(8,128)(2,1)S(1)} %shard_map.73.refs_2_.refs_0_), custom_call_target="tpu_custom_call" | custom-call | flops 1000 | bytes 1000 | tf_op jit(solution)/shard_map/pallas_call | solution.py:219
  45.1 1.8 %collective-permute-done.12.refs_1_ = bf16[27,16,128]{2,1,0:T(8,128)(2,1)S(1)} collective-permute-done((bf16[27,16,128]{2,1,0:T(8,128)(2,1)S(1)}, bf16[27,16,128]{2,1,0:T(8,128)(2,1)S(1)}, u32[]{:S(2)}, u32[]{:S(2)}) %collective-permute-start.12) | collective-permute-done | bytes 110624 | tf_op jit(solution)/shard_map/ppermute | solution.py:496
  47.0 5.1 %collective-permute-done.13.got_ref = bf16[36,16,128]{2,1,0:T(8,128)(2,1)S(1)} collective-permute-done((bf16[36,16,128]{2,1,0:T(8,128)(2,1)S(1)}, bf16[36,16,128]{2,1,0:T(8,128)(2,1)S(1)}, u32[]{:S(2)}, u32[]{:S(2)}) %collective-permute-start.13) | collective-permute-done | bytes 147488 | tf_op jit(solution)/shard_map/ppermute | solution.py:496
  52.1 0.8 %shard_map.76 = f32[27,16,256]{2,1,0:T(8,128)} custom-call(bf16[36,16,128]{2,1,0:T(8,128)(2,1)S(1)} %shard_map.75.mine_ref, bf16[36,16,128]{2,1,0:T(8,128)(2,1)S(1)} %collective-permute-done.13.got_ref), custom_call_target="tpu_custom_call" | custom-call | flops 1000 | bytes 1000 | tf_op jit(solution)/shard_map/pallas_call | solution.py:365
  (24 shorter events, 0.6 us)
Async XLA Ops:
  2.8 8.9 %collective-permute-start = (bf16[256,256]{1,0:T(8,128)(2,1)}, bf16[256,256]{1,0:T(8,128)(2,1)S(1)}, u32[]{:S(2)}, u32[]{:S(2)}) collective-permute-start(bf16[256,256]{1,0:T(8,128)(2,1)} %shard_map.59), channel_id=1, source_target_pairs={{0,1},{1,2},{2,3},{4,5},{5,6},{6,7},{8,9},{9,10},{10,11},{12,13},{... | collective-permute-start | bytes 393224 | tf_op jit(solution)/shard_map/ppermute | solution.py:516
  7.7 1.5 %copy-start = (bf16[3,3,3,128,256]{4,3,2,1,0:T(8,128)(2,1)S(1)}, bf16[3,3,3,128,256]{4,3,2,1,0:T(8,128)(2,1)}, u32[]{:S(2)}) copy-start(bf16[3,3,3,128,256]{4,3,2,1,0:T(8,128)(2,1)} %refs_2_.1) | copy-start | bytes 5308420
  9.2 1.2 %copy-start.2 = (bf16[1,4,32,32,128]{4,3,2,1,0:T(8,128)(2,1)S(1)}, bf16[1,4,32,32,128]{4,3,2,1,0:T(8,128)(2,1)}, u32[]{:S(2)}) copy-start(bf16[1,4,32,32,128]{4,3,2,1,0:T(8,128)(2,1)} %volume_ref.3) | copy-start | bytes 3145732
  10.4 1.4 %copy-start.3 = (bf16[1,2,16,16,256]{4,3,2,1,0:T(8,128)(2,1)S(1)}, bf16[1,2,16,16,256]{4,3,2,1,0:T(8,128)(2,1)}, u32[]{:S(2)}) copy-start(bf16[1,2,16,16,256]{4,3,2,1,0:T(8,128)(2,1)} %param.5) | copy-start | bytes 786436
  12.9 7.9 %copy-start.1 = (bf16[3,3,3,128,256]{4,3,2,1,0:T(8,128)(2,1)S(1)}, bf16[3,3,3,128,256]{4,3,2,1,0:T(8,128)(2,1)}, u32[]{:S(2)}) copy-start(bf16[3,3,3,128,256]{4,3,2,1,0:T(8,128)(2,1)} %refs_2_.1) | copy-start | bytes 5308420
  12.9 2.1 %collective-permute-start.1 = (bf16[36,4,16,128]{3,2,1,0:T(8,128)(2,1)S(1)}, bf16[36,4,16,128]{3,2,1,0:T(8,128)(2,1)S(1)}, u32[]{:S(2)}, u32[]{:S(2)}) collective-permute-start(bf16[36,4,16,128]{3,2,1,0:T(8,128)(2,1)S(1)} %get-tuple-element.38), channel_id=1, source_target_pairs={{0,4},{1,5},{2,6},{3,7},{4,0},{5,1},{6,2},{7,3},{8,12},{9,13},{10,... | collective-permute-start | bytes 1769480 | tf_op jit(solution)/shard_map/ppermute | solution.py:496
  13.0 7.8 %collective-permute-start.3 = (bf16[256,256]{1,0:T(8,128)(2,1)S(1)}, bf16[256,256]{1,0:T(8,128)(2,1)S(1)}, u32[]{:S(2)}, u32[]{:S(2)}) collective-permute-start(bf16[256,256]{1,0:T(8,128)(2,1)S(1)} %slice.3), channel_id=1, source_target_pairs={{1,0},{2,1},{3,2},{5,4},{6,5},{7,6},{9,8},{10,9},{11,10},{13,12},{... | collective-permute-start | bytes 393224 | tf_op jit(solution)/shard_map/ppermute | solution.py:516
  15.2 8.8 %collective-permute-start.2 = (bf16[18,4,16,128]{3,2,1,0:T(8,128)(2,1)S(1)}, bf16[18,4,16,128]{3,2,1,0:T(8,128)(2,1)S(1)}, u32[]{:S(2)}, u32[]{:S(2)}) collective-permute-start(bf16[18,4,16,128]{3,2,1,0:T(8,128)(2,1)S(1)} %get-tuple-element.40.refs_3_), channel_id=1, source_target_pairs={{0,1},{1,0},{2,3},{3,2},{4,6},{5,7},{6,4},{7,5},{8,9},{9,8},{10,11... | collective-permute-start | bytes 884744 | tf_op jit(solution)/shard_map/ppermute | solution.py:496
  23.9 2.5 %collective-permute-start.5 = (bf16[18,4,16,128]{3,2,1,0:T(8,128)(2,1)S(1)}, bf16[18,4,16,128]{3,2,1,0:T(8,128)(2,1)S(1)}, u32[]{:S(2)}, u32[]{:S(2)}) collective-permute-start(bf16[18,4,16,128]{3,2,1,0:T(8,128)(2,1)S(1)} %get-tuple-element.45), channel_id=1, source_target_pairs={{0,4},{1,5},{2,6},{3,7},{4,0},{5,1},{6,2},{7,3},{8,12},{9,13},{10,... | collective-permute-start | bytes 884744 | tf_op jit(solution)/shard_map/ppermute | solution.py:496
  24.1 5.4 %collective-permute-start.4 = (bf16[9,4,16,128]{3,2,1,0:T(8,128)(2,1)S(1)}, bf16[9,4,16,128]{3,2,1,0:T(8,128)(2,1)S(1)}, u32[]{:S(2)}, u32[]{:S(2)}) collective-permute-start(bf16[9,4,16,128]{3,2,1,0:T(8,128)(2,1)S(1)} %get-tuple-element.44.refs_2_), channel_id=1, source_target_pairs={{0,2},{1,3},{2,0},{3,1},{4,5},{5,4},{6,7},{7,6},{8,10},{9,11},{10,... | collective-permute-start | bytes 442376 | tf_op jit(solution)/shard_map/ppermute | solution.py:496
  26.5 7.0 %collective-permute-start.8 = (bf16[18,2,16,128]{3,2,1,0:T(8,128)(2,1)S(1)}, bf16[18,2,16,128]{3,2,1,0:T(8,128)(2,1)S(1)}, u32[]{:S(2)}, u32[]{:S(2)}) collective-permute-start(bf16[18,2,16,128]{3,2,1,0:T(8,128)(2,1)S(1)} %get-tuple-element.46.refs_2_), channel_id=1, source_target_pairs={{0,8},{1,9},{2,10},{3,11},{4,12},{5,13},{6,14},{7,15},{8,0},{9,1},... | collective-permute-start | bytes 442376 | tf_op jit(solution)/shard_map/ppermute | solution.py:496
  29.6 9.7 %collective-permute-start.6 = (bf16[1,2,4,64,128]{4,3,2,1,0:T(8,128)(2,1)S(1)}, bf16[1,2,4,64,128]{4,3,2,1,0:T(8,128)(2,1)S(1)}, u32[]{:S(2)}, u32[]{:S(2)}) collective-permute-start(bf16[1,2,4,64,128]{4,3,2,1,0:T(8,128)(2,1)S(1)} %get-tuple-element.49.refs_3_), channel_id=1, source_target_pairs={{0,1},{1,0},{2,3},{3,2},{4,6},{5,7},{6,4},{7,5},{8,9},{9,8},{10,11... | collective-permute-start | bytes 393224 | tf_op jit(solution)/shard_map/ppermute | solution.py:496
  31.9 5.1 %collective-permute-start.7 = (bf16[9,2,16,128]{3,2,1,0:T(8,128)(2,1)S(1)}, bf16[9,2,16,128]{3,2,1,0:T(8,128)(2,1)S(1)}, u32[]{:S(2)}, u32[]{:S(2)}) collective-permute-start(bf16[9,2,16,128]{3,2,1,0:T(8,128)(2,1)S(1)} %get-tuple-element.47.refs_1_.refs_2_), channel_id=1, source_target_pairs={{0,8},{1,9},{2,10},{3,11},{4,12},{5,13},{6,14},{7,15},{8,0},{9,1},... | collective-permute-start | bytes 221192 | tf_op jit(solution)/shard_map/ppermute | solution.py:496
  33.6 7.0 %collective-permute-start.11 = (bf16[18,1,16,128]{3,2,1,0:T(8,128)(2,1)S(1)}, bf16[18,1,16,128]{3,2,1,0:T(8,128)(2,1)S(1)}, u32[]{:S(2)}, u32[]{:S(2)}) collective-permute-start(bf16[18,1,16,128]{3,2,1,0:T(8,128)(2,1)S(1)} %get-tuple-element.52.refs_2_), channel_id=1, source_target_pairs={{0,16},{1,17},{2,18},{3,19},{4,20},{5,21},{6,22},{7,23},{8,24},{9,... | collective-permute-start | bytes 221192 | tf_op jit(solution)/shard_map/ppermute | solution.py:496
  37.1 4.9 %collective-permute-start.10 = (bf16[9,1,16,128]{3,2,1,0:T(8,128)(2,1)S(1)}, bf16[9,1,16,128]{3,2,1,0:T(8,128)(2,1)S(1)}, u32[]{:S(2)}, u32[]{:S(2)}) collective-permute-start(bf16[9,1,16,128]{3,2,1,0:T(8,128)(2,1)S(1)} %get-tuple-element.53.refs_2_), channel_id=1, source_target_pairs={{0,16},{1,17},{2,18},{3,19},{4,20},{5,21},{6,22},{7,23},{8,24},{9,... | collective-permute-start | bytes 110600 | tf_op jit(solution)/shard_map/ppermute | solution.py:496
  39.3 5.0 %collective-permute-start.9 = (bf16[2,1,4,64,128]{4,3,2,1,0:T(8,128)(2,1)S(1)}, bf16[2,1,4,64,128]{4,3,2,1,0:T(8,128)(2,1)S(1)}, u32[]{:S(2)}, u32[]{:S(2)}) collective-permute-start(bf16[2,1,4,64,128]{4,3,2,1,0:T(8,128)(2,1)S(1)} %get-tuple-element.55.refs_4_), channel_id=1, source_target_pairs={{0,2},{1,3},{2,0},{3,1},{4,5},{5,4},{6,7},{7,6},{8,10},{9,11},{10,... | collective-permute-start | bytes 393224 | tf_op jit(solution)/shard_map/ppermute | solution.py:496
  42.1 4.8 %collective-permute-start.12 = (bf16[27,16,128]{2,1,0:T(8,128)(2,1)S(1)}, bf16[27,16,128]{2,1,0:T(8,128)(2,1)S(1)}, u32[]{:S(2)}, u32[]{:S(2)}) collective-permute-start(bf16[27,16,128]{2,1,0:T(8,128)(2,1)S(1)} %shard_map.73.refs_2_.refs_0_), channel_id=1, source_target_pairs={{0,2},{1,3},{2,0},{3,1},{4,5},{5,4},{6,7},{7,6},{8,10},{9,11},{10,... | collective-permute-start | bytes 331784 | tf_op jit(solution)/shard_map/ppermute | solution.py:496
  46.9 5.2 %collective-permute-start.13 = (bf16[36,16,128]{2,1,0:T(8,128)(2,1)S(1)}, bf16[36,16,128]{2,1,0:T(8,128)(2,1)S(1)}, u32[]{:S(2)}, u32[]{:S(2)}) collective-permute-start(bf16[36,16,128]{2,1,0:T(8,128)(2,1)S(1)} %shard_map.75.mine_ref), channel_id=1, source_target_pairs={{0,1},{1,0},{2,3},{3,2},{4,6},{5,7},{6,4},{7,5},{8,9},{9,8},{10,11... | collective-permute-start | bytes 442376 | tf_op jit(solution)/shard_map/ppermute | solution.py:496

commit v6 on v5

--- a/solution.py
+++ b/solution.py
@@ -12,10 +12,12 @@
 F32 = jnp.float32
 VMEM_LIMIT = 20 * 1024 * 1024
 DONE = (8, 128)
+PLANE_PARTS = 4
+SPACER = 6 * 10**9
 VMEM_WHOLE = 63 * 1024 * 1024
 
 
-def call(kernel, out_shape, scratch=(), in_specs=None, limit=VMEM_LIMIT, order=(), inputs=0):
+def call(kernel, out_shape, scratch=(), in_specs=None, limit=VMEM_LIMIT, order=(), inputs=0, flops=1000):
     extra = {} if in_specs is None else {"in_specs": in_specs}
     if order:
         whole = pl.BlockSpec(memory_space=pltpu.VMEM)
@@ -30,7 +32,7 @@
         out_shape=out_shape,
         scratch_shapes=list(scratch),
         compiler_params=pltpu.CompilerParams(vmem_limit_bytes=limit),
-        cost_estimate=pl.CostEstimate(flops=1000, bytes_accessed=1000, transcendentals=0),
+        cost_estimate=pl.CostEstimate(flops=flops, bytes_accessed=1000, transcendentals=0),
         **extra,
     )
 
@@ -89,16 +91,25 @@
 
 def halo_kernel(volume_ref, kernel_ref, share_ref, plane, weights, wide, sems):
     planes, height, width, chans = volume_ref.shape[1:]
-    first = pltpu.make_async_copy(volume_ref.at[0, planes - 1], plane, sems.at[0])
-    second = pltpu.make_async_copy(kernel_ref.at[0], weights, sems.at[1])
-    first.start()
-    second.start()
-    first.wait()
+    part = height // PLANE_PARTS
+    rows = [pl.ds(index * part, part) for index in range(PLANE_PARTS)]
+    copies = [
+        pltpu.make_async_copy(volume_ref.at[0, planes - 1, row], plane.at[row], sems.at[index])
+        for index, row in enumerate(rows)
+    ]
+    loads = [
+        pltpu.make_async_copy(kernel_ref.at[0, kh], weights.at[kh], sems.at[PLANE_PARTS + kh])
+        for kh in range(3)
+    ]
+    for copy in copies + loads:
+        copy.start()
+    for copy in copies:
+        copy.wait()
     even, odd = spread_plane(plane[...], wide)
     above = jnp.concatenate([jnp.zeros_like(odd[:1]), odd[:-1]], axis=0)
-    second.wait()
     total = None
     for kh, rows in enumerate((above, even, odd)):
+        loads[kh].wait()
         lhs = rows.reshape(height * width // 4, 3 * chans)
         rhs = weights[kh].reshape(3 * chans, weights.shape[-1])
         term = jnp.dot(lhs, rhs, preferred_element_type=F32)
@@ -116,7 +127,7 @@
             pltpu.VMEM((height, width, chans), BF16),
             pltpu.VMEM((3, 3, chans, co), BF16),
             pltpu.VMEM((height * width + 16, chans), F32),
-            pltpu.SemaphoreType.DMA((2,)),
+            pltpu.SemaphoreType.DMA((PLANE_PARTS + 3,)),
         ],
         [pl.BlockSpec(memory_space=pltpu.HBM)] * 2,
         VMEM_WHOLE,
@@ -199,25 +210,26 @@
     )(preact, share, cotangent)
 
 
-def switched_kernel(space, cores, kept_ref, got_ref, out_ref, done_ref):
+def switched_kernel(space, cores, came, kept_ref, got_ref, out_ref, done_ref):
     done_ref[...] = jnp.zeros_like(done_ref)
     half = space // 2
+    rows = kept_ref.shape[1]
     strips = kept_ref.shape[0] // half
     for source in range(space):
         place = relative_place(source, space, cores)
+        far = place // half
         for strip in range(strips):
             column = (source * strips + strip) * 128
-            far = place // half
             row = (place % half) * strips + strip
-            out_ref[:, column : column + 128] = jnp.where(far == 1, got_ref[row], kept_ref[row])
-
-
-def switched_of(kept, got, space, cores, order):
+            there = got_ref[pl.ds(pl.multiple_of(came + row * rows, rows), rows), :]
+            out_ref[:, column : column + 128] = jnp.where(far == 1, there, kept_ref[row])
+
+
+def switched_of(kept, got, came, space, cores, order):
     group = kept.shape[-2]
     kept = kept.reshape(-1, group, 128)
-    got = got.reshape(-1, group, 128)
-    return call(
-        functools.partial(switched_kernel, space, cores),
+    return call(
+        functools.partial(switched_kernel, space, cores, came),
         (
             jax.ShapeDtypeStruct((group, 2 * kept.shape[0] * 128), BF16),
             jax.ShapeDtypeStruct(DONE, F32),
@@ -246,72 +258,106 @@
     return ((units // 2, chips) if axis == "space" else (units, chips // 2)) + tuple(shape[2:])
 
 
-def add_kernel(now, then, cores, value_ref, got_ref, *outs):
-    if now is None:
-        total = value_ref[...]
-    else:
-        total = value_ref[:, side(*now, cores)]
-    total = total.reshape(got_ref.shape) + got_ref[...].astype(F32)
+def add_kernel(now, then, cores, value_ref, *refs):
+    keep_ref, sent_ref = refs[-2:]
+    got = jnp.concatenate([ref[...] for ref in refs[:-2]], axis=0).astype(F32)
+    total = value_ref[...] if now is None else value_ref[:, side(*now, cores)]
+    total = total.reshape(got.shape) + got
     if then is None:
-        outs[0][...] = total.astype(BF16)
+        keep_ref[...] = total
+        sent_ref[...] = total.astype(BF16)
         return
-    keep_ref, sent_ref = outs
     keep_ref[...] = total.reshape(keep_ref.shape)
     sent_ref[...] = keep_ref[:, 1 - side(*then, cores)].reshape(sent_ref.shape).astype(BF16)
 
 
-def add_stage(value, got, now, then, cores, order=()):
-    shape = got.shape
+def add_stage(value, got, now, then, cores, order=(), flops=1000):
+    shape = (sum(piece.shape[0] for piece in got),) + got[0].shape[1:]
     if then is None:
-        outs = jax.ShapeDtypeStruct(shape, BF16)
+        outs = (jax.ShapeDtypeStruct(shape, F32), jax.ShapeDtypeStruct(shape, BF16))
     else:
         outs = (
             jax.ShapeDtypeStruct(halves_of(shape, then[0]), F32),
             jax.ShapeDtypeStruct(half_shape(shape, then[0]), BF16),
         )
     return call(
-        functools.partial(add_kernel, now, then, cores), outs, order=order, inputs=2
-    )(value, got, *order)
-
-
-def switch_kernel(stage, cores, first_ref, *refs):
-    got_ref = refs[0] if len(refs) == 3 else None
+        functools.partial(add_kernel, now, then, cores),
+        outs,
+        order=order,
+        inputs=1 + len(got),
+        flops=flops,
+    )(value, *got, *order)
+
+
+def switch_kernel(stage, cores, came, first_ref, *refs):
     stay_ref, out_ref = refs[-2:]
+    refs = list(refs[:-2])
     bit = side("space", stage, cores)
-    sources = first_ref.shape[0]
-    for part, ref in enumerate((first_ref, got_ref)):
-        if ref is not None:
-            for source in range(sources):
-                stay_ref[part * sources + source] = ref[source, bit]
-                out_ref[part * sources + source] = ref[source, 1 - bit]
-
-
-def switch_stage(first, got, stage, cores, order):
-    sources, targets = first.shape[:2]
-    split = (sources, 2, targets // 2) + first.shape[2:]
-    operands = (first.reshape(split),) + ((got.reshape(split),) if got is not None else ())
-    shape = jax.ShapeDtypeStruct((sources * len(operands), targets // 2) + first.shape[2:], BF16)
-    return call(
-        functools.partial(switch_kernel, stage, cores),
-        (shape, shape),
+    sources, _, targets, strips, rows, lanes = first_ref.shape
+    half = targets * strips * rows
+    if came is None:
+        ahead = out_ref.shape[0] - sources * half
+    else:
+        ahead = out_ref.shape[0] - 2 * sources * half
+    rider = refs.pop() if ahead else None
+    if rider is not None:
+        out_ref[pl.ds(0, ahead), :] = rider[...]
+    place = ahead
+    for source in range(sources):
+        stay_ref[source] = first_ref[source, bit]
+        out_ref[pl.ds(place, half), :] = first_ref[source, 1 - bit].reshape(half, lanes)
+        place += half
+    if came is not None:
+        got_ref = refs[0]
+        for source in range(sources):
+            base = came + source * 2 * half
+            mine = got_ref[pl.ds(pl.multiple_of(base + bit * half, rows), half), :]
+            stay_ref[sources + source] = mine.reshape(targets, strips, rows, lanes)
+            out_ref[pl.ds(place, half), :] = got_ref[
+                pl.ds(pl.multiple_of(base + (1 - bit) * half, rows), half), :
+            ]
+            place += half
+
+
+def switch_stage(first, got, came, rider, stage, cores, order):
+    sources, targets, strips, rows, lanes = first.shape
+    operands = (first.reshape(sources, 2, targets // 2, strips, rows, lanes),)
+    total = sources * (1 if got is None else 2)
+    count = total * targets // 2 * strips * rows
+    if got is not None:
+        operands += (got,)
+    if rider is not None:
+        operands += (rider.reshape(-1, lanes),)
+        count += operands[-1].shape[0]
+    return call(
+        functools.partial(switch_kernel, stage, cores, None if got is None else came),
+        (
+            jax.ShapeDtypeStruct((total, targets // 2, strips, rows, lanes), BF16),
+            jax.ShapeDtypeStruct((count, lanes), BF16),
+        ),
         order=order,
         inputs=len(operands),
     )(*operands, *order)
 
 
-def gather_kernel(early_count, mine_ref, got_ref, out_ref):
-    out_ref[pl.ds(0, early_count)] = mine_ref[pl.ds(0, early_count)]
-    out_ref[pl.ds(early_count, early_count)] = got_ref[pl.ds(0, early_count)]
-    late = mine_ref.shape[0] - early_count
-    rows = pl.ds(early_count, late)
-    total = mine_ref[rows].astype(F32) + got_ref[rows].astype(F32)
-    out_ref[pl.ds(2 * early_count, late)] = total.astype(BF16)
-
-
-def gather_stage(mine, got, early_count, order):
-    shape = (mine.shape[0] + early_count,) + mine.shape[1:]
-    return call(
-        functools.partial(gather_kernel, early_count),
+def gather_kernel(early, add_late, mine_ref, got_ref, out_ref):
+    late = mine_ref.shape[0] - early
+    rows = pl.ds(early, late)
+    out_ref[pl.ds(0, early)] = mine_ref[pl.ds(0, early)]
+    out_ref[pl.ds(early, early)] = got_ref[pl.ds(0, early)]
+    if add_late:
+        total = mine_ref[rows].astype(F32) + got_ref[rows].astype(F32)
+        out_ref[pl.ds(2 * early, late)] = total.astype(BF16)
+    else:
+        out_ref[pl.ds(2 * early, late)] = mine_ref[rows]
+        out_ref[pl.ds(2 * early + late, late)] = got_ref[rows]
+
+
+def gather_stage(mine, got, early, add_late, order=()):
+    late = mine.shape[0] - early
+    shape = (2 * early + (late if add_late else 2 * late),) + mine.shape[1:]
+    return call(
+        functools.partial(gather_kernel, early, add_late),
         jax.ShapeDtypeStruct(shape, BF16),
         order=order,
         inputs=2,
@@ -332,38 +378,48 @@
         jax.ShapeDtypeStruct(shape, BF16),
         order=order,
         inputs=3,
+        flops=SPACER,
     )(value, got, late, *order)
 
 
-def kernel_grad_out_kernel(space, cores, early_units, share, mine_ref, got_ref, out_ref):
+def kernel_grad_out_kernel(space, cores, early_units, late_units, mine_ref, got_ref, out_ref):
     halves = out_ref.shape[-1] // 128
-    count = mine_ref.shape[0]
-    late_units = out_ref.shape[0] * halves - early_units
-    near = share * (space // 2)
+    half = space // 2
+    share = -(-early_units // space)
+    late_share = late_units if space == 2 else -(-late_units // half)
 
     def put(index, value):
-        tap, half = divmod(index, halves)
-        out_ref[tap, :, half * 128 : (half + 1) * 128] = value
-
-    for index in range(late_units):
-        row = near + index
-        put(index, mine_ref[row].astype(F32) + got_ref[row].astype(F32))
+        tap, part = divmod(index, halves)
+        out_ref[tap, :, part * 128 : (part + 1) * 128] = value
+
     for group in range(space):
         place = relative_group(group, space, cores)
-        far = place // (space // 2)
-        row = (place % (space // 2)) * share
+        far, row = place // half, (place % half) * share
         for unit in range(share):
             index = group * share + unit
             if index < early_units:
                 value = jnp.where(far == 1, got_ref[row + unit], mine_ref[row + unit])
                 put(late_units + index, value.astype(F32))
+    base = half * share
+    if space == 2:
+        for unit in range(late_units):
+            put(unit, mine_ref[base + unit].astype(F32) + got_ref[base + unit].astype(F32))
+        return
+    inner = half // 2
+    for group in range(half):
+        place = relative_group(2 * group, space, cores) // 2
+        far, row = place // inner, base + (place % inner) * late_share
+        for unit in range(late_share):
+            index = group * late_share + unit
+            if index < late_units:
+                value = jnp.where(far == 1, got_ref[row + unit], mine_ref[row + unit])
+                put(index, value.astype(F32))
 
 
 def kernel_grad_out(mine, got, early_units, late_units, space, cores, co):
     taps = (early_units + late_units) * 128 // co
-    share = -(-early_units // space)
-    return call(
-        functools.partial(kernel_grad_out_kernel, space, cores, early_units, share),
+    return call(
+        functools.partial(kernel_grad_out_kernel, space, cores, early_units, late_units),
         jax.ShapeDtypeStruct((taps, mine.shape[1], co), F32),
     )(mine, got)
 
@@ -386,13 +442,17 @@
                 put(kw * halves + half, chip, keep, send)
 
 
-def kernel_grad_kernel(kds, cores, chips, scale, even_ref, odd_ref, grads_ref, *refs):
+def kernel_grad_kernel(kds, cores, chips, scale, parts, even_ref, odd_ref, grads_ref, *refs):
     above_ref = refs[0] if 0 in kds else None
-    keep_ref, send_ref = refs[-2:]
+    keep_ref, send_refs = refs[-1 - parts], refs[-parts:]
+    size = send_refs[0].shape[0]
     outs = even_ref.shape[0] // 2
     cells = even_ref.shape[1] * even_ref.shape[2]
     core = lax.axis_index("dp") % cores
     per_row = 3 * (grads_ref.shape[1] // 128)
+    for unit in range(len(kds) * 3 * per_row, keep_ref.shape[0]):
+        keep_ref[unit] = jnp.zeros(keep_ref.shape[1:], F32)
+        send_refs[unit // size][unit % size] = jnp.zeros(keep_ref.shape[1:], BF16)
     for place, kd in enumerate(kds):
         if kd == 0:
             planes = [2 * d - 1 for d in range(1, outs + 1)]
@@ -409,20 +469,22 @@
 
             def put(unit, chip, keep, send, base=(place * 3 + kh) * per_row):
                 keep_ref[base + unit, chip] = keep
-                send_ref[base + unit, chip] = send.astype(BF16)
+                send_refs[(base + unit) // size][(base + unit) % size, chip] = send.astype(BF16)
 
             store_units(product, scale, core, cores, chips, put)
 
 
-def kernel_grad_part(even, odd, grads, above, kds, cores, chips, scale, order=()):
+def kernel_grad_part(even, odd, grads, above, kds, cores, chips, scale, multiple, parts=1, order=()):
     chans = even.shape[-1] // 3
     co = grads.shape[-1]
     units = len(kds) * 9 * (co // 128)
+    units += -units % math.lcm(multiple, parts)
     shape = (units, chips, chans // (cores * chips), 128)
     operands = (even, odd, grads) + ((above,) if 0 in kds else ())
     return call(
-        functools.partial(kernel_grad_kernel, kds, cores, chips, scale),
-        (jax.ShapeDtypeStruct(shape, F32), jax.ShapeDtypeStruct(shape, BF16)),
+        functools.partial(kernel_grad_kernel, kds, cores, chips, scale, parts),
+        (jax.ShapeDtypeStruct(shape, F32),)
+        + (jax.ShapeDtypeStruct((units // parts,) + shape[1:], BF16),) * parts,
         order=order,
         inputs=len(operands),
     )(*operands, *order)
@@ -520,17 +582,9 @@
     return exchange_space(value, stage, cores) if axis == "space" else exchange_chips(value, stage, cores)
 
 
-def add_cores(keep, send, then, cores, order=()):
-    if cores == 1:
-        got = jnp.zeros_like(send)
-    else:
-        got = exchange(send, lambda i, j: (i ^ 1, j))
+def add_cores(keep, sends, then, cores, order=()):
+    got = tuple(exchange(send, lambda i, j: (i ^ 1, j)) if cores == 2 else 0 * send for send in sends)
     return add_stage(keep, got, None, then, cores, order)
-
-
-def pad_units(value, space):
-    extra = -value.shape[0] % space
-    return jnp.pad(value, ((0, extra),) + ((0, 0),) * (value.ndim - 1)) if extra else value
 
 
 def body(volume, kernel, cotangent):
@@ -551,67 +605,60 @@
     grads, flipped = activation(preact, share, cotangent.reshape(outs * cells, co), space, cores)
     above = neighbour(grads[:cells], -1)
 
-    early = kernel_grad_part(even, odd, grads, None, (1, 2), cores, chips, scale)
-    early_units = early[0].shape[0]
-    early = [pad_units(half, space) for half in early]
+    early = kernel_grad_part(even, odd, grads, None, (1, 2), cores, chips, scale, space)
+    early_units, late_units = 18 * (co // 128), 9 * (co // 128)
     plan = over_space + over_chips
-    late_plan = list(over_chips)
+    late_plan = over_chips + over_space[:-1]
     switch_plan = list(over_space)
-    value, sent = add_cores(*early, plan[0], cores)
-    late_state = stay = moved = None
-    late_units = volume_grad = None
-    late_ready = None
+    value, sent = add_cores(early[0], early[1:], plan[0], cores)
+    stay, moved, came = flipped[None], None, 0
+    late_now = late_value = late_got = late_half = None
     for place, now in enumerate(plan):
         got = exchange_stage(sent, *now, cores)
         tokens = []
         if place == 0:
-            volume_grad, done = volume_grad_of(grads, above, kernel, height, width, (sent,))
-            late = kernel_grad_part(even, odd, grads, above, (0,), cores, chips, scale, (done,))
-            late_units = late[0].shape[0]
-            tokens.append(late[0])
-        elif late_ready is None:
-            if late_state is None:
-                then = late_plan[0] if late_plan else None
-                result = add_cores(*late, then, cores, (sent,))
-            else:
-                then = late_plan[0] if late_plan else None
-                result = add_stage(*late_state, late_now, then, cores, (sent,))
-            if then is None:
-                late_ready = result
-                tokens.append(late_ready)
-            else:
+            late = kernel_grad_part(even, odd, grads, above, (0,), cores, chips, scale, space // 2, 2, (sent,))
+            volume_grad, done = volume_grad_of(grads, above, kernel, height, width, (late[1],))
+            late_value, late_sent = add_cores(late[0], late[1:], late_plan[0], cores, (done,))
+        elif late_now is not None:
+            then = late_plan[0] if late_plan else None
+            late_value, late_sent = add_stage(late_value, late_got, late_now, then, cores, (sent,))
+        if late_plan and late_plan[0][0] == "chips":
+            late_now = late_plan.pop(0)
+            late_got = (exchange_stage(late_sent, *late_now, cores),)
+            tokens.append(late_sent)
+        elif late_plan or switch_plan:
+            rider = None
+            if late_plan:
                 late_now = late_plan.pop(0)
-                late_state = (result[0], exchange_stage(result[1], *late_now, cores))
-                tokens.append(result[1])
-        if place >= len(over_space) and switch_plan:
+                rider = late_sent
+            elif late_now is not None:
+                late_now, late_half = None, late_sent
             _, stage = switch_plan.pop(0)
-            if stay is None:
-                stay = flipped[None]
-            stay, out = switch_stage(stay, moved, stage, cores, (sent,))
+            stay, out = switch_stage(stay, moved, came, rider, stage, cores, (sent,))
             moved = exchange_space(out, stage, cores)
+            came = 0
+            if rider is not None:
+                came = rider.size // rider.shape[-1]
+                late_got = (moved[:came].reshape(rider.shape),)
             tokens.append(out)
         if place + 1 < len(plan):
-            value, sent = add_stage(value, got, now, plan[place + 1], cores, tuple(tokens))
-    while late_ready is None:
-        then = late_plan[0] if late_plan else None
-        result = add_stage(*late_state, late_now, then, cores)
-        if then is None:
-            late_ready = result
-        else:
-            late_now = late_plan.pop(0)
-            late_state = (result[0], exchange_stage(result[1], *late_now, cores))
-
-    mine = join(value, got, late_ready, plan[-1], cores, tuple(tokens))
-    share_units = mine.shape[0] - late_units
+            weight = SPACER if place >= len(over_space) else 1000
+            value, sent = add_stage(value, (got,), now, plan[place + 1], cores, tuple(tokens), weight)
+    if late_half is None:
+        late_half = add_stage(late_value, late_got, late_now, None, cores)[1]
+
+    mine = join(value, got, late_half, plan[-1], cores, tuple(tokens))
+    early_rows = mine.shape[0] - late_half.shape[0]
     switched = None
     for step, (_, stage) in enumerate(reversed(over_space)):
         got = exchange_space(mine, stage, cores)
         order = ()
         if switched is None:
-            switched, done = switched_of(stay, moved, space, cores, (mine,))
+            switched, done = switched_of(stay, moved, came, space, cores, (mine,))
             order = (done,)
         if step + 1 < len(over_space):
-            mine = gather_stage(mine, got, share_units << step, order)
+            mine = gather_stage(mine, got, early_rows << step, step == 0, order)
     kernel_grad = kernel_grad_out(mine, got, early_units, late_units, space, cores, co)
 
     return (

time: 53.2 us -> 59.6 us (1.12)
  starting transfers between devices: 22.3 us -> 26.5 us
  waiting for transfers between devices: 17.2 us -> 18.5 us
  Pallas kernels: 9.95 us -> 10.8 us
    ppermute x12 -> x13, starting transfers between devices: 16 us -> 20.2 us  [exchange(): return lax.ppermute(value, ('dp', 'space'), pairs)]
    ppermute x2, waiting for transfers between devices: 3.44 us -> 6.61 us  [neighbour(): lax.ppermute(value, 'space', [(source, source + steps) for source in rang...]
    ppermute x12 -> x13, waiting for transfers between devices: 13.8 us -> 11.9 us  [exchange(): return lax.ppermute(value, ('dp', 'space'), pairs)]
    pallas_call x7 -> x8, Pallas kernels: 0.48 us -> 1.11 us  [add_stage(): call(functools.partial(add_kernel, now, then, cores), outs, order=order,...]
  transfers between devices with their start and end apart: 14 -> 15, of which waited for: 9 -> 8; matrix products, arithmetic and copies ran while one was open for 0% -> 0% of each run, Pallas kernels for 11% -> 11%
where the time goes in v6:
time: 59.6 us; the launch traced here: 59.3 us
  starting transfers between devices  26.5 us (44%)
  waiting for transfers between devices  18.5 us (31%)
  Pallas kernels  10.8 us (18%)
  local copies, waits for them, and re-layouts  2.72 us (5%)
  between operations  0.81 us (1%)
    ppermute x13, starting transfers between devices, exchange(): return lax.ppermute(value, ('dp', 'space'), pairs)  20.2 us
    ppermute x13, waiting for transfers between devices, exchange(): return lax.ppermute(value, ('dp', 'space'), pairs)  11.9 us
    ppermute x2, waiting for transfers between devices, neighbour(): lax.ppermute(value, 'space', [(source, source + steps) for source in rang...  6.61 us
    ppermute x2, starting transfers between devices, neighbour(): lax.ppermute(value, 'space', [(source, source + steps) for source in rang...  6.27 us
    unnamed x8, local copies, waits for them, and re-layouts  2.71 us
    pallas_call x1, Pallas kernels, volume_grad_of(): call(volume_grad_kernel, (jax.ShapeDtypeStruct(shape, BF16), jax.ShapeDty...  2.59 us
    pallas_call x1, Pallas kernels, halo_share(): call(halo_kernel, jax.ShapeDtypeStruct((height * width // 4, co), BF16),...  2.41 us
    pallas_call x1, Pallas kernels, partial_preact(): call(preact_kernel, (jax.ShapeDtypeStruct((planes // 2 * cells, co), F32)...  1.37 us
  transfers between devices with their start and end apart: 15, of which 8 were waited for; matrix products, arithmetic and copies ran while one was open for 0% of the time, Pallas kernels for 11%

profile of v6, /device:TPU:0, one launch (start us, length us, event | category | flops | bytes accessed | tf_op | source)
XLA Modules:
  0.0 59.3 jit_solution(15986066285530348474)
XLA Ops:
  0.6 2.4 %shard_map.59 = bf16[256,256]{1,0:T(8,128)(2,1)} custom-call(bf16[1,4,32,32,128]{4,3,2,1,0:T(8,128)(2,1)} %volume_ref.3, bf16[3,3,3,128,256]{4,3,2,1,0:T(8,128)(2,1)} %refs_2_.1), custom_call_target="tpu_custom_call" | custom-call | flops 1000 | bytes 1000 | tf_op jit(solution)/shard_map/pallas_call | solution.py:123
  3.0 4.8 %collective-permute-start = (bf16[256,256]{1,0:T(8,128)(2,1)}, bf16[256,256]{1,0:T(8,128)(2,1)S(1)}, u32[]{:S(2)}, u32[]{:S(2)}) collective-permute-start(bf16[256,256]{1,0:T(8,128)(2,1)} %shard_map.59), channel_id=1, source_target_pairs={{0,1},{1,2},{2,3},{4,5},{5,6},{6,7},{8,9},{9,10},{10,11},{12,13},{... | collective-permute-start | bytes 393224 | tf_op jit(solution)/shard_map/ppermute | solution.py:578
  7.9 1.5 %copy-done = bf16[3,3,3,128,256]{4,3,2,1,0:T(8,128)(2,1)S(1)} copy-done((bf16[3,3,3,128,256]{4,3,2,1,0:T(8,128)(2,1)S(1)}, bf16[3,3,3,128,256]{4,3,2,1,0:T(8,128)(2,1)}, u32[]{:S(2)}) %copy-start) | copy-done | bytes 1769496
  9.4 1.2 %copy-done.2 = bf16[1,4,32,32,128]{4,3,2,1,0:T(8,128)(2,1)S(1)} copy-done((bf16[1,4,32,32,128]{4,3,2,1,0:T(8,128)(2,1)S(1)}, bf16[1,4,32,32,128]{4,3,2,1,0:T(8,128)(2,1)}, u32[]{:S(2)}) %copy-start.2) | copy-done | bytes 1048600
  10.6 1.4 %shard_map.58 = (f32[512,256]{1,0:T(8,128)S(1)}, bf16[4,16,16,384]{3,2,1,0:T(8,128)(2,1)S(1)}, bf16[4,17,16,384]{3,2,1,0:T(8,128)(2,1)S(1)}) custom-call(bf16[1,4,32,32,128]{4,3,2,1,0:T(8,128)(2,1)S(1)} %copy-done.2, bf16[3,3,3,128,256]{4,3,2,1,0:T(8,128)(2,1)S(1)} %copy-done), custom_call_target="tpu_custom_call" | custom-call | flops 1000 | bytes 1000 | tf_op jit(solution)/shard_map/pallas_call | solution.py:169
  12.0 0.3 shard_map.60
  12.3 0.8 %shard_map.61 = (f32[36,4,16,128]{3,2,1,0:T(8,128)S(1)}, bf16[36,4,16,128]{3,2,1,0:T(8,128)(2,1)S(1)}) custom-call(bf16[4,16,16,384]{3,2,1,0:T(8,128)(2,1)S(1)} %get-tuple-element.38.even_ref.refs_0_, bf16[4,17,16,384]{3,2,1,0:T(8,128)(2,1)S(1)} %get-tuple-element.39.odd_ref.refs_1_, bf16[512,256]{1,0:T(8,128)(2,1)S(1)} %get-tuple-element.40.grads_ref.refs_2_.refs_0_), custom_call_target="tpu_custom_call" | custom-call | flops 1000 | bytes 1000 | tf_op jit(solution)/shard_map/pallas_call | solution.py:484
  13.2 2.0 %collective-permute-done.2.refs_0_ = bf16[36,4,16,128]{3,2,1,0:T(8,128)(2,1)S(1)} collective-permute-done((bf16[36,4,16,128]{3,2,1,0:T(8,128)(2,1)S(1)}, bf16[36,4,16,128]{3,2,1,0:T(8,128)(2,1)S(1)}, u32[]{:S(2)}, u32[]{:S(2)}) %collective-permute-start.2) | collective-permute-done | bytes 589856 | tf_op jit(solution)/shard_map/ppermute | solution.py:558
  15.2 0.2 shard_map.62
  15.4 1.6 %collective-permute-start.6 = (bf16[18,4,16,128]{3,2,1,0:T(8,128)(2,1)S(1)}, bf16[18,4,16,128]{3,2,1,0:T(8,128)(2,1)S(1)}, u32[]{:S(2)}, u32[]{:S(2)}) collective-permute-start(bf16[18,4,16,128]{3,2,1,0:T(8,128)(2,1)S(1)} %get-tuple-element.43.refs_4_), channel_id=1, source_target_pairs={{0,1},{1,0},{2,3},{3,2},{4,6},{5,7},{6,4},{7,5},{8,9},{9,8},{10,11... | collective-permute-start | bytes 884744 | tf_op jit(solution)/shard_map/ppermute | solution.py:558
  16.9 1.4 %collective-permute-start.1 = (bf16[256,256]{1,0:T(8,128)(2,1)S(1)}, bf16[256,256]{1,0:T(8,128)(2,1)S(1)}, u32[]{:S(2)}, u32[]{:S(2)}) collective-permute-start(bf16[256,256]{1,0:T(8,128)(2,1)S(1)} %slice.6), channel_id=1, source_target_pairs={{1,0},{2,1},{3,2},{5,4},{6,5},{7,6},{9,8},{10,9},{11,10},{13,12},{... | collective-permute-start | bytes 393224 | tf_op jit(solution)/shard_map/ppermute | solution.py:578
  18.4 6.6 %collective-permute-done.1.refs_3_.refs_1_ = bf16[256,256]{1,0:T(8,128)(2,1)S(1)} collective-permute-done((bf16[256,256]{1,0:T(8,128)(2,1)S(1)}, bf16[256,256]{1,0:T(8,128)(2,1)S(1)}, u32[]{:S(2)}, u32[]{:S(2)}) %collective-permute-start.1) | collective-permute-done | bytes 131104 | tf_op jit(solution)/shard_map/ppermute | solution.py:578
  25.0 0.5 shard_map.63
  25.6 0.5 collective-permute-start.4
  26.1 2.6 %shard_map.64 = (bf16[4,16,2,32,128]{4,3,2,1,0:T(8,128)(2,1)}, f32[8,128]{1,0:T(8,128)S(1)}) custom-call(bf16[512,256]{1,0:T(8,128)(2,1)S(1)} %get-tuple-element.40.grads_ref.refs_2_.refs_0_, bf16[256,256]{1,0:T(8,128)(2,1)S(1)} %collective-permute-done.1.refs_3_.refs_1_, bf16[3,3,3,128,256]{4,3,2,1,0:T(8,128)(2,1)S(1)} %copy-done.1, ...), custom_call_target="tpu_custom_call" | custom-call | flops 1000 | bytes 1000 | tf_op jit(solution)/shard_map/pallas_call | solution.py:539
  28.8 1.6 %collective-permute-start.5 = (bf16[18,2,16,128]{3,2,1,0:T(8,128)(2,1)S(1)}, bf16[18,2,16,128]{3,2,1,0:T(8,128)(2,1)S(1)}, u32[]{:S(2)}, u32[]{:S(2)}) collective-permute-start(bf16[18,2,16,128]{3,2,1,0:T(8,128)(2,1)S(1)} %get-tuple-element.49.refs_2_), channel_id=1, source_target_pairs={{0,8},{1,9},{2,10},{3,11},{4,12},{5,13},{6,14},{7,15},{8,0},{9,1},... | collective-permute-start | bytes 442376 | tf_op jit(solution)/shard_map/ppermute | solution.py:558
  30.5 2.3 %collective-permute-start.8 = (bf16[9,4,16,128]{3,2,1,0:T(8,128)(2,1)S(1)}, bf16[9,4,16,128]{3,2,1,0:T(8,128)(2,1)S(1)}, u32[]{:S(2)}, u32[]{:S(2)}) collective-permute-start(bf16[9,4,16,128]{3,2,1,0:T(8,128)(2,1)S(1)} %get-tuple-element.51.refs_2_), channel_id=1, source_target_pairs={{0,2},{1,3},{2,0},{3,1},{4,5},{5,4},{6,7},{7,6},{8,10},{9,11},{10,... | collective-permute-start | bytes 442376 | tf_op jit(solution)/shard_map/ppermute | solution.py:558
  32.8 1.9 %collective-permute-done.5.refs_1_ = bf16[18,2,16,128]{3,2,1,0:T(8,128)(2,1)S(1)} collective-permute-done((bf16[18,2,16,128]{3,2,1,0:T(8,128)(2,1)S(1)}, bf16[18,2,16,128]{3,2,1,0:T(8,128)(2,1)S(1)}, u32[]{:S(2)}, u32[]{:S(2)}) %collective-permute-start.5) | collective-permute-done | bytes 147488 | tf_op jit(solution)/shard_map/ppermute | solution.py:558
  34.7 2.7 %collective-permute-start.7 = (bf16[18,1,16,128]{3,2,1,0:T(8,128)(2,1)S(1)}, bf16[18,1,16,128]{3,2,1,0:T(8,128)(2,1)S(1)}, u32[]{:S(2)}, u32[]{:S(2)}) collective-permute-start(bf16[18,1,16,128]{3,2,1,0:T(8,128)(2,1)S(1)} %get-tuple-element.53.refs_2_), channel_id=1, source_target_pairs={{0,16},{1,17},{2,18},{3,19},{4,20},{5,21},{6,22},{7,23},{8,24},{9,... | collective-permute-start | bytes 221192 | tf_op jit(solution)/shard_map/ppermute | solution.py:558
  37.4 1.6 %collective-permute-start.10 = (bf16[9,2,16,128]{3,2,1,0:T(8,128)(2,1)S(1)}, bf16[9,2,16,128]{3,2,1,0:T(8,128)(2,1)S(1)}, u32[]{:S(2)}, u32[]{:S(2)}) collective-permute-start(bf16[9,2,16,128]{3,2,1,0:T(8,128)(2,1)S(1)} %get-tuple-element.55.refs_2_), channel_id=1, source_target_pairs={{0,8},{1,9},{2,10},{3,11},{4,12},{5,13},{6,14},{7,15},{8,0},{9,1},... | collective-permute-start | bytes 221192 | tf_op jit(solution)/shard_map/ppermute | solution.py:558
  39.1 1.1 %collective-permute-done.7.refs_1_ = bf16[18,1,16,128]{3,2,1,0:T(8,128)(2,1)S(1)} collective-permute-done((bf16[18,1,16,128]{3,2,1,0:T(8,128)(2,1)S(1)}, bf16[18,1,16,128]{3,2,1,0:T(8,128)(2,1)S(1)}, u32[]{:S(2)}, u32[]{:S(2)}) %collective-permute-start.7) | collective-permute-done | bytes 73760 | tf_op jit(solution)/shard_map/ppermute | solution.py:558
  40.3 2.3 %collective-permute-start.9 = (bf16[656,128]{1,0:T(8,128)(2,1)S(1)}, bf16[656,128]{1,0:T(8,128)(2,1)S(1)}, u32[]{:S(2)}, u32[]{:S(2)}) collective-permute-start(bf16[656,128]{1,0:T(8,128)(2,1)S(1)} %get-tuple-element.58.refs_2_), channel_id=1, source_target_pairs={{0,1},{1,0},{2,3},{3,2},{4,6},{5,7},{6,4},{7,5},{8,9},{9,8},{10,11... | collective-permute-start | bytes 503816 | tf_op jit(solution)/shard_map/ppermute | solution.py:558
  42.6 3.0 %collective-permute-start.12 = (bf16[9,1,16,128]{3,2,1,0:T(8,128)(2,1)S(1)}, bf16[9,1,16,128]{3,2,1,0:T(8,128)(2,1)S(1)}, u32[]{:S(2)}, u32[]{:S(2)}) collective-permute-start(bf16[9,1,16,128]{3,2,1,0:T(8,128)(2,1)S(1)} %get-tuple-element.60.refs_2_), channel_id=1, source_target_pairs={{0,16},{1,17},{2,18},{3,19},{4,20},{5,21},{6,22},{7,23},{8,24},{9,... | collective-permute-start | bytes 110600 | tf_op jit(solution)/shard_map/ppermute | solution.py:558
  45.7 0.5 collective-permute-done.9.refs_1_
  46.2 2.4 %collective-permute-start.11 = (bf16[512,128]{1,0:T(8,128)(2,1)S(1)}, bf16[512,128]{1,0:T(8,128)(2,1)S(1)}, u32[]{:S(2)}, u32[]{:S(2)}) collective-permute-start(bf16[512,128]{1,0:T(8,128)(2,1)S(1)} %get-tuple-element.62.refs_3_), channel_id=1, source_target_pairs={{0,2},{1,3},{2,0},{3,1},{4,5},{5,4},{6,7},{7,6},{8,10},{9,11},{10,... | collective-permute-start | bytes 393224 | tf_op jit(solution)/shard_map/ppermute | solution.py:558
  48.5 0.6 %shard_map.73 = (f32[9,1,16,128]{3,2,1,0:T(8,128)}, bf16[9,1,16,128]{3,2,1,0:T(8,128)(2,1)S(1)}) custom-call(f32[1,2,9,16,128]{4,3,2,1,0:T(8,128)S(1)} %get-tuple-element.64.refs_0_, bf16[9,1,16,128]{3,2,1,0:T(8,128)(2,1)S(1)} %bitcast.11, bf16[9,1,16,128]{3,2,1,0:T(8,128)(2,1)S(1)} %get-tuple-element.60.refs_2_), custom_call_target="tpu_custom_call" | custom-call | flops 1000 | bytes 1000 | tf_op jit(solution)/shard_map/pallas_call | solution.py:283
  49.3 2.7 %collective-permute-done.11.refs_1_ = bf16[512,128]{1,0:T(8,128)(2,1)S(1)} collective-permute-done((bf16[512,128]{1,0:T(8,128)(2,1)S(1)}, bf16[512,128]{1,0:T(8,128)(2,1)S(1)}, u32[]{:S(2)}, u32[]{:S(2)}) %collective-permute-start.11) | collective-permute-done | bytes 131104 | tf_op jit(solution)/shard_map/ppermute | solution.py:558
  52.0 0.8 %shard_map.75 = (bf16[64,2048]{1,0:T(8,128)(2,1)}, f32[8,128]{1,0:T(8,128)S(1)}) custom-call(bf16[8,64,128]{2,1,0:T(8,128)(2,1)S(1)} %bitcast.12, bf16[512,128]{1,0:T(8,128)(2,1)S(1)} %collective-permute-done.11.refs_1_, bf16[18,16,128]{2,1,0:T(8,128)(2,1)S(1)} %shard_map.74.refs_2_.refs_0_), custom_call_target="tpu_custom_call" | custom-call | flops 1000 | bytes 1000 | tf_op jit(solution)/shard_map/pallas_call | solution.py:231
  52.8 0.9 %collective-permute-done.13.refs_1_ = bf16[18,16,128]{2,1,0:T(8,128)(2,1)S(1)} collective-permute-done((bf16[18,16,128]{2,1,0:T(8,128)(2,1)S(1)}, bf16[18,16,128]{2,1,0:T(8,128)(2,1)S(1)}, u32[]{:S(2)}, u32[]{:S(2)}) %collective-permute-start.13) | collective-permute-done | bytes 73760 | tf_op jit(solution)/shard_map/ppermute | solution.py:558
  53.7 1.9 %collective-permute-start.14 = (bf16[27,16,128]{2,1,0:T(8,128)(2,1)S(1)}, bf16[27,16,128]{2,1,0:T(8,128)(2,1)S(1)}, u32[]{:S(2)}, u32[]{:S(2)}) collective-permute-start(bf16[27,16,128]{2,1,0:T(8,128)(2,1)S(1)} %shard_map.76.mine_ref), channel_id=1, source_target_pairs={{0,1},{1,0},{2,3},{3,2},{4,6},{5,7},{6,4},{7,5},{8,9},{9,8},{10,11... | collective-permute-start | bytes 331784 | tf_op jit(solution)/shard_map/ppermute | solution.py:558
  55.6 2.9 %collective-permute-done.14.got_ref = bf16[27,16,128]{2,1,0:T(8,128)(2,1)S(1)} collective-permute-done((bf16[27,16,128]{2,1,0:T(8,128)(2,1)S(1)}, bf16[27,16,128]{2,1,0:T(8,128)(2,1)S(1)}, u32[]{:S(2)}, u32[]{:S(2)}) %collective-permute-start.14) | collective-permute-done | bytes 110624 | tf_op jit(solution)/shard_map/ppermute | solution.py:558
  58.5 0.8 %shard_map.77 = f32[27,16,256]{2,1,0:T(8,128)} custom-call(bf16[27,16,128]{2,1,0:T(8,128)(2,1)S(1)} %shard_map.76.mine_ref, bf16[27,16,128]{2,1,0:T(8,128)(2,1)S(1)} %collective-permute-done.14.got_ref), custom_call_target="tpu_custom_call" | custom-call | flops 1000 | bytes 1000 | tf_op jit(solution)/shard_map/pallas_call | solution.py:421
  (28 shorter events, 0.7 us)
Async XLA Ops:
  3.0 8.9 %collective-permute-start = (bf16[256,256]{1,0:T(8,128)(2,1)}, bf16[256,256]{1,0:T(8,128)(2,1)S(1)}, u32[]{:S(2)}, u32[]{:S(2)}) collective-permute-start(bf16[256,256]{1,0:T(8,128)(2,1)} %shard_map.59), channel_id=1, source_target_pairs={{0,1},{1,2},{2,3},{4,5},{5,6},{6,7},{8,9},{9,10},{10,11},{12,13},{... | collective-permute-start | bytes 393224 | tf_op jit(solution)/shard_map/ppermute | solution.py:578
  7.9 1.5 %copy-start = (bf16[3,3,3,128,256]{4,3,2,1,0:T(8,128)(2,1)S(1)}, bf16[3,3,3,128,256]{4,3,2,1,0:T(8,128)(2,1)}, u32[]{:S(2)}) copy-start(bf16[3,3,3,128,256]{4,3,2,1,0:T(8,128)(2,1)} %refs_2_.1) | copy-start | bytes 5308420
  9.4 1.2 %copy-start.2 = (bf16[1,4,32,32,128]{4,3,2,1,0:T(8,128)(2,1)S(1)}, bf16[1,4,32,32,128]{4,3,2,1,0:T(8,128)(2,1)}, u32[]{:S(2)}) copy-start(bf16[1,4,32,32,128]{4,3,2,1,0:T(8,128)(2,1)} %volume_ref.3) | copy-start | bytes 3145732
  10.6 1.4 %copy-start.3 = (bf16[1,2,16,16,256]{4,3,2,1,0:T(8,128)(2,1)S(1)}, bf16[1,2,16,16,256]{4,3,2,1,0:T(8,128)(2,1)}, u32[]{:S(2)}) copy-start(bf16[1,2,16,16,256]{4,3,2,1,0:T(8,128)(2,1)} %param.5) | copy-start | bytes 786436
  13.1 2.1 %collective-permute-start.2 = (bf16[36,4,16,128]{3,2,1,0:T(8,128)(2,1)S(1)}, bf16[36,4,16,128]{3,2,1,0:T(8,128)(2,1)S(1)}, u32[]{:S(2)}, u32[]{:S(2)}) collective-permute-start(bf16[36,4,16,128]{3,2,1,0:T(8,128)(2,1)S(1)} %get-tuple-element.42), channel_id=1, source_target_pairs={{0,4},{1,5},{2,6},{3,7},{4,0},{5,1},{6,2},{7,3},{8,12},{9,13},{10,... | collective-permute-start | bytes 1769480 | tf_op jit(solution)/shard_map/ppermute | solution.py:558
  15.4 15.1 %collective-permute-start.6 = (bf16[18,4,16,128]{3,2,1,0:T(8,128)(2,1)S(1)}, bf16[18,4,16,128]{3,2,1,0:T(8,128)(2,1)S(1)}, u32[]{:S(2)}, u32[]{:S(2)}) collective-permute-start(bf16[18,4,16,128]{3,2,1,0:T(8,128)(2,1)S(1)} %get-tuple-element.43.refs_4_), channel_id=1, source_target_pairs={{0,1},{1,0},{2,3},{3,2},{4,6},{5,7},{6,4},{7,5},{8,9},{9,8},{10,11... | collective-permute-start | bytes 884744 | tf_op jit(solution)/shard_map/ppermute | solution.py:558
  16.9 9.2 %copy-start.1 = (bf16[3,3,3,128,256]{4,3,2,1,0:T(8,128)(2,1)S(1)}, bf16[3,3,3,128,256]{4,3,2,1,0:T(8,128)(2,1)}, u32[]{:S(2)}) copy-start(bf16[3,3,3,128,256]{4,3,2,1,0:T(8,128)(2,1)} %refs_2_.1) | copy-start | bytes 5308420
  16.9 8.0 %collective-permute-start.1 = (bf16[256,256]{1,0:T(8,128)(2,1)S(1)}, bf16[256,256]{1,0:T(8,128)(2,1)S(1)}, u32[]{:S(2)}, u32[]{:S(2)}) collective-permute-start(bf16[256,256]{1,0:T(8,128)(2,1)S(1)} %slice.6), channel_id=1, source_target_pairs={{1,0},{2,1},{3,2},{5,4},{6,5},{7,6},{9,8},{10,9},{11,10},{13,12},{... | collective-permute-start | bytes 393224 | tf_op jit(solution)/shard_map/ppermute | solution.py:578
  25.5 3.2 %collective-permute-start.3 = (bf16[9,4,16,128]{3,2,1,0:T(8,128)(2,1)S(1)}, bf16[9,4,16,128]{3,2,1,0:T(8,128)(2,1)S(1)}, u32[]{:S(2)}, u32[]{:S(2)}) collective-permute-start(bf16[9,4,16,128]{3,2,1,0:T(8,128)(2,1)S(1)} %get-tuple-element.45.refs_3_), channel_id=1, source_target_pairs={{0,4},{1,5},{2,6},{3,7},{4,0},{5,1},{6,2},{7,3},{8,12},{9,13},{10,... | collective-permute-start | bytes 442376 | tf_op jit(solution)/shard_map/ppermute | solution.py:558
  25.6 3.1 %collective-permute-start.4 = (bf16[9,4,16,128]{3,2,1,0:T(8,128)(2,1)S(1)}, bf16[9,4,16,128]{3,2,1,0:T(8,128)(2,1)S(1)}, u32[]{:S(2)}, u32[]{:S(2)}) collective-permute-start(bf16[9,4,16,128]{3,2,1,0:T(8,128)(2,1)S(1)} %get-tuple-element.46), channel_id=1, source_target_pairs={{0,4},{1,5},{2,6},{3,7},{4,0},{5,1},{6,2},{7,3},{8,12},{9,13},{10,... | collective-permute-start | bytes 442376 | tf_op jit(solution)/shard_map/ppermute | solution.py:558
  28.8 5.9 %collective-permute-start.5 = (bf16[18,2,16,128]{3,2,1,0:T(8,128)(2,1)S(1)}, bf16[18,2,16,128]{3,2,1,0:T(8,128)(2,1)S(1)}, u32[]{:S(2)}, u32[]{:S(2)}) collective-permute-start(bf16[18,2,16,128]{3,2,1,0:T(8,128)(2,1)S(1)} %get-tuple-element.49.refs_2_), channel_id=1, source_target_pairs={{0,8},{1,9},{2,10},{3,11},{4,12},{5,13},{6,14},{7,15},{8,0},{9,1},... | collective-permute-start | bytes 442376 | tf_op jit(solution)/shard_map/ppermute | solution.py:558
  30.5 6.9 %collective-permute-start.8 = (bf16[9,4,16,128]{3,2,1,0:T(8,128)(2,1)S(1)}, bf16[9,4,16,128]{3,2,1,0:T(8,128)(2,1)S(1)}, u32[]{:S(2)}, u32[]{:S(2)}) collective-permute-start(bf16[9,4,16,128]{3,2,1,0:T(8,128)(2,1)S(1)} %get-tuple-element.51.refs_2_), channel_id=1, source_target_pairs={{0,2},{1,3},{2,0},{3,1},{4,5},{5,4},{6,7},{7,6},{8,10},{9,11},{10,... | collective-permute-start | bytes 442376 | tf_op jit(solution)/shard_map/ppermute | solution.py:558
  34.7 5.5 %collective-permute-start.7 = (bf16[18,1,16,128]{3,2,1,0:T(8,128)(2,1)S(1)}, bf16[18,1,16,128]{3,2,1,0:T(8,128)(2,1)S(1)}, u32[]{:S(2)}, u32[]{:S(2)}) collective-permute-start(bf16[18,1,16,128]{3,2,1,0:T(8,128)(2,1)S(1)} %get-tuple-element.53.refs_2_), channel_id=1, source_target_pairs={{0,16},{1,17},{2,18},{3,19},{4,20},{5,21},{6,22},{7,23},{8,24},{9,... | collective-permute-start | bytes 221192 | tf_op jit(solution)/shard_map/ppermute | solution.py:558
  37.4 5.2 %collective-permute-start.10 = (bf16[9,2,16,128]{3,2,1,0:T(8,128)(2,1)S(1)}, bf16[9,2,16,128]{3,2,1,0:T(8,128)(2,1)S(1)}, u32[]{:S(2)}, u32[]{:S(2)}) collective-permute-start(bf16[9,2,16,128]{3,2,1,0:T(8,128)(2,1)S(1)} %get-tuple-element.55.refs_2_), channel_id=1, source_target_pairs={{0,8},{1,9},{2,10},{3,11},{4,12},{5,13},{6,14},{7,15},{8,0},{9,1},... | collective-permute-start | bytes 221192 | tf_op jit(solution)/shard_map/ppermute | solution.py:558
  40.3 5.9 %collective-permute-start.9 = (bf16[656,128]{1,0:T(8,128)(2,1)S(1)}, bf16[656,128]{1,0:T(8,128)(2,1)S(1)}, u32[]{:S(2)}, u32[]{:S(2)}) collective-permute-start(bf16[656,128]{1,0:T(8,128)(2,1)S(1)} %get-tuple-element.58.refs_2_), channel_id=1, source_target_pairs={{0,1},{1,0},{2,3},{3,2},{4,6},{5,7},{6,4},{7,5},{8,9},{9,8},{10,11... | collective-permute-start | bytes 503816 | tf_op jit(solution)/shard_map/ppermute | solution.py:558
  42.6 6.6 %collective-permute-start.12 = (bf16[9,1,16,128]{3,2,1,0:T(8,128)(2,1)S(1)}, bf16[9,1,16,128]{3,2,1,0:T(8,128)(2,1)S(1)}, u32[]{:S(2)}, u32[]{:S(2)}) collective-permute-start(bf16[9,1,16,128]{3,2,1,0:T(8,128)(2,1)S(1)} %get-tuple-element.60.refs_2_), channel_id=1, source_target_pairs={{0,16},{1,17},{2,18},{3,19},{4,20},{5,21},{6,22},{7,23},{8,24},{9,... | collective-permute-start | bytes 110600 | tf_op jit(solution)/shard_map/ppermute | solution.py:558
  46.2 5.8 %collective-permute-start.11 = (bf16[512,128]{1,0:T(8,128)(2,1)S(1)}, bf16[512,128]{1,0:T(8,128)(2,1)S(1)}, u32[]{:S(2)}, u32[]{:S(2)}) collective-permute-start(bf16[512,128]{1,0:T(8,128)(2,1)S(1)} %get-tuple-element.62.refs_3_), channel_id=1, source_target_pairs={{0,2},{1,3},{2,0},{3,1},{4,5},{5,4},{6,7},{7,6},{8,10},{9,11},{10,... | collective-permute-start | bytes 393224 | tf_op jit(solution)/shard_map/ppermute | solution.py:558
  49.2 4.4 %collective-permute-start.13 = (bf16[18,16,128]{2,1,0:T(8,128)(2,1)S(1)}, bf16[18,16,128]{2,1,0:T(8,128)(2,1)S(1)}, u32[]{:S(2)}, u32[]{:S(2)}) collective-permute-start(bf16[18,16,128]{2,1,0:T(8,128)(2,1)S(1)} %shard_map.74.refs_2_.refs_0_), channel_id=1, source_target_pairs={{0,2},{1,3},{2,0},{3,1},{4,5},{5,4},{6,7},{7,6},{8,10},{9,11},{10,... | collective-permute-start | bytes 221192 | tf_op jit(solution)/shard_map/ppermute | solution.py:558
  53.7 4.8 %collective-permute-start.14 = (bf16[27,16,128]{2,1,0:T(8,128)(2,1)S(1)}, bf16[27,16,128]{2,1,0:T(8,128)(2,1)S(1)}, u32[]{:S(2)}, u32[]{:S(2)}) collective-permute-start(bf16[27,16,128]{2,1,0:T(8,128)(2,1)S(1)} %shard_map.76.mine_ref), channel_id=1, source_target_pairs={{0,1},{1,0},{2,3},{3,2},{4,6},{5,7},{6,4},{7,5},{8,9},{9,8},{10,11... | collective-permute-start | bytes 331784 | tf_op jit(solution)/shard_map/ppermute | solution.py:558

commit v7 on v6

--- a/solution.py
+++ b/solution.py
@@ -12,9 +12,9 @@
 F32 = jnp.float32
 VMEM_LIMIT = 20 * 1024 * 1024
 DONE = (8, 128)
-PLANE_PARTS = 4
+PLANE_PARTS = 1
 SPACER = 6 * 10**9
-VMEM_WHOLE = 63 * 1024 * 1024
+VMEM_WHOLE = 60 * 1024 * 1024
 
 
 def call(kernel, out_shape, scratch=(), in_specs=None, limit=VMEM_LIMIT, order=(), inputs=0, flops=1000):
@@ -259,22 +259,22 @@
 
 
 def add_kernel(now, then, cores, value_ref, *refs):
-    keep_ref, sent_ref = refs[-2:]
-    got = jnp.concatenate([ref[...] for ref in refs[:-2]], axis=0).astype(F32)
+    outs = 1 if then is None else 2
+    got = jnp.concatenate([ref[...] for ref in refs[:-outs]], axis=0).astype(F32)
     total = value_ref[...] if now is None else value_ref[:, side(*now, cores)]
     total = total.reshape(got.shape) + got
     if then is None:
-        keep_ref[...] = total
-        sent_ref[...] = total.astype(BF16)
+        refs[-1][...] = total.astype(BF16)
         return
+    keep_ref, sent_ref = refs[-2:]
     keep_ref[...] = total.reshape(keep_ref.shape)
     sent_ref[...] = keep_ref[:, 1 - side(*then, cores)].reshape(sent_ref.shape).astype(BF16)
 
 
-def add_stage(value, got, now, then, cores, order=(), flops=1000):
+def add_stage(value, got, now, then, cores, order=()):
     shape = (sum(piece.shape[0] for piece in got),) + got[0].shape[1:]
     if then is None:
-        outs = (jax.ShapeDtypeStruct(shape, F32), jax.ShapeDtypeStruct(shape, BF16))
+        outs = jax.ShapeDtypeStruct(shape, BF16)
     else:
         outs = (
             jax.ShapeDtypeStruct(halves_of(shape, then[0]), F32),
@@ -285,7 +285,6 @@
         outs,
         order=order,
         inputs=1 + len(got),
-        flops=flops,
     )(value, *got, *order)
 
 
@@ -340,25 +339,18 @@
     )(*operands, *order)
 
 
-def gather_kernel(early, add_late, mine_ref, got_ref, out_ref):
-    late = mine_ref.shape[0] - early
-    rows = pl.ds(early, late)
+def gather_kernel(early, mine_ref, got_ref, out_ref):
+    rows = pl.ds(early, mine_ref.shape[0] - early)
     out_ref[pl.ds(0, early)] = mine_ref[pl.ds(0, early)]
     out_ref[pl.ds(early, early)] = got_ref[pl.ds(0, early)]
-    if add_late:
-        total = mine_ref[rows].astype(F32) + got_ref[rows].astype(F32)
-        out_ref[pl.ds(2 * early, late)] = total.astype(BF16)
-    else:
-        out_ref[pl.ds(2 * early, late)] = mine_ref[rows]
-        out_ref[pl.ds(2 * early + late, late)] = got_ref[rows]
-
-
-def gather_stage(mine, got, early, add_late, order=()):
-    late = mine.shape[0] - early
-    shape = (2 * early + (late if add_late else 2 * late),) + mine.shape[1:]
-    return call(
-        functools.partial(gather_kernel, early, add_late),
-        jax.ShapeDtypeStruct(shape, BF16),
+    total = mine_ref[rows].astype(F32) + got_ref[rows].astype(F32)
+    out_ref[pl.ds(2 * early, total.shape[0])] = total.astype(BF16)
+
+
+def gather_stage(mine, got, early, order=()):
+    return call(
+        functools.partial(gather_kernel, early),
+        jax.ShapeDtypeStruct((mine.shape[0] + early,) + mine.shape[1:], BF16),
         order=order,
         inputs=2,
     )(mine, got, *order)
@@ -386,12 +378,14 @@
     halves = out_ref.shape[-1] // 128
     half = space // 2
     share = -(-early_units // space)
-    late_share = late_units if space == 2 else -(-late_units // half)
 
     def put(index, value):
         tap, part = divmod(index, halves)
         out_ref[tap, :, part * 128 : (part + 1) * 128] = value
 
+    for unit in range(late_units):
+        row = half * share + unit
+        put(unit, mine_ref[row].astype(F32) + got_ref[row].astype(F32))
     for group in range(space):
         place = relative_group(group, space, cores)
         far, row = place // half, (place % half) * share
@@ -400,28 +394,16 @@
             if index < early_units:
                 value = jnp.where(far == 1, got_ref[row + unit], mine_ref[row + unit])
                 put(late_units + index, value.astype(F32))
-    base = half * share
-    if space == 2:
-        for unit in range(late_units):
-            put(unit, mine_ref[base + unit].astype(F32) + got_ref[base + unit].astype(F32))
-        return
-    inner = half // 2
-    for group in range(half):
-        place = relative_group(2 * group, space, cores) // 2
-        far, row = place // inner, base + (place % inner) * late_share
-        for unit in range(late_share):
-            index = group * late_share + unit
-            if index < late_units:
-                value = jnp.where(far == 1, got_ref[row + unit], mine_ref[row + unit])
-                put(index, value.astype(F32))
-
-
-def kernel_grad_out(mine, got, early_units, late_units, space, cores, co):
+
+
+def kernel_grad_out(mine, got, early_units, late_units, space, cores, co, order):
     taps = (early_units + late_units) * 128 // co
     return call(
         functools.partial(kernel_grad_out_kernel, space, cores, early_units, late_units),
         jax.ShapeDtypeStruct((taps, mine.shape[1], co), F32),
-    )(mine, got)
+        order=order,
+        inputs=2,
+    )(mine, got, *order)
 
 
 def store_units(product, scale, core, cores, chips, put):
@@ -608,58 +590,56 @@
     early = kernel_grad_part(even, odd, grads, None, (1, 2), cores, chips, scale, space)
     early_units, late_units = 18 * (co // 128), 9 * (co // 128)
     plan = over_space + over_chips
-    late_plan = over_chips + over_space[:-1]
-    switch_plan = list(over_space)
     value, sent = add_cores(early[0], early[1:], plan[0], cores)
-    stay, moved, came = flipped[None], None, 0
-    late_now = late_value = late_got = late_half = None
+    late_plan, late_now, late_half = list(over_chips), None, None
+    switch_at = [len(over_space) - 1 + 2 * stage for stage in range(len(over_space))]
+    stay, moved = flipped[None], None
     for place, now in enumerate(plan):
         got = exchange_stage(sent, *now, cores)
-        tokens = []
+        tokens = [sent]
         if place == 0:
-            late = kernel_grad_part(even, odd, grads, above, (0,), cores, chips, scale, space // 2, 2, (sent,))
-            volume_grad, done = volume_grad_of(grads, above, kernel, height, width, (late[1],))
-            late_value, late_sent = add_cores(late[0], late[1:], late_plan[0], cores, (done,))
-        elif late_now is not None:
-            then = late_plan[0] if late_plan else None
-            late_value, late_sent = add_stage(late_value, late_got, late_now, then, cores, (sent,))
-        if late_plan and late_plan[0][0] == "chips":
-            late_now = late_plan.pop(0)
-            late_got = (exchange_stage(late_sent, *late_now, cores),)
-            tokens.append(late_sent)
-        elif late_plan or switch_plan:
-            rider = None
-            if late_plan:
-                late_now = late_plan.pop(0)
-                rider = late_sent
-            elif late_now is not None:
-                late_now, late_half = None, late_sent
-            _, stage = switch_plan.pop(0)
-            stay, out = switch_stage(stay, moved, came, rider, stage, cores, (sent,))
+            late = kernel_grad_part(even, odd, grads, above, (0,), cores, chips, scale, 1, 1, (sent,))
+            tokens.append(late[1])
+        elif late_half is None:
+            then = late_plan.pop(0) if late_plan else None
+            if late_now is None:
+                result = add_cores(late[0], late[1:], then, cores, (sent,))
+            else:
+                result = add_stage(late_value, late_got, late_now, then, cores, (sent,))
+            late_now = then
+            if then is None:
+                late_half = result
+            else:
+                late_value, late_sent = result
+                late_got = (exchange_stage(late_sent, *then, cores),)
+                tokens.append(late_sent)
+        if switch_at and place == switch_at[0]:
+            stage = len(over_space) - len(switch_at)
+            switch_at.pop(0)
+            stay, out = switch_stage(stay, moved, 0, None, stage, cores, (tokens[-1],))
             moved = exchange_space(out, stage, cores)
-            came = 0
-            if rider is not None:
-                came = rider.size // rider.shape[-1]
-                late_got = (moved[:came].reshape(rider.shape),)
             tokens.append(out)
         if place + 1 < len(plan):
-            weight = SPACER if place >= len(over_space) else 1000
-            value, sent = add_stage(value, (got,), now, plan[place + 1], cores, tuple(tokens), weight)
+            value, sent = add_stage(value, (got,), now, plan[place + 1], cores, tuple(tokens[1:]))
+    for stage in range(len(over_space) - len(switch_at), len(over_space)):
+        stay, out = switch_stage(stay, moved, 0, None, stage, cores, (sent,))
+        moved = exchange_space(out, stage, cores)
     if late_half is None:
-        late_half = add_stage(late_value, late_got, late_now, None, cores)[1]
-
-    mine = join(value, got, late_half, plan[-1], cores, tuple(tokens))
+        late_half = add_stage(late_value, late_got, late_now, None, cores)
+
+    mine = join(value, got, late_half, plan[-1], cores, tuple(tokens[1:]))
     early_rows = mine.shape[0] - late_half.shape[0]
     switched = None
     for step, (_, stage) in enumerate(reversed(over_space)):
         got = exchange_space(mine, stage, cores)
         order = ()
         if switched is None:
-            switched, done = switched_of(stay, moved, came, space, cores, (mine,))
+            switched, done = switched_of(stay, moved, 0, space, cores, (mine,))
             order = (done,)
         if step + 1 < len(over_space):
-            mine = gather_stage(mine, got, early_rows << step, step == 0, order)
-    kernel_grad = kernel_grad_out(mine, got, early_units, late_units, space, cores, co)
+            mine = gather_stage(mine, got, early_rows << step, order)
+    volume_grad, done = volume_grad_of(grads, above, kernel, height, width, (mine,))
+    kernel_grad = kernel_grad_out(mine, got, early_units, late_units, space, cores, co, (done,))
 
     return (
         switched[None],

time: 59.6 us -> 53.6 us (0.90)
  local copies, waits for them, and re-layouts: 2.72 us -> 0.03 us
  starting transfers between devices: 26.5 us -> 24.9 us
  waiting for transfers between devices: 18.5 us -> 17.4 us
  Pallas kernels: 10.8 us -> 10.2 us
    unnamed x8 -> x6, local copies, waits for them, and re-layouts: 2.71 us -> 0.01 us
    ppermute x13 -> x12, starting transfers between devices: 20.2 us -> 18.6 us  [exchange(): return lax.ppermute(value, ('dp', 'space'), pairs)]
    ppermute x2, waiting for transfers between devices: 6.61 us -> 5.49 us  [neighbour(): lax.ppermute(value, 'space', [(source, source + steps) for source in rang...]
    pallas_call x8 -> x7, Pallas kernels: 1.11 us -> 0.46 us  [add_stage(): call(functools.partial(add_kernel, now, then, cores), outs, order=order,...]
    ppermute x13 -> x12, waiting for transfers between devices: 11.9 us -> 12 us  [exchange(): return lax.ppermute(value, ('dp', 'space'), pairs)]
  transfers between devices with their start and end apart: 15 -> 14, of which waited for: 8 -> 10; matrix products, arithmetic and copies ran while one was open for 0% -> 0% of each run, Pallas kernels for 11% -> 11%
where the time goes in v7:
time: 53.6 us; the launch traced here: 53.4 us
  starting transfers between devices  24.9 us (46%)
  waiting for transfers between devices  17.4 us (32%)
  Pallas kernels  10.2 us (19%)
  between operations  0.81 us (2%)
    ppermute x12, starting transfers between devices, exchange(): return lax.ppermute(value, ('dp', 'space'), pairs)  18.6 us
    ppermute x12, waiting for transfers between devices, exchange(): return lax.ppermute(value, ('dp', 'space'), pairs)  12 us
    ppermute x2, starting transfers between devices, neighbour(): lax.ppermute(value, 'space', [(source, source + steps) for source in rang...  6.27 us
    ppermute x2, waiting for transfers between devices, neighbour(): lax.ppermute(value, 'space', [(source, source + steps) for source in rang...  5.49 us
    pallas_call x1, Pallas kernels, volume_grad_of(): call(volume_grad_kernel, (jax.ShapeDtypeStruct(shape, BF16), jax.ShapeDty...  2.59 us
    pallas_call x1, Pallas kernels, halo_share(): call(halo_kernel, jax.ShapeDtypeStruct((height * width // 4, co), BF16),...  2.47 us
    pallas_call x1, Pallas kernels, partial_preact(): call(preact_kernel, (jax.ShapeDtypeStruct((planes // 2 * cells, co), F32)...  1.38 us
    pallas_call x2, Pallas kernels, kernel_grad_part(): call(functools.partial(kernel_grad_kernel, kds, cores, chips, scale, part...  1.35 us
  transfers between devices with their start and end apart: 14, of which 10 were waited for; matrix products, arithmetic and copies ran while one was open for 0% of the time, Pallas kernels for 11%

profile of v7, /device:TPU:0, one launch (start us, length us, event | category | flops | bytes accessed | tf_op | source)
XLA Modules:
  0.0 53.4 jit_solution(4691312779660602834)
XLA Ops:
  0.6 2.5 %shard_map.59 = bf16[256,256]{1,0:T(8,128)(2,1)} custom-call(bf16[1,4,32,32,128]{4,3,2,1,0:T(8,128)(2,1)} %volume_ref.3, bf16[3,3,3,128,256]{4,3,2,1,0:T(8,128)(2,1)} %refs_2_.1), custom_call_target="tpu_custom_call" | custom-call | flops 1000 | bytes 1000 | tf_op jit(solution)/shard_map/pallas_call | solution.py:123
  3.1 5.0 %collective-permute-start = (bf16[256,256]{1,0:T(8,128)(2,1)}, bf16[256,256]{1,0:T(8,128)(2,1)S(1)}, u32[]{:S(2)}, u32[]{:S(2)}) collective-permute-start(bf16[256,256]{1,0:T(8,128)(2,1)} %shard_map.59), channel_id=1, source_target_pairs={{0,1},{1,2},{2,3},{4,5},{5,6},{6,7},{8,9},{9,10},{10,11},{12,13},{... | collective-permute-start | bytes 393224 | tf_op jit(solution)/shard_map/ppermute | solution.py:560
  8.2 1.4 %shard_map.58 = (f32[512,256]{1,0:T(8,128)S(1)}, bf16[4,16,16,384]{3,2,1,0:T(8,128)(2,1)S(1)}, bf16[4,17,16,384]{3,2,1,0:T(8,128)(2,1)S(1)}) custom-call(bf16[1,4,32,32,128]{4,3,2,1,0:T(8,128)(2,1)S(1)} %copy-done.1, bf16[3,3,3,128,256]{4,3,2,1,0:T(8,128)(2,1)S(1)} %copy-done), custom_call_target="tpu_custom_call" | custom-call | flops 1000 | bytes 1000 | tf_op jit(solution)/shard_map/pallas_call | solution.py:169
  9.5 1.6 %collective-permute-done.share_ref = bf16[256,256]{1,0:T(8,128)(2,1)S(1)} collective-permute-done((bf16[256,256]{1,0:T(8,128)(2,1)}, bf16[256,256]{1,0:T(8,128)(2,1)S(1)}, u32[]{:S(2)}, u32[]{:S(2)}) %collective-permute-start) | collective-permute-done | bytes 131104 | tf_op jit(solution)/shard_map/ppermute | solution.py:560
  11.2 0.3 shard_map.60
  11.5 0.8 %shard_map.61 = (f32[36,4,16,128]{3,2,1,0:T(8,128)S(1)}, bf16[36,4,16,128]{3,2,1,0:T(8,128)(2,1)S(1)}) custom-call(bf16[4,16,16,384]{3,2,1,0:T(8,128)(2,1)S(1)} %get-tuple-element.34.even_ref.refs_0_, bf16[4,17,16,384]{3,2,1,0:T(8,128)(2,1)S(1)} %get-tuple-element.35.odd_ref.refs_1_, bf16[512,256]{1,0:T(8,128)(2,1)S(1)} %get-tuple-element.36.grads_ref.refs_2_.refs_0_), custom_call_target="tpu_custom_call" | custom-call | flops 1000 | bytes 1000 | tf_op jit(solution)/shard_map/pallas_call | solution.py:466
  12.4 1.3 %collective-permute-start.1 = (bf16[256,256]{1,0:T(8,128)(2,1)S(1)}, bf16[256,256]{1,0:T(8,128)(2,1)S(1)}, u32[]{:S(2)}, u32[]{:S(2)}) collective-permute-start(bf16[256,256]{1,0:T(8,128)(2,1)S(1)} %slice.3), channel_id=1, source_target_pairs={{1,0},{2,1},{3,2},{5,4},{6,5},{7,6},{9,8},{10,9},{11,10},{13,12},{... | collective-permute-start | bytes 393224 | tf_op jit(solution)/shard_map/ppermute | solution.py:560
  13.7 0.7 %collective-permute-done.2.refs_0_ = bf16[36,4,16,128]{3,2,1,0:T(8,128)(2,1)S(1)} collective-permute-done((bf16[36,4,16,128]{3,2,1,0:T(8,128)(2,1)S(1)}, bf16[36,4,16,128]{3,2,1,0:T(8,128)(2,1)S(1)}, u32[]{:S(2)}, u32[]{:S(2)}) %collective-permute-start.2) | collective-permute-done | bytes 589856 | tf_op jit(solution)/shard_map/ppermute | solution.py:540
  14.4 0.2 shard_map.62
  14.5 2.4 %collective-permute-start.4 = (bf16[18,4,16,128]{3,2,1,0:T(8,128)(2,1)S(1)}, bf16[18,4,16,128]{3,2,1,0:T(8,128)(2,1)S(1)}, u32[]{:S(2)}, u32[]{:S(2)}) collective-permute-start(bf16[18,4,16,128]{3,2,1,0:T(8,128)(2,1)S(1)} %get-tuple-element.39.refs_4_), channel_id=1, source_target_pairs={{0,1},{1,0},{2,3},{3,2},{4,6},{5,7},{6,4},{7,5},{8,9},{9,8},{10,11... | collective-permute-start | bytes 884744 | tf_op jit(solution)/shard_map/ppermute | solution.py:540
  17.0 3.9 %collective-permute-done.1.refs_3_.refs_1_ = bf16[256,256]{1,0:T(8,128)(2,1)S(1)} collective-permute-done((bf16[256,256]{1,0:T(8,128)(2,1)S(1)}, bf16[256,256]{1,0:T(8,128)(2,1)S(1)}, u32[]{:S(2)}, u32[]{:S(2)}) %collective-permute-start.1) | collective-permute-done | bytes 131104 | tf_op jit(solution)/shard_map/ppermute | solution.py:560
  20.8 0.5 shard_map.63
  21.4 2.6 %collective-permute-done.4.refs_1_ = bf16[18,4,16,128]{3,2,1,0:T(8,128)(2,1)S(1)} collective-permute-done((bf16[18,4,16,128]{3,2,1,0:T(8,128)(2,1)S(1)}, bf16[18,4,16,128]{3,2,1,0:T(8,128)(2,1)S(1)}, u32[]{:S(2)}, u32[]{:S(2)}) %collective-permute-start.4) | collective-permute-done | bytes 294944 | tf_op jit(solution)/shard_map/ppermute | solution.py:540
  24.0 0.1 shard_map.64
  24.1 2.7 %collective-permute-start.6 = (bf16[9,4,16,128]{3,2,1,0:T(8,128)(2,1)S(1)}, bf16[9,4,16,128]{3,2,1,0:T(8,128)(2,1)S(1)}, u32[]{:S(2)}, u32[]{:S(2)}) collective-permute-start(bf16[9,4,16,128]{3,2,1,0:T(8,128)(2,1)S(1)} %get-tuple-element.43.refs_2_), channel_id=1, source_target_pairs={{0,2},{1,3},{2,0},{3,1},{4,5},{5,4},{6,7},{7,6},{8,10},{9,11},{10,... | collective-permute-start | bytes 442376 | tf_op jit(solution)/shard_map/ppermute | solution.py:540
  26.8 0.1 shard_map.65
  26.9 1.6 %collective-permute-start.8 = (bf16[18,2,16,128]{3,2,1,0:T(8,128)(2,1)S(1)}, bf16[18,2,16,128]{3,2,1,0:T(8,128)(2,1)S(1)}, u32[]{:S(2)}, u32[]{:S(2)}) collective-permute-start(bf16[18,2,16,128]{3,2,1,0:T(8,128)(2,1)S(1)} %get-tuple-element.44.refs_1_.refs_2_), channel_id=1, source_target_pairs={{0,8},{1,9},{2,10},{3,11},{4,12},{5,13},{6,14},{7,15},{8,0},{9,1},... | collective-permute-start | bytes 442376 | tf_op jit(solution)/shard_map/ppermute | solution.py:540
  28.5 0.6 %collective-permute-start.5 = (bf16[512,128]{1,0:T(8,128)(2,1)S(1)}, bf16[512,128]{1,0:T(8,128)(2,1)S(1)}, u32[]{:S(2)}, u32[]{:S(2)}) collective-permute-start(bf16[512,128]{1,0:T(8,128)(2,1)S(1)} %get-tuple-element.46.refs_3_), channel_id=1, source_target_pairs={{0,1},{1,0},{2,3},{3,2},{4,6},{5,7},{6,4},{7,5},{8,9},{9,8},{10,11... | collective-permute-start | bytes 393224 | tf_op jit(solution)/shard_map/ppermute | solution.py:540
  29.2 1.6 %collective-permute-done.6.refs_1_ = bf16[9,4,16,128]{3,2,1,0:T(8,128)(2,1)S(1)} collective-permute-done((bf16[9,4,16,128]{3,2,1,0:T(8,128)(2,1)S(1)}, bf16[9,4,16,128]{3,2,1,0:T(8,128)(2,1)S(1)}, u32[]{:S(2)}, u32[]{:S(2)}) %collective-permute-start.6) | collective-permute-done | bytes 147488 | tf_op jit(solution)/shard_map/ppermute | solution.py:540
  30.8 1.4 %collective-permute-start.7 = (bf16[9,2,16,128]{3,2,1,0:T(8,128)(2,1)S(1)}, bf16[9,2,16,128]{3,2,1,0:T(8,128)(2,1)S(1)}, u32[]{:S(2)}, u32[]{:S(2)}) collective-permute-start(bf16[9,2,16,128]{3,2,1,0:T(8,128)(2,1)S(1)} %get-tuple-element.49.refs_2_), channel_id=1, source_target_pairs={{0,8},{1,9},{2,10},{3,11},{4,12},{5,13},{6,14},{7,15},{8,0},{9,1},... | collective-permute-start | bytes 221192 | tf_op jit(solution)/shard_map/ppermute | solution.py:540
  32.2 0.3 collective-permute-done.8.refs_1_
  32.6 2.7 %collective-permute-start.11 = (bf16[18,1,16,128]{3,2,1,0:T(8,128)(2,1)S(1)}, bf16[18,1,16,128]{3,2,1,0:T(8,128)(2,1)S(1)}, u32[]{:S(2)}, u32[]{:S(2)}) collective-permute-start(bf16[18,1,16,128]{3,2,1,0:T(8,128)(2,1)S(1)} %get-tuple-element.51.refs_2_), channel_id=1, source_target_pairs={{0,16},{1,17},{2,18},{3,19},{4,20},{5,21},{6,22},{7,23},{8,24},{9,... | collective-permute-start | bytes 221192 | tf_op jit(solution)/shard_map/ppermute | solution.py:540
  35.2 0.7 %collective-permute-done.7.refs_1_ = bf16[9,2,16,128]{3,2,1,0:T(8,128)(2,1)S(1)} collective-permute-done((bf16[9,2,16,128]{3,2,1,0:T(8,128)(2,1)S(1)}, bf16[9,2,16,128]{3,2,1,0:T(8,128)(2,1)S(1)}, u32[]{:S(2)}, u32[]{:S(2)}) %collective-permute-start.7) | collective-permute-done | bytes 73760 | tf_op jit(solution)/shard_map/ppermute | solution.py:540
  36.0 1.9 %collective-permute-start.10 = (bf16[9,1,16,128]{3,2,1,0:T(8,128)(2,1)S(1)}, bf16[9,1,16,128]{3,2,1,0:T(8,128)(2,1)S(1)}, u32[]{:S(2)}, u32[]{:S(2)}) collective-permute-start(bf16[9,1,16,128]{3,2,1,0:T(8,128)(2,1)S(1)} %get-tuple-element.52.refs_2_), channel_id=1, source_target_pairs={{0,16},{1,17},{2,18},{3,19},{4,20},{5,21},{6,22},{7,23},{8,24},{9,... | collective-permute-start | bytes 110600 | tf_op jit(solution)/shard_map/ppermute | solution.py:540
  37.9 2.6 %collective-permute-start.9 = (bf16[512,128]{1,0:T(8,128)(2,1)S(1)}, bf16[512,128]{1,0:T(8,128)(2,1)S(1)}, u32[]{:S(2)}, u32[]{:S(2)}) collective-permute-start(bf16[512,128]{1,0:T(8,128)(2,1)S(1)} %get-tuple-element.54.refs_3_), channel_id=1, source_target_pairs={{0,2},{1,3},{2,0},{3,1},{4,5},{5,4},{6,7},{7,6},{8,10},{9,11},{10,... | collective-permute-start | bytes 393224 | tf_op jit(solution)/shard_map/ppermute | solution.py:540
  40.5 0.4 collective-permute-done.10.refs_1_
  41.0 2.5 %collective-permute-start.12 = (bf16[27,16,128]{2,1,0:T(8,128)(2,1)S(1)}, bf16[27,16,128]{2,1,0:T(8,128)(2,1)S(1)}, u32[]{:S(2)}, u32[]{:S(2)}) collective-permute-start(bf16[27,16,128]{2,1,0:T(8,128)(2,1)S(1)} %shard_map.72.refs_2_.refs_0_), channel_id=1, source_target_pairs={{0,2},{1,3},{2,0},{3,1},{4,5},{5,4},{6,7},{7,6},{8,10},{9,11},{10,... | collective-permute-start | bytes 331784 | tf_op jit(solution)/shard_map/ppermute | solution.py:540
  43.4 0.8 %shard_map.73 = (bf16[64,2048]{1,0:T(8,128)(2,1)}, f32[8,128]{1,0:T(8,128)S(1)}) custom-call(bf16[8,64,128]{2,1,0:T(8,128)(2,1)S(1)} %bitcast.9, bf16[512,128]{1,0:T(8,128)(2,1)S(1)} %collective-permute-done.9.refs_1_, bf16[27,16,128]{2,1,0:T(8,128)(2,1)S(1)} %shard_map.72.refs_2_.refs_0_), custom_call_target="tpu_custom_call" | custom-call | flops 1000 | bytes 1000 | tf_op jit(solution)/shard_map/pallas_call | solution.py:231
  44.2 3.1 %collective-permute-done.12.refs_1_ = bf16[27,16,128]{2,1,0:T(8,128)(2,1)S(1)} collective-permute-done((bf16[27,16,128]{2,1,0:T(8,128)(2,1)S(1)}, bf16[27,16,128]{2,1,0:T(8,128)(2,1)S(1)}, u32[]{:S(2)}, u32[]{:S(2)}) %collective-permute-start.12) | collective-permute-done | bytes 110624 | tf_op jit(solution)/shard_map/ppermute | solution.py:540
  47.4 2.6 %shard_map.75 = (bf16[4,16,2,32,128]{4,3,2,1,0:T(8,128)(2,1)}, f32[8,128]{1,0:T(8,128)S(1)}) custom-call(bf16[512,256]{1,0:T(8,128)(2,1)S(1)} %get-tuple-element.36.grads_ref.refs_2_.refs_0_, bf16[256,256]{1,0:T(8,128)(2,1)S(1)} %collective-permute-done.1.refs_3_.refs_1_, bf16[3,3,3,128,256]{4,3,2,1,0:T(8,128)(2,1)S(1)} %copy-done, ...), custom_call_target="tpu_custom_call" | custom-call | flops 1000 | bytes 1000 | tf_op jit(solution)/shard_map/pallas_call | solution.py:521
  50.0 2.5 %collective-permute-done.13.refs_1_ = bf16[36,16,128]{2,1,0:T(8,128)(2,1)S(1)} collective-permute-done((bf16[36,16,128]{2,1,0:T(8,128)(2,1)S(1)}, bf16[36,16,128]{2,1,0:T(8,128)(2,1)S(1)}, u32[]{:S(2)}, u32[]{:S(2)}) %collective-permute-start.13) | collective-permute-done | bytes 147488 | tf_op jit(solution)/shard_map/ppermute | solution.py:540
  52.6 0.8 %shard_map.76 = f32[27,16,256]{2,1,0:T(8,128)} custom-call(bf16[36,16,128]{2,1,0:T(8,128)(2,1)S(1)} %shard_map.74.refs_3_.refs_0_, bf16[36,16,128]{2,1,0:T(8,128)(2,1)S(1)} %collective-permute-done.13.refs_1_, f32[8,128]{1,0:T(8,128)S(1)} %get-tuple-element.60.refs_2_), custom_call_target="tpu_custom_call" | custom-call | flops 1000 | bytes 1000 | tf_op jit(solution)/shard_map/pallas_call | solution.py:401
  (22 shorter events, 0.5 us)
Async XLA Ops:
  0.6 7.5 %copy-start.1 = (bf16[1,4,32,32,128]{4,3,2,1,0:T(8,128)(2,1)S(1)}, bf16[1,4,32,32,128]{4,3,2,1,0:T(8,128)(2,1)}, u32[]{:S(2)}) copy-start(bf16[1,4,32,32,128]{4,3,2,1,0:T(8,128)(2,1)} %volume_ref.3) | copy-start | bytes 3145732
  0.6 7.5 %copy-start = (bf16[3,3,3,128,256]{4,3,2,1,0:T(8,128)(2,1)S(1)}, bf16[3,3,3,128,256]{4,3,2,1,0:T(8,128)(2,1)}, u32[]{:S(2)}) copy-start(bf16[3,3,3,128,256]{4,3,2,1,0:T(8,128)(2,1)} %refs_2_.1) | copy-start | bytes 5308420
  3.1 8.1 %copy-start.2 = (bf16[1,2,16,16,256]{4,3,2,1,0:T(8,128)(2,1)S(1)}, bf16[1,2,16,16,256]{4,3,2,1,0:T(8,128)(2,1)}, u32[]{:S(2)}) copy-start(bf16[1,2,16,16,256]{4,3,2,1,0:T(8,128)(2,1)} %param.5) | copy-start | bytes 786436
  3.1 8.0 %collective-permute-start = (bf16[256,256]{1,0:T(8,128)(2,1)}, bf16[256,256]{1,0:T(8,128)(2,1)S(1)}, u32[]{:S(2)}, u32[]{:S(2)}) collective-permute-start(bf16[256,256]{1,0:T(8,128)(2,1)} %shard_map.59), channel_id=1, source_target_pairs={{0,1},{1,2},{2,3},{4,5},{5,6},{6,7},{8,9},{9,10},{10,11},{12,13},{... | collective-permute-start | bytes 393224 | tf_op jit(solution)/shard_map/ppermute | solution.py:560
  12.3 2.1 %collective-permute-start.2 = (bf16[36,4,16,128]{3,2,1,0:T(8,128)(2,1)S(1)}, bf16[36,4,16,128]{3,2,1,0:T(8,128)(2,1)S(1)}, u32[]{:S(2)}, u32[]{:S(2)}) collective-permute-start(bf16[36,4,16,128]{3,2,1,0:T(8,128)(2,1)S(1)} %get-tuple-element.38), channel_id=1, source_target_pairs={{0,4},{1,5},{2,6},{3,7},{4,0},{5,1},{6,2},{7,3},{8,12},{9,13},{10,... | collective-permute-start | bytes 1769480 | tf_op jit(solution)/shard_map/ppermute | solution.py:540
  12.4 8.4 %collective-permute-start.1 = (bf16[256,256]{1,0:T(8,128)(2,1)S(1)}, bf16[256,256]{1,0:T(8,128)(2,1)S(1)}, u32[]{:S(2)}, u32[]{:S(2)}) collective-permute-start(bf16[256,256]{1,0:T(8,128)(2,1)S(1)} %slice.3), channel_id=1, source_target_pairs={{1,0},{2,1},{3,2},{5,4},{6,5},{7,6},{9,8},{10,9},{11,10},{13,12},{... | collective-permute-start | bytes 393224 | tf_op jit(solution)/shard_map/ppermute | solution.py:560
  14.5 9.4 %collective-permute-start.4 = (bf16[18,4,16,128]{3,2,1,0:T(8,128)(2,1)S(1)}, bf16[18,4,16,128]{3,2,1,0:T(8,128)(2,1)S(1)}, u32[]{:S(2)}, u32[]{:S(2)}) collective-permute-start(bf16[18,4,16,128]{3,2,1,0:T(8,128)(2,1)S(1)} %get-tuple-element.39.refs_4_), channel_id=1, source_target_pairs={{0,1},{1,0},{2,3},{3,2},{4,6},{5,7},{6,4},{7,5},{8,9},{9,8},{10,11... | collective-permute-start | bytes 884744 | tf_op jit(solution)/shard_map/ppermute | solution.py:540
  21.3 5.4 %collective-permute-start.3 = (bf16[18,4,16,128]{3,2,1,0:T(8,128)(2,1)S(1)}, bf16[18,4,16,128]{3,2,1,0:T(8,128)(2,1)S(1)}, u32[]{:S(2)}, u32[]{:S(2)}) collective-permute-start(bf16[18,4,16,128]{3,2,1,0:T(8,128)(2,1)S(1)} %get-tuple-element.41.refs_2_), channel_id=1, source_target_pairs={{0,4},{1,5},{2,6},{3,7},{4,0},{5,1},{6,2},{7,3},{8,12},{9,13},{10,... | collective-permute-start | bytes 884744 | tf_op jit(solution)/shard_map/ppermute | solution.py:540
  24.1 6.7 %collective-permute-start.6 = (bf16[9,4,16,128]{3,2,1,0:T(8,128)(2,1)S(1)}, bf16[9,4,16,128]{3,2,1,0:T(8,128)(2,1)S(1)}, u32[]{:S(2)}, u32[]{:S(2)}) collective-permute-start(bf16[9,4,16,128]{3,2,1,0:T(8,128)(2,1)S(1)} %get-tuple-element.43.refs_2_), channel_id=1, source_target_pairs={{0,2},{1,3},{2,0},{3,1},{4,5},{5,4},{6,7},{7,6},{8,10},{9,11},{10,... | collective-permute-start | bytes 442376 | tf_op jit(solution)/shard_map/ppermute | solution.py:540
  26.9 5.7 %collective-permute-start.8 = (bf16[18,2,16,128]{3,2,1,0:T(8,128)(2,1)S(1)}, bf16[18,2,16,128]{3,2,1,0:T(8,128)(2,1)S(1)}, u32[]{:S(2)}, u32[]{:S(2)}) collective-permute-start(bf16[18,2,16,128]{3,2,1,0:T(8,128)(2,1)S(1)} %get-tuple-element.44.refs_1_.refs_2_), channel_id=1, source_target_pairs={{0,8},{1,9},{2,10},{3,11},{4,12},{5,13},{6,14},{7,15},{8,0},{9,1},... | collective-permute-start | bytes 442376 | tf_op jit(solution)/shard_map/ppermute | solution.py:540
  28.5 9.4 %collective-permute-start.5 = (bf16[512,128]{1,0:T(8,128)(2,1)S(1)}, bf16[512,128]{1,0:T(8,128)(2,1)S(1)}, u32[]{:S(2)}, u32[]{:S(2)}) collective-permute-start(bf16[512,128]{1,0:T(8,128)(2,1)S(1)} %get-tuple-element.46.refs_3_), channel_id=1, source_target_pairs={{0,1},{1,0},{2,3},{3,2},{4,6},{5,7},{6,4},{7,5},{8,9},{9,8},{10,11... | collective-permute-start | bytes 393224 | tf_op jit(solution)/shard_map/ppermute | solution.py:540
  30.8 5.2 %collective-permute-start.7 = (bf16[9,2,16,128]{3,2,1,0:T(8,128)(2,1)S(1)}, bf16[9,2,16,128]{3,2,1,0:T(8,128)(2,1)S(1)}, u32[]{:S(2)}, u32[]{:S(2)}) collective-permute-start(bf16[9,2,16,128]{3,2,1,0:T(8,128)(2,1)S(1)} %get-tuple-element.49.refs_2_), channel_id=1, source_target_pairs={{0,8},{1,9},{2,10},{3,11},{4,12},{5,13},{6,14},{7,15},{8,0},{9,1},... | collective-permute-start | bytes 221192 | tf_op jit(solution)/shard_map/ppermute | solution.py:540
  32.6 7.9 %collective-permute-start.11 = (bf16[18,1,16,128]{3,2,1,0:T(8,128)(2,1)S(1)}, bf16[18,1,16,128]{3,2,1,0:T(8,128)(2,1)S(1)}, u32[]{:S(2)}, u32[]{:S(2)}) collective-permute-start(bf16[18,1,16,128]{3,2,1,0:T(8,128)(2,1)S(1)} %get-tuple-element.51.refs_2_), channel_id=1, source_target_pairs={{0,16},{1,17},{2,18},{3,19},{4,20},{5,21},{6,22},{7,23},{8,24},{9,... | collective-permute-start | bytes 221192 | tf_op jit(solution)/shard_map/ppermute | solution.py:540
  36.0 4.9 %collective-permute-start.10 = (bf16[9,1,16,128]{3,2,1,0:T(8,128)(2,1)S(1)}, bf16[9,1,16,128]{3,2,1,0:T(8,128)(2,1)S(1)}, u32[]{:S(2)}, u32[]{:S(2)}) collective-permute-start(bf16[9,1,16,128]{3,2,1,0:T(8,128)(2,1)S(1)} %get-tuple-element.52.refs_2_), channel_id=1, source_target_pairs={{0,16},{1,17},{2,18},{3,19},{4,20},{5,21},{6,22},{7,23},{8,24},{9,... | collective-permute-start | bytes 110600 | tf_op jit(solution)/shard_map/ppermute | solution.py:540
  37.9 5.5 %collective-permute-start.9 = (bf16[512,128]{1,0:T(8,128)(2,1)S(1)}, bf16[512,128]{1,0:T(8,128)(2,1)S(1)}, u32[]{:S(2)}, u32[]{:S(2)}) collective-permute-start(bf16[512,128]{1,0:T(8,128)(2,1)S(1)} %get-tuple-element.54.refs_3_), channel_id=1, source_target_pairs={{0,2},{1,3},{2,0},{3,1},{4,5},{5,4},{6,7},{7,6},{8,10},{9,11},{10,... | collective-permute-start | bytes 393224 | tf_op jit(solution)/shard_map/ppermute | solution.py:540
  41.0 6.4 %collective-permute-start.12 = (bf16[27,16,128]{2,1,0:T(8,128)(2,1)S(1)}, bf16[27,16,128]{2,1,0:T(8,128)(2,1)S(1)}, u32[]{:S(2)}, u32[]{:S(2)}) collective-permute-start(bf16[27,16,128]{2,1,0:T(8,128)(2,1)S(1)} %shard_map.72.refs_2_.refs_0_), channel_id=1, source_target_pairs={{0,2},{1,3},{2,0},{3,1},{4,5},{5,4},{6,7},{7,6},{8,10},{9,11},{10,... | collective-permute-start | bytes 331784 | tf_op jit(solution)/shard_map/ppermute | solution.py:540
  47.4 5.2 %collective-permute-start.13 = (bf16[36,16,128]{2,1,0:T(8,128)(2,1)S(1)}, bf16[36,16,128]{2,1,0:T(8,128)(2,1)S(1)}, u32[]{:S(2)}, u32[]{:S(2)}) collective-permute-start(bf16[36,16,128]{2,1,0:T(8,128)(2,1)S(1)} %shard_map.74.refs_3_.refs_0_), channel_id=1, source_target_pairs={{0,1},{1,0},{2,3},{3,2},{4,6},{5,7},{6,4},{7,5},{8,9},{9,8},{10,11... | collective-permute-start | bytes 442376 | tf_op jit(solution)/shard_map/ppermute | solution.py:540

commit v8 on v7

--- a/solution.py
+++ b/solution.py
@@ -13,7 +13,7 @@
 VMEM_LIMIT = 20 * 1024 * 1024
 DONE = (8, 128)
 PLANE_PARTS = 1
-SPACER = 6 * 10**9
+SPACER = 7 * 10**8
 VMEM_WHOLE = 60 * 1024 * 1024
 
 
@@ -271,7 +271,7 @@
     sent_ref[...] = keep_ref[:, 1 - side(*then, cores)].reshape(sent_ref.shape).astype(BF16)
 
 
-def add_stage(value, got, now, then, cores, order=()):
+def add_stage(value, got, now, then, cores, order=(), flops=1000):
     shape = (sum(piece.shape[0] for piece in got),) + got[0].shape[1:]
     if then is None:
         outs = jax.ShapeDtypeStruct(shape, BF16)
@@ -285,6 +285,7 @@
         outs,
         order=order,
         inputs=1 + len(got),
+        flops=flops,
     )(value, *got, *order)
 
 
@@ -339,71 +340,72 @@
     )(*operands, *order)
 
 
-def gather_kernel(early, mine_ref, got_ref, out_ref):
+def gather_kernel(early, mine_ref, got_ref, *outs):
     rows = pl.ds(early, mine_ref.shape[0] - early)
-    out_ref[pl.ds(0, early)] = mine_ref[pl.ds(0, early)]
-    out_ref[pl.ds(early, early)] = got_ref[pl.ds(0, early)]
+    outs[0][pl.ds(0, early)] = mine_ref[pl.ds(0, early)]
+    outs[0][pl.ds(early, early)] = got_ref[pl.ds(0, early)]
     total = mine_ref[rows].astype(F32) + got_ref[rows].astype(F32)
-    out_ref[pl.ds(2 * early, total.shape[0])] = total.astype(BF16)
-
-
-def gather_stage(mine, got, early, order=()):
-    return call(
-        functools.partial(gather_kernel, early),
-        jax.ShapeDtypeStruct((mine.shape[0] + early,) + mine.shape[1:], BF16),
-        order=order,
-        inputs=2,
-    )(mine, got, *order)
-
-
-def join_kernel(now, cores, value_ref, got_ref, late_ref, out_ref):
-    total = value_ref[:, side(*now, cores)].reshape(got_ref.shape) + got_ref[...].astype(F32)
-    early = total.shape[0]
-    out_ref[pl.ds(0, early)] = total.reshape((early,) + out_ref.shape[1:]).astype(BF16)
-    out_ref[pl.ds(early, late_ref.shape[0])] = late_ref[...].reshape((-1,) + out_ref.shape[1:])
-
-
-def join(value, got, late, now, cores, order):
-    shape = (got.shape[0] + late.shape[0],) + got.shape[2:]
-    return call(
-        functools.partial(join_kernel, now, cores),
-        jax.ShapeDtypeStruct(shape, BF16),
+    if len(outs) == 2:
+        outs[1][...] = total
+    else:
+        outs[0][pl.ds(2 * early, total.shape[0])] = total.astype(BF16)
+
+
+def gather_stage(mine, got, early, last, order=()):
+    late, rest = mine.shape[0] - early, mine.shape[1:]
+    if last:
+        outs = (
+            jax.ShapeDtypeStruct((2 * early,) + rest, BF16),
+            jax.ShapeDtypeStruct((late,) + rest, F32),
+        )
+    else:
+        outs = (jax.ShapeDtypeStruct((2 * early + late,) + rest, BF16),)
+    return call(functools.partial(gather_kernel, early), outs, order=order, inputs=2)(mine, got, *order)
+
+
+def join_kernel(early_ref, late_ref, got_ref, out_ref):
+    early = early_ref.shape[0]
+    total = late_ref[...].astype(F32) + got_ref[...].astype(F32)
+    out_ref[pl.ds(0, early)] = early_ref[...].reshape((early,) + out_ref.shape[1:])
+    out_ref[pl.ds(early, total.shape[0])] = total.reshape((-1,) + out_ref.shape[1:]).astype(BF16)
+
+
+def join(early, late, got, order):
+    return call(
+        join_kernel,
+        jax.ShapeDtypeStruct((early.shape[0] + late.shape[0],) + got.shape[2:], BF16),
         order=order,
         inputs=3,
-        flops=SPACER,
-    )(value, got, late, *order)
-
-
-def kernel_grad_out_kernel(space, cores, early_units, late_units, mine_ref, got_ref, out_ref):
+    )(early, late, got, *order)
+
+
+def kernel_grad_out_kernel(space, cores, early_units, mine_ref, got_ref, late_ref, out_ref):
     halves = out_ref.shape[-1] // 128
     half = space // 2
     share = -(-early_units // space)
+    late_units = late_ref.shape[0]
 
     def put(index, value):
         tap, part = divmod(index, halves)
-        out_ref[tap, :, part * 128 : (part + 1) * 128] = value
+        out_ref[tap, :, part * 128 : (part + 1) * 128] = value.astype(F32)
 
     for unit in range(late_units):
-        row = half * share + unit
-        put(unit, mine_ref[row].astype(F32) + got_ref[row].astype(F32))
+        put(unit, late_ref[unit])
     for group in range(space):
         place = relative_group(group, space, cores)
         far, row = place // half, (place % half) * share
         for unit in range(share):
             index = group * share + unit
             if index < early_units:
-                value = jnp.where(far == 1, got_ref[row + unit], mine_ref[row + unit])
-                put(late_units + index, value.astype(F32))
-
-
-def kernel_grad_out(mine, got, early_units, late_units, space, cores, co, order):
-    taps = (early_units + late_units) * 128 // co
-    return call(
-        functools.partial(kernel_grad_out_kernel, space, cores, early_units, late_units),
+                put(late_units + index, jnp.where(far == 1, got_ref[row + unit], mine_ref[row + unit]))
+
+
+def kernel_grad_out(mine, got, late, early_units, space, cores, co):
+    taps = (early_units + late.shape[0]) * 128 // co
+    return call(
+        functools.partial(kernel_grad_out_kernel, space, cores, early_units),
         jax.ShapeDtypeStruct((taps, mine.shape[1], co), F32),
-        order=order,
-        inputs=2,
-    )(mine, got, *order)
+    )(mine, got, late)
 
 
 def store_units(product, scale, core, cores, chips, put):
@@ -588,11 +590,11 @@
     above = neighbour(grads[:cells], -1)
 
     early = kernel_grad_part(even, odd, grads, None, (1, 2), cores, chips, scale, space)
-    early_units, late_units = 18 * (co // 128), 9 * (co // 128)
+    early_units = 18 * (co // 128)
     plan = over_space + over_chips
     value, sent = add_cores(early[0], early[1:], plan[0], cores)
     late_plan, late_now, late_half = list(over_chips), None, None
-    switch_at = [len(over_space) - 1 + 2 * stage for stage in range(len(over_space))]
+    switch_at = [len(over_space) - 1 + stage for stage in range(len(over_space))]
     stay, moved = flipped[None], None
     for place, now in enumerate(plan):
         got = exchange_stage(sent, *now, cores)
@@ -626,20 +628,19 @@
         moved = exchange_space(out, stage, cores)
     if late_half is None:
         late_half = add_stage(late_value, late_got, late_now, None, cores)
-
-    mine = join(value, got, late_half, plan[-1], cores, tuple(tokens[1:]))
-    early_rows = mine.shape[0] - late_half.shape[0]
-    switched = None
+    late_got = exchange_space(late_half, 0, cores)
+    early_sum = add_stage(value, (got,), plan[-1], None, cores, (late_half,), SPACER)
+
+    switched, done = switched_of(stay, moved, 0, space, cores, (late_half,))
+    mine = join(early_sum, late_half, late_got, (done,))
+    early_rows = early_sum.shape[0]
+    volume_grad, done = volume_grad_of(grads, above, kernel, height, width, (mine,))
     for step, (_, stage) in enumerate(reversed(over_space)):
         got = exchange_space(mine, stage, cores)
-        order = ()
-        if switched is None:
-            switched, done = switched_of(stay, moved, 0, space, cores, (mine,))
-            order = (done,)
-        if step + 1 < len(over_space):
-            mine = gather_stage(mine, got, early_rows << step, order)
-    volume_grad, done = volume_grad_of(grads, above, kernel, height, width, (mine,))
-    kernel_grad = kernel_grad_out(mine, got, early_units, late_units, space, cores, co, (done,))
+        order = () if step else (done,)
+        if stage:
+            mine, *late_sum = gather_stage(mine, got, early_rows << step, stage == 1, order)
+    kernel_grad = kernel_grad_out(mine, got, late_sum[0], early_units, space, cores, co)
 
     return (
         switched[None],

time: 53.6 us -> 54 us (level)
  starting transfers between devices: 24.9 us -> 25.5 us
    ppermute x12 -> x13, starting transfers between devices: 18.6 us -> 19.2 us  [exchange(): return lax.ppermute(value, ('dp', 'space'), pairs)]
    ppermute x12 -> x13, waiting for transfers between devices: 12 us -> 11.7 us  [exchange(): return lax.ppermute(value, ('dp', 'space'), pairs)]
  transfers between devices with their start and end apart: 14 -> 15, of which waited for: 10 -> 9; matrix products, arithmetic and copies ran while one was open for 0% -> 0% of each run, Pallas kernels for 11% -> 11%
where the time goes in v8:
time: 54 us; the launch traced here: 53.8 us
  starting transfers between devices  25.5 us (47%)
  waiting for transfers between devices  17.2 us (32%)
  Pallas kernels  10.3 us (19%)
  between operations  0.82 us (2%)
    ppermute x13, starting transfers between devices, exchange(): return lax.ppermute(value, ('dp', 'space'), pairs)  19.2 us
    ppermute x13, waiting for transfers between devices, exchange(): return lax.ppermute(value, ('dp', 'space'), pairs)  11.7 us
    ppermute x2, starting transfers between devices, neighbour(): lax.ppermute(value, 'space', [(source, source + steps) for source in rang...  6.27 us
    ppermute x2, waiting for transfers between devices, neighbour(): lax.ppermute(value, 'space', [(source, source + steps) for source in rang...  5.49 us
    pallas_call x1, Pallas kernels, volume_grad_of(): call(volume_grad_kernel, (jax.ShapeDtypeStruct(shape, BF16), jax.ShapeDty...  2.59 us
    pallas_call x1, Pallas kernels, halo_share(): call(halo_kernel, jax.ShapeDtypeStruct((height * width // 4, co), BF16),...  2.47 us
    pallas_call x1, Pallas kernels, partial_preact(): call(preact_kernel, (jax.ShapeDtypeStruct((planes // 2 * cells, co), F32)...  1.38 us
    pallas_call x2, Pallas kernels, kernel_grad_part(): call(functools.partial(kernel_grad_kernel, kds, cores, chips, scale, part...  1.35 us
  transfers between devices with their start and end apart: 15, of which 9 were waited for; matrix products, arithmetic and copies ran while one was open for 0% of the time, Pallas kernels for 11%

profile of v8, /device:TPU:0, one launch (start us, length us, event | category | flops | bytes accessed | tf_op | source)
XLA Modules:
  0.0 53.8 jit_solution(4338611623937934993)
XLA Ops:
  0.6 2.5 %shard_map.59 = bf16[256,256]{1,0:T(8,128)(2,1)} custom-call(bf16[1,4,32,32,128]{4,3,2,1,0:T(8,128)(2,1)} %volume_ref.3, bf16[3,3,3,128,256]{4,3,2,1,0:T(8,128)(2,1)} %refs_2_.1), custom_call_target="tpu_custom_call" | custom-call | flops 1000 | bytes 1000 | tf_op jit(solution)/shard_map/pallas_call | solution.py:123
  3.1 5.0 %collective-permute-start = (bf16[256,256]{1,0:T(8,128)(2,1)}, bf16[256,256]{1,0:T(8,128)(2,1)S(1)}, u32[]{:S(2)}, u32[]{:S(2)}) collective-permute-start(bf16[256,256]{1,0:T(8,128)(2,1)} %shard_map.59), channel_id=1, source_target_pairs={{0,1},{1,2},{2,3},{4,5},{5,6},{6,7},{8,9},{9,10},{10,11},{12,13},{... | collective-permute-start | bytes 393224 | tf_op jit(solution)/shard_map/ppermute | solution.py:562
  8.2 1.4 %shard_map.58 = (f32[512,256]{1,0:T(8,128)S(1)}, bf16[4,16,16,384]{3,2,1,0:T(8,128)(2,1)S(1)}, bf16[4,17,16,384]{3,2,1,0:T(8,128)(2,1)S(1)}) custom-call(bf16[1,4,32,32,128]{4,3,2,1,0:T(8,128)(2,1)S(1)} %copy-done.1, bf16[3,3,3,128,256]{4,3,2,1,0:T(8,128)(2,1)S(1)} %copy-done), custom_call_target="tpu_custom_call" | custom-call | flops 1000 | bytes 1000 | tf_op jit(solution)/shard_map/pallas_call | solution.py:169
  9.5 1.6 %collective-permute-done.share_ref = bf16[256,256]{1,0:T(8,128)(2,1)S(1)} collective-permute-done((bf16[256,256]{1,0:T(8,128)(2,1)}, bf16[256,256]{1,0:T(8,128)(2,1)S(1)}, u32[]{:S(2)}, u32[]{:S(2)}) %collective-permute-start) | collective-permute-done | bytes 131104 | tf_op jit(solution)/shard_map/ppermute | solution.py:562
  11.2 0.3 shard_map.60
  11.5 0.8 %shard_map.61 = (f32[36,4,16,128]{3,2,1,0:T(8,128)S(1)}, bf16[36,4,16,128]{3,2,1,0:T(8,128)(2,1)S(1)}) custom-call(bf16[4,16,16,384]{3,2,1,0:T(8,128)(2,1)S(1)} %get-tuple-element.36.even_ref.refs_0_, bf16[4,17,16,384]{3,2,1,0:T(8,128)(2,1)S(1)} %get-tuple-element.37.odd_ref.refs_1_, bf16[512,256]{1,0:T(8,128)(2,1)S(1)} %get-tuple-element.38.grads_ref.refs_2_.refs_0_), custom_call_target="tpu_custom_call" | custom-call | flops 1000 | bytes 1000 | tf_op jit(solution)/shard_map/pallas_call | solution.py:468
  12.4 1.3 %collective-permute-start.1 = (bf16[256,256]{1,0:T(8,128)(2,1)S(1)}, bf16[256,256]{1,0:T(8,128)(2,1)S(1)}, u32[]{:S(2)}, u32[]{:S(2)}) collective-permute-start(bf16[256,256]{1,0:T(8,128)(2,1)S(1)} %slice.3), channel_id=1, source_target_pairs={{1,0},{2,1},{3,2},{5,4},{6,5},{7,6},{9,8},{10,9},{11,10},{13,12},{... | collective-permute-start | bytes 393224 | tf_op jit(solution)/shard_map/ppermute | solution.py:562
  13.7 0.7 %collective-permute-done.2.refs_0_ = bf16[36,4,16,128]{3,2,1,0:T(8,128)(2,1)S(1)} collective-permute-done((bf16[36,4,16,128]{3,2,1,0:T(8,128)(2,1)S(1)}, bf16[36,4,16,128]{3,2,1,0:T(8,128)(2,1)S(1)}, u32[]{:S(2)}, u32[]{:S(2)}) %collective-permute-start.2) | collective-permute-done | bytes 589856 | tf_op jit(solution)/shard_map/ppermute | solution.py:542
  14.4 0.2 shard_map.62
  14.5 2.4 %collective-permute-start.4 = (bf16[18,4,16,128]{3,2,1,0:T(8,128)(2,1)S(1)}, bf16[18,4,16,128]{3,2,1,0:T(8,128)(2,1)S(1)}, u32[]{:S(2)}, u32[]{:S(2)}) collective-permute-start(bf16[18,4,16,128]{3,2,1,0:T(8,128)(2,1)S(1)} %get-tuple-element.41.refs_4_), channel_id=1, source_target_pairs={{0,1},{1,0},{2,3},{3,2},{4,6},{5,7},{6,4},{7,5},{8,9},{9,8},{10,11... | collective-permute-start | bytes 884744 | tf_op jit(solution)/shard_map/ppermute | solution.py:542
  17.0 3.9 %collective-permute-done.1.refs_3_.refs_1_ = bf16[256,256]{1,0:T(8,128)(2,1)S(1)} collective-permute-done((bf16[256,256]{1,0:T(8,128)(2,1)S(1)}, bf16[256,256]{1,0:T(8,128)(2,1)S(1)}, u32[]{:S(2)}, u32[]{:S(2)}) %collective-permute-start.1) | collective-permute-done | bytes 131104 | tf_op jit(solution)/shard_map/ppermute | solution.py:562
  20.8 0.5 shard_map.63
  21.4 2.6 %collective-permute-done.4.refs_1_ = bf16[18,4,16,128]{3,2,1,0:T(8,128)(2,1)S(1)} collective-permute-done((bf16[18,4,16,128]{3,2,1,0:T(8,128)(2,1)S(1)}, bf16[18,4,16,128]{3,2,1,0:T(8,128)(2,1)S(1)}, u32[]{:S(2)}, u32[]{:S(2)}) %collective-permute-start.4) | collective-permute-done | bytes 294944 | tf_op jit(solution)/shard_map/ppermute | solution.py:542
  24.1 2.7 %collective-permute-start.7 = (bf16[9,4,16,128]{3,2,1,0:T(8,128)(2,1)S(1)}, bf16[9,4,16,128]{3,2,1,0:T(8,128)(2,1)S(1)}, u32[]{:S(2)}, u32[]{:S(2)}) collective-permute-start(bf16[9,4,16,128]{3,2,1,0:T(8,128)(2,1)S(1)} %get-tuple-element.45.refs_2_), channel_id=1, source_target_pairs={{0,2},{1,3},{2,0},{3,1},{4,5},{5,4},{6,7},{7,6},{8,10},{9,11},{10,... | collective-permute-start | bytes 442376 | tf_op jit(solution)/shard_map/ppermute | solution.py:542
  26.8 0.1 shard_map.65
  26.9 1.6 %collective-permute-start.6 = (bf16[18,2,16,128]{3,2,1,0:T(8,128)(2,1)S(1)}, bf16[18,2,16,128]{3,2,1,0:T(8,128)(2,1)S(1)}, u32[]{:S(2)}, u32[]{:S(2)}) collective-permute-start(bf16[18,2,16,128]{3,2,1,0:T(8,128)(2,1)S(1)} %get-tuple-element.46.refs_1_.refs_2_), channel_id=1, source_target_pairs={{0,8},{1,9},{2,10},{3,11},{4,12},{5,13},{6,14},{7,15},{8,0},{9,1},... | collective-permute-start | bytes 442376 | tf_op jit(solution)/shard_map/ppermute | solution.py:542
  28.5 0.6 %collective-permute-start.5 = (bf16[512,128]{1,0:T(8,128)(2,1)S(1)}, bf16[512,128]{1,0:T(8,128)(2,1)S(1)}, u32[]{:S(2)}, u32[]{:S(2)}) collective-permute-start(bf16[512,128]{1,0:T(8,128)(2,1)S(1)} %get-tuple-element.48.refs_3_), channel_id=1, source_target_pairs={{0,1},{1,0},{2,3},{3,2},{4,6},{5,7},{6,4},{7,5},{8,9},{9,8},{10,11... | collective-permute-start | bytes 393224 | tf_op jit(solution)/shard_map/ppermute | solution.py:542
  29.2 1.6 %collective-permute-done.7.refs_1_ = bf16[9,4,16,128]{3,2,1,0:T(8,128)(2,1)S(1)} collective-permute-done((bf16[9,4,16,128]{3,2,1,0:T(8,128)(2,1)S(1)}, bf16[9,4,16,128]{3,2,1,0:T(8,128)(2,1)S(1)}, u32[]{:S(2)}, u32[]{:S(2)}) %collective-permute-start.7) | collective-permute-done | bytes 147488 | tf_op jit(solution)/shard_map/ppermute | solution.py:542
  30.8 1.4 %collective-permute-start.10 = (bf16[9,2,16,128]{3,2,1,0:T(8,128)(2,1)S(1)}, bf16[9,2,16,128]{3,2,1,0:T(8,128)(2,1)S(1)}, u32[]{:S(2)}, u32[]{:S(2)}) collective-permute-start(bf16[9,2,16,128]{3,2,1,0:T(8,128)(2,1)S(1)} %get-tuple-element.51.refs_2_), channel_id=1, source_target_pairs={{0,8},{1,9},{2,10},{3,11},{4,12},{5,13},{6,14},{7,15},{8,0},{9,1},... | collective-permute-start | bytes 221192 | tf_op jit(solution)/shard_map/ppermute | solution.py:542
  32.2 0.3 collective-permute-done.6.refs_1_
  32.6 2.7 %collective-permute-start.9 = (bf16[18,1,16,128]{3,2,1,0:T(8,128)(2,1)S(1)}, bf16[18,1,16,128]{3,2,1,0:T(8,128)(2,1)S(1)}, u32[]{:S(2)}, u32[]{:S(2)}) collective-permute-start(bf16[18,1,16,128]{3,2,1,0:T(8,128)(2,1)S(1)} %get-tuple-element.52.refs_2_), channel_id=1, source_target_pairs={{0,16},{1,17},{2,18},{3,19},{4,20},{5,21},{6,22},{7,23},{8,24},{9,... | collective-permute-start | bytes 221192 | tf_op jit(solution)/shard_map/ppermute | solution.py:542
  35.3 1.8 %collective-permute-start.8 = (bf16[512,128]{1,0:T(8,128)(2,1)S(1)}, bf16[512,128]{1,0:T(8,128)(2,1)S(1)}, u32[]{:S(2)}, u32[]{:S(2)}) collective-permute-start(bf16[512,128]{1,0:T(8,128)(2,1)S(1)} %get-tuple-element.54.refs_3_), channel_id=1, source_target_pairs={{0,2},{1,3},{2,0},{3,1},{4,5},{5,4},{6,7},{7,6},{8,10},{9,11},{10,... | collective-permute-start | bytes 393224 | tf_op jit(solution)/shard_map/ppermute | solution.py:542
  37.1 0.8 %collective-permute-start.11 = (bf16[9,1,16,128]{3,2,1,0:T(8,128)(2,1)S(1)}, bf16[9,1,16,128]{3,2,1,0:T(8,128)(2,1)S(1)}, u32[]{:S(2)}, u32[]{:S(2)}) collective-permute-start(bf16[9,1,16,128]{3,2,1,0:T(8,128)(2,1)S(1)} %get-tuple-element.57.refs_2_), channel_id=1, source_target_pairs={{0,16},{1,17},{2,18},{3,19},{4,20},{5,21},{6,22},{7,23},{8,24},{9,... | collective-permute-start | bytes 110600 | tf_op jit(solution)/shard_map/ppermute | solution.py:542
  37.9 1.5 %collective-permute-start.12 = (bf16[18,1,16,128]{3,2,1,0:T(8,128)(2,1)S(1)}, bf16[18,1,16,128]{3,2,1,0:T(8,128)(2,1)S(1)}, u32[]{:S(2)}, u32[]{:S(2)}) collective-permute-start(bf16[18,1,16,128]{3,2,1,0:T(8,128)(2,1)S(1)} %shard_map.71.refs_2_.refs_1_), channel_id=1, source_target_pairs={{0,1},{1,0},{2,3},{3,2},{4,6},{5,7},{6,4},{7,5},{8,9},{9,8},{10,11... | collective-permute-start | bytes 221192 | tf_op jit(solution)/shard_map/ppermute | solution.py:542
  39.5 2.6 %collective-permute-done.11.refs_1_ = bf16[9,1,16,128]{3,2,1,0:T(8,128)(2,1)S(1)} collective-permute-done((bf16[9,1,16,128]{3,2,1,0:T(8,128)(2,1)S(1)}, bf16[9,1,16,128]{3,2,1,0:T(8,128)(2,1)S(1)}, u32[]{:S(2)}, u32[]{:S(2)}) %collective-permute-start.11) | collective-permute-done | bytes 36896 | tf_op jit(solution)/shard_map/ppermute | solution.py:542
  42.1 0.8 %shard_map.72 = (bf16[64,2048]{1,0:T(8,128)(2,1)}, f32[8,128]{1,0:T(8,128)S(1)}) custom-call(bf16[8,64,128]{2,1,0:T(8,128)(2,1)S(1)} %bitcast.9, bf16[512,128]{1,0:T(8,128)(2,1)S(1)} %collective-permute-done.8.refs_1_, bf16[18,1,16,128]{3,2,1,0:T(8,128)(2,1)S(1)} %shard_map.71.refs_2_.refs_1_), custom_call_target="tpu_custom_call" | custom-call | flops 1000 | bytes 1000 | tf_op jit(solution)/shard_map/pallas_call | solution.py:231
  42.9 2.0 %collective-permute-start.13 = (bf16[27,16,128]{2,1,0:T(8,128)(2,1)S(1)}, bf16[27,16,128]{2,1,0:T(8,128)(2,1)S(1)}, u32[]{:S(2)}, u32[]{:S(2)}) collective-permute-start(bf16[27,16,128]{2,1,0:T(8,128)(2,1)S(1)} %shard_map.74.refs_3_.refs_0_), channel_id=1, source_target_pairs={{0,2},{1,3},{2,0},{3,1},{4,5},{5,4},{6,7},{7,6},{8,10},{9,11},{10,... | collective-permute-start | bytes 331784 | tf_op jit(solution)/shard_map/ppermute | solution.py:542
  44.9 2.6 %shard_map.75 = (bf16[4,16,2,32,128]{4,3,2,1,0:T(8,128)(2,1)}, f32[8,128]{1,0:T(8,128)S(1)}) custom-call(bf16[512,256]{1,0:T(8,128)(2,1)S(1)} %get-tuple-element.38.grads_ref.refs_2_.refs_0_, bf16[256,256]{1,0:T(8,128)(2,1)S(1)} %collective-permute-done.1.refs_3_.refs_1_, bf16[3,3,3,128,256]{4,3,2,1,0:T(8,128)(2,1)S(1)} %copy-done, ...), custom_call_target="tpu_custom_call" | custom-call | flops 1000 | bytes 1000 | tf_op jit(solution)/shard_map/pallas_call | solution.py:523
  47.5 1.0 %collective-permute-done.13.refs_1_ = bf16[27,16,128]{2,1,0:T(8,128)(2,1)S(1)} collective-permute-done((bf16[27,16,128]{2,1,0:T(8,128)(2,1)S(1)}, bf16[27,16,128]{2,1,0:T(8,128)(2,1)S(1)}, u32[]{:S(2)}, u32[]{:S(2)}) %collective-permute-start.13) | collective-permute-done | bytes 110624 | tf_op jit(solution)/shard_map/ppermute | solution.py:542
  48.5 1.5 %collective-permute-start.14 = (bf16[18,16,128]{2,1,0:T(8,128)(2,1)S(1)}, bf16[18,16,128]{2,1,0:T(8,128)(2,1)S(1)}, u32[]{:S(2)}, u32[]{:S(2)}) collective-permute-start(bf16[18,16,128]{2,1,0:T(8,128)(2,1)S(1)} %get-tuple-element.63.mine_ref), channel_id=1, source_target_pairs={{0,1},{1,0},{2,3},{3,2},{4,6},{5,7},{6,4},{7,5},{8,9},{9,8},{10,11... | collective-permute-start | bytes 221192 | tf_op jit(solution)/shard_map/ppermute | solution.py:542
  50.0 3.0 %collective-permute-done.14.got_ref = bf16[18,16,128]{2,1,0:T(8,128)(2,1)S(1)} collective-permute-done((bf16[18,16,128]{2,1,0:T(8,128)(2,1)S(1)}, bf16[18,16,128]{2,1,0:T(8,128)(2,1)S(1)}, u32[]{:S(2)}, u32[]{:S(2)}) %collective-permute-start.14) | collective-permute-done | bytes 73760 | tf_op jit(solution)/shard_map/ppermute | solution.py:542
  53.0 0.8 %shard_map.77 = f32[27,16,256]{2,1,0:T(8,128)} custom-call(bf16[18,16,128]{2,1,0:T(8,128)(2,1)S(1)} %get-tuple-element.63.mine_ref, bf16[18,16,128]{2,1,0:T(8,128)(2,1)S(1)} %collective-permute-done.14.got_ref, f32[18,16,128]{2,1,0:T(8,128)S(1)} %get-tuple-element.64.late_ref), custom_call_target="tpu_custom_call" | custom-call | flops 1000 | bytes 1000 | tf_op jit(solution)/shard_map/pallas_call | solution.py:405
  (25 shorter events, 0.5 us)
Async XLA Ops:
  0.6 7.5 %copy-start.1 = (bf16[1,4,32,32,128]{4,3,2,1,0:T(8,128)(2,1)S(1)}, bf16[1,4,32,32,128]{4,3,2,1,0:T(8,128)(2,1)}, u32[]{:S(2)}) copy-start(bf16[1,4,32,32,128]{4,3,2,1,0:T(8,128)(2,1)} %volume_ref.3) | copy-start | bytes 3145732
  0.6 7.5 %copy-start = (bf16[3,3,3,128,256]{4,3,2,1,0:T(8,128)(2,1)S(1)}, bf16[3,3,3,128,256]{4,3,2,1,0:T(8,128)(2,1)}, u32[]{:S(2)}) copy-start(bf16[3,3,3,128,256]{4,3,2,1,0:T(8,128)(2,1)} %refs_2_.1) | copy-start | bytes 5308420
  3.1 8.1 %copy-start.2 = (bf16[1,2,16,16,256]{4,3,2,1,0:T(8,128)(2,1)S(1)}, bf16[1,2,16,16,256]{4,3,2,1,0:T(8,128)(2,1)}, u32[]{:S(2)}) copy-start(bf16[1,2,16,16,256]{4,3,2,1,0:T(8,128)(2,1)} %param.5) | copy-start | bytes 786436
  3.1 8.0 %collective-permute-start = (bf16[256,256]{1,0:T(8,128)(2,1)}, bf16[256,256]{1,0:T(8,128)(2,1)S(1)}, u32[]{:S(2)}, u32[]{:S(2)}) collective-permute-start(bf16[256,256]{1,0:T(8,128)(2,1)} %shard_map.59), channel_id=1, source_target_pairs={{0,1},{1,2},{2,3},{4,5},{5,6},{6,7},{8,9},{9,10},{10,11},{12,13},{... | collective-permute-start | bytes 393224 | tf_op jit(solution)/shard_map/ppermute | solution.py:562
  12.3 2.1 %collective-permute-start.2 = (bf16[36,4,16,128]{3,2,1,0:T(8,128)(2,1)S(1)}, bf16[36,4,16,128]{3,2,1,0:T(8,128)(2,1)S(1)}, u32[]{:S(2)}, u32[]{:S(2)}) collective-permute-start(bf16[36,4,16,128]{3,2,1,0:T(8,128)(2,1)S(1)} %get-tuple-element.40), channel_id=1, source_target_pairs={{0,4},{1,5},{2,6},{3,7},{4,0},{5,1},{6,2},{7,3},{8,12},{9,13},{10,... | collective-permute-start | bytes 1769480 | tf_op jit(solution)/shard_map/ppermute | solution.py:542
  12.4 8.4 %collective-permute-start.1 = (bf16[256,256]{1,0:T(8,128)(2,1)S(1)}, bf16[256,256]{1,0:T(8,128)(2,1)S(1)}, u32[]{:S(2)}, u32[]{:S(2)}) collective-permute-start(bf16[256,256]{1,0:T(8,128)(2,1)S(1)} %slice.3), channel_id=1, source_target_pairs={{1,0},{2,1},{3,2},{5,4},{6,5},{7,6},{9,8},{10,9},{11,10},{13,12},{... | collective-permute-start | bytes 393224 | tf_op jit(solution)/shard_map/ppermute | solution.py:562
  14.5 9.4 %collective-permute-start.4 = (bf16[18,4,16,128]{3,2,1,0:T(8,128)(2,1)S(1)}, bf16[18,4,16,128]{3,2,1,0:T(8,128)(2,1)S(1)}, u32[]{:S(2)}, u32[]{:S(2)}) collective-permute-start(bf16[18,4,16,128]{3,2,1,0:T(8,128)(2,1)S(1)} %get-tuple-element.41.refs_4_), channel_id=1, source_target_pairs={{0,1},{1,0},{2,3},{3,2},{4,6},{5,7},{6,4},{7,5},{8,9},{9,8},{10,11... | collective-permute-start | bytes 884744 | tf_op jit(solution)/shard_map/ppermute | solution.py:542
  21.3 5.4 %collective-permute-start.3 = (bf16[18,4,16,128]{3,2,1,0:T(8,128)(2,1)S(1)}, bf16[18,4,16,128]{3,2,1,0:T(8,128)(2,1)S(1)}, u32[]{:S(2)}, u32[]{:S(2)}) collective-permute-start(bf16[18,4,16,128]{3,2,1,0:T(8,128)(2,1)S(1)} %get-tuple-element.43.refs_2_), channel_id=1, source_target_pairs={{0,4},{1,5},{2,6},{3,7},{4,0},{5,1},{6,2},{7,3},{8,12},{9,13},{10,... | collective-permute-start | bytes 884744 | tf_op jit(solution)/shard_map/ppermute | solution.py:542
  24.1 6.7 %collective-permute-start.7 = (bf16[9,4,16,128]{3,2,1,0:T(8,128)(2,1)S(1)}, bf16[9,4,16,128]{3,2,1,0:T(8,128)(2,1)S(1)}, u32[]{:S(2)}, u32[]{:S(2)}) collective-permute-start(bf16[9,4,16,128]{3,2,1,0:T(8,128)(2,1)S(1)} %get-tuple-element.45.refs_2_), channel_id=1, source_target_pairs={{0,2},{1,3},{2,0},{3,1},{4,5},{5,4},{6,7},{7,6},{8,10},{9,11},{10,... | collective-permute-start | bytes 442376 | tf_op jit(solution)/shard_map/ppermute | solution.py:542
  26.9 5.7 %collective-permute-start.6 = (bf16[18,2,16,128]{3,2,1,0:T(8,128)(2,1)S(1)}, bf16[18,2,16,128]{3,2,1,0:T(8,128)(2,1)S(1)}, u32[]{:S(2)}, u32[]{:S(2)}) collective-permute-start(bf16[18,2,16,128]{3,2,1,0:T(8,128)(2,1)S(1)} %get-tuple-element.46.refs_1_.refs_2_), channel_id=1, source_target_pairs={{0,8},{1,9},{2,10},{3,11},{4,12},{5,13},{6,14},{7,15},{8,0},{9,1},... | collective-permute-start | bytes 442376 | tf_op jit(solution)/shard_map/ppermute | solution.py:542
  28.5 6.7 %collective-permute-start.5 = (bf16[512,128]{1,0:T(8,128)(2,1)S(1)}, bf16[512,128]{1,0:T(8,128)(2,1)S(1)}, u32[]{:S(2)}, u32[]{:S(2)}) collective-permute-start(bf16[512,128]{1,0:T(8,128)(2,1)S(1)} %get-tuple-element.48.refs_3_), channel_id=1, source_target_pairs={{0,1},{1,0},{2,3},{3,2},{4,6},{5,7},{6,4},{7,5},{8,9},{9,8},{10,11... | collective-permute-start | bytes 393224 | tf_op jit(solution)/shard_map/ppermute | solution.py:542
  30.8 6.3 %collective-permute-start.10 = (bf16[9,2,16,128]{3,2,1,0:T(8,128)(2,1)S(1)}, bf16[9,2,16,128]{3,2,1,0:T(8,128)(2,1)S(1)}, u32[]{:S(2)}, u32[]{:S(2)}) collective-permute-start(bf16[9,2,16,128]{3,2,1,0:T(8,128)(2,1)S(1)} %get-tuple-element.51.refs_2_), channel_id=1, source_target_pairs={{0,8},{1,9},{2,10},{3,11},{4,12},{5,13},{6,14},{7,15},{8,0},{9,1},... | collective-permute-start | bytes 221192 | tf_op jit(solution)/shard_map/ppermute | solution.py:542
  32.6 5.3 %collective-permute-start.9 = (bf16[18,1,16,128]{3,2,1,0:T(8,128)(2,1)S(1)}, bf16[18,1,16,128]{3,2,1,0:T(8,128)(2,1)S(1)}, u32[]{:S(2)}, u32[]{:S(2)}) collective-permute-start(bf16[18,1,16,128]{3,2,1,0:T(8,128)(2,1)S(1)} %get-tuple-element.52.refs_2_), channel_id=1, source_target_pairs={{0,16},{1,17},{2,18},{3,19},{4,20},{5,21},{6,22},{7,23},{8,24},{9,... | collective-permute-start | bytes 221192 | tf_op jit(solution)/shard_map/ppermute | solution.py:542
  35.3 6.8 %collective-permute-start.8 = (bf16[512,128]{1,0:T(8,128)(2,1)S(1)}, bf16[512,128]{1,0:T(8,128)(2,1)S(1)}, u32[]{:S(2)}, u32[]{:S(2)}) collective-permute-start(bf16[512,128]{1,0:T(8,128)(2,1)S(1)} %get-tuple-element.54.refs_3_), channel_id=1, source_target_pairs={{0,2},{1,3},{2,0},{3,1},{4,5},{5,4},{6,7},{7,6},{8,10},{9,11},{10,... | collective-permute-start | bytes 393224 | tf_op jit(solution)/shard_map/ppermute | solution.py:542
  37.1 4.9 %collective-permute-start.11 = (bf16[9,1,16,128]{3,2,1,0:T(8,128)(2,1)S(1)}, bf16[9,1,16,128]{3,2,1,0:T(8,128)(2,1)S(1)}, u32[]{:S(2)}, u32[]{:S(2)}) collective-permute-start(bf16[9,1,16,128]{3,2,1,0:T(8,128)(2,1)S(1)} %get-tuple-element.57.refs_2_), channel_id=1, source_target_pairs={{0,16},{1,17},{2,18},{3,19},{4,20},{5,21},{6,22},{7,23},{8,24},{9,... | collective-permute-start | bytes 110600 | tf_op jit(solution)/shard_map/ppermute | solution.py:542
  37.9 5.0 %collective-permute-start.12 = (bf16[18,1,16,128]{3,2,1,0:T(8,128)(2,1)S(1)}, bf16[18,1,16,128]{3,2,1,0:T(8,128)(2,1)S(1)}, u32[]{:S(2)}, u32[]{:S(2)}) collective-permute-start(bf16[18,1,16,128]{3,2,1,0:T(8,128)(2,1)S(1)} %shard_map.71.refs_2_.refs_1_), channel_id=1, source_target_pairs={{0,1},{1,0},{2,3},{3,2},{4,6},{5,7},{6,4},{7,5},{8,9},{9,8},{10,11... | collective-permute-start | bytes 221192 | tf_op jit(solution)/shard_map/ppermute | solution.py:542
  42.9 5.6 %collective-permute-start.13 = (bf16[27,16,128]{2,1,0:T(8,128)(2,1)S(1)}, bf16[27,16,128]{2,1,0:T(8,128)(2,1)S(1)}, u32[]{:S(2)}, u32[]{:S(2)}) collective-permute-start(bf16[27,16,128]{2,1,0:T(8,128)(2,1)S(1)} %shard_map.74.refs_3_.refs_0_), channel_id=1, source_target_pairs={{0,2},{1,3},{2,0},{3,1},{4,5},{5,4},{6,7},{7,6},{8,10},{9,11},{10,... | collective-permute-start | bytes 331784 | tf_op jit(solution)/shard_map/ppermute | solution.py:542
  48.5 4.4 %collective-permute-start.14 = (bf16[18,16,128]{2,1,0:T(8,128)(2,1)S(1)}, bf16[18,16,128]{2,1,0:T(8,128)(2,1)S(1)}, u32[]{:S(2)}, u32[]{:S(2)}) collective-permute-start(bf16[18,16,128]{2,1,0:T(8,128)(2,1)S(1)} %get-tuple-element.63.mine_ref), channel_id=1, source_target_pairs={{0,1},{1,0},{2,3},{3,2},{4,6},{5,7},{6,4},{7,5},{8,9},{9,8},{10,11... | collective-permute-start | bytes 221192 | tf_op jit(solution)/shard_map/ppermute | solution.py:542

commit v9 on v7

--- a/solution.py
+++ b/solution.py
@@ -14,7 +14,7 @@
 DONE = (8, 128)
 PLANE_PARTS = 1
 SPACER = 6 * 10**9
-VMEM_WHOLE = 60 * 1024 * 1024
+VMEM_WHOLE = 63 * 1024 * 1024
 
 
 def call(kernel, out_shape, scratch=(), in_specs=None, limit=VMEM_LIMIT, order=(), inputs=0, flops=1000):
@@ -177,37 +177,37 @@
     )(volume, kernel)
 
 
-def activation_kernel(space, cores, preact_ref, share_ref, cotangent_ref, grad_ref, flipped_ref):
-    cells, co = share_ref.shape
-    count = preact_ref.shape[0] // cells
-    group = co // space
-    strips = cells // 128
-    for d in range(count):
-        rows = pl.ds(d * cells, cells)
-        value = preact_ref[rows, :]
-        if d == 0:
-            value = value + share_ref[...].astype(F32)
-        sig = jax.nn.sigmoid(value)
-        slope = sig * (1.0 + value * (1.0 - sig))
-        grad_ref[rows, :] = (cotangent_ref[rows, :].astype(F32) * slope).astype(BF16)
-        flipped = (value * sig).T.astype(BF16)
-        for target in range(space):
-            place = staged_place(target, space, cores)
-            for strip in range(strips):
-                flipped_ref[place, d * strips + strip] = flipped[
-                    target * group : (target + 1) * group, strip * 128 : (strip + 1) * 128
-                ]
-
-
-def activation(preact, share, cotangent, space, cores):
-    cells, co = preact.shape
-    return call(
-        functools.partial(activation_kernel, space, cores),
+def activation_kernel(space, cores, start, preact_ref, cotangent_ref, *refs):
+    grad_ref, flipped_ref = refs[-2:]
+    share_ref = refs[0] if len(refs) == 3 else None
+    co = preact_ref.shape[1]
+    count = grad_ref.shape[0]
+    group, strips = co // space, flipped_ref.shape[1]
+    rows = pl.ds(start, count)
+    value = preact_ref[rows, :]
+    if share_ref is not None:
+        value = value + share_ref[...].astype(F32)
+    sig = jax.nn.sigmoid(value)
+    slope = sig * (1.0 + value * (1.0 - sig))
+    grad_ref[...] = (cotangent_ref[rows, :].astype(F32) * slope).astype(BF16)
+    flipped = (value * sig).T.astype(BF16)
+    for target in range(space):
+        place = staged_place(target, space, cores)
+        for strip in range(strips):
+            flipped_ref[place, strip] = flipped[
+                target * group : (target + 1) * group, strip * 128 : (strip + 1) * 128
+            ]
+
+
+def activation(preact, cotangent, share, start, count, space, cores):
+    co = preact.shape[1]
+    return call(
+        functools.partial(activation_kernel, space, cores, start),
         (
-            jax.ShapeDtypeStruct((cells, co), BF16),
-            jax.ShapeDtypeStruct((space, cells // 128, co // space, 128), BF16),
+            jax.ShapeDtypeStruct((count, co), BF16),
+            jax.ShapeDtypeStruct((space, count // 128, co // space, 128), BF16),
         ),
-    )(preact, share, cotangent)
+    )(preact, cotangent, *(() if share is None else (share,)))
 
 
 def switched_kernel(space, cores, came, kept_ref, got_ref, out_ref, done_ref):
@@ -271,7 +271,7 @@
     sent_ref[...] = keep_ref[:, 1 - side(*then, cores)].reshape(sent_ref.shape).astype(BF16)
 
 
-def add_stage(value, got, now, then, cores, order=()):
+def add_stage(value, got, now, then, cores, order=(), flops=1000):
     shape = (sum(piece.shape[0] for piece in got),) + got[0].shape[1:]
     if then is None:
         outs = jax.ShapeDtypeStruct(shape, BF16)
@@ -285,6 +285,7 @@
         outs,
         order=order,
         inputs=1 + len(got),
+        flops=flops,
     )(value, *got, *order)
 
 
@@ -424,64 +425,88 @@
                 put(kw * halves + half, chip, keep, send)
 
 
-def kernel_grad_kernel(kds, cores, chips, scale, parts, even_ref, odd_ref, grads_ref, *refs):
-    above_ref = refs[0] if 0 in kds else None
-    keep_ref, send_refs = refs[-1 - parts], refs[-parts:]
-    size = send_refs[0].shape[0]
+def tap_products(even_ref, odd_ref, planes, rhs, put):
+    for kh in range(3):
+        lhs = [tap_rows(even_ref, odd_ref, plane, kh) for plane in planes]
+        put(
+            kh,
+            lax.dot_general(
+                jnp.concatenate(lhs, axis=0), rhs, (((0,), (0,)), ((), ())), preferred_element_type=F32
+            ),
+        )
+
+
+def ahead_kernel(even_ref, odd_ref, rest_ref, out_ref):
     outs = even_ref.shape[0] // 2
-    cells = even_ref.shape[1] * even_ref.shape[2]
+    for place, kd in enumerate((1, 2)):
+        planes = [2 * d - 1 + kd for d in range(1, outs)]
+
+        def put(kh, product, base=3 * place):
+            out_ref[base + kh] = product
+
+        tap_products(even_ref, odd_ref, planes, rest_ref[...], put)
+
+
+def early_ahead(even, odd, rest):
+    return call(
+        ahead_kernel, jax.ShapeDtypeStruct((6, even.shape[-1], rest.shape[-1]), F32)
+    )(even, odd, rest)
+
+
+def kernel_grad_kernel(early, cores, chips, scale, even_ref, odd_ref, grads_ref, other_ref, keep_ref, send_ref):
+    outs = even_ref.shape[0] // 2
     core = lax.axis_index("dp") % cores
     per_row = 3 * (grads_ref.shape[1] // 128)
+    kds = (1, 2) if early else (0,)
     for unit in range(len(kds) * 3 * per_row, keep_ref.shape[0]):
         keep_ref[unit] = jnp.zeros(keep_ref.shape[1:], F32)
-        send_refs[unit // size][unit % size] = jnp.zeros(keep_ref.shape[1:], BF16)
+        send_ref[unit] = jnp.zeros(keep_ref.shape[1:], BF16)
     for place, kd in enumerate(kds):
-        if kd == 0:
+        if early:
+            planes, rhs = [kd - 1], grads_ref[...]
+        else:
             planes = [2 * d - 1 for d in range(1, outs + 1)]
-            rhs = [grads_ref[pl.ds(d * cells, cells), :] for d in range(1, outs)] + [above_ref[...]]
-            rhs = jnp.concatenate(rhs, axis=0)
-        else:
-            planes = [2 * d - 1 + kd for d in range(outs)]
-            rhs = grads_ref[...]
-        for kh in range(3):
-            lhs = [tap_rows(even_ref, odd_ref, plane, kh) for plane in planes]
-            product = lax.dot_general(
-                jnp.concatenate(lhs, axis=0), rhs, (((0,), (0,)), ((), ())), preferred_element_type=F32
-            )
-
-            def put(unit, chip, keep, send, base=(place * 3 + kh) * per_row):
-                keep_ref[base + unit, chip] = keep
-                send_refs[(base + unit) // size][(base + unit) % size, chip] = send.astype(BF16)
+            rhs = jnp.concatenate([grads_ref[...], other_ref[...]], axis=0)
+
+        def take(kh, product, base=3 * place):
+            if early:
+                product = product + other_ref[base + kh]
+
+            def put(unit, chip, keep, send):
+                keep_ref[(base + kh) * per_row + unit, chip] = keep
+                send_ref[(base + kh) * per_row + unit, chip] = send.astype(BF16)
 
             store_units(product, scale, core, cores, chips, put)
 
-
-def kernel_grad_part(even, odd, grads, above, kds, cores, chips, scale, multiple, parts=1, order=()):
+        tap_products(even_ref, odd_ref, planes, rhs, take)
+
+
+def kernel_grad_part(even, odd, grads, other, early, cores, chips, scale, multiple, order=()):
     chans = even.shape[-1] // 3
-    co = grads.shape[-1]
-    units = len(kds) * 9 * (co // 128)
-    units += -units % math.lcm(multiple, parts)
+    units = (18 if early else 9) * (grads.shape[-1] // 128)
+    units += -units % multiple
     shape = (units, chips, chans // (cores * chips), 128)
-    operands = (even, odd, grads) + ((above,) if 0 in kds else ())
-    return call(
-        functools.partial(kernel_grad_kernel, kds, cores, chips, scale, parts),
-        (jax.ShapeDtypeStruct(shape, F32),)
-        + (jax.ShapeDtypeStruct((units // parts,) + shape[1:], BF16),) * parts,
-        order=order,
-        inputs=len(operands),
-    )(*operands, *order)
-
-
-def volume_grad_kernel(grads_ref, above_ref, kernel_ref, out_ref, done_ref, shifted, wide):
+    return call(
+        functools.partial(kernel_grad_kernel, early, cores, chips, scale),
+        (jax.ShapeDtypeStruct(shape, F32), jax.ShapeDtypeStruct(shape, BF16)),
+        order=order,
+        inputs=4,
+    )(even, odd, grads, other, *order)
+
+
+def volume_grad_kernel(first_ref, rest_ref, above_ref, kernel_ref, out_ref, done_ref, shifted, wide):
     done_ref[...] = jnp.zeros_like(done_ref)
     planes, h2, _, width, chans = out_ref.shape
     w2 = width // 2
     cells = h2 * w2
     outs = planes // 2
-    co = grads_ref.shape[1]
+    co = first_ref.shape[1]
     here, right = [], []
     for d in range(outs + 1):
-        plane = grads_ref[pl.ds(d * cells, cells), :] if d < outs else above_ref[...]
+        if 0 < d < outs:
+            plane = rest_ref[pl.ds((d - 1) * cells, cells), :]
+        else:
+            plane = (first_ref if d == 0 else above_ref)[...]
         shifted[pl.ds(0, cells), :] = plane.astype(F32)
         moved = shifted[pl.ds(1, cells), :]
         column = lax.broadcasted_iota(jnp.int32, moved.shape, 0) % w2
@@ -513,8 +538,8 @@
             out_ref[plane, :, odd_row] = wide[...].reshape(h2, width, chans).astype(BF16)
 
 
-def volume_grad_of(grads, above, kernel, height, width, order=()):
-    cells, co = grads.shape
+def volume_grad_of(first, rest, above, kernel, height, width, order=()):
+    cells, co = first.shape[0] + rest.shape[0], first.shape[1]
     chans = kernel.shape[3]
     planes = 2 * cells * 4 // (height * width)
     shape = (planes, height // 2, 2, width, chans)
@@ -526,8 +551,8 @@
             pltpu.VMEM((height * width // 2, chans), F32),
         ],
         order=order,
-        inputs=3,
-    )(grads, above, kernel, *order)
+        inputs=4,
+    )(first, rest, above, kernel, *order)
 
 
 def exchange(value, partner):
@@ -584,10 +609,14 @@
 
     share = neighbour(halo_share(volume, kernel), 1)
     preact, even, odd = partial_preact(volume, kernel)
-    grads, flipped = activation(preact, share, cotangent.reshape(outs * cells, co), space, cores)
-    above = neighbour(grads[:cells], -1)
-
-    early = kernel_grad_part(even, odd, grads, None, (1, 2), cores, chips, scale, space)
+    cotangent = cotangent.reshape(outs * cells, co)
+    rest, flipped_rest = activation(preact, cotangent, None, cells, (outs - 1) * cells, space, cores)
+    products = early_ahead(even, odd, rest)
+    first, flipped = activation(preact, cotangent, share, 0, cells, space, cores)
+    flipped = jnp.concatenate([flipped, flipped_rest], axis=1)
+    above = neighbour(first, -1)
+
+    early = kernel_grad_part(even, odd, first, products, True, cores, chips, scale, space)
     early_units, late_units = 18 * (co // 128), 9 * (co // 128)
     plan = over_space + over_chips
     value, sent = add_cores(early[0], early[1:], plan[0], cores)
@@ -598,7 +627,7 @@
         got = exchange_stage(sent, *now, cores)
         tokens = [sent]
         if place == 0:
-            late = kernel_grad_part(even, odd, grads, above, (0,), cores, chips, scale, 1, 1, (sent,))
+            late = kernel_grad_part(even, odd, rest, above, False, cores, chips, scale, 1, (sent,))
             tokens.append(late[1])
         elif late_half is None:
             then = late_plan.pop(0) if late_plan else None
@@ -620,7 +649,10 @@
             moved = exchange_space(out, stage, cores)
             tokens.append(out)
         if place + 1 < len(plan):
-            value, sent = add_stage(value, (got,), now, plan[place + 1], cores, tuple(tokens[1:]))
+            weight = SPACER if place >= len(over_space) else 1000
+            value, sent = add_stage(
+                value, (got,), now, plan[place + 1], cores, tuple(tokens[1:]), weight
+            )
     for stage in range(len(over_space) - len(switch_at), len(over_space)):
         stay, out = switch_stage(stay, moved, 0, None, stage, cores, (sent,))
         moved = exchange_space(out, stage, cores)
@@ -638,7 +670,7 @@
             order = (done,)
         if step + 1 < len(over_space):
             mine = gather_stage(mine, got, early_rows << step, order)
-    volume_grad, done = volume_grad_of(grads, above, kernel, height, width, (mine,))
+    volume_grad, done = volume_grad_of(first, rest, above, kernel, height, width, (mine,))
     kernel_grad = kernel_grad_out(mine, got, early_units, late_units, space, cores, co, (done,))
 
     return (

time: 53.6 us -> 51.9 us (0.968)
  local copies, waits for them, and re-layouts: 0.03 us -> 2.7 us
  waiting for transfers between devices: 17.4 us -> 14.8 us
  starting transfers between devices: 24.9 us -> 22.9 us
    unnamed x6 -> x8, local copies, waits for them, and re-layouts: 0.01 us -> 2.7 us
    ppermute x2, waiting for transfers between devices: 5.49 us -> 3.59 us  [neighbour(): lax.ppermute(value, 'space', [(source, source + steps) for source in rang...]
    ppermute x12, starting transfers between devices: 18.6 us -> 16.7 us  [exchange(): return lax.ppermute(value, ('dp', 'space'), pairs)]
    ppermute x12, waiting for transfers between devices: 12 us -> 11.2 us  [exchange(): return lax.ppermute(value, ('dp', 'space'), pairs)]
    pallas_call x3 -> x5, Pallas kernels: 1.62 us -> 1.91 us  [the longest x2 1.04 us: kernel_grad_part(): call(functools.partial(kernel_grad_kernel, early, cores, chips, scale), (...]
  transfers between devices with their start and end apart: 14 -> 14, of which waited for: 10 -> 8; matrix products, arithmetic and copies ran while one was open for 0% -> 0% of each run, Pallas kernels for 11% -> 13%
where the time goes in v9:
time: 51.9 us; the launch traced here: 51.7 us
  starting transfers between devices  22.9 us (44%)
  waiting for transfers between devices  14.8 us (29%)
  Pallas kernels  10.4 us (20%)
  local copies, waits for them, and re-layouts  2.7 us (5%)
  between operations  0.8 us (2%)
    ppermute x12, starting transfers between devices, exchange(): return lax.ppermute(value, ('dp', 'space'), pairs)  16.7 us
    ppermute x12, waiting for transfers between devices, exchange(): return lax.ppermute(value, ('dp', 'space'), pairs)  11.2 us
    ppermute x2, starting transfers between devices, neighbour(): lax.ppermute(value, 'space', [(source, source + steps) for source in rang...  6.14 us
    ppermute x2, waiting for transfers between devices, neighbour(): lax.ppermute(value, 'space', [(source, source + steps) for source in rang...  3.59 us
    unnamed x8, local copies, waits for them, and re-layouts  2.7 us
    pallas_call x1, Pallas kernels, volume_grad_of(): call(volume_grad_kernel, (jax.ShapeDtypeStruct(shape, BF16), jax.ShapeDty...  2.63 us
    pallas_call x1, Pallas kernels, halo_share(): call(halo_kernel, jax.ShapeDtypeStruct((height * width // 4, co), BF16),...  2.33 us
    pallas_call x1, Pallas kernels, partial_preact(): call(preact_kernel, (jax.ShapeDtypeStruct((planes // 2 * cells, co), F32)...  1.38 us
  transfers between devices with their start and end apart: 14, of which 8 were waited for; matrix products, arithmetic and copies ran while one was open for 0% of the time, Pallas kernels for 13%

profile of v9, /device:TPU:0, one launch (start us, length us, event | category | flops | bytes accessed | tf_op | source)
XLA Modules:
  0.0 51.7 jit_solution(7737409509292289721)
XLA Ops:
  0.6 2.3 %shard_map.59 = bf16[256,256]{1,0:T(8,128)(2,1)} custom-call(bf16[1,4,32,32,128]{4,3,2,1,0:T(8,128)(2,1)} %volume_ref.3, bf16[3,3,3,128,256]{4,3,2,1,0:T(8,128)(2,1)} %refs_3_.1), custom_call_target="tpu_custom_call" | custom-call | flops 1000 | bytes 1000 | tf_op jit(solution)/shard_map/pallas_call | solution.py:123
  3.0 4.8 %collective-permute-start = (bf16[256,256]{1,0:T(8,128)(2,1)}, bf16[256,256]{1,0:T(8,128)(2,1)S(1)}, u32[]{:S(2)}, u32[]{:S(2)}) collective-permute-start(bf16[256,256]{1,0:T(8,128)(2,1)} %shard_map.59), channel_id=1, source_target_pairs={{0,1},{1,2},{2,3},{4,5},{5,6},{6,7},{8,9},{9,10},{10,11},{12,13},{... | collective-permute-start | bytes 393224 | tf_op jit(solution)/shard_map/ppermute | solution.py:585
  7.8 1.5 %copy-done = bf16[3,3,3,128,256]{4,3,2,1,0:T(8,128)(2,1)S(1)} copy-done((bf16[3,3,3,128,256]{4,3,2,1,0:T(8,128)(2,1)S(1)}, bf16[3,3,3,128,256]{4,3,2,1,0:T(8,128)(2,1)}, u32[]{:S(2)}) %copy-start) | copy-done | bytes 1769496
  9.3 1.2 %copy-done.2 = bf16[1,4,32,32,128]{4,3,2,1,0:T(8,128)(2,1)S(1)} copy-done((bf16[1,4,32,32,128]{4,3,2,1,0:T(8,128)(2,1)S(1)}, bf16[1,4,32,32,128]{4,3,2,1,0:T(8,128)(2,1)}, u32[]{:S(2)}) %copy-start.2) | copy-done | bytes 1048600
  10.5 1.4 %shard_map.58 = (f32[512,256]{1,0:T(8,128)S(1)}, bf16[4,16,16,384]{3,2,1,0:T(8,128)(2,1)S(1)}, bf16[4,17,16,384]{3,2,1,0:T(8,128)(2,1)S(1)}) custom-call(bf16[1,4,32,32,128]{4,3,2,1,0:T(8,128)(2,1)S(1)} %copy-done.2, bf16[3,3,3,128,256]{4,3,2,1,0:T(8,128)(2,1)S(1)} %copy-done), custom_call_target="tpu_custom_call" | custom-call | flops 1000 | bytes 1000 | tf_op jit(solution)/shard_map/pallas_call | solution.py:169
  11.9 0.2 shard_map.61
  12.1 0.5 %shard_map.62.other_ref = f32[6,384,256]{2,1,0:T(8,128)S(1)} custom-call(bf16[4,16,16,384]{3,2,1,0:T(8,128)(2,1)S(1)} %get-tuple-element.37.even_ref.refs_0_, bf16[4,17,16,384]{3,2,1,0:T(8,128)(2,1)S(1)} %get-tuple-element.38.odd_ref.refs_1_, bf16[256,256]{1,0:T(8,128)(2,1)S(1)} %get-tuple-element.39.rest_ref.refs_2_.refs_1_), custom_call_target="tpu_custom_call" | custom-call | flops 1000 | bytes 1000 | tf_op jit(solution)/shard_map/pallas_call | solution.py:451
  12.6 0.2 shard_map.60
  12.8 0.5 %shard_map.63 = (f32[36,4,16,128]{3,2,1,0:T(8,128)S(1)}, bf16[36,4,16,128]{3,2,1,0:T(8,128)(2,1)S(1)}) custom-call(bf16[4,16,16,384]{3,2,1,0:T(8,128)(2,1)S(1)} %get-tuple-element.37.even_ref.refs_0_, bf16[4,17,16,384]{3,2,1,0:T(8,128)(2,1)S(1)} %get-tuple-element.38.odd_ref.refs_1_, bf16[256,256]{1,0:T(8,128)(2,1)S(1)} %get-tuple-element.40.grads_ref.refs_0_, ...), custom_call_target="tpu_custom_call" | custom-call | flops 1000 | bytes 1000 | tf_op jit(solution)/shard_map/pallas_call | solution.py:489
  13.4 1.3 %collective-permute-start.1 = (bf16[256,256]{1,0:T(8,128)(2,1)S(1)}, bf16[256,256]{1,0:T(8,128)(2,1)S(1)}, u32[]{:S(2)}, u32[]{:S(2)}) collective-permute-start(bf16[256,256]{1,0:T(8,128)(2,1)S(1)} %get-tuple-element.40.grads_ref.refs_0_), channel_id=1, source_target_pairs={{1,0},{2,1},{3,2},{5,4},{6,5},{7,6},{9,8},{10,9},{11,10},{13,12},{... | collective-permute-start | bytes 393224 | tf_op jit(solution)/shard_map/ppermute | solution.py:585
  14.7 0.7 %collective-permute-done.2.refs_0_ = bf16[36,4,16,128]{3,2,1,0:T(8,128)(2,1)S(1)} collective-permute-done((bf16[36,4,16,128]{3,2,1,0:T(8,128)(2,1)S(1)}, bf16[36,4,16,128]{3,2,1,0:T(8,128)(2,1)S(1)}, u32[]{:S(2)}, u32[]{:S(2)}) %collective-permute-start.2) | collective-permute-done | bytes 589856 | tf_op jit(solution)/shard_map/ppermute | solution.py:565
  15.6 2.0 %collective-permute-start.4 = (bf16[18,4,16,128]{3,2,1,0:T(8,128)(2,1)S(1)}, bf16[18,4,16,128]{3,2,1,0:T(8,128)(2,1)S(1)}, u32[]{:S(2)}, u32[]{:S(2)}) collective-permute-start(bf16[18,4,16,128]{3,2,1,0:T(8,128)(2,1)S(1)} %get-tuple-element.43.refs_4_), channel_id=1, source_target_pairs={{0,1},{1,0},{2,3},{3,2},{4,6},{5,7},{6,4},{7,5},{8,9},{9,8},{10,11... | collective-permute-start | bytes 884744 | tf_op jit(solution)/shard_map/ppermute | solution.py:565
  17.6 3.6 %collective-permute-done.1.refs_3_.refs_2_ = bf16[256,256]{1,0:T(8,128)(2,1)S(1)} collective-permute-done((bf16[256,256]{1,0:T(8,128)(2,1)S(1)}, bf16[256,256]{1,0:T(8,128)(2,1)S(1)}, u32[]{:S(2)}, u32[]{:S(2)}) %collective-permute-start.1) | collective-permute-done | bytes 131104 | tf_op jit(solution)/shard_map/ppermute | solution.py:585
  21.2 0.5 %shard_map.65 = (f32[18,4,16,128]{3,2,1,0:T(8,128)S(1)}, bf16[18,4,16,128]{3,2,1,0:T(8,128)(2,1)S(1)}) custom-call(bf16[4,16,16,384]{3,2,1,0:T(8,128)(2,1)S(1)} %get-tuple-element.37.even_ref.refs_0_, bf16[4,17,16,384]{3,2,1,0:T(8,128)(2,1)S(1)} %get-tuple-element.38.odd_ref.refs_1_, bf16[256,256]{1,0:T(8,128)(2,1)S(1)} %get-tuple-element.39.rest_ref.refs_2_.refs_1_, ...), custom_call_target="tpu_custom_call" | custom-call | flops 1000 | bytes 1000 | tf_op jit(solution)/shard_map/pallas_call | solution.py:489
  21.8 2.6 %collective-permute-done.4.refs_1_ = bf16[18,4,16,128]{3,2,1,0:T(8,128)(2,1)S(1)} collective-permute-done((bf16[18,4,16,128]{3,2,1,0:T(8,128)(2,1)S(1)}, bf16[18,4,16,128]{3,2,1,0:T(8,128)(2,1)S(1)}, u32[]{:S(2)}, u32[]{:S(2)}) %collective-permute-start.4) | collective-permute-done | bytes 294944 | tf_op jit(solution)/shard_map/ppermute | solution.py:565
  24.4 1.6 %collective-permute-start.6 = (bf16[9,4,16,128]{3,2,1,0:T(8,128)(2,1)S(1)}, bf16[9,4,16,128]{3,2,1,0:T(8,128)(2,1)S(1)}, u32[]{:S(2)}, u32[]{:S(2)}) collective-permute-start(bf16[9,4,16,128]{3,2,1,0:T(8,128)(2,1)S(1)} %get-tuple-element.47.refs_2_), channel_id=1, source_target_pairs={{0,2},{1,3},{2,0},{3,1},{4,5},{5,4},{6,7},{7,6},{8,10},{9,11},{10,... | collective-permute-start | bytes 442376 | tf_op jit(solution)/shard_map/ppermute | solution.py:565
  26.1 1.6 %collective-permute-start.8 = (bf16[18,2,16,128]{3,2,1,0:T(8,128)(2,1)S(1)}, bf16[18,2,16,128]{3,2,1,0:T(8,128)(2,1)S(1)}, u32[]{:S(2)}, u32[]{:S(2)}) collective-permute-start(bf16[18,2,16,128]{3,2,1,0:T(8,128)(2,1)S(1)} %get-tuple-element.48.refs_1_.refs_2_), channel_id=1, source_target_pairs={{0,8},{1,9},{2,10},{3,11},{4,12},{5,13},{6,14},{7,15},{8,0},{9,1},... | collective-permute-start | bytes 442376 | tf_op jit(solution)/shard_map/ppermute | solution.py:565
  27.9 1.8 %collective-permute-done.6.refs_1_ = bf16[9,4,16,128]{3,2,1,0:T(8,128)(2,1)S(1)} collective-permute-done((bf16[9,4,16,128]{3,2,1,0:T(8,128)(2,1)S(1)}, bf16[9,4,16,128]{3,2,1,0:T(8,128)(2,1)S(1)}, u32[]{:S(2)}, u32[]{:S(2)}) %collective-permute-start.6) | collective-permute-done | bytes 147488 | tf_op jit(solution)/shard_map/ppermute | solution.py:565
  29.7 1.6 %collective-permute-start.7 = (bf16[9,2,16,128]{3,2,1,0:T(8,128)(2,1)S(1)}, bf16[9,2,16,128]{3,2,1,0:T(8,128)(2,1)S(1)}, u32[]{:S(2)}, u32[]{:S(2)}) collective-permute-start(bf16[9,2,16,128]{3,2,1,0:T(8,128)(2,1)S(1)} %get-tuple-element.53.refs_2_), channel_id=1, source_target_pairs={{0,8},{1,9},{2,10},{3,11},{4,12},{5,13},{6,14},{7,15},{8,0},{9,1},... | collective-permute-start | bytes 221192 | tf_op jit(solution)/shard_map/ppermute | solution.py:565
  31.3 1.0 %collective-permute-start.5 = (bf16[512,128]{1,0:T(8,128)(2,1)S(1)}, bf16[512,128]{1,0:T(8,128)(2,1)S(1)}, u32[]{:S(2)}, u32[]{:S(2)}) collective-permute-start(bf16[512,128]{1,0:T(8,128)(2,1)S(1)} %get-tuple-element.50.refs_3_), channel_id=1, source_target_pairs={{0,1},{1,0},{2,3},{3,2},{4,6},{5,7},{6,4},{7,5},{8,9},{9,8},{10,11... | collective-permute-start | bytes 393224 | tf_op jit(solution)/shard_map/ppermute | solution.py:565
  32.4 2.7 %collective-permute-start.11 = (bf16[18,1,16,128]{3,2,1,0:T(8,128)(2,1)S(1)}, bf16[18,1,16,128]{3,2,1,0:T(8,128)(2,1)S(1)}, u32[]{:S(2)}, u32[]{:S(2)}) collective-permute-start(bf16[18,1,16,128]{3,2,1,0:T(8,128)(2,1)S(1)} %get-tuple-element.55.refs_2_), channel_id=1, source_target_pairs={{0,16},{1,17},{2,18},{3,19},{4,20},{5,21},{6,22},{7,23},{8,24},{9,... | collective-permute-start | bytes 221192 | tf_op jit(solution)/shard_map/ppermute | solution.py:565
  35.1 2.2 %collective-permute-start.10 = (bf16[9,1,16,128]{3,2,1,0:T(8,128)(2,1)S(1)}, bf16[9,1,16,128]{3,2,1,0:T(8,128)(2,1)S(1)}, u32[]{:S(2)}, u32[]{:S(2)}) collective-permute-start(bf16[9,1,16,128]{3,2,1,0:T(8,128)(2,1)S(1)} %get-tuple-element.56.refs_2_), channel_id=1, source_target_pairs={{0,16},{1,17},{2,18},{3,19},{4,20},{5,21},{6,22},{7,23},{8,24},{9,... | collective-permute-start | bytes 110600 | tf_op jit(solution)/shard_map/ppermute | solution.py:565
  37.3 1.1 %collective-permute-start.9 = (bf16[512,128]{1,0:T(8,128)(2,1)S(1)}, bf16[512,128]{1,0:T(8,128)(2,1)S(1)}, u32[]{:S(2)}, u32[]{:S(2)}) collective-permute-start(bf16[512,128]{1,0:T(8,128)(2,1)S(1)} %get-tuple-element.58.refs_3_), channel_id=1, source_target_pairs={{0,2},{1,3},{2,0},{3,1},{4,5},{5,4},{6,7},{7,6},{8,10},{9,11},{10,... | collective-permute-start | bytes 393224 | tf_op jit(solution)/shard_map/ppermute | solution.py:565
  38.4 0.9 %collective-permute-done.11.refs_1_ = bf16[18,1,16,128]{3,2,1,0:T(8,128)(2,1)S(1)} collective-permute-done((bf16[18,1,16,128]{3,2,1,0:T(8,128)(2,1)S(1)}, bf16[18,1,16,128]{3,2,1,0:T(8,128)(2,1)S(1)}, u32[]{:S(2)}, u32[]{:S(2)}) %collective-permute-start.11) | collective-permute-done | bytes 73760 | tf_op jit(solution)/shard_map/ppermute | solution.py:565
  39.3 0.7 %collective-permute-done.10.refs_1_ = bf16[9,1,16,128]{3,2,1,0:T(8,128)(2,1)S(1)} collective-permute-done((bf16[9,1,16,128]{3,2,1,0:T(8,128)(2,1)S(1)}, bf16[9,1,16,128]{3,2,1,0:T(8,128)(2,1)S(1)}, u32[]{:S(2)}, u32[]{:S(2)}) %collective-permute-start.10) | collective-permute-done | bytes 36896 | tf_op jit(solution)/shard_map/ppermute | solution.py:565
  40.0 2.4 %collective-permute-start.12 = (bf16[27,16,128]{2,1,0:T(8,128)(2,1)S(1)}, bf16[27,16,128]{2,1,0:T(8,128)(2,1)S(1)}, u32[]{:S(2)}, u32[]{:S(2)}) collective-permute-start(bf16[27,16,128]{2,1,0:T(8,128)(2,1)S(1)} %shard_map.74.refs_2_.refs_0_), channel_id=1, source_target_pairs={{0,2},{1,3},{2,0},{3,1},{4,5},{5,4},{6,7},{7,6},{8,10},{9,11},{10,... | collective-permute-start | bytes 331784 | tf_op jit(solution)/shard_map/ppermute | solution.py:565
  42.4 0.8 %shard_map.75 = (bf16[64,2048]{1,0:T(8,128)(2,1)}, f32[8,128]{1,0:T(8,128)S(1)}) custom-call(bf16[8,64,128]{2,1,0:T(8,128)(2,1)S(1)} %bitcast.10, bf16[512,128]{1,0:T(8,128)(2,1)S(1)} %collective-permute-done.9.refs_1_, bf16[27,16,128]{2,1,0:T(8,128)(2,1)S(1)} %shard_map.74.refs_2_.refs_0_), custom_call_target="tpu_custom_call" | custom-call | flops 1000 | bytes 1000 | tf_op jit(solution)/shard_map/pallas_call | solution.py:231
  43.2 2.4 %collective-permute-done.12.refs_1_ = bf16[27,16,128]{2,1,0:T(8,128)(2,1)S(1)} collective-permute-done((bf16[27,16,128]{2,1,0:T(8,128)(2,1)S(1)}, bf16[27,16,128]{2,1,0:T(8,128)(2,1)S(1)}, u32[]{:S(2)}, u32[]{:S(2)}) %collective-permute-start.12) | collective-permute-done | bytes 110624 | tf_op jit(solution)/shard_map/ppermute | solution.py:565
  45.6 0.4 collective-permute-start.13
  46.0 2.6 %shard_map.77 = (bf16[4,16,2,32,128]{4,3,2,1,0:T(8,128)(2,1)}, f32[8,128]{1,0:T(8,128)S(1)}) custom-call(bf16[256,256]{1,0:T(8,128)(2,1)S(1)} %get-tuple-element.40.grads_ref.refs_0_, bf16[256,256]{1,0:T(8,128)(2,1)S(1)} %get-tuple-element.39.rest_ref.refs_2_.refs_1_, bf16[256,256]{1,0:T(8,128)(2,1)S(1)} %collective-permute-done.1.refs_3_.refs_2_, ...), custom_call_target="tpu_custom_call" | custom-call | flops 1000 | bytes 1000 | tf_op jit(solution)/shard_map/pallas_call | solution.py:546
  48.6 2.2 %collective-permute-done.13.refs_1_ = bf16[36,16,128]{2,1,0:T(8,128)(2,1)S(1)} collective-permute-done((bf16[36,16,128]{2,1,0:T(8,128)(2,1)S(1)}, bf16[36,16,128]{2,1,0:T(8,128)(2,1)S(1)}, u32[]{:S(2)}, u32[]{:S(2)}) %collective-permute-start.13) | collective-permute-done | bytes 147488 | tf_op jit(solution)/shard_map/ppermute | solution.py:565
  50.8 0.8 %shard_map.78 = f32[27,16,256]{2,1,0:T(8,128)} custom-call(bf16[36,16,128]{2,1,0:T(8,128)(2,1)S(1)} %shard_map.76.refs_4_.refs_0_, bf16[36,16,128]{2,1,0:T(8,128)(2,1)S(1)} %collective-permute-done.13.refs_1_, f32[8,128]{1,0:T(8,128)S(1)} %get-tuple-element.64.refs_2_), custom_call_target="tpu_custom_call" | custom-call | flops 1000 | bytes 1000 | tf_op jit(solution)/shard_map/pallas_call | solution.py:402
  (26 shorter events, 0.8 us)
Async XLA Ops:
  3.0 9.7 %collective-permute-start = (bf16[256,256]{1,0:T(8,128)(2,1)}, bf16[256,256]{1,0:T(8,128)(2,1)S(1)}, u32[]{:S(2)}, u32[]{:S(2)}) collective-permute-start(bf16[256,256]{1,0:T(8,128)(2,1)} %shard_map.59), channel_id=1, source_target_pairs={{0,1},{1,2},{2,3},{4,5},{5,6},{6,7},{8,9},{9,10},{10,11},{12,13},{... | collective-permute-start | bytes 393224 | tf_op jit(solution)/shard_map/ppermute | solution.py:585
  7.8 1.5 %copy-start = (bf16[3,3,3,128,256]{4,3,2,1,0:T(8,128)(2,1)S(1)}, bf16[3,3,3,128,256]{4,3,2,1,0:T(8,128)(2,1)}, u32[]{:S(2)}) copy-start(bf16[3,3,3,128,256]{4,3,2,1,0:T(8,128)(2,1)} %refs_3_.1) | copy-start | bytes 5308420
  9.3 1.2 %copy-start.2 = (bf16[1,4,32,32,128]{4,3,2,1,0:T(8,128)(2,1)S(1)}, bf16[1,4,32,32,128]{4,3,2,1,0:T(8,128)(2,1)}, u32[]{:S(2)}) copy-start(bf16[1,4,32,32,128]{4,3,2,1,0:T(8,128)(2,1)} %volume_ref.3) | copy-start | bytes 3145732
  10.5 1.4 %copy-start.3 = (bf16[1,2,16,16,256]{4,3,2,1,0:T(8,128)(2,1)S(1)}, bf16[1,2,16,16,256]{4,3,2,1,0:T(8,128)(2,1)}, u32[]{:S(2)}) copy-start(bf16[1,2,16,16,256]{4,3,2,1,0:T(8,128)(2,1)} %param.5) | copy-start | bytes 786436
  13.3 2.1 %collective-permute-start.2 = (bf16[36,4,16,128]{3,2,1,0:T(8,128)(2,1)S(1)}, bf16[36,4,16,128]{3,2,1,0:T(8,128)(2,1)S(1)}, u32[]{:S(2)}, u32[]{:S(2)}) collective-permute-start(bf16[36,4,16,128]{3,2,1,0:T(8,128)(2,1)S(1)} %get-tuple-element.42), channel_id=1, source_target_pairs={{0,4},{1,5},{2,6},{3,7},{4,0},{5,1},{6,2},{7,3},{8,12},{9,13},{10,... | collective-permute-start | bytes 1769480 | tf_op jit(solution)/shard_map/ppermute | solution.py:565
  13.4 7.8 %collective-permute-start.1 = (bf16[256,256]{1,0:T(8,128)(2,1)S(1)}, bf16[256,256]{1,0:T(8,128)(2,1)S(1)}, u32[]{:S(2)}, u32[]{:S(2)}) collective-permute-start(bf16[256,256]{1,0:T(8,128)(2,1)S(1)} %get-tuple-element.40.grads_ref.refs_0_), channel_id=1, source_target_pairs={{1,0},{2,1},{3,2},{5,4},{6,5},{7,6},{9,8},{10,9},{11,10},{13,12},{... | collective-permute-start | bytes 393224 | tf_op jit(solution)/shard_map/ppermute | solution.py:585
  15.6 8.8 %collective-permute-start.4 = (bf16[18,4,16,128]{3,2,1,0:T(8,128)(2,1)S(1)}, bf16[18,4,16,128]{3,2,1,0:T(8,128)(2,1)S(1)}, u32[]{:S(2)}, u32[]{:S(2)}) collective-permute-start(bf16[18,4,16,128]{3,2,1,0:T(8,128)(2,1)S(1)} %get-tuple-element.43.refs_4_), channel_id=1, source_target_pairs={{0,1},{1,0},{2,3},{3,2},{4,6},{5,7},{6,4},{7,5},{8,9},{9,8},{10,11... | collective-permute-start | bytes 884744 | tf_op jit(solution)/shard_map/ppermute | solution.py:565
  21.7 4.3 %collective-permute-start.3 = (bf16[18,4,16,128]{3,2,1,0:T(8,128)(2,1)S(1)}, bf16[18,4,16,128]{3,2,1,0:T(8,128)(2,1)S(1)}, u32[]{:S(2)}, u32[]{:S(2)}) collective-permute-start(bf16[18,4,16,128]{3,2,1,0:T(8,128)(2,1)S(1)} %get-tuple-element.45.refs_2_), channel_id=1, source_target_pairs={{0,4},{1,5},{2,6},{3,7},{4,0},{5,1},{6,2},{7,3},{8,12},{9,13},{10,... | collective-permute-start | bytes 884744 | tf_op jit(solution)/shard_map/ppermute | solution.py:565
  24.4 5.2 %collective-permute-start.6 = (bf16[9,4,16,128]{3,2,1,0:T(8,128)(2,1)S(1)}, bf16[9,4,16,128]{3,2,1,0:T(8,128)(2,1)S(1)}, u32[]{:S(2)}, u32[]{:S(2)}) collective-permute-start(bf16[9,4,16,128]{3,2,1,0:T(8,128)(2,1)S(1)} %get-tuple-element.47.refs_2_), channel_id=1, source_target_pairs={{0,2},{1,3},{2,0},{3,1},{4,5},{5,4},{6,7},{7,6},{8,10},{9,11},{10,... | collective-permute-start | bytes 442376 | tf_op jit(solution)/shard_map/ppermute | solution.py:565
  26.1 6.2 %collective-permute-start.8 = (bf16[18,2,16,128]{3,2,1,0:T(8,128)(2,1)S(1)}, bf16[18,2,16,128]{3,2,1,0:T(8,128)(2,1)S(1)}, u32[]{:S(2)}, u32[]{:S(2)}) collective-permute-start(bf16[18,2,16,128]{3,2,1,0:T(8,128)(2,1)S(1)} %get-tuple-element.48.refs_1_.refs_2_), channel_id=1, source_target_pairs={{0,8},{1,9},{2,10},{3,11},{4,12},{5,13},{6,14},{7,15},{8,0},{9,1},... | collective-permute-start | bytes 442376 | tf_op jit(solution)/shard_map/ppermute | solution.py:565
  29.7 5.3 %collective-permute-start.7 = (bf16[9,2,16,128]{3,2,1,0:T(8,128)(2,1)S(1)}, bf16[9,2,16,128]{3,2,1,0:T(8,128)(2,1)S(1)}, u32[]{:S(2)}, u32[]{:S(2)}) collective-permute-start(bf16[9,2,16,128]{3,2,1,0:T(8,128)(2,1)S(1)} %get-tuple-element.53.refs_2_), channel_id=1, source_target_pairs={{0,8},{1,9},{2,10},{3,11},{4,12},{5,13},{6,14},{7,15},{8,0},{9,1},... | collective-permute-start | bytes 221192 | tf_op jit(solution)/shard_map/ppermute | solution.py:565
  31.3 5.9 %collective-permute-start.5 = (bf16[512,128]{1,0:T(8,128)(2,1)S(1)}, bf16[512,128]{1,0:T(8,128)(2,1)S(1)}, u32[]{:S(2)}, u32[]{:S(2)}) collective-permute-start(bf16[512,128]{1,0:T(8,128)(2,1)S(1)} %get-tuple-element.50.refs_3_), channel_id=1, source_target_pairs={{0,1},{1,0},{2,3},{3,2},{4,6},{5,7},{6,4},{7,5},{8,9},{9,8},{10,11... | collective-permute-start | bytes 393224 | tf_op jit(solution)/shard_map/ppermute | solution.py:565
  32.4 6.9 %collective-permute-start.11 = (bf16[18,1,16,128]{3,2,1,0:T(8,128)(2,1)S(1)}, bf16[18,1,16,128]{3,2,1,0:T(8,128)(2,1)S(1)}, u32[]{:S(2)}, u32[]{:S(2)}) collective-permute-start(bf16[18,1,16,128]{3,2,1,0:T(8,128)(2,1)S(1)} %get-tuple-element.55.refs_2_), channel_id=1, source_target_pairs={{0,16},{1,17},{2,18},{3,19},{4,20},{5,21},{6,22},{7,23},{8,24},{9,... | collective-permute-start | bytes 221192 | tf_op jit(solution)/shard_map/ppermute | solution.py:565
  35.1 4.9 %collective-permute-start.10 = (bf16[9,1,16,128]{3,2,1,0:T(8,128)(2,1)S(1)}, bf16[9,1,16,128]{3,2,1,0:T(8,128)(2,1)S(1)}, u32[]{:S(2)}, u32[]{:S(2)}) collective-permute-start(bf16[9,1,16,128]{3,2,1,0:T(8,128)(2,1)S(1)} %get-tuple-element.56.refs_2_), channel_id=1, source_target_pairs={{0,16},{1,17},{2,18},{3,19},{4,20},{5,21},{6,22},{7,23},{8,24},{9,... | collective-permute-start | bytes 110600 | tf_op jit(solution)/shard_map/ppermute | solution.py:565
  37.3 5.1 %collective-permute-start.9 = (bf16[512,128]{1,0:T(8,128)(2,1)S(1)}, bf16[512,128]{1,0:T(8,128)(2,1)S(1)}, u32[]{:S(2)}, u32[]{:S(2)}) collective-permute-start(bf16[512,128]{1,0:T(8,128)(2,1)S(1)} %get-tuple-element.58.refs_3_), channel_id=1, source_target_pairs={{0,2},{1,3},{2,0},{3,1},{4,5},{5,4},{6,7},{7,6},{8,10},{9,11},{10,... | collective-permute-start | bytes 393224 | tf_op jit(solution)/shard_map/ppermute | solution.py:565
  40.0 6.0 %copy-start.1 = (bf16[3,3,3,128,256]{4,3,2,1,0:T(8,128)(2,1)S(1)}, bf16[3,3,3,128,256]{4,3,2,1,0:T(8,128)(2,1)}, u32[]{:S(2)}) copy-start(bf16[3,3,3,128,256]{4,3,2,1,0:T(8,128)(2,1)} %refs_3_.1) | copy-start | bytes 5308420
  40.0 5.6 %collective-permute-start.12 = (bf16[27,16,128]{2,1,0:T(8,128)(2,1)S(1)}, bf16[27,16,128]{2,1,0:T(8,128)(2,1)S(1)}, u32[]{:S(2)}, u32[]{:S(2)}) collective-permute-start(bf16[27,16,128]{2,1,0:T(8,128)(2,1)S(1)} %shard_map.74.refs_2_.refs_0_), channel_id=1, source_target_pairs={{0,2},{1,3},{2,0},{3,1},{4,5},{5,4},{6,7},{7,6},{8,10},{9,11},{10,... | collective-permute-start | bytes 331784 | tf_op jit(solution)/shard_map/ppermute | solution.py:565
  45.6 5.2 %collective-permute-start.13 = (bf16[36,16,128]{2,1,0:T(8,128)(2,1)S(1)}, bf16[36,16,128]{2,1,0:T(8,128)(2,1)S(1)}, u32[]{:S(2)}, u32[]{:S(2)}) collective-permute-start(bf16[36,16,128]{2,1,0:T(8,128)(2,1)S(1)} %shard_map.76.refs_4_.refs_0_), channel_id=1, source_target_pairs={{0,1},{1,0},{2,3},{3,2},{4,6},{5,7},{6,4},{7,5},{8,9},{9,8},{10,11... | collective-permute-start | bytes 442376 | tf_op jit(solution)/shard_map/ppermute | solution.py:565

commit v10 on v9

--- a/solution.py
+++ b/solution.py
@@ -14,7 +14,7 @@
 DONE = (8, 128)
 PLANE_PARTS = 1
 SPACER = 6 * 10**9
-VMEM_WHOLE = 63 * 1024 * 1024
+VMEM_WHOLE = 60 * 1024 * 1024
 
 
 def call(kernel, out_shape, scratch=(), in_specs=None, limit=VMEM_LIMIT, order=(), inputs=0, flops=1000):

time: 51.9 us -> 50.9 us (0.981)
  starting transfers between devices: 22.9 us -> 25.6 us
  local copies, waits for them, and re-layouts: 2.7 us -> 0.01 us
  waiting for transfers between devices: 14.8 us -> 13.8 us
    unnamed x8 -> x6, local copies, waits for them, and re-layouts: 2.7 us -> 0.01 us
    ppermute x12, starting transfers between devices: 16.7 us -> 19.3 us  [exchange(): return lax.ppermute(value, ('dp', 'space'), pairs)]
    ppermute x12, waiting for transfers between devices: 11.2 us -> 8.99 us  [exchange(): return lax.ppermute(value, ('dp', 'space'), pairs)]
    ppermute x2, waiting for transfers between devices: 3.59 us -> 4.76 us  [neighbour(): lax.ppermute(value, 'space', [(source, source + steps) for source in rang...]
  transfers between devices with their start and end apart: 14 -> 14, of which waited for: 8 -> 10; matrix products, arithmetic and copies ran while one was open for 0% -> 0% of each run, Pallas kernels for 13% -> 13%
where the time goes in v10:
time: 50.9 us; the launch traced here: 50.8 us
  starting transfers between devices  25.6 us (50%)
  waiting for transfers between devices  13.8 us (27%)
  Pallas kernels  10.5 us (21%)
  between operations  0.83 us (2%)
    ppermute x12, starting transfers between devices, exchange(): return lax.ppermute(value, ('dp', 'space'), pairs)  19.3 us
    ppermute x12, waiting for transfers between devices, exchange(): return lax.ppermute(value, ('dp', 'space'), pairs)  8.99 us
    ppermute x2, starting transfers between devices, neighbour(): lax.ppermute(value, 'space', [(source, source + steps) for source in rang...  6.27 us
    ppermute x2, waiting for transfers between devices, neighbour(): lax.ppermute(value, 'space', [(source, source + steps) for source in rang...  4.76 us
    pallas_call x1, Pallas kernels, volume_grad_of(): call(volume_grad_kernel, (jax.ShapeDtypeStruct(shape, BF16), jax.ShapeDty...  2.59 us
    pallas_call x1, Pallas kernels, halo_share(): call(halo_kernel, jax.ShapeDtypeStruct((height * width // 4, co), BF16),...  2.47 us
    pallas_call x1, Pallas kernels, partial_preact(): call(preact_kernel, (jax.ShapeDtypeStruct((planes // 2 * cells, co), F32)...  1.38 us
    pallas_call x2, Pallas kernels, kernel_grad_part(): call(functools.partial(kernel_grad_kernel, early, cores, chips, scale), (...  1.04 us
  transfers between devices with their start and end apart: 14, of which 10 were waited for; matrix products, arithmetic and copies ran while one was open for 0% of the time, Pallas kernels for 13%

profile of v10, /device:TPU:0, one launch (start us, length us, event | category | flops | bytes accessed | tf_op | source)
XLA Modules:
  0.0 50.8 jit_solution(16195729965815760384)
XLA Ops:
  0.6 2.5 %shard_map.59 = bf16[256,256]{1,0:T(8,128)(2,1)} custom-call(bf16[1,4,32,32,128]{4,3,2,1,0:T(8,128)(2,1)} %volume_ref.3, bf16[3,3,3,128,256]{4,3,2,1,0:T(8,128)(2,1)} %refs_3_.1), custom_call_target="tpu_custom_call" | custom-call | flops 1000 | bytes 1000 | tf_op jit(solution)/shard_map/pallas_call | solution.py:123
  3.1 5.0 %collective-permute-start = (bf16[256,256]{1,0:T(8,128)(2,1)}, bf16[256,256]{1,0:T(8,128)(2,1)S(1)}, u32[]{:S(2)}, u32[]{:S(2)}) collective-permute-start(bf16[256,256]{1,0:T(8,128)(2,1)} %shard_map.59), channel_id=1, source_target_pairs={{0,1},{1,2},{2,3},{4,5},{5,6},{6,7},{8,9},{9,10},{10,11},{12,13},{... | collective-permute-start | bytes 393224 | tf_op jit(solution)/shard_map/ppermute | solution.py:585
  8.2 1.4 %shard_map.58 = (f32[512,256]{1,0:T(8,128)S(1)}, bf16[4,16,16,384]{3,2,1,0:T(8,128)(2,1)S(1)}, bf16[4,17,16,384]{3,2,1,0:T(8,128)(2,1)S(1)}) custom-call(bf16[1,4,32,32,128]{4,3,2,1,0:T(8,128)(2,1)S(1)} %copy-done.1, bf16[3,3,3,128,256]{4,3,2,1,0:T(8,128)(2,1)S(1)} %copy-done), custom_call_target="tpu_custom_call" | custom-call | flops 1000 | bytes 1000 | tf_op jit(solution)/shard_map/pallas_call | solution.py:169
  9.5 0.2 shard_map.61
  9.7 0.5 %shard_map.62.other_ref = f32[6,384,256]{2,1,0:T(8,128)S(1)} custom-call(bf16[4,16,16,384]{3,2,1,0:T(8,128)(2,1)S(1)} %get-tuple-element.37.even_ref.refs_0_, bf16[4,17,16,384]{3,2,1,0:T(8,128)(2,1)S(1)} %get-tuple-element.38.odd_ref.refs_1_, bf16[256,256]{1,0:T(8,128)(2,1)S(1)} %get-tuple-element.39.rest_ref.refs_2_.refs_1_), custom_call_target="tpu_custom_call" | custom-call | flops 1000 | bytes 1000 | tf_op jit(solution)/shard_map/pallas_call | solution.py:451
  10.2 0.9 %collective-permute-done.refs_0_ = bf16[256,256]{1,0:T(8,128)(2,1)S(1)} collective-permute-done((bf16[256,256]{1,0:T(8,128)(2,1)}, bf16[256,256]{1,0:T(8,128)(2,1)S(1)}, u32[]{:S(2)}, u32[]{:S(2)}) %collective-permute-start) | collective-permute-done | bytes 131104 | tf_op jit(solution)/shard_map/ppermute | solution.py:585
  11.2 0.2 shard_map.60
  11.4 0.5 %shard_map.63 = (f32[36,4,16,128]{3,2,1,0:T(8,128)S(1)}, bf16[36,4,16,128]{3,2,1,0:T(8,128)(2,1)S(1)}) custom-call(bf16[4,16,16,384]{3,2,1,0:T(8,128)(2,1)S(1)} %get-tuple-element.37.even_ref.refs_0_, bf16[4,17,16,384]{3,2,1,0:T(8,128)(2,1)S(1)} %get-tuple-element.38.odd_ref.refs_1_, bf16[256,256]{1,0:T(8,128)(2,1)S(1)} %get-tuple-element.40.grads_ref.refs_0_, ...), custom_call_target="tpu_custom_call" | custom-call | flops 1000 | bytes 1000 | tf_op jit(solution)/shard_map/pallas_call | solution.py:489
  12.0 1.3 %collective-permute-start.1 = (bf16[256,256]{1,0:T(8,128)(2,1)S(1)}, bf16[256,256]{1,0:T(8,128)(2,1)S(1)}, u32[]{:S(2)}, u32[]{:S(2)}) collective-permute-start(bf16[256,256]{1,0:T(8,128)(2,1)S(1)} %get-tuple-element.40.grads_ref.refs_0_), channel_id=1, source_target_pairs={{1,0},{2,1},{3,2},{5,4},{6,5},{7,6},{9,8},{10,9},{11,10},{13,12},{... | collective-permute-start | bytes 393224 | tf_op jit(solution)/shard_map/ppermute | solution.py:585
  13.3 0.7 %collective-permute-done.2.refs_0_ = bf16[36,4,16,128]{3,2,1,0:T(8,128)(2,1)S(1)} collective-permute-done((bf16[36,4,16,128]{3,2,1,0:T(8,128)(2,1)S(1)}, bf16[36,4,16,128]{3,2,1,0:T(8,128)(2,1)S(1)}, u32[]{:S(2)}, u32[]{:S(2)}) %collective-permute-start.2) | collective-permute-done | bytes 589856 | tf_op jit(solution)/shard_map/ppermute | solution.py:565
  14.1 2.4 %collective-permute-start.4 = (bf16[18,4,16,128]{3,2,1,0:T(8,128)(2,1)S(1)}, bf16[18,4,16,128]{3,2,1,0:T(8,128)(2,1)S(1)}, u32[]{:S(2)}, u32[]{:S(2)}) collective-permute-start(bf16[18,4,16,128]{3,2,1,0:T(8,128)(2,1)S(1)} %get-tuple-element.43.refs_4_), channel_id=1, source_target_pairs={{0,1},{1,0},{2,3},{3,2},{4,6},{5,7},{6,4},{7,5},{8,9},{9,8},{10,11... | collective-permute-start | bytes 884744 | tf_op jit(solution)/shard_map/ppermute | solution.py:565
  16.6 3.8 %collective-permute-done.1.refs_3_.refs_2_ = bf16[256,256]{1,0:T(8,128)(2,1)S(1)} collective-permute-done((bf16[256,256]{1,0:T(8,128)(2,1)S(1)}, bf16[256,256]{1,0:T(8,128)(2,1)S(1)}, u32[]{:S(2)}, u32[]{:S(2)}) %collective-permute-start.1) | collective-permute-done | bytes 131104 | tf_op jit(solution)/shard_map/ppermute | solution.py:585
  20.4 0.5 %shard_map.65 = (f32[18,4,16,128]{3,2,1,0:T(8,128)S(1)}, bf16[18,4,16,128]{3,2,1,0:T(8,128)(2,1)S(1)}) custom-call(bf16[4,16,16,384]{3,2,1,0:T(8,128)(2,1)S(1)} %get-tuple-element.37.even_ref.refs_0_, bf16[4,17,16,384]{3,2,1,0:T(8,128)(2,1)S(1)} %get-tuple-element.38.odd_ref.refs_1_, bf16[256,256]{1,0:T(8,128)(2,1)S(1)} %get-tuple-element.39.rest_ref.refs_2_.refs_1_, ...), custom_call_target="tpu_custom_call" | custom-call | flops 1000 | bytes 1000 | tf_op jit(solution)/shard_map/pallas_call | solution.py:489
  21.0 2.6 %collective-permute-done.4.refs_1_ = bf16[18,4,16,128]{3,2,1,0:T(8,128)(2,1)S(1)} collective-permute-done((bf16[18,4,16,128]{3,2,1,0:T(8,128)(2,1)S(1)}, bf16[18,4,16,128]{3,2,1,0:T(8,128)(2,1)S(1)}, u32[]{:S(2)}, u32[]{:S(2)}) %collective-permute-start.4) | collective-permute-done | bytes 294944 | tf_op jit(solution)/shard_map/ppermute | solution.py:565
  23.6 2.7 %collective-permute-start.6 = (bf16[9,4,16,128]{3,2,1,0:T(8,128)(2,1)S(1)}, bf16[9,4,16,128]{3,2,1,0:T(8,128)(2,1)S(1)}, u32[]{:S(2)}, u32[]{:S(2)}) collective-permute-start(bf16[9,4,16,128]{3,2,1,0:T(8,128)(2,1)S(1)} %get-tuple-element.47.refs_2_), channel_id=1, source_target_pairs={{0,2},{1,3},{2,0},{3,1},{4,5},{5,4},{6,7},{7,6},{8,10},{9,11},{10,... | collective-permute-start | bytes 442376 | tf_op jit(solution)/shard_map/ppermute | solution.py:565
  26.5 1.6 %collective-permute-start.8 = (bf16[18,2,16,128]{3,2,1,0:T(8,128)(2,1)S(1)}, bf16[18,2,16,128]{3,2,1,0:T(8,128)(2,1)S(1)}, u32[]{:S(2)}, u32[]{:S(2)}) collective-permute-start(bf16[18,2,16,128]{3,2,1,0:T(8,128)(2,1)S(1)} %get-tuple-element.48.refs_1_.refs_2_), channel_id=1, source_target_pairs={{0,8},{1,9},{2,10},{3,11},{4,12},{5,13},{6,14},{7,15},{8,0},{9,1},... | collective-permute-start | bytes 442376 | tf_op jit(solution)/shard_map/ppermute | solution.py:565
  28.2 1.3 %collective-permute-done.6.refs_1_ = bf16[9,4,16,128]{3,2,1,0:T(8,128)(2,1)S(1)} collective-permute-done((bf16[9,4,16,128]{3,2,1,0:T(8,128)(2,1)S(1)}, bf16[9,4,16,128]{3,2,1,0:T(8,128)(2,1)S(1)}, u32[]{:S(2)}, u32[]{:S(2)}) %collective-permute-start.6) | collective-permute-done | bytes 147488 | tf_op jit(solution)/shard_map/ppermute | solution.py:565
  29.5 1.6 %collective-permute-start.7 = (bf16[9,2,16,128]{3,2,1,0:T(8,128)(2,1)S(1)}, bf16[9,2,16,128]{3,2,1,0:T(8,128)(2,1)S(1)}, u32[]{:S(2)}, u32[]{:S(2)}) collective-permute-start(bf16[9,2,16,128]{3,2,1,0:T(8,128)(2,1)S(1)} %get-tuple-element.53.refs_2_), channel_id=1, source_target_pairs={{0,8},{1,9},{2,10},{3,11},{4,12},{5,13},{6,14},{7,15},{8,0},{9,1},... | collective-permute-start | bytes 221192 | tf_op jit(solution)/shard_map/ppermute | solution.py:565
  31.2 0.6 %collective-permute-start.5 = (bf16[512,128]{1,0:T(8,128)(2,1)S(1)}, bf16[512,128]{1,0:T(8,128)(2,1)S(1)}, u32[]{:S(2)}, u32[]{:S(2)}) collective-permute-start(bf16[512,128]{1,0:T(8,128)(2,1)S(1)} %get-tuple-element.50.refs_3_), channel_id=1, source_target_pairs={{0,1},{1,0},{2,3},{3,2},{4,6},{5,7},{6,4},{7,5},{8,9},{9,8},{10,11... | collective-permute-start | bytes 393224 | tf_op jit(solution)/shard_map/ppermute | solution.py:565
  31.7 0.4 collective-permute-done.8.refs_1_
  32.2 2.7 %collective-permute-start.11 = (bf16[18,1,16,128]{3,2,1,0:T(8,128)(2,1)S(1)}, bf16[18,1,16,128]{3,2,1,0:T(8,128)(2,1)S(1)}, u32[]{:S(2)}, u32[]{:S(2)}) collective-permute-start(bf16[18,1,16,128]{3,2,1,0:T(8,128)(2,1)S(1)} %get-tuple-element.55.refs_2_), channel_id=1, source_target_pairs={{0,16},{1,17},{2,18},{3,19},{4,20},{5,21},{6,22},{7,23},{8,24},{9,... | collective-permute-start | bytes 221192 | tf_op jit(solution)/shard_map/ppermute | solution.py:565
  34.9 2.4 %collective-permute-start.10 = (bf16[9,1,16,128]{3,2,1,0:T(8,128)(2,1)S(1)}, bf16[9,1,16,128]{3,2,1,0:T(8,128)(2,1)S(1)}, u32[]{:S(2)}, u32[]{:S(2)}) collective-permute-start(bf16[9,1,16,128]{3,2,1,0:T(8,128)(2,1)S(1)} %get-tuple-element.56.refs_2_), channel_id=1, source_target_pairs={{0,16},{1,17},{2,18},{3,19},{4,20},{5,21},{6,22},{7,23},{8,24},{9,... | collective-permute-start | bytes 110600 | tf_op jit(solution)/shard_map/ppermute | solution.py:565
  37.3 1.8 %collective-permute-start.9 = (bf16[512,128]{1,0:T(8,128)(2,1)S(1)}, bf16[512,128]{1,0:T(8,128)(2,1)S(1)}, u32[]{:S(2)}, u32[]{:S(2)}) collective-permute-start(bf16[512,128]{1,0:T(8,128)(2,1)S(1)} %get-tuple-element.58.refs_3_), channel_id=1, source_target_pairs={{0,2},{1,3},{2,0},{3,1},{4,5},{5,4},{6,7},{7,6},{8,10},{9,11},{10,... | collective-permute-start | bytes 393224 | tf_op jit(solution)/shard_map/ppermute | solution.py:565
  39.0 0.7 %collective-permute-done.10.refs_1_ = bf16[9,1,16,128]{3,2,1,0:T(8,128)(2,1)S(1)} collective-permute-done((bf16[9,1,16,128]{3,2,1,0:T(8,128)(2,1)S(1)}, bf16[9,1,16,128]{3,2,1,0:T(8,128)(2,1)S(1)}, u32[]{:S(2)}, u32[]{:S(2)}) %collective-permute-start.10) | collective-permute-done | bytes 36896 | tf_op jit(solution)/shard_map/ppermute | solution.py:565
  39.8 1.7 %collective-permute-start.12 = (bf16[27,16,128]{2,1,0:T(8,128)(2,1)S(1)}, bf16[27,16,128]{2,1,0:T(8,128)(2,1)S(1)}, u32[]{:S(2)}, u32[]{:S(2)}) collective-permute-start(bf16[27,16,128]{2,1,0:T(8,128)(2,1)S(1)} %shard_map.74.refs_2_.refs_0_), channel_id=1, source_target_pairs={{0,2},{1,3},{2,0},{3,1},{4,5},{5,4},{6,7},{7,6},{8,10},{9,11},{10,... | collective-permute-start | bytes 331784 | tf_op jit(solution)/shard_map/ppermute | solution.py:565
  41.5 0.8 %collective-permute-done.9.refs_1_ = bf16[512,128]{1,0:T(8,128)(2,1)S(1)} collective-permute-done((bf16[512,128]{1,0:T(8,128)(2,1)S(1)}, bf16[512,128]{1,0:T(8,128)(2,1)S(1)}, u32[]{:S(2)}, u32[]{:S(2)}) %collective-permute-start.9) | collective-permute-done | bytes 131104 | tf_op jit(solution)/shard_map/ppermute | solution.py:565
  42.3 0.8 %shard_map.75 = (bf16[64,2048]{1,0:T(8,128)(2,1)}, f32[8,128]{1,0:T(8,128)S(1)}) custom-call(bf16[8,64,128]{2,1,0:T(8,128)(2,1)S(1)} %bitcast.10, bf16[512,128]{1,0:T(8,128)(2,1)S(1)} %collective-permute-done.9.refs_1_, bf16[27,16,128]{2,1,0:T(8,128)(2,1)S(1)} %shard_map.74.refs_2_.refs_0_), custom_call_target="tpu_custom_call" | custom-call | flops 1000 | bytes 1000 | tf_op jit(solution)/shard_map/pallas_call | solution.py:231
  43.1 1.6 %collective-permute-done.12.refs_1_ = bf16[27,16,128]{2,1,0:T(8,128)(2,1)S(1)} collective-permute-done((bf16[27,16,128]{2,1,0:T(8,128)(2,1)S(1)}, bf16[27,16,128]{2,1,0:T(8,128)(2,1)S(1)}, u32[]{:S(2)}, u32[]{:S(2)}) %collective-permute-start.12) | collective-permute-done | bytes 110624 | tf_op jit(solution)/shard_map/ppermute | solution.py:565
  44.7 1.7 %collective-permute-start.13 = (bf16[36,16,128]{2,1,0:T(8,128)(2,1)S(1)}, bf16[36,16,128]{2,1,0:T(8,128)(2,1)S(1)}, u32[]{:S(2)}, u32[]{:S(2)}) collective-permute-start(bf16[36,16,128]{2,1,0:T(8,128)(2,1)S(1)} %shard_map.76.refs_4_.refs_0_), channel_id=1, source_target_pairs={{0,1},{1,0},{2,3},{3,2},{4,6},{5,7},{6,4},{7,5},{8,9},{9,8},{10,11... | collective-permute-start | bytes 442376 | tf_op jit(solution)/shard_map/ppermute | solution.py:565
  46.4 2.6 %shard_map.77 = (bf16[4,16,2,32,128]{4,3,2,1,0:T(8,128)(2,1)}, f32[8,128]{1,0:T(8,128)S(1)}) custom-call(bf16[256,256]{1,0:T(8,128)(2,1)S(1)} %get-tuple-element.40.grads_ref.refs_0_, bf16[256,256]{1,0:T(8,128)(2,1)S(1)} %get-tuple-element.39.rest_ref.refs_2_.refs_1_, bf16[256,256]{1,0:T(8,128)(2,1)S(1)} %collective-permute-done.1.refs_3_.refs_2_, ...), custom_call_target="tpu_custom_call" | custom-call | flops 1000 | bytes 1000 | tf_op jit(solution)/shard_map/pallas_call | solution.py:546
  49.0 1.0 %collective-permute-done.13.refs_1_ = bf16[36,16,128]{2,1,0:T(8,128)(2,1)S(1)} collective-permute-done((bf16[36,16,128]{2,1,0:T(8,128)(2,1)S(1)}, bf16[36,16,128]{2,1,0:T(8,128)(2,1)S(1)}, u32[]{:S(2)}, u32[]{:S(2)}) %collective-permute-start.13) | collective-permute-done | bytes 147488 | tf_op jit(solution)/shard_map/ppermute | solution.py:565
  49.9 0.8 %shard_map.78 = f32[27,16,256]{2,1,0:T(8,128)} custom-call(bf16[36,16,128]{2,1,0:T(8,128)(2,1)S(1)} %shard_map.76.refs_4_.refs_0_, bf16[36,16,128]{2,1,0:T(8,128)(2,1)S(1)} %collective-permute-done.13.refs_1_, f32[8,128]{1,0:T(8,128)S(1)} %get-tuple-element.64.refs_2_), custom_call_target="tpu_custom_call" | custom-call | flops 1000 | bytes 1000 | tf_op jit(solution)/shard_map/pallas_call | solution.py:402
  (24 shorter events, 0.8 us)
Async XLA Ops:
  0.6 7.5 %copy-start.1 = (bf16[1,4,32,32,128]{4,3,2,1,0:T(8,128)(2,1)S(1)}, bf16[1,4,32,32,128]{4,3,2,1,0:T(8,128)(2,1)}, u32[]{:S(2)}) copy-start(bf16[1,4,32,32,128]{4,3,2,1,0:T(8,128)(2,1)} %volume_ref.3) | copy-start | bytes 3145732
  0.6 7.5 %copy-start = (bf16[3,3,3,128,256]{4,3,2,1,0:T(8,128)(2,1)S(1)}, bf16[3,3,3,128,256]{4,3,2,1,0:T(8,128)(2,1)}, u32[]{:S(2)}) copy-start(bf16[3,3,3,128,256]{4,3,2,1,0:T(8,128)(2,1)} %refs_3_.1) | copy-start | bytes 5308420
  3.1 6.4 %copy-start.2 = (bf16[1,2,16,16,256]{4,3,2,1,0:T(8,128)(2,1)S(1)}, bf16[1,2,16,16,256]{4,3,2,1,0:T(8,128)(2,1)}, u32[]{:S(2)}) copy-start(bf16[1,2,16,16,256]{4,3,2,1,0:T(8,128)(2,1)} %param.5) | copy-start | bytes 786436
  3.1 8.0 %collective-permute-start = (bf16[256,256]{1,0:T(8,128)(2,1)}, bf16[256,256]{1,0:T(8,128)(2,1)S(1)}, u32[]{:S(2)}, u32[]{:S(2)}) collective-permute-start(bf16[256,256]{1,0:T(8,128)(2,1)} %shard_map.59), channel_id=1, source_target_pairs={{0,1},{1,2},{2,3},{4,5},{5,6},{6,7},{8,9},{9,10},{10,11},{12,13},{... | collective-permute-start | bytes 393224 | tf_op jit(solution)/shard_map/ppermute | solution.py:585
  11.9 2.1 %collective-permute-start.2 = (bf16[36,4,16,128]{3,2,1,0:T(8,128)(2,1)S(1)}, bf16[36,4,16,128]{3,2,1,0:T(8,128)(2,1)S(1)}, u32[]{:S(2)}, u32[]{:S(2)}) collective-permute-start(bf16[36,4,16,128]{3,2,1,0:T(8,128)(2,1)S(1)} %get-tuple-element.42), channel_id=1, source_target_pairs={{0,4},{1,5},{2,6},{3,7},{4,0},{5,1},{6,2},{7,3},{8,12},{9,13},{10,... | collective-permute-start | bytes 1769480 | tf_op jit(solution)/shard_map/ppermute | solution.py:565
  12.0 8.4 %collective-permute-start.1 = (bf16[256,256]{1,0:T(8,128)(2,1)S(1)}, bf16[256,256]{1,0:T(8,128)(2,1)S(1)}, u32[]{:S(2)}, u32[]{:S(2)}) collective-permute-start(bf16[256,256]{1,0:T(8,128)(2,1)S(1)} %get-tuple-element.40.grads_ref.refs_0_), channel_id=1, source_target_pairs={{1,0},{2,1},{3,2},{5,4},{6,5},{7,6},{9,8},{10,9},{11,10},{13,12},{... | collective-permute-start | bytes 393224 | tf_op jit(solution)/shard_map/ppermute | solution.py:585
  14.1 9.4 %collective-permute-start.4 = (bf16[18,4,16,128]{3,2,1,0:T(8,128)(2,1)S(1)}, bf16[18,4,16,128]{3,2,1,0:T(8,128)(2,1)S(1)}, u32[]{:S(2)}, u32[]{:S(2)}) collective-permute-start(bf16[18,4,16,128]{3,2,1,0:T(8,128)(2,1)S(1)} %get-tuple-element.43.refs_4_), channel_id=1, source_target_pairs={{0,1},{1,0},{2,3},{3,2},{4,6},{5,7},{6,4},{7,5},{8,9},{9,8},{10,11... | collective-permute-start | bytes 884744 | tf_op jit(solution)/shard_map/ppermute | solution.py:565
  20.9 5.4 %collective-permute-start.3 = (bf16[18,4,16,128]{3,2,1,0:T(8,128)(2,1)S(1)}, bf16[18,4,16,128]{3,2,1,0:T(8,128)(2,1)S(1)}, u32[]{:S(2)}, u32[]{:S(2)}) collective-permute-start(bf16[18,4,16,128]{3,2,1,0:T(8,128)(2,1)S(1)} %get-tuple-element.45.refs_2_), channel_id=1, source_target_pairs={{0,4},{1,5},{2,6},{3,7},{4,0},{5,1},{6,2},{7,3},{8,12},{9,13},{10,... | collective-permute-start | bytes 884744 | tf_op jit(solution)/shard_map/ppermute | solution.py:565
  23.6 5.8 %collective-permute-start.6 = (bf16[9,4,16,128]{3,2,1,0:T(8,128)(2,1)S(1)}, bf16[9,4,16,128]{3,2,1,0:T(8,128)(2,1)S(1)}, u32[]{:S(2)}, u32[]{:S(2)}) collective-permute-start(bf16[9,4,16,128]{3,2,1,0:T(8,128)(2,1)S(1)} %get-tuple-element.47.refs_2_), channel_id=1, source_target_pairs={{0,2},{1,3},{2,0},{3,1},{4,5},{5,4},{6,7},{7,6},{8,10},{9,11},{10,... | collective-permute-start | bytes 442376 | tf_op jit(solution)/shard_map/ppermute | solution.py:565
  26.5 5.7 %collective-permute-start.8 = (bf16[18,2,16,128]{3,2,1,0:T(8,128)(2,1)S(1)}, bf16[18,2,16,128]{3,2,1,0:T(8,128)(2,1)S(1)}, u32[]{:S(2)}, u32[]{:S(2)}) collective-permute-start(bf16[18,2,16,128]{3,2,1,0:T(8,128)(2,1)S(1)} %get-tuple-element.48.refs_1_.refs_2_), channel_id=1, source_target_pairs={{0,8},{1,9},{2,10},{3,11},{4,12},{5,13},{6,14},{7,15},{8,0},{9,1},... | collective-permute-start | bytes 442376 | tf_op jit(solution)/shard_map/ppermute | solution.py:565
  29.5 5.3 %collective-permute-start.7 = (bf16[9,2,16,128]{3,2,1,0:T(8,128)(2,1)S(1)}, bf16[9,2,16,128]{3,2,1,0:T(8,128)(2,1)S(1)}, u32[]{:S(2)}, u32[]{:S(2)}) collective-permute-start(bf16[9,2,16,128]{3,2,1,0:T(8,128)(2,1)S(1)} %get-tuple-element.53.refs_2_), channel_id=1, source_target_pairs={{0,8},{1,9},{2,10},{3,11},{4,12},{5,13},{6,14},{7,15},{8,0},{9,1},... | collective-permute-start | bytes 221192 | tf_op jit(solution)/shard_map/ppermute | solution.py:565
  31.2 6.1 %collective-permute-start.5 = (bf16[512,128]{1,0:T(8,128)(2,1)S(1)}, bf16[512,128]{1,0:T(8,128)(2,1)S(1)}, u32[]{:S(2)}, u32[]{:S(2)}) collective-permute-start(bf16[512,128]{1,0:T(8,128)(2,1)S(1)} %get-tuple-element.50.refs_3_), channel_id=1, source_target_pairs={{0,1},{1,0},{2,3},{3,2},{4,6},{5,7},{6,4},{7,5},{8,9},{9,8},{10,11... | collective-permute-start | bytes 393224 | tf_op jit(solution)/shard_map/ppermute | solution.py:565
  32.2 6.9 %collective-permute-start.11 = (bf16[18,1,16,128]{3,2,1,0:T(8,128)(2,1)S(1)}, bf16[18,1,16,128]{3,2,1,0:T(8,128)(2,1)S(1)}, u32[]{:S(2)}, u32[]{:S(2)}) collective-permute-start(bf16[18,1,16,128]{3,2,1,0:T(8,128)(2,1)S(1)} %get-tuple-element.55.refs_2_), channel_id=1, source_target_pairs={{0,16},{1,17},{2,18},{3,19},{4,20},{5,21},{6,22},{7,23},{8,24},{9,... | collective-permute-start | bytes 221192 | tf_op jit(solution)/shard_map/ppermute | solution.py:565
  34.9 4.9 %collective-permute-start.10 = (bf16[9,1,16,128]{3,2,1,0:T(8,128)(2,1)S(1)}, bf16[9,1,16,128]{3,2,1,0:T(8,128)(2,1)S(1)}, u32[]{:S(2)}, u32[]{:S(2)}) collective-permute-start(bf16[9,1,16,128]{3,2,1,0:T(8,128)(2,1)S(1)} %get-tuple-element.56.refs_2_), channel_id=1, source_target_pairs={{0,16},{1,17},{2,18},{3,19},{4,20},{5,21},{6,22},{7,23},{8,24},{9,... | collective-permute-start | bytes 110600 | tf_op jit(solution)/shard_map/ppermute | solution.py:565
  37.3 5.0 %collective-permute-start.9 = (bf16[512,128]{1,0:T(8,128)(2,1)S(1)}, bf16[512,128]{1,0:T(8,128)(2,1)S(1)}, u32[]{:S(2)}, u32[]{:S(2)}) collective-permute-start(bf16[512,128]{1,0:T(8,128)(2,1)S(1)} %get-tuple-element.58.refs_3_), channel_id=1, source_target_pairs={{0,2},{1,3},{2,0},{3,1},{4,5},{5,4},{6,7},{7,6},{8,10},{9,11},{10,... | collective-permute-start | bytes 393224 | tf_op jit(solution)/shard_map/ppermute | solution.py:565
  39.8 4.9 %collective-permute-start.12 = (bf16[27,16,128]{2,1,0:T(8,128)(2,1)S(1)}, bf16[27,16,128]{2,1,0:T(8,128)(2,1)S(1)}, u32[]{:S(2)}, u32[]{:S(2)}) collective-permute-start(bf16[27,16,128]{2,1,0:T(8,128)(2,1)S(1)} %shard_map.74.refs_2_.refs_0_), channel_id=1, source_target_pairs={{0,2},{1,3},{2,0},{3,1},{4,5},{5,4},{6,7},{7,6},{8,10},{9,11},{10,... | collective-permute-start | bytes 331784 | tf_op jit(solution)/shard_map/ppermute | solution.py:565
  44.7 5.2 %collective-permute-start.13 = (bf16[36,16,128]{2,1,0:T(8,128)(2,1)S(1)}, bf16[36,16,128]{2,1,0:T(8,128)(2,1)S(1)}, u32[]{:S(2)}, u32[]{:S(2)}) collective-permute-start(bf16[36,16,128]{2,1,0:T(8,128)(2,1)S(1)} %shard_map.76.refs_4_.refs_0_), channel_id=1, source_target_pairs={{0,1},{1,0},{2,3},{3,2},{4,6},{5,7},{6,4},{7,5},{8,9},{9,8},{10,11... | collective-permute-start | bytes 442376 | tf_op jit(solution)/shard_map/ppermute | solution.py:565

commit v11 on v10

--- a/solution.py
+++ b/solution.py
@@ -64,8 +64,8 @@
     return bits
 
 
-def odd_core(cores):
-    return lax.axis_index("dp") % cores == 1 if cores == 2 else False
+def far_first(cores):
+    return lax.axis_index("dp") % cores == 0 if cores == 2 else False
 
 
 def reverse_bits(value, bits):
@@ -73,19 +73,19 @@
 
 
 def staged_place(target, space, cores):
-    return jnp.where(odd_core(cores), target, reverse_bits(target, bits_of(space)))
+    return jnp.where(far_first(cores), target, reverse_bits(target, bits_of(space)))
 
 
 def relative_place(source, space, cores):
     bits = bits_of(space)
     off = source ^ lax.axis_index("space")
-    return jnp.where(odd_core(cores), reverse_bits(off, bits), off)
+    return jnp.where(far_first(cores), reverse_bits(off, bits), off)
 
 
 def relative_group(group, space, cores):
     bits = bits_of(space)
     index = lax.axis_index("space")
-    mine = jnp.where(odd_core(cores), index, reverse_bits(index, bits))
+    mine = jnp.where(far_first(cores), index, reverse_bits(index, bits))
     return group ^ mine
 
 
@@ -244,7 +244,7 @@
         return (lax.axis_index("dp") // cores >> stage) & 1
     bits = bits_of(lax.axis_size("space"))
     index = lax.axis_index("space")
-    return jnp.where(odd_core(cores), (index >> (bits - 1 - stage)) & 1, (index >> stage) & 1)
+    return jnp.where(far_first(cores), (index >> (bits - 1 - stage)) & 1, (index >> stage) & 1)
 
 
 def halves_of(shape, axis):
@@ -569,7 +569,7 @@
     bits = bits_of(lax.axis_size("space"))
 
     def partner(i, j):
-        bit = bits - 1 - stage if cores == 2 and i % 2 == 1 else stage
+        bit = bits - 1 - stage if cores == 2 and i % 2 == 0 else stage
         return i, j ^ (1 << bit)
 
     return exchange(value, partner)

time: 50.9 us -> 50.9 us (level)
  waiting for transfers between devices: 13.8 us -> 11.8 us
  starting transfers between devices: 25.6 us -> 27.5 us
    ppermute x12, starting transfers between devices: 19.3 us -> 21.2 us  [exchange(): return lax.ppermute(value, ('dp', 'space'), pairs)]
    ppermute x2, waiting for transfers between devices: 4.76 us -> 3.56 us  [neighbour(): lax.ppermute(value, 'space', [(source, source + steps) for source in rang...]
    ppermute x12, waiting for transfers between devices: 8.99 us -> 8.27 us  [exchange(): return lax.ppermute(value, ('dp', 'space'), pairs)]
  transfers between devices with their start and end apart: 14 -> 14, of which waited for: 10 -> 11; matrix products, arithmetic and copies ran while one was open for 0% -> 0% of each run, Pallas kernels for 13% -> 13%
where the time goes in v11:
time: 50.9 us; the launch traced here: 50.7 us
  starting transfers between devices  27.5 us (54%)
  waiting for transfers between devices  11.8 us (23%)
  Pallas kernels  10.5 us (21%)
  between operations  0.82 us (2%)
    ppermute x12, starting transfers between devices, exchange(): return lax.ppermute(value, ('dp', 'space'), pairs)  21.2 us
    ppermute x12, waiting for transfers between devices, exchange(): return lax.ppermute(value, ('dp', 'space'), pairs)  8.27 us
    ppermute x2, starting transfers between devices, neighbour(): lax.ppermute(value, 'space', [(source, source + steps) for source in rang...  6.27 us
    ppermute x2, waiting for transfers between devices, neighbour(): lax.ppermute(value, 'space', [(source, source + steps) for source in rang...  3.56 us
    pallas_call x1, Pallas kernels, volume_grad_of(): call(volume_grad_kernel, (jax.ShapeDtypeStruct(shape, BF16), jax.ShapeDty...  2.59 us
    pallas_call x1, Pallas kernels, halo_share(): call(halo_kernel, jax.ShapeDtypeStruct((height * width // 4, co), BF16),...  2.47 us
    pallas_call x1, Pallas kernels, partial_preact(): call(preact_kernel, (jax.ShapeDtypeStruct((planes // 2 * cells, co), F32)...  1.38 us
    pallas_call x2, Pallas kernels, kernel_grad_part(): call(functools.partial(kernel_grad_kernel, early, cores, chips, scale), (...  1.04 us
  transfers between devices with their start and end apart: 14, of which 11 were waited for; matrix products, arithmetic and copies ran while one was open for 0% of the time, Pallas kernels for 13%

profile of v11, /device:TPU:0, one launch (start us, length us, event | category | flops | bytes accessed | tf_op | source)
XLA Modules:
  0.0 50.7 jit_solution(14110399241050561393)
XLA Ops:
  0.6 2.5 %shard_map.59 = bf16[256,256]{1,0:T(8,128)(2,1)} custom-call(bf16[1,4,32,32,128]{4,3,2,1,0:T(8,128)(2,1)} %volume_ref.3, bf16[3,3,3,128,256]{4,3,2,1,0:T(8,128)(2,1)} %refs_3_.1), custom_call_target="tpu_custom_call" | custom-call | flops 1000 | bytes 1000 | tf_op jit(solution)/shard_map/pallas_call | solution.py:123
  3.1 5.0 %collective-permute-start = (bf16[256,256]{1,0:T(8,128)(2,1)}, bf16[256,256]{1,0:T(8,128)(2,1)S(1)}, u32[]{:S(2)}, u32[]{:S(2)}) collective-permute-start(bf16[256,256]{1,0:T(8,128)(2,1)} %shard_map.59), channel_id=1, source_target_pairs={{0,1},{1,2},{2,3},{4,5},{5,6},{6,7},{8,9},{9,10},{10,11},{12,13},{... | collective-permute-start | bytes 393224 | tf_op jit(solution)/shard_map/ppermute | solution.py:585
  8.2 1.4 %shard_map.58 = (f32[512,256]{1,0:T(8,128)S(1)}, bf16[4,16,16,384]{3,2,1,0:T(8,128)(2,1)S(1)}, bf16[4,17,16,384]{3,2,1,0:T(8,128)(2,1)S(1)}) custom-call(bf16[1,4,32,32,128]{4,3,2,1,0:T(8,128)(2,1)S(1)} %copy-done.1, bf16[3,3,3,128,256]{4,3,2,1,0:T(8,128)(2,1)S(1)} %copy-done), custom_call_target="tpu_custom_call" | custom-call | flops 1000 | bytes 1000 | tf_op jit(solution)/shard_map/pallas_call | solution.py:169
  9.7 0.5 %shard_map.62.other_ref = f32[6,384,256]{2,1,0:T(8,128)S(1)} custom-call(bf16[4,16,16,384]{3,2,1,0:T(8,128)(2,1)S(1)} %get-tuple-element.37.even_ref.refs_0_, bf16[4,17,16,384]{3,2,1,0:T(8,128)(2,1)S(1)} %get-tuple-element.38.odd_ref.refs_1_, bf16[256,256]{1,0:T(8,128)(2,1)S(1)} %get-tuple-element.39.rest_ref.refs_2_.refs_1_), custom_call_target="tpu_custom_call" | custom-call | flops 1000 | bytes 1000 | tf_op jit(solution)/shard_map/pallas_call | solution.py:451
  10.2 0.9 %collective-permute-done.refs_0_ = bf16[256,256]{1,0:T(8,128)(2,1)S(1)} collective-permute-done((bf16[256,256]{1,0:T(8,128)(2,1)}, bf16[256,256]{1,0:T(8,128)(2,1)S(1)}, u32[]{:S(2)}, u32[]{:S(2)}) %collective-permute-start) | collective-permute-done | bytes 131104 | tf_op jit(solution)/shard_map/ppermute | solution.py:585
  11.2 0.2 shard_map.60
  11.4 0.5 %shard_map.63 = (f32[36,4,16,128]{3,2,1,0:T(8,128)S(1)}, bf16[36,4,16,128]{3,2,1,0:T(8,128)(2,1)S(1)}) custom-call(bf16[4,16,16,384]{3,2,1,0:T(8,128)(2,1)S(1)} %get-tuple-element.37.even_ref.refs_0_, bf16[4,17,16,384]{3,2,1,0:T(8,128)(2,1)S(1)} %get-tuple-element.38.odd_ref.refs_1_, bf16[256,256]{1,0:T(8,128)(2,1)S(1)} %get-tuple-element.40.grads_ref.refs_0_, ...), custom_call_target="tpu_custom_call" | custom-call | flops 1000 | bytes 1000 | tf_op jit(solution)/shard_map/pallas_call | solution.py:489
  12.0 1.3 %collective-permute-start.1 = (bf16[256,256]{1,0:T(8,128)(2,1)S(1)}, bf16[256,256]{1,0:T(8,128)(2,1)S(1)}, u32[]{:S(2)}, u32[]{:S(2)}) collective-permute-start(bf16[256,256]{1,0:T(8,128)(2,1)S(1)} %get-tuple-element.40.grads_ref.refs_0_), channel_id=1, source_target_pairs={{1,0},{2,1},{3,2},{5,4},{6,5},{7,6},{9,8},{10,9},{11,10},{13,12},{... | collective-permute-start | bytes 393224 | tf_op jit(solution)/shard_map/ppermute | solution.py:585
  13.3 0.7 %collective-permute-done.2.refs_0_ = bf16[36,4,16,128]{3,2,1,0:T(8,128)(2,1)S(1)} collective-permute-done((bf16[36,4,16,128]{3,2,1,0:T(8,128)(2,1)S(1)}, bf16[36,4,16,128]{3,2,1,0:T(8,128)(2,1)S(1)}, u32[]{:S(2)}, u32[]{:S(2)}) %collective-permute-start.2) | collective-permute-done | bytes 589856 | tf_op jit(solution)/shard_map/ppermute | solution.py:565
  14.1 3.8 %collective-permute-start.4 = (bf16[18,4,16,128]{3,2,1,0:T(8,128)(2,1)S(1)}, bf16[18,4,16,128]{3,2,1,0:T(8,128)(2,1)S(1)}, u32[]{:S(2)}, u32[]{:S(2)}) collective-permute-start(bf16[18,4,16,128]{3,2,1,0:T(8,128)(2,1)S(1)} %get-tuple-element.43.refs_4_), channel_id=1, source_target_pairs={{0,2},{1,3},{2,0},{3,1},{4,5},{5,4},{6,7},{7,6},{8,10},{9,11},{10,... | collective-permute-start | bytes 884744 | tf_op jit(solution)/shard_map/ppermute | solution.py:565
  18.0 2.6 %collective-permute-done.1.refs_3_.refs_2_ = bf16[256,256]{1,0:T(8,128)(2,1)S(1)} collective-permute-done((bf16[256,256]{1,0:T(8,128)(2,1)S(1)}, bf16[256,256]{1,0:T(8,128)(2,1)S(1)}, u32[]{:S(2)}, u32[]{:S(2)}) %collective-permute-start.1) | collective-permute-done | bytes 131104 | tf_op jit(solution)/shard_map/ppermute | solution.py:585
  20.6 0.5 %shard_map.65 = (f32[18,4,16,128]{3,2,1,0:T(8,128)S(1)}, bf16[18,4,16,128]{3,2,1,0:T(8,128)(2,1)S(1)}) custom-call(bf16[4,16,16,384]{3,2,1,0:T(8,128)(2,1)S(1)} %get-tuple-element.37.even_ref.refs_0_, bf16[4,17,16,384]{3,2,1,0:T(8,128)(2,1)S(1)} %get-tuple-element.38.odd_ref.refs_1_, bf16[256,256]{1,0:T(8,128)(2,1)S(1)} %get-tuple-element.39.rest_ref.refs_2_.refs_1_, ...), custom_call_target="tpu_custom_call" | custom-call | flops 1000 | bytes 1000 | tf_op jit(solution)/shard_map/pallas_call | solution.py:489
  21.2 1.5 %collective-permute-done.4.refs_1_ = bf16[18,4,16,128]{3,2,1,0:T(8,128)(2,1)S(1)} collective-permute-done((bf16[18,4,16,128]{3,2,1,0:T(8,128)(2,1)S(1)}, bf16[18,4,16,128]{3,2,1,0:T(8,128)(2,1)S(1)}, u32[]{:S(2)}, u32[]{:S(2)}) %collective-permute-start.4) | collective-permute-done | bytes 294944 | tf_op jit(solution)/shard_map/ppermute | solution.py:565
  22.8 3.6 %collective-permute-start.6 = (bf16[9,4,16,128]{3,2,1,0:T(8,128)(2,1)S(1)}, bf16[9,4,16,128]{3,2,1,0:T(8,128)(2,1)S(1)}, u32[]{:S(2)}, u32[]{:S(2)}) collective-permute-start(bf16[9,4,16,128]{3,2,1,0:T(8,128)(2,1)S(1)} %get-tuple-element.47.refs_2_), channel_id=1, source_target_pairs={{0,1},{1,0},{2,3},{3,2},{4,6},{5,7},{6,4},{7,5},{8,9},{9,8},{10,11... | collective-permute-start | bytes 442376 | tf_op jit(solution)/shard_map/ppermute | solution.py:565
  26.4 1.6 %collective-permute-start.8 = (bf16[18,2,16,128]{3,2,1,0:T(8,128)(2,1)S(1)}, bf16[18,2,16,128]{3,2,1,0:T(8,128)(2,1)S(1)}, u32[]{:S(2)}, u32[]{:S(2)}) collective-permute-start(bf16[18,2,16,128]{3,2,1,0:T(8,128)(2,1)S(1)} %get-tuple-element.48.refs_1_.refs_2_), channel_id=1, source_target_pairs={{0,8},{1,9},{2,10},{3,11},{4,12},{5,13},{6,14},{7,15},{8,0},{9,1},... | collective-permute-start | bytes 442376 | tf_op jit(solution)/shard_map/ppermute | solution.py:565
  28.1 1.3 %collective-permute-done.6.refs_1_ = bf16[9,4,16,128]{3,2,1,0:T(8,128)(2,1)S(1)} collective-permute-done((bf16[9,4,16,128]{3,2,1,0:T(8,128)(2,1)S(1)}, bf16[9,4,16,128]{3,2,1,0:T(8,128)(2,1)S(1)}, u32[]{:S(2)}, u32[]{:S(2)}) %collective-permute-start.6) | collective-permute-done | bytes 147488 | tf_op jit(solution)/shard_map/ppermute | solution.py:565
  29.5 1.6 %collective-permute-start.7 = (bf16[9,2,16,128]{3,2,1,0:T(8,128)(2,1)S(1)}, bf16[9,2,16,128]{3,2,1,0:T(8,128)(2,1)S(1)}, u32[]{:S(2)}, u32[]{:S(2)}) collective-permute-start(bf16[9,2,16,128]{3,2,1,0:T(8,128)(2,1)S(1)} %get-tuple-element.53.refs_2_), channel_id=1, source_target_pairs={{0,8},{1,9},{2,10},{3,11},{4,12},{5,13},{6,14},{7,15},{8,0},{9,1},... | collective-permute-start | bytes 221192 | tf_op jit(solution)/shard_map/ppermute | solution.py:565
  31.1 0.5 %collective-permute-start.5 = (bf16[512,128]{1,0:T(8,128)(2,1)S(1)}, bf16[512,128]{1,0:T(8,128)(2,1)S(1)}, u32[]{:S(2)}, u32[]{:S(2)}) collective-permute-start(bf16[512,128]{1,0:T(8,128)(2,1)S(1)} %get-tuple-element.50.refs_3_), channel_id=1, source_target_pairs={{0,2},{1,3},{2,0},{3,1},{4,5},{5,4},{6,7},{7,6},{8,10},{9,11},{10,... | collective-permute-start | bytes 393224 | tf_op jit(solution)/shard_map/ppermute | solution.py:565
  31.7 0.5 collective-permute-done.8.refs_1_
  32.2 2.7 %collective-permute-start.11 = (bf16[18,1,16,128]{3,2,1,0:T(8,128)(2,1)S(1)}, bf16[18,1,16,128]{3,2,1,0:T(8,128)(2,1)S(1)}, u32[]{:S(2)}, u32[]{:S(2)}) collective-permute-start(bf16[18,1,16,128]{3,2,1,0:T(8,128)(2,1)S(1)} %get-tuple-element.55.refs_2_), channel_id=1, source_target_pairs={{0,16},{1,17},{2,18},{3,19},{4,20},{5,21},{6,22},{7,23},{8,24},{9,... | collective-permute-start | bytes 221192 | tf_op jit(solution)/shard_map/ppermute | solution.py:565
  34.9 2.4 %collective-permute-start.10 = (bf16[9,1,16,128]{3,2,1,0:T(8,128)(2,1)S(1)}, bf16[9,1,16,128]{3,2,1,0:T(8,128)(2,1)S(1)}, u32[]{:S(2)}, u32[]{:S(2)}) collective-permute-start(bf16[9,1,16,128]{3,2,1,0:T(8,128)(2,1)S(1)} %get-tuple-element.56.refs_2_), channel_id=1, source_target_pairs={{0,16},{1,17},{2,18},{3,19},{4,20},{5,21},{6,22},{7,23},{8,24},{9,... | collective-permute-start | bytes 110600 | tf_op jit(solution)/shard_map/ppermute | solution.py:565
  37.3 1.4 %collective-permute-start.9 = (bf16[512,128]{1,0:T(8,128)(2,1)S(1)}, bf16[512,128]{1,0:T(8,128)(2,1)S(1)}, u32[]{:S(2)}, u32[]{:S(2)}) collective-permute-start(bf16[512,128]{1,0:T(8,128)(2,1)S(1)} %get-tuple-element.58.refs_3_), channel_id=1, source_target_pairs={{0,1},{1,0},{2,3},{3,2},{4,6},{5,7},{6,4},{7,5},{8,9},{9,8},{10,11... | collective-permute-start | bytes 393224 | tf_op jit(solution)/shard_map/ppermute | solution.py:565
  38.7 0.2 collective-permute-done.11.refs_1_
  38.9 0.9 %collective-permute-done.10.refs_1_ = bf16[9,1,16,128]{3,2,1,0:T(8,128)(2,1)S(1)} collective-permute-done((bf16[9,1,16,128]{3,2,1,0:T(8,128)(2,1)S(1)}, bf16[9,1,16,128]{3,2,1,0:T(8,128)(2,1)S(1)}, u32[]{:S(2)}, u32[]{:S(2)}) %collective-permute-start.10) | collective-permute-done | bytes 36896 | tf_op jit(solution)/shard_map/ppermute | solution.py:565
  39.8 1.9 %collective-permute-start.12 = (bf16[27,16,128]{2,1,0:T(8,128)(2,1)S(1)}, bf16[27,16,128]{2,1,0:T(8,128)(2,1)S(1)}, u32[]{:S(2)}, u32[]{:S(2)}) collective-permute-start(bf16[27,16,128]{2,1,0:T(8,128)(2,1)S(1)} %shard_map.74.refs_2_.refs_0_), channel_id=1, source_target_pairs={{0,1},{1,0},{2,3},{3,2},{4,6},{5,7},{6,4},{7,5},{8,9},{9,8},{10,11... | collective-permute-start | bytes 331784 | tf_op jit(solution)/shard_map/ppermute | solution.py:565
  41.8 0.6 %collective-permute-done.9.refs_1_ = bf16[512,128]{1,0:T(8,128)(2,1)S(1)} collective-permute-done((bf16[512,128]{1,0:T(8,128)(2,1)S(1)}, bf16[512,128]{1,0:T(8,128)(2,1)S(1)}, u32[]{:S(2)}, u32[]{:S(2)}) %collective-permute-start.9) | collective-permute-done | bytes 131104 | tf_op jit(solution)/shard_map/ppermute | solution.py:565
  42.4 0.8 %shard_map.75 = (bf16[64,2048]{1,0:T(8,128)(2,1)}, f32[8,128]{1,0:T(8,128)S(1)}) custom-call(bf16[8,64,128]{2,1,0:T(8,128)(2,1)S(1)} %bitcast.10, bf16[512,128]{1,0:T(8,128)(2,1)S(1)} %collective-permute-done.9.refs_1_, bf16[27,16,128]{2,1,0:T(8,128)(2,1)S(1)} %shard_map.74.refs_2_.refs_0_), custom_call_target="tpu_custom_call" | custom-call | flops 1000 | bytes 1000 | tf_op jit(solution)/shard_map/pallas_call | solution.py:231
  43.2 1.5 %collective-permute-done.12.refs_1_ = bf16[27,16,128]{2,1,0:T(8,128)(2,1)S(1)} collective-permute-done((bf16[27,16,128]{2,1,0:T(8,128)(2,1)S(1)}, bf16[27,16,128]{2,1,0:T(8,128)(2,1)S(1)}, u32[]{:S(2)}, u32[]{:S(2)}) %collective-permute-start.12) | collective-permute-done | bytes 110624 | tf_op jit(solution)/shard_map/ppermute | solution.py:565
  44.7 1.5 %collective-permute-start.13 = (bf16[36,16,128]{2,1,0:T(8,128)(2,1)S(1)}, bf16[36,16,128]{2,1,0:T(8,128)(2,1)S(1)}, u32[]{:S(2)}, u32[]{:S(2)}) collective-permute-start(bf16[36,16,128]{2,1,0:T(8,128)(2,1)S(1)} %shard_map.76.refs_4_.refs_0_), channel_id=1, source_target_pairs={{0,2},{1,3},{2,0},{3,1},{4,5},{5,4},{6,7},{7,6},{8,10},{9,11},{10,... | collective-permute-start | bytes 442376 | tf_op jit(solution)/shard_map/ppermute | solution.py:565
  46.1 2.6 %shard_map.77 = (bf16[4,16,2,32,128]{4,3,2,1,0:T(8,128)(2,1)}, f32[8,128]{1,0:T(8,128)S(1)}) custom-call(bf16[256,256]{1,0:T(8,128)(2,1)S(1)} %get-tuple-element.40.grads_ref.refs_0_, bf16[256,256]{1,0:T(8,128)(2,1)S(1)} %get-tuple-element.39.rest_ref.refs_2_.refs_1_, bf16[256,256]{1,0:T(8,128)(2,1)S(1)} %collective-permute-done.1.refs_3_.refs_2_, ...), custom_call_target="tpu_custom_call" | custom-call | flops 1000 | bytes 1000 | tf_op jit(solution)/shard_map/pallas_call | solution.py:546
  48.7 1.2 %collective-permute-done.13.refs_1_ = bf16[36,16,128]{2,1,0:T(8,128)(2,1)S(1)} collective-permute-done((bf16[36,16,128]{2,1,0:T(8,128)(2,1)S(1)}, bf16[36,16,128]{2,1,0:T(8,128)(2,1)S(1)}, u32[]{:S(2)}, u32[]{:S(2)}) %collective-permute-start.13) | collective-permute-done | bytes 147488 | tf_op jit(solution)/shard_map/ppermute | solution.py:565
  49.9 0.8 %shard_map.78 = f32[27,16,256]{2,1,0:T(8,128)} custom-call(bf16[36,16,128]{2,1,0:T(8,128)(2,1)S(1)} %shard_map.76.refs_4_.refs_0_, bf16[36,16,128]{2,1,0:T(8,128)(2,1)S(1)} %collective-permute-done.13.refs_1_, f32[8,128]{1,0:T(8,128)S(1)} %get-tuple-element.64.refs_2_), custom_call_target="tpu_custom_call" | custom-call | flops 1000 | bytes 1000 | tf_op jit(solution)/shard_map/pallas_call | solution.py:402
  (24 shorter events, 0.9 us)
Async XLA Ops:
  0.6 7.5 %copy-start.1 = (bf16[1,4,32,32,128]{4,3,2,1,0:T(8,128)(2,1)S(1)}, bf16[1,4,32,32,128]{4,3,2,1,0:T(8,128)(2,1)}, u32[]{:S(2)}) copy-start(bf16[1,4,32,32,128]{4,3,2,1,0:T(8,128)(2,1)} %volume_ref.3) | copy-start | bytes 3145732
  0.6 7.5 %copy-start = (bf16[3,3,3,128,256]{4,3,2,1,0:T(8,128)(2,1)S(1)}, bf16[3,3,3,128,256]{4,3,2,1,0:T(8,128)(2,1)}, u32[]{:S(2)}) copy-start(bf16[3,3,3,128,256]{4,3,2,1,0:T(8,128)(2,1)} %refs_3_.1) | copy-start | bytes 5308420
  3.1 6.4 %copy-start.2 = (bf16[1,2,16,16,256]{4,3,2,1,0:T(8,128)(2,1)S(1)}, bf16[1,2,16,16,256]{4,3,2,1,0:T(8,128)(2,1)}, u32[]{:S(2)}) copy-start(bf16[1,2,16,16,256]{4,3,2,1,0:T(8,128)(2,1)} %param.5) | copy-start | bytes 786436
  3.1 8.0 %collective-permute-start = (bf16[256,256]{1,0:T(8,128)(2,1)}, bf16[256,256]{1,0:T(8,128)(2,1)S(1)}, u32[]{:S(2)}, u32[]{:S(2)}) collective-permute-start(bf16[256,256]{1,0:T(8,128)(2,1)} %shard_map.59), channel_id=1, source_target_pairs={{0,1},{1,2},{2,3},{4,5},{5,6},{6,7},{8,9},{9,10},{10,11},{12,13},{... | collective-permute-start | bytes 393224 | tf_op jit(solution)/shard_map/ppermute | solution.py:585
  11.9 2.1 %collective-permute-start.2 = (bf16[36,4,16,128]{3,2,1,0:T(8,128)(2,1)S(1)}, bf16[36,4,16,128]{3,2,1,0:T(8,128)(2,1)S(1)}, u32[]{:S(2)}, u32[]{:S(2)}) collective-permute-start(bf16[36,4,16,128]{3,2,1,0:T(8,128)(2,1)S(1)} %get-tuple-element.42), channel_id=1, source_target_pairs={{0,4},{1,5},{2,6},{3,7},{4,0},{5,1},{6,2},{7,3},{8,12},{9,13},{10,... | collective-permute-start | bytes 1769480 | tf_op jit(solution)/shard_map/ppermute | solution.py:565
  12.0 8.6 %collective-permute-start.1 = (bf16[256,256]{1,0:T(8,128)(2,1)S(1)}, bf16[256,256]{1,0:T(8,128)(2,1)S(1)}, u32[]{:S(2)}, u32[]{:S(2)}) collective-permute-start(bf16[256,256]{1,0:T(8,128)(2,1)S(1)} %get-tuple-element.40.grads_ref.refs_0_), channel_id=1, source_target_pairs={{1,0},{2,1},{3,2},{5,4},{6,5},{7,6},{9,8},{10,9},{11,10},{13,12},{... | collective-permute-start | bytes 393224 | tf_op jit(solution)/shard_map/ppermute | solution.py:585
  14.1 8.5 %collective-permute-start.4 = (bf16[18,4,16,128]{3,2,1,0:T(8,128)(2,1)S(1)}, bf16[18,4,16,128]{3,2,1,0:T(8,128)(2,1)S(1)}, u32[]{:S(2)}, u32[]{:S(2)}) collective-permute-start(bf16[18,4,16,128]{3,2,1,0:T(8,128)(2,1)S(1)} %get-tuple-element.43.refs_4_), channel_id=1, source_target_pairs={{0,2},{1,3},{2,0},{3,1},{4,5},{5,4},{6,7},{7,6},{8,10},{9,11},{10,... | collective-permute-start | bytes 884744 | tf_op jit(solution)/shard_map/ppermute | solution.py:565
  21.1 5.2 %collective-permute-start.3 = (bf16[18,4,16,128]{3,2,1,0:T(8,128)(2,1)S(1)}, bf16[18,4,16,128]{3,2,1,0:T(8,128)(2,1)S(1)}, u32[]{:S(2)}, u32[]{:S(2)}) collective-permute-start(bf16[18,4,16,128]{3,2,1,0:T(8,128)(2,1)S(1)} %get-tuple-element.45.refs_2_), channel_id=1, source_target_pairs={{0,4},{1,5},{2,6},{3,7},{4,0},{5,1},{6,2},{7,3},{8,12},{9,13},{10,... | collective-permute-start | bytes 884744 | tf_op jit(solution)/shard_map/ppermute | solution.py:565
  22.8 6.7 %collective-permute-start.6 = (bf16[9,4,16,128]{3,2,1,0:T(8,128)(2,1)S(1)}, bf16[9,4,16,128]{3,2,1,0:T(8,128)(2,1)S(1)}, u32[]{:S(2)}, u32[]{:S(2)}) collective-permute-start(bf16[9,4,16,128]{3,2,1,0:T(8,128)(2,1)S(1)} %get-tuple-element.47.refs_2_), channel_id=1, source_target_pairs={{0,1},{1,0},{2,3},{3,2},{4,6},{5,7},{6,4},{7,5},{8,9},{9,8},{10,11... | collective-permute-start | bytes 442376 | tf_op jit(solution)/shard_map/ppermute | solution.py:565
  26.4 5.7 %collective-permute-start.8 = (bf16[18,2,16,128]{3,2,1,0:T(8,128)(2,1)S(1)}, bf16[18,2,16,128]{3,2,1,0:T(8,128)(2,1)S(1)}, u32[]{:S(2)}, u32[]{:S(2)}) collective-permute-start(bf16[18,2,16,128]{3,2,1,0:T(8,128)(2,1)S(1)} %get-tuple-element.48.refs_1_.refs_2_), channel_id=1, source_target_pairs={{0,8},{1,9},{2,10},{3,11},{4,12},{5,13},{6,14},{7,15},{8,0},{9,1},... | collective-permute-start | bytes 442376 | tf_op jit(solution)/shard_map/ppermute | solution.py:565
  29.5 5.3 %collective-permute-start.7 = (bf16[9,2,16,128]{3,2,1,0:T(8,128)(2,1)S(1)}, bf16[9,2,16,128]{3,2,1,0:T(8,128)(2,1)S(1)}, u32[]{:S(2)}, u32[]{:S(2)}) collective-permute-start(bf16[9,2,16,128]{3,2,1,0:T(8,128)(2,1)S(1)} %get-tuple-element.53.refs_2_), channel_id=1, source_target_pairs={{0,8},{1,9},{2,10},{3,11},{4,12},{5,13},{6,14},{7,15},{8,0},{9,1},... | collective-permute-start | bytes 221192 | tf_op jit(solution)/shard_map/ppermute | solution.py:565
  31.1 6.2 %collective-permute-start.5 = (bf16[512,128]{1,0:T(8,128)(2,1)S(1)}, bf16[512,128]{1,0:T(8,128)(2,1)S(1)}, u32[]{:S(2)}, u32[]{:S(2)}) collective-permute-start(bf16[512,128]{1,0:T(8,128)(2,1)S(1)} %get-tuple-element.50.refs_3_), channel_id=1, source_target_pairs={{0,2},{1,3},{2,0},{3,1},{4,5},{5,4},{6,7},{7,6},{8,10},{9,11},{10,... | collective-permute-start | bytes 393224 | tf_op jit(solution)/shard_map/ppermute | solution.py:565
  32.2 6.7 %collective-permute-start.11 = (bf16[18,1,16,128]{3,2,1,0:T(8,128)(2,1)S(1)}, bf16[18,1,16,128]{3,2,1,0:T(8,128)(2,1)S(1)}, u32[]{:S(2)}, u32[]{:S(2)}) collective-permute-start(bf16[18,1,16,128]{3,2,1,0:T(8,128)(2,1)S(1)} %get-tuple-element.55.refs_2_), channel_id=1, source_target_pairs={{0,16},{1,17},{2,18},{3,19},{4,20},{5,21},{6,22},{7,23},{8,24},{9,... | collective-permute-start | bytes 221192 | tf_op jit(solution)/shard_map/ppermute | solution.py:565
  34.9 4.9 %collective-permute-start.10 = (bf16[9,1,16,128]{3,2,1,0:T(8,128)(2,1)S(1)}, bf16[9,1,16,128]{3,2,1,0:T(8,128)(2,1)S(1)}, u32[]{:S(2)}, u32[]{:S(2)}) collective-permute-start(bf16[9,1,16,128]{3,2,1,0:T(8,128)(2,1)S(1)} %get-tuple-element.56.refs_2_), channel_id=1, source_target_pairs={{0,16},{1,17},{2,18},{3,19},{4,20},{5,21},{6,22},{7,23},{8,24},{9,... | collective-permute-start | bytes 110600 | tf_op jit(solution)/shard_map/ppermute | solution.py:565
  37.3 5.0 %collective-permute-start.9 = (bf16[512,128]{1,0:T(8,128)(2,1)S(1)}, bf16[512,128]{1,0:T(8,128)(2,1)S(1)}, u32[]{:S(2)}, u32[]{:S(2)}) collective-permute-start(bf16[512,128]{1,0:T(8,128)(2,1)S(1)} %get-tuple-element.58.refs_3_), channel_id=1, source_target_pairs={{0,1},{1,0},{2,3},{3,2},{4,6},{5,7},{6,4},{7,5},{8,9},{9,8},{10,11... | collective-permute-start | bytes 393224 | tf_op jit(solution)/shard_map/ppermute | solution.py:565
  39.8 4.8 %collective-permute-start.12 = (bf16[27,16,128]{2,1,0:T(8,128)(2,1)S(1)}, bf16[27,16,128]{2,1,0:T(8,128)(2,1)S(1)}, u32[]{:S(2)}, u32[]{:S(2)}) collective-permute-start(bf16[27,16,128]{2,1,0:T(8,128)(2,1)S(1)} %shard_map.74.refs_2_.refs_0_), channel_id=1, source_target_pairs={{0,1},{1,0},{2,3},{3,2},{4,6},{5,7},{6,4},{7,5},{8,9},{9,8},{10,11... | collective-permute-start | bytes 331784 | tf_op jit(solution)/shard_map/ppermute | solution.py:565
  44.7 5.2 %collective-permute-start.13 = (bf16[36,16,128]{2,1,0:T(8,128)(2,1)S(1)}, bf16[36,16,128]{2,1,0:T(8,128)(2,1)S(1)}, u32[]{:S(2)}, u32[]{:S(2)}) collective-permute-start(bf16[36,16,128]{2,1,0:T(8,128)(2,1)S(1)} %shard_map.76.refs_4_.refs_0_), channel_id=1, source_target_pairs={{0,2},{1,3},{2,0},{3,1},{4,5},{5,4},{6,7},{7,6},{8,10},{9,11},{10,... | collective-permute-start | bytes 442376 | tf_op jit(solution)/shard_map/ppermute | solution.py:565

commit v12 on v11

--- a/solution.py
+++ b/solution.py
@@ -241,9 +241,11 @@
 
 def side(axis, stage, cores):
     if axis == "chips":
-        return (lax.axis_index("dp") // cores >> stage) & 1
-    bits = bits_of(lax.axis_size("space"))
-    index = lax.axis_index("space")
+        bits = bits_of(lax.axis_size("dp") // cores)
+        index = lax.axis_index("dp") // cores
+    else:
+        bits = bits_of(lax.axis_size("space"))
+        index = lax.axis_index("space")
     return jnp.where(far_first(cores), (index >> (bits - 1 - stage)) & 1, (index >> stage) & 1)
 
 
@@ -456,6 +458,10 @@
 def kernel_grad_kernel(early, cores, chips, scale, even_ref, odd_ref, grads_ref, other_ref, keep_ref, send_ref):
     outs = even_ref.shape[0] // 2
     core = lax.axis_index("dp") % cores
+    mine = far_first(cores)
+    bits = bits_of(chips)
+    places = [jnp.where(mine, reverse_bits(chip, bits), chip) for chip in range(chips)]
+    others = [jnp.where(mine, chip, reverse_bits(chip, bits)) for chip in range(chips)]
     per_row = 3 * (grads_ref.shape[1] // 128)
     kds = (1, 2) if early else (0,)
     for unit in range(len(kds) * 3 * per_row, keep_ref.shape[0]):
@@ -473,8 +479,8 @@
                 product = product + other_ref[base + kh]
 
             def put(unit, chip, keep, send):
-                keep_ref[(base + kh) * per_row + unit, chip] = keep
-                send_ref[(base + kh) * per_row + unit, chip] = send.astype(BF16)
+                keep_ref[(base + kh) * per_row + unit, places[chip]] = keep
+                send_ref[(base + kh) * per_row + unit, others[chip]] = send.astype(BF16)
 
             store_units(product, scale, core, cores, chips, put)
 
@@ -575,8 +581,14 @@
     return exchange(value, partner)
 
 
-def exchange_chips(value, bit, cores):
-    return exchange(value, lambda i, j: (i ^ (cores << bit), j))
+def exchange_chips(value, stage, cores):
+    bits = bits_of(lax.axis_size("dp") // cores)
+
+    def partner(i, j):
+        bit = bits - 1 - stage if cores == 2 and i % 2 == 0 else stage
+        return i ^ (cores << bit), j
+
+    return exchange(value, partner)
 
 
 def neighbour(value, steps):

time: 50.9 us -> 53.3 us (1.047)
  waiting for transfers between devices: 11.8 us -> 14.8 us
    ppermute x12, waiting for transfers between devices: 8.27 us -> 11.2 us  [exchange(): return lax.ppermute(value, ('dp', 'space'), pairs)]
  transfers between devices with their start and end apart: 14 -> 14, of which waited for: 11 -> 11; matrix products, arithmetic and copies ran while one was open for 0% -> 0% of each run, Pallas kernels for 13% -> 12%
where the time goes in v12:
time: 53.3 us; the launch traced here: 53.2 us
  starting transfers between devices  27 us (51%)
  waiting for transfers between devices  14.8 us (28%)
  Pallas kernels  10.5 us (20%)
  between operations  0.83 us (2%)
    ppermute x12, starting transfers between devices, exchange(): return lax.ppermute(value, ('dp', 'space'), pairs)  20.7 us
    ppermute x12, waiting for transfers between devices, exchange(): return lax.ppermute(value, ('dp', 'space'), pairs)  11.2 us
    ppermute x2, starting transfers between devices, neighbour(): lax.ppermute(value, 'space', [(source, source + steps) for source in rang...  6.27 us
    ppermute x2, waiting for transfers between devices, neighbour(): lax.ppermute(value, 'space', [(source, source + steps) for source in rang...  3.56 us
    pallas_call x1, Pallas kernels, volume_grad_of(): call(volume_grad_kernel, (jax.ShapeDtypeStruct(shape, BF16), jax.ShapeDty...  2.59 us
    pallas_call x1, Pallas kernels, halo_share(): call(halo_kernel, jax.ShapeDtypeStruct((height * width // 4, co), BF16),...  2.47 us
    pallas_call x1, Pallas kernels, partial_preact(): call(preact_kernel, (jax.ShapeDtypeStruct((planes // 2 * cells, co), F32)...  1.38 us
  transfers between devices with their start and end apart: 14, of which 11 were waited for; matrix products, arithmetic and copies ran while one was open for 0% of the time, Pallas kernels for 12%

profile of v12, /device:TPU:0, one launch (start us, length us, event | category | flops | bytes accessed | tf_op | source)
XLA Modules:
  0.0 53.2 jit_solution(14898321168142453037)
XLA Ops:
  0.6 2.5 %shard_map.59 = bf16[256,256]{1,0:T(8,128)(2,1)} custom-call(bf16[1,4,32,32,128]{4,3,2,1,0:T(8,128)(2,1)} %volume_ref.3, bf16[3,3,3,128,256]{4,3,2,1,0:T(8,128)(2,1)} %refs_3_.1), custom_call_target="tpu_custom_call" | custom-call | flops 1000 | bytes 1000 | tf_op jit(solution)/shard_map/pallas_call | solution.py:123
  3.1 5.0 %collective-permute-start = (bf16[256,256]{1,0:T(8,128)(2,1)}, bf16[256,256]{1,0:T(8,128)(2,1)S(1)}, u32[]{:S(2)}, u32[]{:S(2)}) collective-permute-start(bf16[256,256]{1,0:T(8,128)(2,1)} %shard_map.59), channel_id=1, source_target_pairs={{0,1},{1,2},{2,3},{4,5},{5,6},{6,7},{8,9},{9,10},{10,11},{12,13},{... | collective-permute-start | bytes 393224 | tf_op jit(solution)/shard_map/ppermute | solution.py:597
  8.2 1.4 %shard_map.58 = (f32[512,256]{1,0:T(8,128)S(1)}, bf16[4,16,16,384]{3,2,1,0:T(8,128)(2,1)S(1)}, bf16[4,17,16,384]{3,2,1,0:T(8,128)(2,1)S(1)}) custom-call(bf16[1,4,32,32,128]{4,3,2,1,0:T(8,128)(2,1)S(1)} %copy-done.1, bf16[3,3,3,128,256]{4,3,2,1,0:T(8,128)(2,1)S(1)} %copy-done), custom_call_target="tpu_custom_call" | custom-call | flops 1000 | bytes 1000 | tf_op jit(solution)/shard_map/pallas_call | solution.py:169
  9.5 0.2 shard_map.61
  9.7 0.5 shard_map.62.other_ref
  10.2 0.9 %collective-permute-done.refs_0_ = bf16[256,256]{1,0:T(8,128)(2,1)S(1)} collective-permute-done((bf16[256,256]{1,0:T(8,128)(2,1)}, bf16[256,256]{1,0:T(8,128)(2,1)S(1)}, u32[]{:S(2)}, u32[]{:S(2)}) %collective-permute-start) | collective-permute-done | bytes 131104 | tf_op jit(solution)/shard_map/ppermute | solution.py:597
  11.2 0.2 shard_map.60
  11.4 0.5 shard_map.63
  12.0 1.3 %collective-permute-start.1 = (bf16[256,256]{1,0:T(8,128)(2,1)S(1)}, bf16[256,256]{1,0:T(8,128)(2,1)S(1)}, u32[]{:S(2)}, u32[]{:S(2)}) collective-permute-start(bf16[256,256]{1,0:T(8,128)(2,1)S(1)} %get-tuple-element.40.grads_ref.refs_0_), channel_id=1, source_target_pairs={{1,0},{2,1},{3,2},{5,4},{6,5},{7,6},{9,8},{10,9},{11,10},{13,12},{... | collective-permute-start | bytes 393224 | tf_op jit(solution)/shard_map/ppermute | solution.py:597
  13.3 0.7 %collective-permute-done.2.refs_0_ = bf16[36,4,16,128]{3,2,1,0:T(8,128)(2,1)S(1)} collective-permute-done((bf16[36,4,16,128]{3,2,1,0:T(8,128)(2,1)S(1)}, bf16[36,4,16,128]{3,2,1,0:T(8,128)(2,1)S(1)}, u32[]{:S(2)}, u32[]{:S(2)}) %collective-permute-start.2) | collective-permute-done | bytes 589856 | tf_op jit(solution)/shard_map/ppermute | solution.py:571
  14.1 3.8 %collective-permute-start.4 = (bf16[18,4,16,128]{3,2,1,0:T(8,128)(2,1)S(1)}, bf16[18,4,16,128]{3,2,1,0:T(8,128)(2,1)S(1)}, u32[]{:S(2)}, u32[]{:S(2)}) collective-permute-start(bf16[18,4,16,128]{3,2,1,0:T(8,128)(2,1)S(1)} %get-tuple-element.43.refs_4_), channel_id=1, source_target_pairs={{0,2},{1,3},{2,0},{3,1},{4,5},{5,4},{6,7},{7,6},{8,10},{9,11},{10,... | collective-permute-start | bytes 884744 | tf_op jit(solution)/shard_map/ppermute | solution.py:571
  18.0 2.6 %collective-permute-done.1.refs_3_.refs_2_ = bf16[256,256]{1,0:T(8,128)(2,1)S(1)} collective-permute-done((bf16[256,256]{1,0:T(8,128)(2,1)S(1)}, bf16[256,256]{1,0:T(8,128)(2,1)S(1)}, u32[]{:S(2)}, u32[]{:S(2)}) %collective-permute-start.1) | collective-permute-done | bytes 131104 | tf_op jit(solution)/shard_map/ppermute | solution.py:597
  20.6 0.5 shard_map.65
  21.2 1.5 %collective-permute-done.4.refs_1_ = bf16[18,4,16,128]{3,2,1,0:T(8,128)(2,1)S(1)} collective-permute-done((bf16[18,4,16,128]{3,2,1,0:T(8,128)(2,1)S(1)}, bf16[18,4,16,128]{3,2,1,0:T(8,128)(2,1)S(1)}, u32[]{:S(2)}, u32[]{:S(2)}) %collective-permute-start.4) | collective-permute-done | bytes 294944 | tf_op jit(solution)/shard_map/ppermute | solution.py:571
  22.8 3.6 %collective-permute-start.6 = (bf16[9,4,16,128]{3,2,1,0:T(8,128)(2,1)S(1)}, bf16[9,4,16,128]{3,2,1,0:T(8,128)(2,1)S(1)}, u32[]{:S(2)}, u32[]{:S(2)}) collective-permute-start(bf16[9,4,16,128]{3,2,1,0:T(8,128)(2,1)S(1)} %get-tuple-element.47.refs_2_), channel_id=1, source_target_pairs={{0,1},{1,0},{2,3},{3,2},{4,6},{5,7},{6,4},{7,5},{8,9},{9,8},{10,11... | collective-permute-start | bytes 442376 | tf_op jit(solution)/shard_map/ppermute | solution.py:571
  26.4 2.7 %collective-permute-start.8 = (bf16[18,2,16,128]{3,2,1,0:T(8,128)(2,1)S(1)}, bf16[18,2,16,128]{3,2,1,0:T(8,128)(2,1)S(1)}, u32[]{:S(2)}, u32[]{:S(2)}) collective-permute-start(bf16[18,2,16,128]{3,2,1,0:T(8,128)(2,1)S(1)} %get-tuple-element.48.refs_1_.refs_2_), channel_id=1, source_target_pairs={{0,16},{1,17},{2,18},{3,19},{4,12},{5,13},{6,14},{7,15},{8,24},{9,... | collective-permute-start | bytes 442376 | tf_op jit(solution)/shard_map/ppermute | solution.py:571
  29.2 0.3 collective-permute-done.6.refs_1_
  29.5 2.7 %collective-permute-start.7 = (bf16[9,2,16,128]{3,2,1,0:T(8,128)(2,1)S(1)}, bf16[9,2,16,128]{3,2,1,0:T(8,128)(2,1)S(1)}, u32[]{:S(2)}, u32[]{:S(2)}) collective-permute-start(bf16[9,2,16,128]{3,2,1,0:T(8,128)(2,1)S(1)} %get-tuple-element.53.refs_2_), channel_id=1, source_target_pairs={{0,16},{1,17},{2,18},{3,19},{4,12},{5,13},{6,14},{7,15},{8,24},{9,... | collective-permute-start | bytes 221192 | tf_op jit(solution)/shard_map/ppermute | solution.py:571
  32.2 0.5 collective-permute-start.5
  32.7 1.4 %collective-permute-done.8.refs_1_ = bf16[18,2,16,128]{3,2,1,0:T(8,128)(2,1)S(1)} collective-permute-done((bf16[18,2,16,128]{3,2,1,0:T(8,128)(2,1)S(1)}, bf16[18,2,16,128]{3,2,1,0:T(8,128)(2,1)S(1)}, u32[]{:S(2)}, u32[]{:S(2)}) %collective-permute-start.8) | collective-permute-done | bytes 147488 | tf_op jit(solution)/shard_map/ppermute | solution.py:571
  34.1 2.5 %collective-permute-start.11 = (bf16[18,1,16,128]{3,2,1,0:T(8,128)(2,1)S(1)}, bf16[18,1,16,128]{3,2,1,0:T(8,128)(2,1)S(1)}, u32[]{:S(2)}, u32[]{:S(2)}) collective-permute-start(bf16[18,1,16,128]{3,2,1,0:T(8,128)(2,1)S(1)} %get-tuple-element.55.refs_2_), channel_id=1, source_target_pairs={{0,8},{1,9},{2,10},{3,11},{4,20},{5,21},{6,22},{7,23},{8,0},{9,1},... | collective-permute-start | bytes 221192 | tf_op jit(solution)/shard_map/ppermute | solution.py:571
  36.6 0.7 %collective-permute-done.7.refs_1_ = bf16[9,2,16,128]{3,2,1,0:T(8,128)(2,1)S(1)} collective-permute-done((bf16[9,2,16,128]{3,2,1,0:T(8,128)(2,1)S(1)}, bf16[9,2,16,128]{3,2,1,0:T(8,128)(2,1)S(1)}, u32[]{:S(2)}, u32[]{:S(2)}) %collective-permute-start.7) | collective-permute-done | bytes 73760 | tf_op jit(solution)/shard_map/ppermute | solution.py:571
  37.3 1.4 %collective-permute-start.10 = (bf16[9,1,16,128]{3,2,1,0:T(8,128)(2,1)S(1)}, bf16[9,1,16,128]{3,2,1,0:T(8,128)(2,1)S(1)}, u32[]{:S(2)}, u32[]{:S(2)}) collective-permute-start(bf16[9,1,16,128]{3,2,1,0:T(8,128)(2,1)S(1)} %get-tuple-element.56.refs_2_), channel_id=1, source_target_pairs={{0,8},{1,9},{2,10},{3,11},{4,20},{5,21},{6,22},{7,23},{8,0},{9,1},... | collective-permute-start | bytes 110600 | tf_op jit(solution)/shard_map/ppermute | solution.py:571
  38.7 1.3 %collective-permute-start.9 = (bf16[512,128]{1,0:T(8,128)(2,1)S(1)}, bf16[512,128]{1,0:T(8,128)(2,1)S(1)}, u32[]{:S(2)}, u32[]{:S(2)}) collective-permute-start(bf16[512,128]{1,0:T(8,128)(2,1)S(1)} %get-tuple-element.58.refs_3_), channel_id=1, source_target_pairs={{0,1},{1,0},{2,3},{3,2},{4,6},{5,7},{6,4},{7,5},{8,9},{9,8},{10,11... | collective-permute-start | bytes 393224 | tf_op jit(solution)/shard_map/ppermute | solution.py:571
  40.1 1.2 %collective-permute-done.10.refs_1_ = bf16[9,1,16,128]{3,2,1,0:T(8,128)(2,1)S(1)} collective-permute-done((bf16[9,1,16,128]{3,2,1,0:T(8,128)(2,1)S(1)}, bf16[9,1,16,128]{3,2,1,0:T(8,128)(2,1)S(1)}, u32[]{:S(2)}, u32[]{:S(2)}) %collective-permute-start.10) | collective-permute-done | bytes 36896 | tf_op jit(solution)/shard_map/ppermute | solution.py:571
  41.4 2.0 %collective-permute-start.12 = (bf16[27,16,128]{2,1,0:T(8,128)(2,1)S(1)}, bf16[27,16,128]{2,1,0:T(8,128)(2,1)S(1)}, u32[]{:S(2)}, u32[]{:S(2)}) collective-permute-start(bf16[27,16,128]{2,1,0:T(8,128)(2,1)S(1)} %shard_map.74.refs_2_.refs_0_), channel_id=1, source_target_pairs={{0,1},{1,0},{2,3},{3,2},{4,6},{5,7},{6,4},{7,5},{8,9},{9,8},{10,11... | collective-permute-start | bytes 331784 | tf_op jit(solution)/shard_map/ppermute | solution.py:571
  43.4 0.4 collective-permute-done.9.refs_1_
  43.8 0.8 %shard_map.75 = (bf16[64,2048]{1,0:T(8,128)(2,1)}, f32[8,128]{1,0:T(8,128)S(1)}) custom-call(bf16[8,64,128]{2,1,0:T(8,128)(2,1)S(1)} %bitcast.10, bf16[512,128]{1,0:T(8,128)(2,1)S(1)} %collective-permute-done.9.refs_1_, bf16[27,16,128]{2,1,0:T(8,128)(2,1)S(1)} %shard_map.74.refs_2_.refs_0_), custom_call_target="tpu_custom_call" | custom-call | flops 1000 | bytes 1000 | tf_op jit(solution)/shard_map/pallas_call | solution.py:231
  44.6 2.5 %collective-permute-done.12.refs_1_ = bf16[27,16,128]{2,1,0:T(8,128)(2,1)S(1)} collective-permute-done((bf16[27,16,128]{2,1,0:T(8,128)(2,1)S(1)}, bf16[27,16,128]{2,1,0:T(8,128)(2,1)S(1)}, u32[]{:S(2)}, u32[]{:S(2)}) %collective-permute-start.12) | collective-permute-done | bytes 110624 | tf_op jit(solution)/shard_map/ppermute | solution.py:571
  47.2 2.6 %shard_map.77 = (bf16[4,16,2,32,128]{4,3,2,1,0:T(8,128)(2,1)}, f32[8,128]{1,0:T(8,128)S(1)}) custom-call(bf16[256,256]{1,0:T(8,128)(2,1)S(1)} %get-tuple-element.40.grads_ref.refs_0_, bf16[256,256]{1,0:T(8,128)(2,1)S(1)} %get-tuple-element.39.rest_ref.refs_2_.refs_1_, bf16[256,256]{1,0:T(8,128)(2,1)S(1)} %collective-permute-done.1.refs_3_.refs_2_, ...), custom_call_target="tpu_custom_call" | custom-call | flops 1000 | bytes 1000 | tf_op jit(solution)/shard_map/pallas_call | solution.py:552
  49.8 2.5 %collective-permute-done.13.refs_1_ = bf16[36,16,128]{2,1,0:T(8,128)(2,1)S(1)} collective-permute-done((bf16[36,16,128]{2,1,0:T(8,128)(2,1)S(1)}, bf16[36,16,128]{2,1,0:T(8,128)(2,1)S(1)}, u32[]{:S(2)}, u32[]{:S(2)}) %collective-permute-start.13) | collective-permute-done | bytes 147488 | tf_op jit(solution)/shard_map/ppermute | solution.py:571
  52.3 0.8 %shard_map.78 = f32[27,16,256]{2,1,0:T(8,128)} custom-call(bf16[36,16,128]{2,1,0:T(8,128)(2,1)S(1)} %shard_map.76.refs_4_.refs_0_, bf16[36,16,128]{2,1,0:T(8,128)(2,1)S(1)} %collective-permute-done.13.refs_1_, f32[8,128]{1,0:T(8,128)S(1)} %get-tuple-element.64.refs_2_), custom_call_target="tpu_custom_call" | custom-call | flops 1000 | bytes 1000 | tf_op jit(solution)/shard_map/pallas_call | solution.py:404
  (24 shorter events, 0.8 us)
Async XLA Ops:
  0.6 7.5 %copy-start.1 = (bf16[1,4,32,32,128]{4,3,2,1,0:T(8,128)(2,1)S(1)}, bf16[1,4,32,32,128]{4,3,2,1,0:T(8,128)(2,1)}, u32[]{:S(2)}) copy-start(bf16[1,4,32,32,128]{4,3,2,1,0:T(8,128)(2,1)} %volume_ref.3) | copy-start | bytes 3145732
  0.6 7.5 %copy-start = (bf16[3,3,3,128,256]{4,3,2,1,0:T(8,128)(2,1)S(1)}, bf16[3,3,3,128,256]{4,3,2,1,0:T(8,128)(2,1)}, u32[]{:S(2)}) copy-start(bf16[3,3,3,128,256]{4,3,2,1,0:T(8,128)(2,1)} %refs_3_.1) | copy-start | bytes 5308420
  3.1 6.4 %copy-start.2 = (bf16[1,2,16,16,256]{4,3,2,1,0:T(8,128)(2,1)S(1)}, bf16[1,2,16,16,256]{4,3,2,1,0:T(8,128)(2,1)}, u32[]{:S(2)}) copy-start(bf16[1,2,16,16,256]{4,3,2,1,0:T(8,128)(2,1)} %param.5) | copy-start | bytes 786436
  3.1 8.0 %collective-permute-start = (bf16[256,256]{1,0:T(8,128)(2,1)}, bf16[256,256]{1,0:T(8,128)(2,1)S(1)}, u32[]{:S(2)}, u32[]{:S(2)}) collective-permute-start(bf16[256,256]{1,0:T(8,128)(2,1)} %shard_map.59), channel_id=1, source_target_pairs={{0,1},{1,2},{2,3},{4,5},{5,6},{6,7},{8,9},{9,10},{10,11},{12,13},{... | collective-permute-start | bytes 393224 | tf_op jit(solution)/shard_map/ppermute | solution.py:597
  11.9 2.1 %collective-permute-start.2 = (bf16[36,4,16,128]{3,2,1,0:T(8,128)(2,1)S(1)}, bf16[36,4,16,128]{3,2,1,0:T(8,128)(2,1)S(1)}, u32[]{:S(2)}, u32[]{:S(2)}) collective-permute-start(bf16[36,4,16,128]{3,2,1,0:T(8,128)(2,1)S(1)} %get-tuple-element.42), channel_id=1, source_target_pairs={{0,4},{1,5},{2,6},{3,7},{4,0},{5,1},{6,2},{7,3},{8,12},{9,13},{10,... | collective-permute-start | bytes 1769480 | tf_op jit(solution)/shard_map/ppermute | solution.py:571
  12.0 8.6 %collective-permute-start.1 = (bf16[256,256]{1,0:T(8,128)(2,1)S(1)}, bf16[256,256]{1,0:T(8,128)(2,1)S(1)}, u32[]{:S(2)}, u32[]{:S(2)}) collective-permute-start(bf16[256,256]{1,0:T(8,128)(2,1)S(1)} %get-tuple-element.40.grads_ref.refs_0_), channel_id=1, source_target_pairs={{1,0},{2,1},{3,2},{5,4},{6,5},{7,6},{9,8},{10,9},{11,10},{13,12},{... | collective-permute-start | bytes 393224 | tf_op jit(solution)/shard_map/ppermute | solution.py:597
  14.1 8.5 %collective-permute-start.4 = (bf16[18,4,16,128]{3,2,1,0:T(8,128)(2,1)S(1)}, bf16[18,4,16,128]{3,2,1,0:T(8,128)(2,1)S(1)}, u32[]{:S(2)}, u32[]{:S(2)}) collective-permute-start(bf16[18,4,16,128]{3,2,1,0:T(8,128)(2,1)S(1)} %get-tuple-element.43.refs_4_), channel_id=1, source_target_pairs={{0,2},{1,3},{2,0},{3,1},{4,5},{5,4},{6,7},{7,6},{8,10},{9,11},{10,... | collective-permute-start | bytes 884744 | tf_op jit(solution)/shard_map/ppermute | solution.py:571
  21.1 5.2 %collective-permute-start.3 = (bf16[18,4,16,128]{3,2,1,0:T(8,128)(2,1)S(1)}, bf16[18,4,16,128]{3,2,1,0:T(8,128)(2,1)S(1)}, u32[]{:S(2)}, u32[]{:S(2)}) collective-permute-start(bf16[18,4,16,128]{3,2,1,0:T(8,128)(2,1)S(1)} %get-tuple-element.45.refs_2_), channel_id=1, source_target_pairs={{0,4},{1,5},{2,6},{3,7},{4,0},{5,1},{6,2},{7,3},{8,12},{9,13},{10,... | collective-permute-start | bytes 884744 | tf_op jit(solution)/shard_map/ppermute | solution.py:571
  22.8 6.7 %collective-permute-start.6 = (bf16[9,4,16,128]{3,2,1,0:T(8,128)(2,1)S(1)}, bf16[9,4,16,128]{3,2,1,0:T(8,128)(2,1)S(1)}, u32[]{:S(2)}, u32[]{:S(2)}) collective-permute-start(bf16[9,4,16,128]{3,2,1,0:T(8,128)(2,1)S(1)} %get-tuple-element.47.refs_2_), channel_id=1, source_target_pairs={{0,1},{1,0},{2,3},{3,2},{4,6},{5,7},{6,4},{7,5},{8,9},{9,8},{10,11... | collective-permute-start | bytes 442376 | tf_op jit(solution)/shard_map/ppermute | solution.py:571
  26.4 7.6 %collective-permute-start.8 = (bf16[18,2,16,128]{3,2,1,0:T(8,128)(2,1)S(1)}, bf16[18,2,16,128]{3,2,1,0:T(8,128)(2,1)S(1)}, u32[]{:S(2)}, u32[]{:S(2)}) collective-permute-start(bf16[18,2,16,128]{3,2,1,0:T(8,128)(2,1)S(1)} %get-tuple-element.48.refs_1_.refs_2_), channel_id=1, source_target_pairs={{0,16},{1,17},{2,18},{3,19},{4,12},{5,13},{6,14},{7,15},{8,24},{9,... | collective-permute-start | bytes 442376 | tf_op jit(solution)/shard_map/ppermute | solution.py:571
  29.5 7.8 %collective-permute-start.7 = (bf16[9,2,16,128]{3,2,1,0:T(8,128)(2,1)S(1)}, bf16[9,2,16,128]{3,2,1,0:T(8,128)(2,1)S(1)}, u32[]{:S(2)}, u32[]{:S(2)}) collective-permute-start(bf16[9,2,16,128]{3,2,1,0:T(8,128)(2,1)S(1)} %get-tuple-element.53.refs_2_), channel_id=1, source_target_pairs={{0,16},{1,17},{2,18},{3,19},{4,12},{5,13},{6,14},{7,15},{8,24},{9,... | collective-permute-start | bytes 221192 | tf_op jit(solution)/shard_map/ppermute | solution.py:571
  32.2 6.6 %collective-permute-start.5 = (bf16[512,128]{1,0:T(8,128)(2,1)S(1)}, bf16[512,128]{1,0:T(8,128)(2,1)S(1)}, u32[]{:S(2)}, u32[]{:S(2)}) collective-permute-start(bf16[512,128]{1,0:T(8,128)(2,1)S(1)} %get-tuple-element.50.refs_3_), channel_id=1, source_target_pairs={{0,2},{1,3},{2,0},{3,1},{4,5},{5,4},{6,7},{7,6},{8,10},{9,11},{10,... | collective-permute-start | bytes 393224 | tf_op jit(solution)/shard_map/ppermute | solution.py:571
  34.1 6.0 %collective-permute-start.11 = (bf16[18,1,16,128]{3,2,1,0:T(8,128)(2,1)S(1)}, bf16[18,1,16,128]{3,2,1,0:T(8,128)(2,1)S(1)}, u32[]{:S(2)}, u32[]{:S(2)}) collective-permute-start(bf16[18,1,16,128]{3,2,1,0:T(8,128)(2,1)S(1)} %get-tuple-element.55.refs_2_), channel_id=1, source_target_pairs={{0,8},{1,9},{2,10},{3,11},{4,20},{5,21},{6,22},{7,23},{8,0},{9,1},... | collective-permute-start | bytes 221192 | tf_op jit(solution)/shard_map/ppermute | solution.py:571
  37.3 4.0 %collective-permute-start.10 = (bf16[9,1,16,128]{3,2,1,0:T(8,128)(2,1)S(1)}, bf16[9,1,16,128]{3,2,1,0:T(8,128)(2,1)S(1)}, u32[]{:S(2)}, u32[]{:S(2)}) collective-permute-start(bf16[9,1,16,128]{3,2,1,0:T(8,128)(2,1)S(1)} %get-tuple-element.56.refs_2_), channel_id=1, source_target_pairs={{0,8},{1,9},{2,10},{3,11},{4,20},{5,21},{6,22},{7,23},{8,0},{9,1},... | collective-permute-start | bytes 110600 | tf_op jit(solution)/shard_map/ppermute | solution.py:571
  38.7 5.0 %collective-permute-start.9 = (bf16[512,128]{1,0:T(8,128)(2,1)S(1)}, bf16[512,128]{1,0:T(8,128)(2,1)S(1)}, u32[]{:S(2)}, u32[]{:S(2)}) collective-permute-start(bf16[512,128]{1,0:T(8,128)(2,1)S(1)} %get-tuple-element.58.refs_3_), channel_id=1, source_target_pairs={{0,1},{1,0},{2,3},{3,2},{4,6},{5,7},{6,4},{7,5},{8,9},{9,8},{10,11... | collective-permute-start | bytes 393224 | tf_op jit(solution)/shard_map/ppermute | solution.py:571
  41.4 5.7 %collective-permute-start.12 = (bf16[27,16,128]{2,1,0:T(8,128)(2,1)S(1)}, bf16[27,16,128]{2,1,0:T(8,128)(2,1)S(1)}, u32[]{:S(2)}, u32[]{:S(2)}) collective-permute-start(bf16[27,16,128]{2,1,0:T(8,128)(2,1)S(1)} %shard_map.74.refs_2_.refs_0_), channel_id=1, source_target_pairs={{0,1},{1,0},{2,3},{3,2},{4,6},{5,7},{6,4},{7,5},{8,9},{9,8},{10,11... | collective-permute-start | bytes 331784 | tf_op jit(solution)/shard_map/ppermute | solution.py:571
  47.1 5.2 %collective-permute-start.13 = (bf16[36,16,128]{2,1,0:T(8,128)(2,1)S(1)}, bf16[36,16,128]{2,1,0:T(8,128)(2,1)S(1)}, u32[]{:S(2)}, u32[]{:S(2)}) collective-permute-start(bf16[36,16,128]{2,1,0:T(8,128)(2,1)S(1)} %shard_map.76.refs_4_.refs_0_), channel_id=1, source_target_pairs={{0,2},{1,3},{2,0},{3,1},{4,5},{5,4},{6,7},{7,6},{8,10},{9,11},{10,... | collective-permute-start | bytes 442376 | tf_op jit(solution)/shard_map/ppermute | solution.py:571

commit v13 on v12

--- a/solution.py
+++ b/solution.py
@@ -66,6 +66,10 @@
 
 def far_first(cores):
     return lax.axis_index("dp") % cores == 0 if cores == 2 else False
+
+
+def side_first(cores):
+    return lax.axis_index("dp") % cores == 1 if cores == 2 else False
 
 
 def reverse_bits(value, bits):
@@ -243,10 +247,12 @@
     if axis == "chips":
         bits = bits_of(lax.axis_size("dp") // cores)
         index = lax.axis_index("dp") // cores
+        top_first = side_first(cores)
     else:
         bits = bits_of(lax.axis_size("space"))
         index = lax.axis_index("space")
-    return jnp.where(far_first(cores), (index >> (bits - 1 - stage)) & 1, (index >> stage) & 1)
+        top_first = far_first(cores)
+    return jnp.where(top_first, (index >> (bits - 1 - stage)) & 1, (index >> stage) & 1)
 
 
 def halves_of(shape, axis):
@@ -458,7 +464,7 @@
 def kernel_grad_kernel(early, cores, chips, scale, even_ref, odd_ref, grads_ref, other_ref, keep_ref, send_ref):
     outs = even_ref.shape[0] // 2
     core = lax.axis_index("dp") % cores
-    mine = far_first(cores)
+    mine = side_first(cores)
     bits = bits_of(chips)
     places = [jnp.where(mine, reverse_bits(chip, bits), chip) for chip in range(chips)]
     others = [jnp.where(mine, chip, reverse_bits(chip, bits)) for chip in range(chips)]
@@ -585,7 +591,7 @@
     bits = bits_of(lax.axis_size("dp") // cores)
 
     def partner(i, j):
-        bit = bits - 1 - stage if cores == 2 and i % 2 == 0 else stage
+        bit = bits - 1 - stage if cores == 2 and i % 2 == 1 else stage
         return i ^ (cores << bit), j
 
     return exchange(value, partner)

time: 53.3 us -> 52.5 us (0.985)
  starting transfers between devices: 27 us -> 25.7 us
    ppermute x12, starting transfers between devices: 20.7 us -> 19.4 us  [exchange(): return lax.ppermute(value, ('dp', 'space'), pairs)]
  transfers between devices with their start and end apart: 14 -> 14, of which waited for: 11 -> 10; matrix products, arithmetic and copies ran while one was open for 0% -> 0% of each run, Pallas kernels for 12% -> 12%
where the time goes in v13:
time: 52.5 us; the launch traced here: 52.3 us
  starting transfers between devices  25.7 us (49%)
  waiting for transfers between devices  15.2 us (29%)
  Pallas kernels  10.5 us (20%)
  between operations  0.83 us (2%)
    ppermute x12, starting transfers between devices, exchange(): return lax.ppermute(value, ('dp', 'space'), pairs)  19.4 us
    ppermute x12, waiting for transfers between devices, exchange(): return lax.ppermute(value, ('dp', 'space'), pairs)  11.6 us
    ppermute x2, starting transfers between devices, neighbour(): lax.ppermute(value, 'space', [(source, source + steps) for source in rang...  6.27 us
    ppermute x2, waiting for transfers between devices, neighbour(): lax.ppermute(value, 'space', [(source, source + steps) for source in rang...  3.56 us
    pallas_call x1, Pallas kernels, volume_grad_of(): call(volume_grad_kernel, (jax.ShapeDtypeStruct(shape, BF16), jax.ShapeDty...  2.59 us
    pallas_call x1, Pallas kernels, halo_share(): call(halo_kernel, jax.ShapeDtypeStruct((height * width // 4, co), BF16),...  2.47 us
    pallas_call x1, Pallas kernels, partial_preact(): call(preact_kernel, (jax.ShapeDtypeStruct((planes // 2 * cells, co), F32)...  1.38 us
  transfers between devices with their start and end apart: 14, of which 10 were waited for; matrix products, arithmetic and copies ran while one was open for 0% of the time, Pallas kernels for 12%

profile of v13, /device:TPU:0, one launch (start us, length us, event | category | flops | bytes accessed | tf_op | source)
XLA Modules:
  0.0 52.3 jit_solution(7255652078919141769)
XLA Ops:
  0.6 2.5 %shard_map.59 = bf16[256,256]{1,0:T(8,128)(2,1)} custom-call(bf16[1,4,32,32,128]{4,3,2,1,0:T(8,128)(2,1)} %volume_ref.3, bf16[3,3,3,128,256]{4,3,2,1,0:T(8,128)(2,1)} %refs_3_.1), custom_call_target="tpu_custom_call" | custom-call | flops 1000 | bytes 1000 | tf_op jit(solution)/shard_map/pallas_call | solution.py:127
  3.1 5.0 %collective-permute-start = (bf16[256,256]{1,0:T(8,128)(2,1)}, bf16[256,256]{1,0:T(8,128)(2,1)S(1)}, u32[]{:S(2)}, u32[]{:S(2)}) collective-permute-start(bf16[256,256]{1,0:T(8,128)(2,1)} %shard_map.59), channel_id=1, source_target_pairs={{0,1},{1,2},{2,3},{4,5},{5,6},{6,7},{8,9},{9,10},{10,11},{12,13},{... | collective-permute-start | bytes 393224 | tf_op jit(solution)/shard_map/ppermute | solution.py:603
  8.2 1.4 %shard_map.58 = (f32[512,256]{1,0:T(8,128)S(1)}, bf16[4,16,16,384]{3,2,1,0:T(8,128)(2,1)S(1)}, bf16[4,17,16,384]{3,2,1,0:T(8,128)(2,1)S(1)}) custom-call(bf16[1,4,32,32,128]{4,3,2,1,0:T(8,128)(2,1)S(1)} %copy-done.1, bf16[3,3,3,128,256]{4,3,2,1,0:T(8,128)(2,1)S(1)} %copy-done), custom_call_target="tpu_custom_call" | custom-call | flops 1000 | bytes 1000 | tf_op jit(solution)/shard_map/pallas_call | solution.py:173
  9.5 0.2 shard_map.61
  9.7 0.5 shard_map.62.other_ref
  10.2 0.9 %collective-permute-done.refs_0_ = bf16[256,256]{1,0:T(8,128)(2,1)S(1)} collective-permute-done((bf16[256,256]{1,0:T(8,128)(2,1)}, bf16[256,256]{1,0:T(8,128)(2,1)S(1)}, u32[]{:S(2)}, u32[]{:S(2)}) %collective-permute-start) | collective-permute-done | bytes 131104 | tf_op jit(solution)/shard_map/ppermute | solution.py:603
  11.2 0.2 shard_map.60
  11.4 0.5 %shard_map.63 = (f32[36,4,16,128]{3,2,1,0:T(8,128)S(1)}, bf16[36,4,16,128]{3,2,1,0:T(8,128)(2,1)S(1)}) custom-call(bf16[4,16,16,384]{3,2,1,0:T(8,128)(2,1)S(1)} %get-tuple-element.37.even_ref.refs_0_, bf16[4,17,16,384]{3,2,1,0:T(8,128)(2,1)S(1)} %get-tuple-element.38.odd_ref.refs_1_, bf16[256,256]{1,0:T(8,128)(2,1)S(1)} %get-tuple-element.40.grads_ref.refs_0_, ...), custom_call_target="tpu_custom_call" | custom-call | flops 1000 | bytes 1000 | tf_op jit(solution)/shard_map/pallas_call | solution.py:501
  12.0 1.3 %collective-permute-start.1 = (bf16[256,256]{1,0:T(8,128)(2,1)S(1)}, bf16[256,256]{1,0:T(8,128)(2,1)S(1)}, u32[]{:S(2)}, u32[]{:S(2)}) collective-permute-start(bf16[256,256]{1,0:T(8,128)(2,1)S(1)} %get-tuple-element.40.grads_ref.refs_0_), channel_id=1, source_target_pairs={{1,0},{2,1},{3,2},{5,4},{6,5},{7,6},{9,8},{10,9},{11,10},{13,12},{... | collective-permute-start | bytes 393224 | tf_op jit(solution)/shard_map/ppermute | solution.py:603
  13.3 0.7 %collective-permute-done.2.refs_0_ = bf16[36,4,16,128]{3,2,1,0:T(8,128)(2,1)S(1)} collective-permute-done((bf16[36,4,16,128]{3,2,1,0:T(8,128)(2,1)S(1)}, bf16[36,4,16,128]{3,2,1,0:T(8,128)(2,1)S(1)}, u32[]{:S(2)}, u32[]{:S(2)}) %collective-permute-start.2) | collective-permute-done | bytes 589856 | tf_op jit(solution)/shard_map/ppermute | solution.py:577
  14.1 3.8 %collective-permute-start.4 = (bf16[18,4,16,128]{3,2,1,0:T(8,128)(2,1)S(1)}, bf16[18,4,16,128]{3,2,1,0:T(8,128)(2,1)S(1)}, u32[]{:S(2)}, u32[]{:S(2)}) collective-permute-start(bf16[18,4,16,128]{3,2,1,0:T(8,128)(2,1)S(1)} %get-tuple-element.43.refs_4_), channel_id=1, source_target_pairs={{0,2},{1,3},{2,0},{3,1},{4,5},{5,4},{6,7},{7,6},{8,10},{9,11},{10,... | collective-permute-start | bytes 884744 | tf_op jit(solution)/shard_map/ppermute | solution.py:577
  18.0 2.6 %collective-permute-done.1.refs_3_.refs_2_ = bf16[256,256]{1,0:T(8,128)(2,1)S(1)} collective-permute-done((bf16[256,256]{1,0:T(8,128)(2,1)S(1)}, bf16[256,256]{1,0:T(8,128)(2,1)S(1)}, u32[]{:S(2)}, u32[]{:S(2)}) %collective-permute-start.1) | collective-permute-done | bytes 131104 | tf_op jit(solution)/shard_map/ppermute | solution.py:603
  20.6 0.5 shard_map.65
  21.2 1.5 %collective-permute-done.4.refs_1_ = bf16[18,4,16,128]{3,2,1,0:T(8,128)(2,1)S(1)} collective-permute-done((bf16[18,4,16,128]{3,2,1,0:T(8,128)(2,1)S(1)}, bf16[18,4,16,128]{3,2,1,0:T(8,128)(2,1)S(1)}, u32[]{:S(2)}, u32[]{:S(2)}) %collective-permute-start.4) | collective-permute-done | bytes 294944 | tf_op jit(solution)/shard_map/ppermute | solution.py:577
  22.8 3.6 %collective-permute-start.6 = (bf16[9,4,16,128]{3,2,1,0:T(8,128)(2,1)S(1)}, bf16[9,4,16,128]{3,2,1,0:T(8,128)(2,1)S(1)}, u32[]{:S(2)}, u32[]{:S(2)}) collective-permute-start(bf16[9,4,16,128]{3,2,1,0:T(8,128)(2,1)S(1)} %get-tuple-element.47.refs_2_), channel_id=1, source_target_pairs={{0,1},{1,0},{2,3},{3,2},{4,6},{5,7},{6,4},{7,5},{8,9},{9,8},{10,11... | collective-permute-start | bytes 442376 | tf_op jit(solution)/shard_map/ppermute | solution.py:577
  26.4 1.6 %collective-permute-start.8 = (bf16[18,2,16,128]{3,2,1,0:T(8,128)(2,1)S(1)}, bf16[18,2,16,128]{3,2,1,0:T(8,128)(2,1)S(1)}, u32[]{:S(2)}, u32[]{:S(2)}) collective-permute-start(bf16[18,2,16,128]{3,2,1,0:T(8,128)(2,1)S(1)} %get-tuple-element.48.refs_1_.refs_2_), channel_id=1, source_target_pairs={{0,8},{1,9},{2,10},{3,11},{4,20},{5,21},{6,22},{7,23},{8,0},{9,1},... | collective-permute-start | bytes 442376 | tf_op jit(solution)/shard_map/ppermute | solution.py:577
  28.1 1.3 %collective-permute-done.6.refs_1_ = bf16[9,4,16,128]{3,2,1,0:T(8,128)(2,1)S(1)} collective-permute-done((bf16[9,4,16,128]{3,2,1,0:T(8,128)(2,1)S(1)}, bf16[9,4,16,128]{3,2,1,0:T(8,128)(2,1)S(1)}, u32[]{:S(2)}, u32[]{:S(2)}) %collective-permute-start.6) | collective-permute-done | bytes 147488 | tf_op jit(solution)/shard_map/ppermute | solution.py:577
  29.5 1.6 %collective-permute-start.7 = (bf16[9,2,16,128]{3,2,1,0:T(8,128)(2,1)S(1)}, bf16[9,2,16,128]{3,2,1,0:T(8,128)(2,1)S(1)}, u32[]{:S(2)}, u32[]{:S(2)}) collective-permute-start(bf16[9,2,16,128]{3,2,1,0:T(8,128)(2,1)S(1)} %get-tuple-element.53.refs_2_), channel_id=1, source_target_pairs={{0,8},{1,9},{2,10},{3,11},{4,20},{5,21},{6,22},{7,23},{8,0},{9,1},... | collective-permute-start | bytes 221192 | tf_op jit(solution)/shard_map/ppermute | solution.py:577
  31.1 0.5 %collective-permute-start.5 = (bf16[512,128]{1,0:T(8,128)(2,1)S(1)}, bf16[512,128]{1,0:T(8,128)(2,1)S(1)}, u32[]{:S(2)}, u32[]{:S(2)}) collective-permute-start(bf16[512,128]{1,0:T(8,128)(2,1)S(1)} %get-tuple-element.50.refs_3_), channel_id=1, source_target_pairs={{0,2},{1,3},{2,0},{3,1},{4,5},{5,4},{6,7},{7,6},{8,10},{9,11},{10,... | collective-permute-start | bytes 393224 | tf_op jit(solution)/shard_map/ppermute | solution.py:577
  31.7 0.6 %collective-permute-done.8.refs_1_ = bf16[18,2,16,128]{3,2,1,0:T(8,128)(2,1)S(1)} collective-permute-done((bf16[18,2,16,128]{3,2,1,0:T(8,128)(2,1)S(1)}, bf16[18,2,16,128]{3,2,1,0:T(8,128)(2,1)S(1)}, u32[]{:S(2)}, u32[]{:S(2)}) %collective-permute-start.8) | collective-permute-done | bytes 147488 | tf_op jit(solution)/shard_map/ppermute | solution.py:577
  32.3 2.6 %collective-permute-start.11 = (bf16[18,1,16,128]{3,2,1,0:T(8,128)(2,1)S(1)}, bf16[18,1,16,128]{3,2,1,0:T(8,128)(2,1)S(1)}, u32[]{:S(2)}, u32[]{:S(2)}) collective-permute-start(bf16[18,1,16,128]{3,2,1,0:T(8,128)(2,1)S(1)} %get-tuple-element.55.refs_2_), channel_id=1, source_target_pairs={{0,16},{1,17},{2,18},{3,19},{4,12},{5,13},{6,14},{7,15},{8,24},{9,... | collective-permute-start | bytes 221192 | tf_op jit(solution)/shard_map/ppermute | solution.py:577
  34.9 1.7 %collective-permute-start.10 = (bf16[9,1,16,128]{3,2,1,0:T(8,128)(2,1)S(1)}, bf16[9,1,16,128]{3,2,1,0:T(8,128)(2,1)S(1)}, u32[]{:S(2)}, u32[]{:S(2)}) collective-permute-start(bf16[9,1,16,128]{3,2,1,0:T(8,128)(2,1)S(1)} %get-tuple-element.56.refs_2_), channel_id=1, source_target_pairs={{0,16},{1,17},{2,18},{3,19},{4,12},{5,13},{6,14},{7,15},{8,24},{9,... | collective-permute-start | bytes 110600 | tf_op jit(solution)/shard_map/ppermute | solution.py:577
  36.6 2.1 %collective-permute-start.9 = (bf16[512,128]{1,0:T(8,128)(2,1)S(1)}, bf16[512,128]{1,0:T(8,128)(2,1)S(1)}, u32[]{:S(2)}, u32[]{:S(2)}) collective-permute-start(bf16[512,128]{1,0:T(8,128)(2,1)S(1)} %get-tuple-element.58.refs_3_), channel_id=1, source_target_pairs={{0,1},{1,0},{2,3},{3,2},{4,6},{5,7},{6,4},{7,5},{8,9},{9,8},{10,11... | collective-permute-start | bytes 393224 | tf_op jit(solution)/shard_map/ppermute | solution.py:577
  38.8 1.4 %collective-permute-done.10.refs_1_ = bf16[9,1,16,128]{3,2,1,0:T(8,128)(2,1)S(1)} collective-permute-done((bf16[9,1,16,128]{3,2,1,0:T(8,128)(2,1)S(1)}, bf16[9,1,16,128]{3,2,1,0:T(8,128)(2,1)S(1)}, u32[]{:S(2)}, u32[]{:S(2)}) %collective-permute-start.10) | collective-permute-done | bytes 36896 | tf_op jit(solution)/shard_map/ppermute | solution.py:577
  40.2 1.0 %collective-permute-start.12 = (bf16[27,16,128]{2,1,0:T(8,128)(2,1)S(1)}, bf16[27,16,128]{2,1,0:T(8,128)(2,1)S(1)}, u32[]{:S(2)}, u32[]{:S(2)}) collective-permute-start(bf16[27,16,128]{2,1,0:T(8,128)(2,1)S(1)} %shard_map.74.refs_2_.refs_0_), channel_id=1, source_target_pairs={{0,1},{1,0},{2,3},{3,2},{4,6},{5,7},{6,4},{7,5},{8,9},{9,8},{10,11... | collective-permute-start | bytes 331784 | tf_op jit(solution)/shard_map/ppermute | solution.py:577
  41.2 0.5 collective-permute-done.9.refs_1_
  41.7 0.8 %shard_map.75 = (bf16[64,2048]{1,0:T(8,128)(2,1)}, f32[8,128]{1,0:T(8,128)S(1)}) custom-call(bf16[8,64,128]{2,1,0:T(8,128)(2,1)S(1)} %bitcast.10, bf16[512,128]{1,0:T(8,128)(2,1)S(1)} %collective-permute-done.9.refs_1_, bf16[27,16,128]{2,1,0:T(8,128)(2,1)S(1)} %shard_map.74.refs_2_.refs_0_), custom_call_target="tpu_custom_call" | custom-call | flops 1000 | bytes 1000 | tf_op jit(solution)/shard_map/pallas_call | solution.py:235
  42.5 3.8 %collective-permute-done.12.refs_1_ = bf16[27,16,128]{2,1,0:T(8,128)(2,1)S(1)} collective-permute-done((bf16[27,16,128]{2,1,0:T(8,128)(2,1)S(1)}, bf16[27,16,128]{2,1,0:T(8,128)(2,1)S(1)}, u32[]{:S(2)}, u32[]{:S(2)}) %collective-permute-start.12) | collective-permute-done | bytes 110624 | tf_op jit(solution)/shard_map/ppermute | solution.py:577
  46.2 0.7 %collective-permute-start.13 = (bf16[36,16,128]{2,1,0:T(8,128)(2,1)S(1)}, bf16[36,16,128]{2,1,0:T(8,128)(2,1)S(1)}, u32[]{:S(2)}, u32[]{:S(2)}) collective-permute-start(bf16[36,16,128]{2,1,0:T(8,128)(2,1)S(1)} %shard_map.76.refs_4_.refs_0_), channel_id=1, source_target_pairs={{0,2},{1,3},{2,0},{3,1},{4,5},{5,4},{6,7},{7,6},{8,10},{9,11},{10,... | collective-permute-start | bytes 442376 | tf_op jit(solution)/shard_map/ppermute | solution.py:577
  46.9 2.6 %shard_map.77 = (bf16[4,16,2,32,128]{4,3,2,1,0:T(8,128)(2,1)}, f32[8,128]{1,0:T(8,128)S(1)}) custom-call(bf16[256,256]{1,0:T(8,128)(2,1)S(1)} %get-tuple-element.40.grads_ref.refs_0_, bf16[256,256]{1,0:T(8,128)(2,1)S(1)} %get-tuple-element.39.rest_ref.refs_2_.refs_1_, bf16[256,256]{1,0:T(8,128)(2,1)S(1)} %collective-permute-done.1.refs_3_.refs_2_, ...), custom_call_target="tpu_custom_call" | custom-call | flops 1000 | bytes 1000 | tf_op jit(solution)/shard_map/pallas_call | solution.py:558
  49.5 1.9 %collective-permute-done.13.refs_1_ = bf16[36,16,128]{2,1,0:T(8,128)(2,1)S(1)} collective-permute-done((bf16[36,16,128]{2,1,0:T(8,128)(2,1)S(1)}, bf16[36,16,128]{2,1,0:T(8,128)(2,1)S(1)}, u32[]{:S(2)}, u32[]{:S(2)}) %collective-permute-start.13) | collective-permute-done | bytes 147488 | tf_op jit(solution)/shard_map/ppermute | solution.py:577
  51.4 0.8 %shard_map.78 = f32[27,16,256]{2,1,0:T(8,128)} custom-call(bf16[36,16,128]{2,1,0:T(8,128)(2,1)S(1)} %shard_map.76.refs_4_.refs_0_, bf16[36,16,128]{2,1,0:T(8,128)(2,1)S(1)} %collective-permute-done.13.refs_1_, f32[8,128]{1,0:T(8,128)S(1)} %get-tuple-element.64.refs_2_), custom_call_target="tpu_custom_call" | custom-call | flops 1000 | bytes 1000 | tf_op jit(solution)/shard_map/pallas_call | solution.py:410
  (24 shorter events, 0.8 us)
Async XLA Ops:
  0.6 7.5 %copy-start.1 = (bf16[1,4,32,32,128]{4,3,2,1,0:T(8,128)(2,1)S(1)}, bf16[1,4,32,32,128]{4,3,2,1,0:T(8,128)(2,1)}, u32[]{:S(2)}) copy-start(bf16[1,4,32,32,128]{4,3,2,1,0:T(8,128)(2,1)} %volume_ref.3) | copy-start | bytes 3145732
  0.6 7.5 %copy-start = (bf16[3,3,3,128,256]{4,3,2,1,0:T(8,128)(2,1)S(1)}, bf16[3,3,3,128,256]{4,3,2,1,0:T(8,128)(2,1)}, u32[]{:S(2)}) copy-start(bf16[3,3,3,128,256]{4,3,2,1,0:T(8,128)(2,1)} %refs_3_.1) | copy-start | bytes 5308420
  3.1 6.4 %copy-start.2 = (bf16[1,2,16,16,256]{4,3,2,1,0:T(8,128)(2,1)S(1)}, bf16[1,2,16,16,256]{4,3,2,1,0:T(8,128)(2,1)}, u32[]{:S(2)}) copy-start(bf16[1,2,16,16,256]{4,3,2,1,0:T(8,128)(2,1)} %param.5) | copy-start | bytes 786436
  3.1 8.0 %collective-permute-start = (bf16[256,256]{1,0:T(8,128)(2,1)}, bf16[256,256]{1,0:T(8,128)(2,1)S(1)}, u32[]{:S(2)}, u32[]{:S(2)}) collective-permute-start(bf16[256,256]{1,0:T(8,128)(2,1)} %shard_map.59), channel_id=1, source_target_pairs={{0,1},{1,2},{2,3},{4,5},{5,6},{6,7},{8,9},{9,10},{10,11},{12,13},{... | collective-permute-start | bytes 393224 | tf_op jit(solution)/shard_map/ppermute | solution.py:603
  11.9 2.1 %collective-permute-start.2 = (bf16[36,4,16,128]{3,2,1,0:T(8,128)(2,1)S(1)}, bf16[36,4,16,128]{3,2,1,0:T(8,128)(2,1)S(1)}, u32[]{:S(2)}, u32[]{:S(2)}) collective-permute-start(bf16[36,4,16,128]{3,2,1,0:T(8,128)(2,1)S(1)} %get-tuple-element.42), channel_id=1, source_target_pairs={{0,4},{1,5},{2,6},{3,7},{4,0},{5,1},{6,2},{7,3},{8,12},{9,13},{10,... | collective-permute-start | bytes 1769480 | tf_op jit(solution)/shard_map/ppermute | solution.py:577
  12.0 8.6 %collective-permute-start.1 = (bf16[256,256]{1,0:T(8,128)(2,1)S(1)}, bf16[256,256]{1,0:T(8,128)(2,1)S(1)}, u32[]{:S(2)}, u32[]{:S(2)}) collective-permute-start(bf16[256,256]{1,0:T(8,128)(2,1)S(1)} %get-tuple-element.40.grads_ref.refs_0_), channel_id=1, source_target_pairs={{1,0},{2,1},{3,2},{5,4},{6,5},{7,6},{9,8},{10,9},{11,10},{13,12},{... | collective-permute-start | bytes 393224 | tf_op jit(solution)/shard_map/ppermute | solution.py:603
  14.1 8.5 %collective-permute-start.4 = (bf16[18,4,16,128]{3,2,1,0:T(8,128)(2,1)S(1)}, bf16[18,4,16,128]{3,2,1,0:T(8,128)(2,1)S(1)}, u32[]{:S(2)}, u32[]{:S(2)}) collective-permute-start(bf16[18,4,16,128]{3,2,1,0:T(8,128)(2,1)S(1)} %get-tuple-element.43.refs_4_), channel_id=1, source_target_pairs={{0,2},{1,3},{2,0},{3,1},{4,5},{5,4},{6,7},{7,6},{8,10},{9,11},{10,... | collective-permute-start | bytes 884744 | tf_op jit(solution)/shard_map/ppermute | solution.py:577
  21.1 5.2 %collective-permute-start.3 = (bf16[18,4,16,128]{3,2,1,0:T(8,128)(2,1)S(1)}, bf16[18,4,16,128]{3,2,1,0:T(8,128)(2,1)S(1)}, u32[]{:S(2)}, u32[]{:S(2)}) collective-permute-start(bf16[18,4,16,128]{3,2,1,0:T(8,128)(2,1)S(1)} %get-tuple-element.45.refs_2_), channel_id=1, source_target_pairs={{0,4},{1,5},{2,6},{3,7},{4,0},{5,1},{6,2},{7,3},{8,12},{9,13},{10,... | collective-permute-start | bytes 884744 | tf_op jit(solution)/shard_map/ppermute | solution.py:577
  22.8 6.7 %collective-permute-start.6 = (bf16[9,4,16,128]{3,2,1,0:T(8,128)(2,1)S(1)}, bf16[9,4,16,128]{3,2,1,0:T(8,128)(2,1)S(1)}, u32[]{:S(2)}, u32[]{:S(2)}) collective-permute-start(bf16[9,4,16,128]{3,2,1,0:T(8,128)(2,1)S(1)} %get-tuple-element.47.refs_2_), channel_id=1, source_target_pairs={{0,1},{1,0},{2,3},{3,2},{4,6},{5,7},{6,4},{7,5},{8,9},{9,8},{10,11... | collective-permute-start | bytes 442376 | tf_op jit(solution)/shard_map/ppermute | solution.py:577
  26.4 5.8 %collective-permute-start.8 = (bf16[18,2,16,128]{3,2,1,0:T(8,128)(2,1)S(1)}, bf16[18,2,16,128]{3,2,1,0:T(8,128)(2,1)S(1)}, u32[]{:S(2)}, u32[]{:S(2)}) collective-permute-start(bf16[18,2,16,128]{3,2,1,0:T(8,128)(2,1)S(1)} %get-tuple-element.48.refs_1_.refs_2_), channel_id=1, source_target_pairs={{0,8},{1,9},{2,10},{3,11},{4,20},{5,21},{6,22},{7,23},{8,0},{9,1},... | collective-permute-start | bytes 442376 | tf_op jit(solution)/shard_map/ppermute | solution.py:577
  29.5 5.4 %collective-permute-start.7 = (bf16[9,2,16,128]{3,2,1,0:T(8,128)(2,1)S(1)}, bf16[9,2,16,128]{3,2,1,0:T(8,128)(2,1)S(1)}, u32[]{:S(2)}, u32[]{:S(2)}) collective-permute-start(bf16[9,2,16,128]{3,2,1,0:T(8,128)(2,1)S(1)} %get-tuple-element.53.refs_2_), channel_id=1, source_target_pairs={{0,8},{1,9},{2,10},{3,11},{4,20},{5,21},{6,22},{7,23},{8,0},{9,1},... | collective-permute-start | bytes 221192 | tf_op jit(solution)/shard_map/ppermute | solution.py:577
  31.1 5.5 %collective-permute-start.5 = (bf16[512,128]{1,0:T(8,128)(2,1)S(1)}, bf16[512,128]{1,0:T(8,128)(2,1)S(1)}, u32[]{:S(2)}, u32[]{:S(2)}) collective-permute-start(bf16[512,128]{1,0:T(8,128)(2,1)S(1)} %get-tuple-element.50.refs_3_), channel_id=1, source_target_pairs={{0,2},{1,3},{2,0},{3,1},{4,5},{5,4},{6,7},{7,6},{8,10},{9,11},{10,... | collective-permute-start | bytes 393224 | tf_op jit(solution)/shard_map/ppermute | solution.py:577
  32.3 6.4 %collective-permute-start.11 = (bf16[18,1,16,128]{3,2,1,0:T(8,128)(2,1)S(1)}, bf16[18,1,16,128]{3,2,1,0:T(8,128)(2,1)S(1)}, u32[]{:S(2)}, u32[]{:S(2)}) collective-permute-start(bf16[18,1,16,128]{3,2,1,0:T(8,128)(2,1)S(1)} %get-tuple-element.55.refs_2_), channel_id=1, source_target_pairs={{0,16},{1,17},{2,18},{3,19},{4,12},{5,13},{6,14},{7,15},{8,24},{9,... | collective-permute-start | bytes 221192 | tf_op jit(solution)/shard_map/ppermute | solution.py:577
  34.9 5.3 %collective-permute-start.10 = (bf16[9,1,16,128]{3,2,1,0:T(8,128)(2,1)S(1)}, bf16[9,1,16,128]{3,2,1,0:T(8,128)(2,1)S(1)}, u32[]{:S(2)}, u32[]{:S(2)}) collective-permute-start(bf16[9,1,16,128]{3,2,1,0:T(8,128)(2,1)S(1)} %get-tuple-element.56.refs_2_), channel_id=1, source_target_pairs={{0,16},{1,17},{2,18},{3,19},{4,12},{5,13},{6,14},{7,15},{8,24},{9,... | collective-permute-start | bytes 110600 | tf_op jit(solution)/shard_map/ppermute | solution.py:577
  36.6 5.0 %collective-permute-start.9 = (bf16[512,128]{1,0:T(8,128)(2,1)S(1)}, bf16[512,128]{1,0:T(8,128)(2,1)S(1)}, u32[]{:S(2)}, u32[]{:S(2)}) collective-permute-start(bf16[512,128]{1,0:T(8,128)(2,1)S(1)} %get-tuple-element.58.refs_3_), channel_id=1, source_target_pairs={{0,1},{1,0},{2,3},{3,2},{4,6},{5,7},{6,4},{7,5},{8,9},{9,8},{10,11... | collective-permute-start | bytes 393224 | tf_op jit(solution)/shard_map/ppermute | solution.py:577
  40.2 6.0 %collective-permute-start.12 = (bf16[27,16,128]{2,1,0:T(8,128)(2,1)S(1)}, bf16[27,16,128]{2,1,0:T(8,128)(2,1)S(1)}, u32[]{:S(2)}, u32[]{:S(2)}) collective-permute-start(bf16[27,16,128]{2,1,0:T(8,128)(2,1)S(1)} %shard_map.74.refs_2_.refs_0_), channel_id=1, source_target_pairs={{0,1},{1,0},{2,3},{3,2},{4,6},{5,7},{6,4},{7,5},{8,9},{9,8},{10,11... | collective-permute-start | bytes 331784 | tf_op jit(solution)/shard_map/ppermute | solution.py:577
  46.2 5.2 %collective-permute-start.13 = (bf16[36,16,128]{2,1,0:T(8,128)(2,1)S(1)}, bf16[36,16,128]{2,1,0:T(8,128)(2,1)S(1)}, u32[]{:S(2)}, u32[]{:S(2)}) collective-permute-start(bf16[36,16,128]{2,1,0:T(8,128)(2,1)S(1)} %shard_map.76.refs_4_.refs_0_), channel_id=1, source_target_pairs={{0,2},{1,3},{2,0},{3,1},{4,5},{5,4},{6,7},{7,6},{8,10},{9,11},{10,... | collective-permute-start | bytes 442376 | tf_op jit(solution)/shard_map/ppermute | solution.py:577
